TPU v7x, 32 devices: a whole 2x2x4 slice. The times are simulated.
32 devices in a mesh: dom: 4 (over z), sub: 8 (over y, x, core).
Axes of the slice: x: 2, y: 2, z: 4, core: 2. Of those that a mesh axis runs over, the one named last changes fastest.
Arguments:
- positions: float32 [3, 16, 64, 128], P(None, 'dom', 'sub'), may hold values from 0 to 1
- velocities: float32 [3, 16, 64, 128], P(None, 'dom', 'sub'), may hold values from -6 to 6
- masses: float32 [16, 64, 128], P('dom', 'sub'), may hold values from 0.0004 to 0.004
- smoothing: float32 [16, 64, 128], P('dom', 'sub'), may hold values from 0.3 to 0.6
- neighbours: int32 [16, 64, 5], P('dom', 'sub'), may hold values from 0 to 8, as said below
- particle_group: int32 [16, 64, 128], P('dom', 'sub'), may hold values from 0 to 1023, as said below
- group_row: int32 [1024], replicated, may hold values from 0 to 1023, as said below
Outputs:
- density: float32 [16, 64, 128], P('dom', 'sub')
- catalog: float32 [17, 1024], P(None, 'sub')
Inputs may be any that keep to these rules, and one draw needn't show every extreme that they name: `neighbours`: each block lists 5 different codes of 0 to 8, the first one 4, the block itself. `particle_group`: a group g is owned by index group_row[g] // 128 of sub; at most 2048 of one device's particles belong to groups of any one owner, and on every device some owner gets exactly 2048 of them. `group_row`: a permutation of the catalog rows.
All inputs are finite; a program needn't handle non-finite values.
Results may differ from a plain program's by a relative error of at most 0.0003.
Values sent between devices are 32-bit elements; how exact they have to be, the bound alone decides.
No kernel may reach another device: no remote copies, remote signals or barrier semaphores. Data moves between devices by JAX's collectives and lax.ppermute only.
A program may use at most 64 MiB of HBM per device.

v0:
```python
import functools
import math

import jax
import jax.numpy as jnp
from jax import lax
from jax.experimental import pallas as pl
from jax.experimental.pallas import tpu as pltpu
from jax.sharding import PartitionSpec as P

F32 = jnp.float32
BF16 = jnp.bfloat16
LANES = 128
EARLY = 16
DENSITY_FACTOR = 21.0 / (16.0 * math.pi) / 256.0
VMEM = pl.BlockSpec(memory_space=pltpu.VMEM)
SMEM = pl.BlockSpec(memory_space=pltpu.SMEM)
NT = (((1,), (1,)), ((), ()))


def params():
    return pltpu.CompilerParams(vmem_limit_bytes=40 * 1024 * 1024)


def rounded(value):
    return value.astype(BF16).astype(F32)


def three_parts(value):
    first = rounded(value)
    rest = value - first
    second = rounded(rest)
    return first, second, rest - second


def spread(numbers, y, count):
    row = jnp.broadcast_to(numbers[y : y + 1, :].astype(F32), (16, LANES)).astype(BF16)
    return jnp.concatenate([row] * (count // 16), axis=0)


def row_numbers(count):
    return lax.broadcasted_iota(jnp.int32, (count, LANES), 0).astype(F32).astype(BF16)


def slot_one_hot(slots, y):
    return jnp.where(
        row_numbers(LANES) == spread(slots, y, LANES), jnp.ones((), BF16), jnp.zeros((), BF16)
    )


def moment_pieces(
    nx_total, ny_total, pos_ref, vel_ref, mass_ref, group_ref, row_ref,
    table_ref, rows_ref, hot_ref, feat_ref, lhs_ref, total_ref,
):
    blocks_x, blocks_y, _ = mass_ref.shape
    owners = table_ref.shape[0]
    table_rows = row_ref.shape[0]
    base_x = (lax.axis_index("dom") * blocks_x).astype(F32)
    base_y = ((2 * lax.axis_index("chip") + lax.axis_index("core")) * blocks_y).astype(F32)
    y_iota = lax.broadcasted_iota(jnp.int32, (blocks_y, LANES), 0).astype(F32)

    def features_of(x):
        group = group_ref[x]
        low = group & (LANES - 1)
        high = group >> 7
        rows = jnp.zeros_like(group)
        for r in range(table_rows):
            line = jnp.broadcast_to(row_ref[r : r + 1, :], group.shape)
            picked = jnp.take_along_axis(line, low, axis=1)
            rows = jnp.where(high == r, picked, rows)
        rows_ref[x] = rows
        mass = mass_ref[x]
        gx = (base_x + float(x) + pos_ref[0, x]) / float(nx_total)
        gy = (base_y + y_iota + pos_ref[1, x]) / float(ny_total)
        gz = pos_ref[2, x]
        vx, vy, vz = vel_ref[0, x], vel_ref[1, x], vel_ref[2, x]
        mx, my, mz = mass * gx, mass * gy, mass * gz
        features = (
            mass, mx, my, mz, mass * vx, mass * vy, mass * vz,
            mass * (gy * vz - gz * vy), mass * (gz * vx - gx * vz), mass * (gx * vy - gy * vx),
            mx * gx, my * gy, mz * gz, mx * gy, mx * gz, my * gz,
        )
        for f, feature in enumerate(features):
            start = (x * EARLY + f) * blocks_y
            feat_ref[start : start + blocks_y, :] = feature

    def operands_of(x, y):
        lanes = slice(y * LANES, (y + 1) * LANES)
        feats = feat_ref[pl.ds(x * EARLY * blocks_y + y, EARLY, stride=blocks_y), :]
        high_part = rounded(feats)
        both = jnp.concatenate([high_part, feats - high_part], axis=0).astype(BF16)
        rows = rows_ref[x]
        owner_row = spread(rows >> 7, y, 2 * EARLY)
        for o in range(owners):
            lhs_ref[x, o * 2 * EARLY : (o + 1) * 2 * EARLY, lanes] = jnp.where(
                owner_row == jnp.asarray(o, BF16), both, jnp.zeros((), BF16)
            )
        hot_ref[x, :, lanes] = slot_one_hot(rows & (LANES - 1), y)

    def add_product(x):
        product = lax.dot_general(lhs_ref[x], hot_ref[x], NT, preferred_element_type=F32)
        total_ref[...] = product if x == 0 else total_ref[...] + product

    def finish():
        total = total_ref[...].reshape(owners, 2 * EARLY, LANES)
        table_ref[...] = total[:, :EARLY, :] + total[:, EARLY:, :]

    pieces = []
    for x in range(blocks_x):
        pieces.append(functools.partial(features_of, x))
        pieces += [functools.partial(operands_of, x, y) for y in range(blocks_y)]
        pieces.append(functools.partial(add_product, x))
    return pieces + [finish]


def target_rows(pos, radius):
    weight = 4.0 / (radius * radius)
    cx, cy, cz = pos[0] - 0.5, pos[1] - 0.5, pos[2] - 0.5
    lines = (
        -2.0 * cx * weight, -2.0 * cy * weight, -2.0 * cz * weight,
        weight, weight, weight,
        (cx * cx + cy * cy + cz * cz) * weight, jnp.zeros_like(weight),
    )
    parts = [three_parts(line) for line in lines]
    return [part[k] for k in range(3) for part in parts]


def target_matrix(coef):
    one, two, three = coef[0:8], coef[8:16], coef[16:24]
    stacked = jnp.concatenate([one, one, two, two, one, three], axis=0)
    return stacked.T.astype(BF16)


def source_matrix(line, root, squares):
    value = jnp.where(squares, line * line, line) * (root * root)
    one, two, three = three_parts(value)
    first = jnp.concatenate([one, two], axis=0).astype(BF16)
    last = jnp.concatenate([three, one], axis=0).astype(BF16)
    return jnp.concatenate([first, first, last], axis=0)


def fifth_root(mass):
    root = jnp.exp(0.2 * jnp.log(mass))
    square = root * root
    return 0.8 * root + 0.2 * mass / (square * square)


def store_source(nat_ref, start, count, columns, mass):
    cx, cy, cz = [column - 0.5 for column in columns]
    one = jnp.ones_like(cx)
    for kind, line in enumerate((cx, cy, cz, cx, cy, cz, one, fifth_root(mass))):
        nat_ref[start + kind * 8 : start + kind * 8 + count, :] = line


def pair_sums(sides, pieces=()):
    rows = 32
    steps = []
    for target, sources, roots, total in sides:
        count = roots.shape[0]
        for first in range(0, count, 2):
            steps.append((target, sources, roots, total, first, min(2, count - first), count))

    def product(step):
        target, sources, _, _, first, width, _ = step
        right = sources[:, first * LANES : (first + width) * LANES]
        return jnp.dot(target[...], right, preferred_element_type=F32)

    ready = product(steps[0])
    chunks = None
    for number, (_, _, roots, total, first, width, count) in enumerate(steps):
        squared = ready
        if number + 1 < len(steps):
            ready = product(steps[number + 1])
        if first == 0:
            chunks = [None] * (LANES // rows)
        limits = []
        for k in range(width):
            root = roots[first + k : first + k + 1, :]
            reach = 4.0 * root
            limits.append(
                [jnp.broadcast_to(line, (rows, LANES)) for line in (root, reach, reach * reach)]
            )
        for r in range(len(chunks)):
            for k, (root, reach, most) in enumerate(limits):
                t = squared[r * rows : (r + 1) * rows, k * LANES : (k + 1) * LANES]
                t = jnp.maximum(jnp.minimum(t, most), 0.0)
                u = pl.reciprocal(lax.rsqrt(t), approx=True)
                f = reach - u
                f = f * f
                f = f * f
                term = f * (root + u)
                chunks[r] = term if chunks[r] is None else chunks[r] + term
        if first + width == count:
            for r, chunk in enumerate(chunks):
                total[r * rows : (r + 1) * rows, :] = chunk
        if number < len(pieces):
            pieces[number]()
    for piece in pieces[len(steps) :]:
        piece()


def column_sums(totals):
    lane = lax.broadcasted_iota(jnp.int32, (LANES, LANES), 1)
    columns = jnp.zeros((LANES, LANES), F32)
    for k, total in enumerate(totals):
        columns = jnp.where(lane == k, jnp.sum(total, axis=1, keepdims=True), columns)
    return columns.T[: len(totals), :]


def square_mask():
    kind = lax.broadcasted_iota(jnp.int32, (8, LANES), 0)
    return (kind >= 3) & (kind < 6)


def block_pairs(
    x_first, x_step, x_count, code_ref, pos_ref, mass_ref, smooth_ref, prev_ref, next_ref,
    out_ref, match_ref, nat_ref, src_ref, shift_ref, tgt_ref, mat_ref, near_ref, root_ref, total_ref,
    pieces=(),
):
    blocks_x, blocks_y, _ = mass_ref.shape
    listed = code_ref.shape[0]
    null = (blocks_x + 2) * blocks_y
    for xe in range(blocks_x + 2):
        if xe == 0 or xe == blocks_x + 1:
            ref = prev_ref if xe == 0 else next_ref
            if ref is None:
                continue
            store_source(nat_ref, xe * 64, blocks_y, [ref[c] for c in range(3)], ref[3])
        else:
            columns = [pos_ref[c, xe - 1] for c in range(3)]
            store_source(nat_ref, xe * 64, blocks_y, columns, mass_ref[xe - 1])
        for y in range(blocks_y):
            src_ref[xe * blocks_y + y] = nat_ref[pl.ds(xe * 64 + y, 8, stride=8), :]
    src_ref[null] = jnp.zeros((8, LANES), F32)
    kind = lax.broadcasted_iota(jnp.int32, (8, LANES), 0)
    for code in range(9):
        along_x = jnp.where((kind == 0) | (kind == 3), float(code // 3 - 1), 0.0)
        along_y = jnp.where((kind == 1) | (kind == 4), float(code % 3 - 1), 0.0)
        shift_ref[code] = along_x + along_y
    squares = square_mask()
    for k in range(x_count):
        x = x_first + k * x_step
        lines = target_rows([pos_ref[c, x] for c in range(3)], smooth_ref[x])
        for row, line in enumerate(lines):
            tgt_ref[k, row * blocks_y : (row + 1) * blocks_y, :] = line

    blocks = [(turn, y) for turn in range(x_count) for y in range(blocks_y)]
    for number, (turn, y) in enumerate(blocks):
        target = target_matrix(tgt_ref[turn, pl.ds(y, 24, stride=blocks_y), :])
        mat_ref[number] = target
        if y == 0:
            match_ref[turn, 0] = target
        if y == blocks_y - 1:
            match_ref[turn, 1] = target
    for number, (turn, y) in enumerate(blocks):
        x = x_first + turn * x_step
        for k in range(listed):
            code = code_ref[k, x, y]
            step_x = (code * 11) >> 5
            near_y = y + code - 3 * step_x - 1
            inside = (near_y >= 0) & (near_y < blocks_y)
            line = src_ref[jnp.where(inside, (x + step_x) * blocks_y + near_y, null)]
            root = jnp.broadcast_to(line[7:8], line.shape)
            near_ref[number, :, k * LANES : (k + 1) * LANES] = source_matrix(
                line + shift_ref[code], root, squares
            )
            root_ref[number, k : k + 1, :] = root[0:1]
    pair_sums(
        [
            (mat_ref.at[n], near_ref.at[n], root_ref.at[n, pl.ds(0, listed)], total_ref.at[n])
            for n in range(len(blocks))
        ],
        pieces,
    )
    for turn in range(x_count):
        out_ref[turn] = column_sums([total_ref[turn * blocks_y + y] for y in range(blocks_y)])


def middle_kernel(
    code_ref, pos_ref, mass_ref, smooth_ref, column_ref, out_ref, match_ref, *scratch
):
    blocks_x, blocks_y, _ = mass_ref.shape
    for side in range(2):
        y = side * (blocks_y - 1)
        for x in range(blocks_x):
            for c in range(3):
                column_ref[side, c, x : x + 1, :] = pos_ref[c, x, y : y + 1, :]
            column_ref[side, 3, x : x + 1, :] = mass_ref[x, y : y + 1, :]
    block_pairs(
        1, 1, blocks_x - 2, code_ref, pos_ref, mass_ref, smooth_ref, None, None,
        out_ref, match_ref, *scratch,
    )


def edge_kernel(
    nx_total, ny_total, code_ref, pos_ref, mass_ref, smooth_ref, prev_ref, next_ref,
    vel_ref, group_ref, row_ref, out_ref, match_ref, table_ref, rows_ref, hot_ref,
    feat_ref, lhs_ref, sum_ref, *scratch
):
    blocks_x = mass_ref.shape[0]
    pieces = moment_pieces(
        nx_total, ny_total, pos_ref, vel_ref, mass_ref, group_ref, row_ref,
        table_ref, rows_ref, hot_ref, feat_ref, lhs_ref, sum_ref,
    )
    block_pairs(
        0, blocks_x - 1, 2, code_ref, pos_ref, mass_ref, smooth_ref, prev_ref, next_ref,
        out_ref, match_ref, *scratch, pieces=pieces,
    )


def pair_scratch(blocks_x, blocks_y, x_count, listed):
    return [
        pltpu.VMEM(((blocks_x + 2) * 64, LANES), F32),
        pltpu.VMEM(((blocks_x + 2) * blocks_y + 1, 8, LANES), F32),
        pltpu.VMEM((9, 8, LANES), F32),
        pltpu.VMEM((x_count, 24 * blocks_y, LANES), F32),
    ] + product_scratch(x_count * blocks_y, listed)


def product_scratch(blocks, listed):
    return [
        pltpu.VMEM((blocks, LANES, 48), BF16),
        pltpu.VMEM((blocks, 48, listed * LANES), BF16),
        pltpu.VMEM((blocks, 8, LANES), F32),
        pltpu.VMEM((blocks, LANES, LANES), F32),
    ]


def rim_kernel(
    code_ref, middle_ref, edge_ref, middle_match_ref, edge_match_ref, mass_ref, smooth_ref,
    low_ref, high_ref, rows_ref, hot_ref, early_ref,
    sum_ref, table_ref, nat_ref, md_ref, lhs_ref, row_sum_ref, near_ref, root_ref, total_ref,
):
    blocks_x, blocks_y, _ = mass_ref.shape
    owners = early_ref.shape[0]
    listed = code_ref.shape[0]
    for side, ref in enumerate((low_ref, high_ref)):
        store_source(nat_ref, side * 64, blocks_x + 2, [ref[c] for c in range(3)], ref[3])
    kind = lax.broadcasted_iota(jnp.int32, (8, LANES), 0)
    squares = square_mask()
    sides = []
    for x in range(blocks_x):
        edge = x == 0 or x == blocks_x - 1
        turn = (1 if x else 0) if edge else x - 1
        sum_ref[x] = (edge_ref if edge else middle_ref)[turn]
        for side in range(2):
            y = side * (blocks_y - 1)
            number = 2 * x + side
            for step_x in range(3):
                wanted = step_x * 3 + side * 2
                found = code_ref[0, x, y] == wanted
                for k in range(1, listed):
                    found = found | (code_ref[k, x, y] == wanted)
                along_x = jnp.where((kind == 0) | (kind == 3), float(step_x - 1), 0.0)
                along_y = jnp.where((kind == 1) | (kind == 4), float(side * 2 - 1), 0.0)
                line = nat_ref[pl.ds(side * 64 + x + step_x, 8, stride=8), :]
                root = jnp.broadcast_to(line[7:8], line.shape) * jnp.where(found, 1.0, 0.0)
                near_ref[number, :, step_x * LANES : (step_x + 1) * LANES] = source_matrix(
                    line + along_x + along_y, root, squares
                )
                root_ref[number, step_x : step_x + 1, :] = root[0:1]
            match_ref = (edge_match_ref if edge else middle_match_ref).at[turn, side]
            sides.append(
                (match_ref, near_ref.at[number], root_ref.at[number, pl.ds(0, 3)], total_ref.at[number])
            )
    owner_ids = lax.broadcasted_iota(jnp.int32, (owners, LANES), 0)
    last = blocks_y - 1

    def put_moments(x, ys):
        radius = smooth_ref[x]
        moment = mass_ref[x] * (sum_ref[x] * DENSITY_FACTOR / (radius * radius * radius))
        high_part = rounded(moment)
        low_part = moment - high_part
        owner = rows_ref[x] >> 7
        for y in ys:
            mine = jnp.broadcast_to(owner[y : y + 1, :], owner_ids.shape) == owner_ids
            lhs_ref[x, :, y * LANES : (y + 1) * LANES] = jnp.concatenate(
                [
                    jnp.where(mine, jnp.broadcast_to(part[y : y + 1, :], mine.shape), 0.0)
                    for part in (high_part, low_part)
                ],
                axis=0,
            ).astype(BF16)

    def inner_moments(x):
        put_moments(x, range(1, last))
        lanes = slice(LANES, last * LANES)
        product = lax.dot_general(
            hot_ref[x, :, lanes], lhs_ref[x, :, lanes], NT, preferred_element_type=F32
        )
        row_sum_ref[...] = product if x == 0 else row_sum_ref[...] + product

    pair_sums(sides, [functools.partial(inner_moments, x) for x in range(blocks_x)])
    sums = column_sums([total_ref[number] for number in range(len(sides))])
    for x in range(blocks_x):
        for side in range(2):
            y = side * last
            sum_ref[x, y : y + 1, :] += sums[2 * x + side : 2 * x + side + 1, :]
        put_moments(x, (0, last))
    ends = [(x, slice(y * LANES, (y + 1) * LANES)) for x in range(blocks_x) for y in (0, last)]
    total = row_sum_ref[...] + lax.dot_general(
        jnp.concatenate([hot_ref[x, :, lanes] for x, lanes in ends], axis=1),
        jnp.concatenate([lhs_ref[x, :, lanes] for x, lanes in ends], axis=1),
        NT,
        preferred_element_type=F32,
    )
    total = total.T
    md_ref[...] = total[:owners] + total[owners:]
    core, my_chip = lax.axis_index("core"), lax.axis_index("chip")
    for other in range(2):
        for step in range(owners // 2):
            owner = 2 * (my_chip ^ step) + (core ^ other)
            table_ref[other, step, :EARLY, :] = early_ref[owner]
            table_ref[other, step, EARLY : EARLY + 1, :] = md_ref[pl.ds(owner, 1), :]


def swap(value, axis, step):
    count = lax.axis_size(axis)
    return lax.ppermute(value, axis, [(i, i ^ step) for i in range(count)])


def neighbours_of(low_edge, high_edge, axis, parity):
    count = lax.axis_size(axis)
    even = parity == 0
    inner = lax.ppermute(
        jnp.where(even, high_edge, low_edge), axis, [(i, i ^ 1) for i in range(count)]
    )
    outer = lax.ppermute(
        jnp.where(even, low_edge, high_edge),
        axis,
        [(i, (i + 1 if i & 1 else i - 1) % count) for i in range(count)],
    )
    return jnp.where(even, outer, inner), jnp.where(even, inner, outer)


def added(parts):
    while len(parts) > 1:
        parts = [sum(parts[k : k + 2][1:], parts[k]) for k in range(0, len(parts), 2)]
    return parts[0]


def to_owner(table):
    table = table[0] + swap(table[1], "core", 1)
    while table.shape[0] > 1:
        ways = min(4, table.shape[0])
        part = table.shape[0] // ways
        table = added(
            [table[:part]]
            + [swap(table[k * part : (k + 1) * part], "chip", k * part) for k in range(1, ways)]
        )
    return table[0]


def summed(value, axis):
    count = lax.axis_size(axis)
    if count & (count - 1):
        return lax.psum(value, axis)
    copies = jnp.broadcast_to(value[None], (count,) + value.shape)
    return added(list(lax.all_to_all(copies, axis, split_axis=0, concat_axis=0, tiled=True)))


def shards(positions, velocities, masses, smoothing, neighbours, particle_group, group_row):
    blocks_x, blocks_y, block_len = masses.shape
    dom_count, sub_count = lax.axis_size("dom"), lax.axis_size("chip") * lax.axis_size("core")
    owners = sub_count
    chunk = blocks_y * block_len
    shape = jax.ShapeDtypeStruct
    codes = neighbours.transpose(2, 0, 1)
    packed = jnp.concatenate([positions, masses[None]], axis=0)
    prev, following = neighbours_of(
        packed[:, 0], packed[:, blocks_x - 1], "dom", lax.axis_index("dom") & 1
    )
    columns, middle, middle_match = pl.pallas_call(
        middle_kernel,
        out_shape=(
            shape((2, 4, blocks_x, LANES), F32),
            shape((blocks_x - 2, blocks_y, LANES), F32),
            shape((blocks_x - 2, 2, LANES, 48), BF16),
        ),
        in_specs=[SMEM] + [VMEM] * 3,
        out_specs=(VMEM,) * 3,
        scratch_shapes=pair_scratch(blocks_x, blocks_y, blocks_x - 2, codes.shape[0]),
        compiler_params=params(),
        cost_estimate=pl.CostEstimate(
            flops=4_000_000_000, bytes_accessed=400_000, transcendentals=1_300_000
        ),
        name="middle_pairs",
    )(codes, positions, masses, smoothing)
    edges = [
        jnp.concatenate([prev[:, y : y + 1], columns[side], following[:, y : y + 1]], axis=1)
        for side, y in ((0, 0), (1, blocks_y - 1))
    ]
    low, high = neighbours_of(*edges, ("chip", "core"), lax.axis_index("core"))
    edge, edge_match, early, rows, hot = pl.pallas_call(
        functools.partial(edge_kernel, blocks_x * dom_count, blocks_y * sub_count),
        out_shape=(
            shape((2, blocks_y, LANES), F32),
            shape((2, 2, LANES, 48), BF16),
            shape((owners, EARLY, LANES), F32),
            shape(masses.shape, jnp.int32),
            shape((blocks_x, LANES, chunk), BF16),
        ),
        in_specs=[SMEM] + [VMEM] * 8,
        out_specs=(VMEM,) * 5,
        scratch_shapes=[
            pltpu.VMEM((blocks_x * EARLY * blocks_y, LANES), F32),
            pltpu.VMEM((blocks_x, owners * 2 * EARLY, chunk), BF16),
            pltpu.VMEM((owners * 2 * EARLY, LANES), F32),
        ]
        + pair_scratch(blocks_x, blocks_y, 2, codes.shape[0]),
        compiler_params=params(),
        cost_estimate=pl.CostEstimate(
            flops=5_000_000_000, bytes_accessed=1_400_000, transcendentals=1_300_000
        ),
        name="edge_pairs_and_moments",
    )(
        codes, positions, masses, smoothing, prev, following,
        velocities, particle_group, group_row.reshape(-1, LANES),
    )
    sums, table = pl.pallas_call(
        rim_kernel,
        out_shape=(shape(masses.shape, F32), shape((2, owners // 2, EARLY + 1, LANES), F32)),
        in_specs=[SMEM] + [VMEM] * 11,
        out_specs=(VMEM, VMEM),
        scratch_shapes=[
            pltpu.VMEM((128, LANES), F32),
            pltpu.VMEM((owners, LANES), F32),
            pltpu.VMEM((blocks_x, 2 * owners, chunk), BF16),
            pltpu.VMEM((LANES, 2 * owners), F32),
        ]
        + product_scratch(2 * blocks_x, 3)[1:],
        compiler_params=params(),
        cost_estimate=pl.CostEstimate(
            flops=200_000_000, bytes_accessed=400_000, transcendentals=400_000
        ),
        name="rim_pairs_and_table",
    )(
        codes, middle, edge, middle_match, edge_match, masses, smoothing, low, high, rows, hot, early
    )
    density = sums * DENSITY_FACTOR / (smoothing * smoothing * smoothing)
    return (density, summed(to_owner(table), "dom"))


def solution(mesh):
    dom_count, sub_count = mesh.devices.shape
    mesh = jax.sharding.Mesh(
        mesh.devices.reshape(dom_count, sub_count // 2, 2), ("dom", "chip", "core")
    )
    sub = ("chip", "core")
    in_specs = (
        P(None, "dom", sub, None),
        P(None, "dom", sub, None),
        P("dom", sub, None),
        P("dom", sub, None),
        P("dom", sub, None),
        P("dom", sub, None),
        P(),
    )
    out_specs = (P("dom", sub, None), P(None, sub))
    return jax.shard_map(shards, mesh=mesh, in_specs=in_specs, out_specs=out_specs, check_vma=False)
```

profile of v0, /device:TPU:0, one launch (start us, length us, event | category | flops | bytes accessed | tf_op | source)
XLA Modules:
  0.0 36.3 jit_solution(4132890713166335883)
XLA Ops:
  0.6 0.0 copy-start.2
  0.6 0.8 %select_bitcast_fusion = (f32[4,8,128]{2,1,0:T(8,128)S(1)}, f32[4,1,8,128]{3,2,0,1:T(8,128)S(1)}, f32[4,1,8,128]{3,2,0,1:T(8,128)S(1)}) fusion(pred[]{:T(512)S(6)} %eq.6, f32[1,4,8,128]{3,2,0,1:T(8,128)} %bitcast.19, f32[3,4,8,128]{3,2,1,0:T(8,128)} %pos_ref.3), kind=kLoop, calls=%fused_computation.8 | loop fusion | flops 12288 | bytes 114689 | tf_op jit(solution)/shard_map/jit(_where)/select_n | solution.py:426
  1.4 0.0 copy-start
  1.4 0.0 copy-start.1
  1.4 0.0 copy-start.3
  1.5 5.1 %collective-permute-start = (f32[4,8,128]{2,1,0:T(8,128)S(1)}, f32[4,8,128]{2,1,0:T(8,128)S(1)}, u32[]{:S(2)}, u32[]{:S(2)}) collective-permute-start(f32[4,8,128]{2,1,0:T(8,128)S(1)} %select_bitcast_fusion.1), channel_id=1, source_target_pairs={{0,24},{8,16},{16,8},{24,0},{1,25},{9,17},{17,9},{25,1},{2,26},{10... | collective-permute-start | bytes 49160 | tf_op jit(solution)/shard_map/ppermute | solution.py:428
  6.6 0.0 collective-permute-start.1
  6.6 0.0 copy-done.2
  6.6 0.0 copy-done
  6.6 0.0 copy-done.1
  6.6 0.0 copy-done.3
  6.6 3.2 %middle_pairs.1 = (f32[2,4,4,128]{3,2,1,0:T(4,128)S(1)}, f32[2,8,128]{2,1,0:T(8,128)S(1)}, bf16[2,2,128,48]{3,2,1,0:T(8,128)(2,1)S(1)}) custom-call(s32[5,4,8]{2,1,0:T(4,128)S(1)} %bitcast.20, f32[3,4,8,128]{3,2,1,0:T(8,128)S(1)} %copy-done.2, f32[4,8,128]{2,1,0:T(8,128)S(1)} %copy-done, f32[4,8,128]{2,1,0:T(8,128)S(1)} %copy-done.1), custom_call_target="tpu_custom_call" | custom-call | flops 4000000000 | bytes 400000 | tf_op jit(solution)/shard_map/middle_pairs/pallas_call | solution.py:473
  9.8 0.0 collective-permute-done
  9.8 0.5 %collective-permute-done.1 = f32[4,8,128]{2,1,0:T(8,128)S(1)} collective-permute-done((f32[4,8,128]{2,1,0:T(8,128)S(1)}, f32[4,8,128]{2,1,0:T(8,128)S(1)}, u32[]{:S(2)}, u32[]{:S(2)}) %collective-permute-start.1) | collective-permute-done | bytes 16416 | tf_op jit(solution)/shard_map/ppermute | solution.py:425
  10.3 0.0 copy-start.4
  10.3 0.0 copy-start.5
  10.4 0.0 copy-start.6
  10.4 0.1 collective-permute-start.3
  10.5 2.5 %collective-permute-start.2 = (f32[4,6,128]{2,1,0:T(8,128)S(1)}, f32[4,6,128]{2,1,0:T(8,128)S(1)}, u32[]{:S(2)}, u32[]{:S(2)}) collective-permute-start(f32[4,6,128]{2,1,0:T(8,128)S(1)} %get-tuple-element.33), channel_id=1, source_target_pairs={{0,7},{1,2},{2,1},{3,4},{4,3},{5,6},{6,5},{7,0},{8,15},{9,10},{10,... | collective-permute-start | bytes 36872 | tf_op jit(solution)/shard_map/ppermute | solution.py:428
  13.0 0.0 copy-done.4
  13.0 0.0 copy-done.5
  13.0 0.0 copy-done.6
  13.0 4.3 %edge_pairs_and_moments.1 = (f32[2,8,128]{2,1,0:T(8,128)S(1)}, bf16[2,2,128,48]{3,2,1,0:T(8,128)(2,1)S(1)}, f32[8,16,128]{2,1,0:T(8,128)S(1)}, s32[4,8,128]{2,1,0:T(8,128)S(1)}, bf16[4,128,1024]{2,1,0:T(8,128)(2,1)S(1)}) custom-call(s32[5,4,8]{2,1,0:T(4,128)S(1)} %bitcast.21, f32[3,4,8,128]{3,2,1,0:T(8,128)S(1)} %copy-done.2, f32[4,8,128]{2,1,0:T(8,128)S(1)} %copy-done, ...), custom_call_target="tpu_custom_call" | custom-call | flops 5000000000 | bytes 1400000 | tf_op jit(solution)/shard_map/edge_pairs_and_moments/pallas_call | solution.py:494
  17.3 0.0 collective-permute-done.3
  17.3 0.0 collective-permute-done.2
  17.3 2.0 %rim_pairs_and_table.1 = (f32[4,8,128]{2,1,0:T(8,128)S(1)}, f32[2,4,17,128]{3,2,1,0:T(8,128)S(1)}) custom-call(s32[5,4,8]{2,1,0:T(4,128)S(1)} %bitcast.22, f32[2,8,128]{2,1,0:T(8,128)S(1)} %get-tuple-element.12.middle_ref, f32[2,8,128]{2,1,0:T(8,128)S(1)} %get-tuple-element.13.edge_ref, bf16[2,2,128,48]{3,2,1,0:T(8,128)(2,1)S(1)} %get-tuple-element.14.middle_match_ref, ...), custom_call_target="tpu_custom_call" | custom-call | flops 200000000 | bytes 400000 | tf_op jit(solution)/shard_map/rim_pairs_and_table/pallas_call | solution.py:520
  19.3 0.1 collective-permute-start.4
  19.4 1.2 %collective-permute-done.4 = f32[4,17,128]{2,1,0:T(8,128)S(1)} collective-permute-done((f32[4,17,128]{2,1,0:T(8,128)S(1)}, f32[4,17,128]{2,1,0:T(8,128)S(1)}, u32[]{:S(2)}, u32[]{:S(2)}) %collective-permute-start.4) | collective-permute-done | bytes 34848 | tf_op jit(solution)/shard_map/ppermute | solution.py:419
  20.6 0.6 %collective-permute-start.7 = (f32[1,17,128]{2,1,0:T(8,128)S(1)}, f32[1,17,128]{2,1,0:T(8,128)S(1)}, u32[]{:S(2)}, u32[]{:S(2)}) collective-permute-start(f32[1,17,128]{2,1,0:T(8,128)S(1)} %get-tuple-element.25), channel_id=1, source_target_pairs={{0,6},{2,4},{4,2},{6,0},{1,7},{3,5},{5,3},{7,1},{8,14},{10,12},{12... | collective-permute-start | bytes 26120 | tf_op jit(solution)/shard_map/ppermute | solution.py:419
  21.3 1.2 %collective-permute-start.6 = (f32[1,17,128]{2,1,0:T(8,128)S(1)}, f32[1,17,128]{2,1,0:T(8,128)S(1)}, u32[]{:S(2)}, u32[]{:S(2)}) collective-permute-start(f32[1,17,128]{2,1,0:T(8,128)S(1)} %get-tuple-element.26), channel_id=1, source_target_pairs={{0,4},{2,6},{4,0},{6,2},{1,5},{3,7},{5,1},{7,3},{8,12},{10,14},{12... | collective-permute-start | bytes 26120 | tf_op jit(solution)/shard_map/ppermute | solution.py:419
  22.4 1.8 %collective-permute-start.5 = (f32[1,17,128]{2,1,0:T(8,128)S(1)}, f32[1,17,128]{2,1,0:T(8,128)S(1)}, u32[]{:S(2)}, u32[]{:S(2)}) collective-permute-start(f32[1,17,128]{2,1,0:T(8,128)S(1)} %get-tuple-element.27), channel_id=1, source_target_pairs={{0,2},{2,0},{4,6},{6,4},{1,3},{3,1},{5,7},{7,5},{8,10},{10,8},{12,... | collective-permute-start | bytes 26120 | tf_op jit(solution)/shard_map/ppermute | solution.py:419
  24.2 1.1 %collective-permute-done.7 = f32[1,17,128]{2,1,0:T(8,128)S(1)} collective-permute-done((f32[1,17,128]{2,1,0:T(8,128)S(1)}, f32[1,17,128]{2,1,0:T(8,128)S(1)}, u32[]{:S(2)}, u32[]{:S(2)}) %collective-permute-start.7) | collective-permute-done | bytes 8736 | tf_op jit(solution)/shard_map/ppermute | solution.py:419
  25.3 0.0 collective-permute-done.6
  25.3 0.8 %collective-permute-done.5 = f32[1,17,128]{2,1,0:T(8,128)S(1)} collective-permute-done((f32[1,17,128]{2,1,0:T(8,128)S(1)}, f32[1,17,128]{2,1,0:T(8,128)S(1)}, u32[]{:S(2)}, u32[]{:S(2)}) %collective-permute-start.5) | collective-permute-done | bytes 8736 | tf_op jit(solution)/shard_map/ppermute | solution.py:419
  26.2 0.6 %broadcast_in_dim.12 = f32[4,17,128]{2,1,0:T(8,128)} broadcast(f32[17,128]{1,0:T(8,128)S(1)} %fusion.6), dimensions={1,2} | broadcast | bytes 43520 | tf_op jit(solution)/shard_map/broadcast_in_dim | solution.py:458
  26.8 3.3 %all-to-all-start = ((f32[4,17,128]{2,1,0:T(8,128)}), f32[4,17,128]{2,1,0:T(8,128)S(1)}, u32[]{:S(2)}, u32[]{:S(2)}) async-start(f32[4,17,128]{2,1,0:T(8,128)} %broadcast_in_dim.12), calls=%async_computation | async-start | bytes 98304 | tf_op jit(solution)/shard_map/all_to_all | solution.py:459
  30.1 0.6 %fusion = f32[4,8,128]{2,1,0:T(8,128)} fusion(f32[4,8,128]{2,1,0:T(8,128)S(1)} %copy-done.1, f32[4,8,128]{2,1,0:T(8,128)S(1)} %get-tuple-element.20), kind=kLoop, calls=%fused_computation.3 | loop fusion | flops 16384 | bytes 49152 | tf_op jit(solution)/shard_map/div | solution.py:540
  30.7 5.0 %all-to-all-done = f32[4,17,128]{2,1,0:T(8,128)S(1)} async-done(((f32[4,17,128]{2,1,0:T(8,128)}), f32[4,17,128]{2,1,0:T(8,128)S(1)}, u32[]{:S(2)}, u32[]{:S(2)}) %all-to-all-start) | async-done | bytes 34848 | tf_op jit(solution)/shard_map/all_to_all | solution.py:459
  35.7 0.6 %fusion.4 = f32[17,128]{1,0:T(8,128)} fusion(f32[4,17,128]{2,1,0:T(8,128)S(1)} %all-to-all-done), kind=kLoop, calls=%fused_computation.14 | loop fusion | flops 6528 | bytes 43520 | tf_op jit(solution)/shard_map/add | solution.py:438
  (10 shorter events, 0.1 us)
Async XLA Ops:
  0.6 5.9 %copy-start.2 = (f32[3,4,8,128]{3,2,1,0:T(8,128)S(1)}, f32[3,4,8,128]{3,2,1,0:T(8,128)}, u32[]{:S(2)}) copy-start(f32[3,4,8,128]{3,2,1,0:T(8,128)} %pos_ref.3) | copy-start | bytes 147460
  1.4 5.2 %copy-start = (f32[4,8,128]{2,1,0:T(8,128)S(1)}, f32[4,8,128]{2,1,0:T(8,128)}, u32[]{:S(2)}) copy-start(f32[4,8,128]{2,1,0:T(8,128)} %mass_ref.5) | copy-start | bytes 49156
  1.4 5.2 %copy-start.1 = (f32[4,8,128]{2,1,0:T(8,128)S(1)}, f32[4,8,128]{2,1,0:T(8,128)}, u32[]{:S(2)}) copy-start(f32[4,8,128]{2,1,0:T(8,128)} %smooth_ref.5) | copy-start | bytes 49156
  1.4 5.2 %copy-start.3 = (s32[4,8,5]{1,0,2:T(4,128)S(1)}, s32[4,8,5]{1,0,2:T(4,128)}, u32[]{:S(2)}) copy-start(s32[4,8,5]{1,0,2:T(4,128)} %param.11) | copy-start | bytes 1924
  1.5 8.3 %collective-permute-start = (f32[4,8,128]{2,1,0:T(8,128)S(1)}, f32[4,8,128]{2,1,0:T(8,128)S(1)}, u32[]{:S(2)}, u32[]{:S(2)}) collective-permute-start(f32[4,8,128]{2,1,0:T(8,128)S(1)} %select_bitcast_fusion.1), channel_id=1, source_target_pairs={{0,24},{8,16},{16,8},{24,0},{1,25},{9,17},{17,9},{25,1},{2,26},{10... | collective-permute-start | bytes 49160 | tf_op jit(solution)/shard_map/ppermute | solution.py:428
  6.6 3.7 %collective-permute-start.1 = (f32[4,8,128]{2,1,0:T(8,128)S(1)}, f32[4,8,128]{2,1,0:T(8,128)S(1)}, u32[]{:S(2)}, u32[]{:S(2)}) collective-permute-start(f32[4,8,128]{2,1,0:T(8,128)S(1)} %get-tuple-element.22), channel_id=1, source_target_pairs={{0,8},{8,0},{16,24},{24,16},{1,9},{9,1},{17,25},{25,17},{2,10},{10... | collective-permute-start | bytes 49160 | tf_op jit(solution)/shard_map/ppermute | solution.py:425
  10.3 2.7 %copy-start.4 = (f32[3,4,8,128]{3,2,1,0:T(8,128)S(1)}, f32[3,4,8,128]{3,2,1,0:T(8,128)}, u32[]{:S(2)}) copy-start(f32[3,4,8,128]{3,2,1,0:T(8,128)} %vel_ref.1) | copy-start | bytes 147460
  10.3 2.7 %copy-start.5 = (s32[4,8,128]{2,1,0:T(8,128)S(1)}, s32[4,8,128]{2,1,0:T(8,128)}, u32[]{:S(2)}) copy-start(s32[4,8,128]{2,1,0:T(8,128)} %group_ref.1) | copy-start | bytes 49156
  10.4 2.6 %copy-start.6 = (s32[1024]{0:T(1024)S(1)}, s32[1024]{0:T(1024)}, u32[]{:S(2)}) copy-start(s32[1024]{0:T(1024)} %param.13) | copy-start | bytes 12292
  10.4 6.9 %collective-permute-start.3 = (f32[4,6,128]{2,1,0:T(8,128)S(1)}, f32[4,6,128]{2,1,0:T(8,128)S(1)}, u32[]{:S(2)}, u32[]{:S(2)}) collective-permute-start(f32[4,6,128]{2,1,0:T(8,128)S(1)} %get-tuple-element.32), channel_id=1, source_target_pairs={{0,1},{1,0},{2,3},{3,2},{4,5},{5,4},{6,7},{7,6},{8,9},{9,8},{10,11... | collective-permute-start | bytes 36872 | tf_op jit(solution)/shard_map/ppermute | solution.py:425
  10.5 6.8 %collective-permute-start.2 = (f32[4,6,128]{2,1,0:T(8,128)S(1)}, f32[4,6,128]{2,1,0:T(8,128)S(1)}, u32[]{:S(2)}, u32[]{:S(2)}) collective-permute-start(f32[4,6,128]{2,1,0:T(8,128)S(1)} %get-tuple-element.33), channel_id=1, source_target_pairs={{0,7},{1,2},{2,1},{3,4},{4,3},{5,6},{6,5},{7,0},{8,15},{9,10},{10,... | collective-permute-start | bytes 36872 | tf_op jit(solution)/shard_map/ppermute | solution.py:428
  19.3 1.3 %collective-permute-start.4 = (f32[4,17,128]{2,1,0:T(8,128)S(1)}, f32[4,17,128]{2,1,0:T(8,128)S(1)}, u32[]{:S(2)}, u32[]{:S(2)}) collective-permute-start(f32[4,17,128]{2,1,0:T(8,128)S(1)} %slice_bitcast_fusion), channel_id=1, source_target_pairs={{0,1},{1,0},{2,3},{3,2},{4,5},{5,4},{6,7},{7,6},{8,9},{9,8},{10,11... | collective-permute-start | bytes 104456 | tf_op jit(solution)/shard_map/ppermute | solution.py:419
  20.6 4.7 %collective-permute-start.7 = (f32[1,17,128]{2,1,0:T(8,128)S(1)}, f32[1,17,128]{2,1,0:T(8,128)S(1)}, u32[]{:S(2)}, u32[]{:S(2)}) collective-permute-start(f32[1,17,128]{2,1,0:T(8,128)S(1)} %get-tuple-element.25), channel_id=1, source_target_pairs={{0,6},{2,4},{4,2},{6,0},{1,7},{3,5},{5,3},{7,1},{8,14},{10,12},{12... | collective-permute-start | bytes 26120 | tf_op jit(solution)/shard_map/ppermute | solution.py:419
  21.3 4.0 %collective-permute-start.6 = (f32[1,17,128]{2,1,0:T(8,128)S(1)}, f32[1,17,128]{2,1,0:T(8,128)S(1)}, u32[]{:S(2)}, u32[]{:S(2)}) collective-permute-start(f32[1,17,128]{2,1,0:T(8,128)S(1)} %get-tuple-element.26), channel_id=1, source_target_pairs={{0,4},{2,6},{4,0},{6,2},{1,5},{3,7},{5,1},{7,3},{8,12},{10,14},{12... | collective-permute-start | bytes 26120 | tf_op jit(solution)/shard_map/ppermute | solution.py:419
  22.4 3.7 %collective-permute-start.5 = (f32[1,17,128]{2,1,0:T(8,128)S(1)}, f32[1,17,128]{2,1,0:T(8,128)S(1)}, u32[]{:S(2)}, u32[]{:S(2)}) collective-permute-start(f32[1,17,128]{2,1,0:T(8,128)S(1)} %get-tuple-element.27), channel_id=1, source_target_pairs={{0,2},{2,0},{4,6},{6,4},{1,3},{3,1},{5,7},{7,5},{8,10},{10,8},{12,... | collective-permute-start | bytes 26120 | tf_op jit(solution)/shard_map/ppermute | solution.py:419
  26.8 8.9 %all-to-all-start = ((f32[4,17,128]{2,1,0:T(8,128)}), f32[4,17,128]{2,1,0:T(8,128)S(1)}, u32[]{:S(2)}, u32[]{:S(2)}) async-start(f32[4,17,128]{2,1,0:T(8,128)} %broadcast_in_dim.12), calls=%async_computation | async-start | bytes 98304 | tf_op jit(solution)/shard_map/all_to_all | solution.py:459
where the time goes:
time: 36.7 us; the launch traced here: 36.3 us
  starting transfers between devices  14.6 us (40%)
  Pallas kernels  9.43 us (26%)
  waiting for transfers between devices  8.73 us (24%)
  other arithmetic  2.05 us (6%)
  between operations  0.81 us (2%)
  local copies, waits for them, and re-layouts  0.68 us (2%)
    ppermute x2, starting transfers between devices, neighbours_of(): lax.ppermute(jnp.where(even, low_edge, high_edge), axis, [(i, (i + 1 if i...  7.66 us
    all_to_all x1, waiting for transfers between devices, summed(): lax.all_to_all(copies, axis, split_axis=0, concat_axis=0, tiled=True)  5.05 us
    pallas_call x1, Pallas kernels, shards(): pl.pallas_call(functools.partial(edge_kernel, blocks_x * dom_count, block...  4.26 us
    ppermute x4, starting transfers between devices, swap(): return lax.ppermute(value, axis, [(i, i ^ step) for i in range(count)])  3.62 us
    all_to_all x1, starting transfers between devices, summed(): lax.all_to_all(copies, axis, split_axis=0, concat_axis=0, tiled=True)  3.27 us
    pallas_call x1, Pallas kernels, shards(): pl.pallas_call(middle_kernel, out_shape=(shape((2, 4, blocks_x, LANES), F...  3.19 us
    ppermute x4, waiting for transfers between devices, swap(): return lax.ppermute(value, axis, [(i, i ^ step) for i in range(count)])  3.16 us
    pallas_call x1, Pallas kernels, shards(): pl.pallas_call(rim_kernel, out_shape=(shape(masses.shape, F32), shape((2,...  1.98 us
  transfers between devices with their start and end apart: 9, of which 5 were waited for; matrix products, arithmetic and copies ran while one was open for 2% of the time, Pallas kernels for 21%

commit v1 on v0

--- a/solution.py
+++ b/solution.py
@@ -48,8 +48,8 @@
     )
 
 
-def moment_pieces(
-    nx_total, ny_total, pos_ref, vel_ref, mass_ref, group_ref, row_ref,
+def moments_kernel(
+    nx_total, ny_total, after_ref, pos_ref, vel_ref, mass_ref, group_ref, row_ref,
     table_ref, rows_ref, hot_ref, feat_ref, lhs_ref, total_ref,
 ):
     blocks_x, blocks_y, _ = mass_ref.shape
@@ -105,12 +105,12 @@
         total = total_ref[...].reshape(owners, 2 * EARLY, LANES)
         table_ref[...] = total[:, :EARLY, :] + total[:, EARLY:, :]
 
-    pieces = []
     for x in range(blocks_x):
-        pieces.append(functools.partial(features_of, x))
-        pieces += [functools.partial(operands_of, x, y) for y in range(blocks_y)]
-        pieces.append(functools.partial(add_product, x))
-    return pieces + [finish]
+        features_of(x)
+        for y in range(blocks_y):
+            operands_of(x, y)
+        add_product(x)
+    finish()
 
 
 def target_rows(pos, radius):
@@ -183,8 +183,8 @@
         for r in range(len(chunks)):
             for k, (root, reach, most) in enumerate(limits):
                 t = squared[r * rows : (r + 1) * rows, k * LANES : (k + 1) * LANES]
-                t = jnp.maximum(jnp.minimum(t, most), 0.0)
-                u = pl.reciprocal(lax.rsqrt(t), approx=True)
+                t = jnp.maximum(jnp.minimum(t, most), 1e-12)
+                u = t * lax.rsqrt(t)
                 f = reach - u
                 f = f * f
                 f = f * f
@@ -212,14 +212,29 @@
     return (kind >= 3) & (kind < 6)
 
 
+def shift_rows(step_x, step_y):
+    kind = lax.broadcasted_iota(jnp.int32, (8, LANES), 0)
+    along_x = jnp.where((kind == 0) | (kind == 3), float(step_x), 0.0)
+    return along_x + jnp.where((kind == 1) | (kind == 4), float(step_y), 0.0)
+
+
+def put_shifts(shift_ref):
+    for code in range(9):
+        shift_ref[code] = shift_rows(code // 3 - 1, code % 3 - 1)
+
+
+def put_source(near_ref, root_ref, number, k, line, shift, squares):
+    root = jnp.broadcast_to(line[7:8], line.shape)
+    near_ref[number, :, k * LANES : (k + 1) * LANES] = source_matrix(line + shift, root, squares)
+    root_ref[number, k : k + 1, :] = root[0:1]
+
+
 def block_pairs(
     x_first, x_step, x_count, code_ref, pos_ref, mass_ref, smooth_ref, prev_ref, next_ref,
-    out_ref, match_ref, nat_ref, src_ref, shift_ref, tgt_ref, mat_ref, near_ref, root_ref, total_ref,
-    pieces=(),
+    out_ref, src_ref, nat_ref, shift_ref, tgt_ref, mat_ref, near_ref, root_ref, total_ref,
 ):
     blocks_x, blocks_y, _ = mass_ref.shape
     listed = code_ref.shape[0]
-    null = (blocks_x + 2) * blocks_y
     for xe in range(blocks_x + 2):
         if xe == 0 or xe == blocks_x + 1:
             ref = prev_ref if xe == 0 else next_ref
@@ -231,53 +246,37 @@
             store_source(nat_ref, xe * 64, blocks_y, columns, mass_ref[xe - 1])
         for y in range(blocks_y):
             src_ref[xe * blocks_y + y] = nat_ref[pl.ds(xe * 64 + y, 8, stride=8), :]
-    src_ref[null] = jnp.zeros((8, LANES), F32)
-    kind = lax.broadcasted_iota(jnp.int32, (8, LANES), 0)
-    for code in range(9):
-        along_x = jnp.where((kind == 0) | (kind == 3), float(code // 3 - 1), 0.0)
-        along_y = jnp.where((kind == 1) | (kind == 4), float(code % 3 - 1), 0.0)
-        shift_ref[code] = along_x + along_y
+    put_shifts(shift_ref)
     squares = square_mask()
-    for k in range(x_count):
-        x = x_first + k * x_step
+    blocks = [(turn, y) for turn in range(x_count) for y in range(1, blocks_y - 1)]
+    for turn in range(x_count):
+        x = x_first + turn * x_step
         lines = target_rows([pos_ref[c, x] for c in range(3)], smooth_ref[x])
         for row, line in enumerate(lines):
-            tgt_ref[k, row * blocks_y : (row + 1) * blocks_y, :] = line
-
-    blocks = [(turn, y) for turn in range(x_count) for y in range(blocks_y)]
+            tgt_ref[turn, row * blocks_y : (row + 1) * blocks_y, :] = line
     for number, (turn, y) in enumerate(blocks):
-        target = target_matrix(tgt_ref[turn, pl.ds(y, 24, stride=blocks_y), :])
-        mat_ref[number] = target
-        if y == 0:
-            match_ref[turn, 0] = target
-        if y == blocks_y - 1:
-            match_ref[turn, 1] = target
+        mat_ref[number] = target_matrix(tgt_ref[turn, pl.ds(y, 24, stride=blocks_y), :])
     for number, (turn, y) in enumerate(blocks):
         x = x_first + turn * x_step
         for k in range(listed):
             code = code_ref[k, x, y]
             step_x = (code * 11) >> 5
-            near_y = y + code - 3 * step_x - 1
-            inside = (near_y >= 0) & (near_y < blocks_y)
-            line = src_ref[jnp.where(inside, (x + step_x) * blocks_y + near_y, null)]
-            root = jnp.broadcast_to(line[7:8], line.shape)
-            near_ref[number, :, k * LANES : (k + 1) * LANES] = source_matrix(
-                line + shift_ref[code], root, squares
-            )
-            root_ref[number, k : k + 1, :] = root[0:1]
+            line = src_ref[(x + step_x) * blocks_y + y + code - 3 * step_x - 1]
+            put_source(near_ref, root_ref, number, k, line, shift_ref[code], squares)
     pair_sums(
         [
             (mat_ref.at[n], near_ref.at[n], root_ref.at[n, pl.ds(0, listed)], total_ref.at[n])
             for n in range(len(blocks))
-        ],
-        pieces,
-    )
+        ]
+    )
+    inner = blocks_y - 2
     for turn in range(x_count):
-        out_ref[turn] = column_sums([total_ref[turn * blocks_y + y] for y in range(blocks_y)])
+        sums = column_sums([total_ref[turn * inner + k] for k in range(inner)])
+        out_ref[turn, 1 : blocks_y - 1, :] = sums
 
 
 def middle_kernel(
-    code_ref, pos_ref, mass_ref, smooth_ref, column_ref, out_ref, match_ref, *scratch
+    code_ref, pos_ref, mass_ref, smooth_ref, group_ref, row_ref, column_ref, out_ref, *scratch
 ):
     blocks_x, blocks_y, _ = mass_ref.shape
     for side in range(2):
@@ -287,34 +286,26 @@
                 column_ref[side, c, x : x + 1, :] = pos_ref[c, x, y : y + 1, :]
             column_ref[side, 3, x : x + 1, :] = mass_ref[x, y : y + 1, :]
     block_pairs(
-        1, 1, blocks_x - 2, code_ref, pos_ref, mass_ref, smooth_ref, None, None,
-        out_ref, match_ref, *scratch,
+        1, 1, blocks_x - 2, code_ref, pos_ref, mass_ref, smooth_ref, None, None, out_ref, *scratch
     )
 
 
 def edge_kernel(
-    nx_total, ny_total, code_ref, pos_ref, mass_ref, smooth_ref, prev_ref, next_ref,
-    vel_ref, group_ref, row_ref, out_ref, match_ref, table_ref, rows_ref, hot_ref,
-    feat_ref, lhs_ref, sum_ref, *scratch
+    code_ref, pos_ref, mass_ref, smooth_ref, prev_ref, next_ref, out_ref, src_ref, *scratch
 ):
     blocks_x = mass_ref.shape[0]
-    pieces = moment_pieces(
-        nx_total, ny_total, pos_ref, vel_ref, mass_ref, group_ref, row_ref,
-        table_ref, rows_ref, hot_ref, feat_ref, lhs_ref, sum_ref,
-    )
     block_pairs(
         0, blocks_x - 1, 2, code_ref, pos_ref, mass_ref, smooth_ref, prev_ref, next_ref,
-        out_ref, match_ref, *scratch, pieces=pieces,
+        out_ref, src_ref, *scratch,
     )
 
 
 def pair_scratch(blocks_x, blocks_y, x_count, listed):
     return [
         pltpu.VMEM(((blocks_x + 2) * 64, LANES), F32),
-        pltpu.VMEM(((blocks_x + 2) * blocks_y + 1, 8, LANES), F32),
         pltpu.VMEM((9, 8, LANES), F32),
         pltpu.VMEM((x_count, 24 * blocks_y, LANES), F32),
-    ] + product_scratch(x_count * blocks_y, listed)
+    ] + product_scratch(x_count * (blocks_y - 2), listed)
 
 
 def product_scratch(blocks, listed):
@@ -327,42 +318,49 @@
 
 
 def rim_kernel(
-    code_ref, middle_ref, edge_ref, middle_match_ref, edge_match_ref, mass_ref, smooth_ref,
+    code_ref, middle_ref, edge_ref, known_ref, pos_ref, mass_ref, smooth_ref,
     low_ref, high_ref, rows_ref, hot_ref, early_ref,
-    sum_ref, table_ref, nat_ref, md_ref, lhs_ref, row_sum_ref, near_ref, root_ref, total_ref,
+    sum_ref, table_ref, nat_ref, src_ref, md_ref, lhs_ref, row_sum_ref,
+    shift_ref, tgt_ref, mat_ref, near_ref, root_ref, total_ref,
 ):
     blocks_x, blocks_y, _ = mass_ref.shape
     owners = early_ref.shape[0]
     listed = code_ref.shape[0]
+    wide = blocks_x + 2
     for side, ref in enumerate((low_ref, high_ref)):
-        store_source(nat_ref, side * 64, blocks_x + 2, [ref[c] for c in range(3)], ref[3])
-    kind = lax.broadcasted_iota(jnp.int32, (8, LANES), 0)
+        store_source(nat_ref, side * 64, wide, [ref[c] for c in range(3)], ref[3])
+        for xe in range(wide):
+            ghost = 5 * side * wide + xe
+            src_ref[ghost] = nat_ref[pl.ds(side * 64 + xe, 8, stride=8), :]
+            for k in range(2):
+                y = k + side * (blocks_y - 2)
+                place = (1 + k + 2 * side) * wide + xe
+                src_ref[place] = known_ref[xe * blocks_y + y]
+    put_shifts(shift_ref)
     squares = square_mask()
-    sides = []
     for x in range(blocks_x):
         edge = x == 0 or x == blocks_x - 1
         turn = (1 if x else 0) if edge else x - 1
         sum_ref[x] = (edge_ref if edge else middle_ref)[turn]
+        lines = target_rows([pos_ref[c, x] for c in range(3)], smooth_ref[x])
+        for row, line in enumerate(lines):
+            tgt_ref[x, row * blocks_y : (row + 1) * blocks_y, :] = line
+    for x in range(blocks_x):
         for side in range(2):
             y = side * (blocks_y - 1)
-            number = 2 * x + side
-            for step_x in range(3):
-                wanted = step_x * 3 + side * 2
-                found = code_ref[0, x, y] == wanted
-                for k in range(1, listed):
-                    found = found | (code_ref[k, x, y] == wanted)
-                along_x = jnp.where((kind == 0) | (kind == 3), float(step_x - 1), 0.0)
-                along_y = jnp.where((kind == 1) | (kind == 4), float(side * 2 - 1), 0.0)
-                line = nat_ref[pl.ds(side * 64 + x + step_x, 8, stride=8), :]
-                root = jnp.broadcast_to(line[7:8], line.shape) * jnp.where(found, 1.0, 0.0)
-                near_ref[number, :, step_x * LANES : (step_x + 1) * LANES] = source_matrix(
-                    line + along_x + along_y, root, squares
-                )
-                root_ref[number, step_x : step_x + 1, :] = root[0:1]
-            match_ref = (edge_match_ref if edge else middle_match_ref).at[turn, side]
-            sides.append(
-                (match_ref, near_ref.at[number], root_ref.at[number, pl.ds(0, 3)], total_ref.at[number])
-            )
+            mat_ref[2 * x + side] = target_matrix(tgt_ref[x, pl.ds(y, 24, stride=blocks_y), :])
+    for x in range(blocks_x):
+        for side in range(2):
+            y = side * (blocks_y - 1)
+            for k in range(listed):
+                code = code_ref[k, x, y]
+                step_x = (code * 11) >> 5
+                line = src_ref[(3 * side + code - 3 * step_x) * wide + x + step_x]
+                put_source(near_ref, root_ref, 2 * x + side, k, line, shift_ref[code], squares)
+    sides = [
+        (mat_ref.at[n], near_ref.at[n], root_ref.at[n, pl.ds(0, listed)], total_ref.at[n])
+        for n in range(2 * blocks_x)
+    ]
     owner_ids = lax.broadcasted_iota(jnp.int32, (owners, LANES), 0)
     last = blocks_y - 1
 
@@ -395,7 +393,7 @@
     for x in range(blocks_x):
         for side in range(2):
             y = side * last
-            sum_ref[x, y : y + 1, :] += sums[2 * x + side : 2 * x + side + 1, :]
+            sum_ref[x, y : y + 1, :] = sums[2 * x + side : 2 * x + side + 1, :]
         put_moments(x, (0, last))
     ends = [(x, slice(y * LANES, (y + 1) * LANES)) for x in range(blocks_x) for y in (0, last)]
     total = row_sum_ref[...] + lax.dot_general(
@@ -455,8 +453,12 @@
     count = lax.axis_size(axis)
     if count & (count - 1):
         return lax.psum(value, axis)
-    copies = jnp.broadcast_to(value[None], (count,) + value.shape)
-    return added(list(lax.all_to_all(copies, axis, split_axis=0, concat_axis=0, tiled=True)))
+    step = 1
+    while step < count:
+        ways = min(4, count // step)
+        value = added([value] + [swap(value, axis, k * step) for k in range(1, ways)])
+        step *= ways
+    return value
 
 
 def shards(positions, velocities, masses, smoothing, neighbours, particle_group, group_row):
@@ -466,57 +468,65 @@
     chunk = blocks_y * block_len
     shape = jax.ShapeDtypeStruct
     codes = neighbours.transpose(2, 0, 1)
+    table_rows = group_row.reshape(-1, LANES)
     packed = jnp.concatenate([positions, masses[None]], axis=0)
     prev, following = neighbours_of(
         packed[:, 0], packed[:, blocks_x - 1], "dom", lax.axis_index("dom") & 1
     )
-    columns, middle, middle_match = pl.pallas_call(
+    sources = ((blocks_x + 2) * blocks_y, 8, LANES)
+    columns, middle = pl.pallas_call(
         middle_kernel,
         out_shape=(
             shape((2, 4, blocks_x, LANES), F32),
             shape((blocks_x - 2, blocks_y, LANES), F32),
-            shape((blocks_x - 2, 2, LANES, 48), BF16),
         ),
-        in_specs=[SMEM] + [VMEM] * 3,
-        out_specs=(VMEM,) * 3,
-        scratch_shapes=pair_scratch(blocks_x, blocks_y, blocks_x - 2, codes.shape[0]),
+        in_specs=[SMEM] + [VMEM] * 5,
+        out_specs=(VMEM,) * 2,
+        scratch_shapes=[pltpu.VMEM(sources, F32)]
+        + pair_scratch(blocks_x, blocks_y, blocks_x - 2, codes.shape[0]),
         compiler_params=params(),
         cost_estimate=pl.CostEstimate(
             flops=4_000_000_000, bytes_accessed=400_000, transcendentals=1_300_000
         ),
         name="middle_pairs",
-    )(codes, positions, masses, smoothing)
+    )(codes, positions, masses, smoothing, particle_group, table_rows)
+    early, rows, hot = pl.pallas_call(
+        functools.partial(moments_kernel, blocks_x * dom_count, blocks_y * sub_count),
+        out_shape=(
+            shape((owners, EARLY, LANES), F32),
+            shape(masses.shape, jnp.int32),
+            shape((blocks_x, LANES, chunk), BF16),
+        ),
+        in_specs=[VMEM] * 6,
+        out_specs=(VMEM,) * 3,
+        scratch_shapes=[
+            pltpu.VMEM((blocks_x * EARLY * blocks_y, LANES), F32),
+            pltpu.VMEM((blocks_x, owners * 2 * EARLY, chunk), BF16),
+            pltpu.VMEM((owners * 2 * EARLY, LANES), F32),
+        ],
+        compiler_params=params(),
+        cost_estimate=pl.CostEstimate(
+            flops=2_000_000_000, bytes_accessed=1_400_000, transcendentals=0
+        ),
+        name="moments_by_row",
+    )(middle, positions, velocities, masses, particle_group, table_rows)
     edges = [
         jnp.concatenate([prev[:, y : y + 1], columns[side], following[:, y : y + 1]], axis=1)
         for side, y in ((0, 0), (1, blocks_y - 1))
     ]
     low, high = neighbours_of(*edges, ("chip", "core"), lax.axis_index("core"))
-    edge, edge_match, early, rows, hot = pl.pallas_call(
-        functools.partial(edge_kernel, blocks_x * dom_count, blocks_y * sub_count),
-        out_shape=(
-            shape((2, blocks_y, LANES), F32),
-            shape((2, 2, LANES, 48), BF16),
-            shape((owners, EARLY, LANES), F32),
-            shape(masses.shape, jnp.int32),
-            shape((blocks_x, LANES, chunk), BF16),
-        ),
-        in_specs=[SMEM] + [VMEM] * 8,
-        out_specs=(VMEM,) * 5,
-        scratch_shapes=[
-            pltpu.VMEM((blocks_x * EARLY * blocks_y, LANES), F32),
-            pltpu.VMEM((blocks_x, owners * 2 * EARLY, chunk), BF16),
-            pltpu.VMEM((owners * 2 * EARLY, LANES), F32),
-        ]
-        + pair_scratch(blocks_x, blocks_y, 2, codes.shape[0]),
+    edge, known = pl.pallas_call(
+        edge_kernel,
+        out_shape=(shape((2, blocks_y, LANES), F32), shape(sources, F32)),
+        in_specs=[SMEM] + [VMEM] * 5,
+        out_specs=(VMEM,) * 2,
+        scratch_shapes=pair_scratch(blocks_x, blocks_y, 2, codes.shape[0]),
         compiler_params=params(),
         cost_estimate=pl.CostEstimate(
-            flops=5_000_000_000, bytes_accessed=1_400_000, transcendentals=1_300_000
+            flops=4_000_000_000, bytes_accessed=400_000, transcendentals=1_300_000
         ),
-        name="edge_pairs_and_moments",
-    )(
-        codes, positions, masses, smoothing, prev, following,
-        velocities, particle_group, group_row.reshape(-1, LANES),
-    )
+        name="edge_pairs",
+    )(codes, positions, masses, smoothing, prev, following)
     sums, table = pl.pallas_call(
         rim_kernel,
         out_shape=(shape(masses.shape, F32), shape((2, owners // 2, EARLY + 1, LANES), F32)),
@@ -524,18 +534,21 @@
         out_specs=(VMEM, VMEM),
         scratch_shapes=[
             pltpu.VMEM((128, LANES), F32),
+            pltpu.VMEM((6 * (blocks_x + 2), 8, LANES), F32),
             pltpu.VMEM((owners, LANES), F32),
             pltpu.VMEM((blocks_x, 2 * owners, chunk), BF16),
             pltpu.VMEM((LANES, 2 * owners), F32),
+            pltpu.VMEM((9, 8, LANES), F32),
+            pltpu.VMEM((blocks_x, 24 * blocks_y, LANES), F32),
         ]
-        + product_scratch(2 * blocks_x, 3)[1:],
+        + product_scratch(2 * blocks_x, codes.shape[0]),
         compiler_params=params(),
         cost_estimate=pl.CostEstimate(
             flops=200_000_000, bytes_accessed=400_000, transcendentals=400_000
         ),
         name="rim_pairs_and_table",
     )(
-        codes, middle, edge, middle_match, edge_match, masses, smoothing, low, high, rows, hot, early
+        codes, middle, edge, known, positions, masses, smoothing, low, high, rows, hot, early
     )
     density = sums * DENSITY_FACTOR / (smoothing * smoothing * smoothing)
     return (density, summed(to_owner(table), "dom"))

time: 36.7 us -> 33.2 us (0.905)
  waiting for transfers between devices: 8.73 us -> 5.57 us
  starting transfers between devices: 14.6 us -> 15.8 us
  Pallas kernels: 9.43 us -> 8.77 us
  local copies, waits for them, and re-layouts: 0.68 us -> 0.06 us
    all_to_all x1 -> x0, waiting for transfers between devices: 5.05 us -> none  [summed(): lax.all_to_all(copies, axis, split_axis=0, concat_axis=0, tiled=True)]
    ppermute x4 -> x7, starting transfers between devices: 3.62 us -> 8.01 us  [swap(): return lax.ppermute(value, axis, [(i, i ^ step) for i in range(count)])]
    all_to_all x1 -> x0, starting transfers between devices: 3.27 us -> none  [summed(): lax.all_to_all(copies, axis, split_axis=0, concat_axis=0, tiled=True)]
    ppermute x4 -> x7, waiting for transfers between devices: 3.16 us -> 5.56 us  [swap(): return lax.ppermute(value, axis, [(i, i ^ step) for i in range(count)])]
    pallas_call x1 -> x2, Pallas kernels: 4.26 us -> 3.64 us  [the longest x1 2.61 us: shards(): pl.pallas_call(edge_kernel, out_shape=(shape((2, blocks_y, LANES), F32),...]
    broadcast_in_dim x1 -> x0, local copies, waits for them, and re-layouts: 0.62 us -> none  [summed(): copies = jnp.broadcast_to(value[None], (count,) + value.shape)]
    pallas_call x1, Pallas kernels: 3.19 us -> 2.62 us  [shards(): pl.pallas_call(middle_kernel, out_shape=(shape((2, 4, blocks_x, LANES), F...]
    pallas_call x1, Pallas kernels: 1.98 us -> 2.5 us  [shards(): pl.pallas_call(rim_kernel, out_shape=(shape(masses.shape, F32), shape((2,...]
  transfers between devices with their start and end apart: 9 -> 11, of which waited for: 5 -> 7; matrix products, arithmetic and copies ran while one was open for 2% -> 2% of each run, Pallas kernels for 21% -> 19%
where the time goes in v1:
time: 33.2 us; the launch traced here: 33 us
  starting transfers between devices  15.8 us (48%)
  Pallas kernels  8.77 us (26%)
  waiting for transfers between devices  5.57 us (17%)
  other arithmetic  2.07 us (6%)
  between operations  0.83 us (2%)
    ppermute x7, starting transfers between devices, swap(): return lax.ppermute(value, axis, [(i, i ^ step) for i in range(count)])  8.01 us
    ppermute x2, starting transfers between devices, neighbours_of(): lax.ppermute(jnp.where(even, low_edge, high_edge), axis, [(i, (i + 1 if i...  7.67 us
    ppermute x7, waiting for transfers between devices, swap(): return lax.ppermute(value, axis, [(i, i ^ step) for i in range(count)])  5.56 us
    pallas_call x1, Pallas kernels, shards(): pl.pallas_call(middle_kernel, out_shape=(shape((2, 4, blocks_x, LANES), F...  2.62 us
    pallas_call x1, Pallas kernels, shards(): pl.pallas_call(edge_kernel, out_shape=(shape((2, blocks_y, LANES), F32),...  2.61 us
    pallas_call x1, Pallas kernels, shards(): pl.pallas_call(rim_kernel, out_shape=(shape(masses.shape, F32), shape((2,...  2.5 us
    pallas_call x1, Pallas kernels, shards(): pl.pallas_call(functools.partial(moments_kernel, blocks_x * dom_count, bl...  1.03 us
    select_n x2, other arithmetic, neighbours_of(): jnp.where(even, high_edge, low_edge)  0.8 us
  transfers between devices with their start and end apart: 11, of which 7 were waited for; matrix products, arithmetic and copies ran while one was open for 2% of the time, Pallas kernels for 19%

profile of v1, /device:TPU:0, one launch (start us, length us, event | category | flops | bytes accessed | tf_op | source)
XLA Modules:
  0.0 33.0 jit_solution(9336172394146532616)
XLA Ops:
  0.6 0.0 copy-start.1
  0.6 0.0 copy-start.2
  0.7 0.0 copy-start.3
  0.7 0.0 copy-start.5
  0.7 0.8 %select_bitcast_fusion = (f32[4,8,128]{2,1,0:T(8,128)S(1)}, f32[4,1,8,128]{3,2,0,1:T(8,128)S(1)}, f32[4,1,8,128]{3,2,0,1:T(8,128)S(1)}) fusion(pred[]{:T(512)S(6)} %eq.6, f32[1,4,8,128]{3,2,0,1:T(8,128)} %bitcast.17, f32[3,4,8,128]{3,2,1,0:T(8,128)} %pos_ref.7), kind=kLoop, calls=%fused_computation.8 | loop fusion | flops 12288 | bytes 114689 | tf_op jit(solution)/shard_map/jit(_where)/select_n | solution.py:424
  1.5 0.0 copy-start
  1.5 0.0 copy-start.6
  1.5 5.1 %collective-permute-start = (f32[4,8,128]{2,1,0:T(8,128)S(1)}, f32[4,8,128]{2,1,0:T(8,128)S(1)}, u32[]{:S(2)}, u32[]{:S(2)}) collective-permute-start(f32[4,8,128]{2,1,0:T(8,128)S(1)} %select_bitcast_fusion.1), channel_id=1, source_target_pairs={{0,24},{8,16},{16,8},{24,0},{1,25},{9,17},{17,9},{25,1},{2,26},{10... | collective-permute-start | bytes 49160 | tf_op jit(solution)/shard_map/ppermute | solution.py:426
  6.6 0.0 collective-permute-start.1
  6.6 0.0 copy-done.1
  6.6 0.0 copy-done.2
  6.6 0.0 copy-done.3
  6.6 0.0 copy-done.5
  6.6 0.0 copy-done
  6.6 0.0 copy-done.6
  6.7 0.0 copy-start.4
  6.7 2.6 %middle_pairs.1 = (f32[2,4,4,128]{3,2,1,0:T(4,128)S(1)}, f32[2,8,128]{2,1,0:T(8,128)S(1)}) custom-call(s32[5,4,8]{2,1,0:T(4,128)S(1)} %bitcast.18, f32[3,4,8,128]{3,2,1,0:T(8,128)S(1)} %copy-done, f32[4,8,128]{2,1,0:T(8,128)S(1)} %copy-done.1, f32[4,8,128]{2,1,0:T(8,128)S(1)} %copy-done.2, s32[4,8,128]{2,1,0:T(8,128)S(1)} %copy-done.5, s32[8,128]{1,0:T(8,128)S(1)} %bitcast.21), custom_call_target="tpu_custom_call" | custom-call | flops 4000000000 | bytes 400000 | tf_op jit(solution)/shard_map/middle_pairs/pallas_call | solution.py:477
  9.3 0.0 copy-done.4
  9.3 1.0 %moments_by_row.1 = (f32[8,16,128]{2,1,0:T(8,128)S(1)}, s32[4,8,128]{2,1,0:T(8,128)S(1)}, bf16[4,128,1024]{2,1,0:T(8,128)(2,1)S(1)}) custom-call(f32[2,8,128]{2,1,0:T(8,128)S(1)} %get-tuple-element.11.after_ref.middle_ref, f32[3,4,8,128]{3,2,1,0:T(8,128)S(1)} %copy-done, f32[3,4,8,128]{3,2,1,0:T(8,128)S(1)} %copy-done.4, f32[4,8,128]{2,1,0:T(8,128)S(1)} %copy-done.1, ...), custom_call_target="tpu_custom_call" | custom-call | flops 2000000000 | bytes 1400000 | tf_op jit(solution)/shard_map/moments_by_row/pallas_call | solution.py:493
  10.3 0.0 collective-permute-done
  10.3 0.0 collective-permute-done.1
  10.4 0.1 collective-permute-start.3
  10.5 2.6 %collective-permute-start.2 = (f32[4,6,128]{2,1,0:T(8,128)S(1)}, f32[4,6,128]{2,1,0:T(8,128)S(1)}, u32[]{:S(2)}, u32[]{:S(2)}) collective-permute-start(f32[4,6,128]{2,1,0:T(8,128)S(1)} %get-tuple-element.31), channel_id=1, source_target_pairs={{0,7},{1,2},{2,1},{3,4},{4,3},{5,6},{6,5},{7,0},{8,15},{9,10},{10,... | collective-permute-start | bytes 36872 | tf_op jit(solution)/shard_map/ppermute | solution.py:426
  13.0 2.6 %edge_pairs.1 = (f32[2,8,128]{2,1,0:T(8,128)S(1)}, f32[48,8,128]{2,1,0:T(8,128)S(1)}) custom-call(s32[5,4,8]{2,1,0:T(4,128)S(1)} %bitcast.19, f32[3,4,8,128]{3,2,1,0:T(8,128)S(1)} %copy-done, f32[4,8,128]{2,1,0:T(8,128)S(1)} %copy-done.1, f32[4,8,128]{2,1,0:T(8,128)S(1)} %copy-done.2, f32[4,8,128]{2,1,0:T(8,128)S(1)} %get-tuple-element.29.prev_ref, ...), custom_call_target="tpu_custom_call" | custom-call | flops 4000000000 | bytes 400000 | tf_op jit(solution)/shard_map/edge_pairs/pallas_call | solution.py:518
  15.7 0.0 collective-permute-done.3
  15.7 0.0 collective-permute-done.2
  15.7 2.5 %rim_pairs_and_table.1 = (f32[4,8,128]{2,1,0:T(8,128)S(1)}, f32[2,4,17,128]{3,2,1,0:T(8,128)S(1)}) custom-call(s32[5,4,8]{2,1,0:T(4,128)S(1)} %bitcast.20, f32[2,8,128]{2,1,0:T(8,128)S(1)} %get-tuple-element.11.after_ref.middle_ref, f32[2,8,128]{2,1,0:T(8,128)S(1)} %get-tuple-element.12.edge_ref, f32[48,8,128]{2,1,0:T(8,128)S(1)} %get-tuple-element.13.known_ref, ...), custom_call_target="tpu_custom_call" | custom-call | flops 200000000 | bytes 400000 | tf_op jit(solution)/shard_map/rim_pairs_and_table/pallas_call | solution.py:530
  18.2 0.1 collective-permute-start.4
  18.3 1.2 %collective-permute-done.4 = f32[4,17,128]{2,1,0:T(8,128)S(1)} collective-permute-done((f32[4,17,128]{2,1,0:T(8,128)S(1)}, f32[4,17,128]{2,1,0:T(8,128)S(1)}, u32[]{:S(2)}, u32[]{:S(2)}) %collective-permute-start.4) | collective-permute-done | bytes 34848 | tf_op jit(solution)/shard_map/ppermute | solution.py:417
  19.5 1.5 %collective-permute-start.7 = (f32[1,17,128]{2,1,0:T(8,128)S(1)}, f32[1,17,128]{2,1,0:T(8,128)S(1)}, u32[]{:S(2)}, u32[]{:S(2)}) collective-permute-start(f32[1,17,128]{2,1,0:T(8,128)S(1)} %get-tuple-element.23), channel_id=1, source_target_pairs={{0,6},{2,4},{4,2},{6,0},{1,7},{3,5},{5,3},{7,1},{8,14},{10,12},{12... | collective-permute-start | bytes 26120 | tf_op jit(solution)/shard_map/ppermute | solution.py:417
  21.1 0.5 %collective-permute-start.6 = (f32[1,17,128]{2,1,0:T(8,128)S(1)}, f32[1,17,128]{2,1,0:T(8,128)S(1)}, u32[]{:S(2)}, u32[]{:S(2)}) collective-permute-start(f32[1,17,128]{2,1,0:T(8,128)S(1)} %get-tuple-element.24), channel_id=1, source_target_pairs={{0,4},{2,6},{4,0},{6,2},{1,5},{3,7},{5,1},{7,3},{8,12},{10,14},{12... | collective-permute-start | bytes 26120 | tf_op jit(solution)/shard_map/ppermute | solution.py:417
  21.6 1.5 %collective-permute-start.5 = (f32[1,17,128]{2,1,0:T(8,128)S(1)}, f32[1,17,128]{2,1,0:T(8,128)S(1)}, u32[]{:S(2)}, u32[]{:S(2)}) collective-permute-start(f32[1,17,128]{2,1,0:T(8,128)S(1)} %get-tuple-element.25), channel_id=1, source_target_pairs={{0,2},{2,0},{4,6},{6,4},{1,3},{3,1},{5,7},{7,5},{8,10},{10,8},{12,... | collective-permute-start | bytes 26120 | tf_op jit(solution)/shard_map/ppermute | solution.py:417
  23.1 1.1 %collective-permute-done.7 = f32[1,17,128]{2,1,0:T(8,128)S(1)} collective-permute-done((f32[1,17,128]{2,1,0:T(8,128)S(1)}, f32[1,17,128]{2,1,0:T(8,128)S(1)}, u32[]{:S(2)}, u32[]{:S(2)}) %collective-permute-start.7) | collective-permute-done | bytes 8736 | tf_op jit(solution)/shard_map/ppermute | solution.py:417
  24.2 0.6 %collective-permute-done.6 = f32[1,17,128]{2,1,0:T(8,128)S(1)} collective-permute-done((f32[1,17,128]{2,1,0:T(8,128)S(1)}, f32[1,17,128]{2,1,0:T(8,128)S(1)}, u32[]{:S(2)}, u32[]{:S(2)}) %collective-permute-start.6) | collective-permute-done | bytes 8736 | tf_op jit(solution)/shard_map/ppermute | solution.py:417
  24.8 0.5 %collective-permute-done.5 = f32[1,17,128]{2,1,0:T(8,128)S(1)} collective-permute-done((f32[1,17,128]{2,1,0:T(8,128)S(1)}, f32[1,17,128]{2,1,0:T(8,128)S(1)}, u32[]{:S(2)}, u32[]{:S(2)}) %collective-permute-start.5) | collective-permute-done | bytes 8736 | tf_op jit(solution)/shard_map/ppermute | solution.py:417
  25.3 1.8 %collective-permute-start.10 = (f32[17,128]{1,0:T(8,128)S(1)}, f32[17,128]{1,0:T(8,128)S(1)}, u32[]{:S(2)}, u32[]{:S(2)}) collective-permute-start(f32[17,128]{1,0:T(8,128)S(1)} %fusion.4), channel_id=1, source_target_pairs={{0,24},{8,16},{16,8},{24,0},{1,25},{9,17},{17,9},{25,1},{2,26},{10... | collective-permute-start | bytes 26120 | tf_op jit(solution)/shard_map/ppermute | solution.py:417
  27.0 1.7 %collective-permute-start.9 = (f32[17,128]{1,0:T(8,128)S(1)}, f32[17,128]{1,0:T(8,128)S(1)}, u32[]{:S(2)}, u32[]{:S(2)}) collective-permute-start(f32[17,128]{1,0:T(8,128)S(1)} %fusion.4), channel_id=1, source_target_pairs={{0,16},{8,24},{16,0},{24,8},{1,17},{9,25},{17,1},{25,9},{2,18},{10... | collective-permute-start | bytes 26120 | tf_op jit(solution)/shard_map/ppermute | solution.py:417
  28.7 0.9 %collective-permute-start.8 = (f32[17,128]{1,0:T(8,128)S(1)}, f32[17,128]{1,0:T(8,128)S(1)}, u32[]{:S(2)}, u32[]{:S(2)}) collective-permute-start(f32[17,128]{1,0:T(8,128)S(1)} %fusion.4), channel_id=1, source_target_pairs={{0,8},{8,0},{16,24},{24,16},{1,9},{9,1},{17,25},{25,17},{2,10},{10... | collective-permute-start | bytes 26120 | tf_op jit(solution)/shard_map/ppermute | solution.py:417
  29.7 0.6 %fusion = f32[4,8,128]{2,1,0:T(8,128)} fusion(f32[4,8,128]{2,1,0:T(8,128)S(1)} %copy-done.2, f32[4,8,128]{2,1,0:T(8,128)S(1)} %get-tuple-element.18), kind=kLoop, calls=%fused_computation.3 | loop fusion | flops 16384 | bytes 49152 | tf_op jit(solution)/shard_map/div | solution.py:553
  30.3 0.5 %collective-permute-done.10 = f32[17,128]{1,0:T(8,128)S(1)} collective-permute-done((f32[17,128]{1,0:T(8,128)S(1)}, f32[17,128]{1,0:T(8,128)S(1)}, u32[]{:S(2)}, u32[]{:S(2)}) %collective-permute-start.10) | collective-permute-done | bytes 8736 | tf_op jit(solution)/shard_map/ppermute | solution.py:417
  30.8 0.9 %collective-permute-done.9 = f32[17,128]{1,0:T(8,128)S(1)} collective-permute-done((f32[17,128]{1,0:T(8,128)S(1)}, f32[17,128]{1,0:T(8,128)S(1)}, u32[]{:S(2)}, u32[]{:S(2)}) %collective-permute-start.9) | collective-permute-done | bytes 8736 | tf_op jit(solution)/shard_map/ppermute | solution.py:417
  31.6 0.8 %collective-permute-done.8 = f32[17,128]{1,0:T(8,128)S(1)} collective-permute-done((f32[17,128]{1,0:T(8,128)S(1)}, f32[17,128]{1,0:T(8,128)S(1)}, u32[]{:S(2)}, u32[]{:S(2)}) %collective-permute-start.8) | collective-permute-done | bytes 8736 | tf_op jit(solution)/shard_map/ppermute | solution.py:417
  32.4 0.6 %add_add_fusion = f32[17,128]{1,0:T(8,128)} fusion(f32[17,128]{1,0:T(8,128)S(1)} %collective-permute-done.9, f32[17,128]{1,0:T(8,128)S(1)} %collective-permute-done.10, f32[17,128]{1,0:T(8,128)S(1)} %fusion.4, f32[17,128]{1,0:T(8,128)S(1)} %collective-permute-done.8), kind=kLoop, calls=%fused_computation.15 | loop fusion | flops 6528 | bytes 43520 | tf_op jit(solution)/shard_map/add | solution.py:436
  (10 shorter events, 0.1 us)
Async XLA Ops:
  0.6 6.0 %copy-start.1 = (f32[4,8,128]{2,1,0:T(8,128)S(1)}, f32[4,8,128]{2,1,0:T(8,128)}, u32[]{:S(2)}) copy-start(f32[4,8,128]{2,1,0:T(8,128)} %mass_ref.7) | copy-start | bytes 49156
  0.6 6.0 %copy-start.2 = (f32[4,8,128]{2,1,0:T(8,128)S(1)}, f32[4,8,128]{2,1,0:T(8,128)}, u32[]{:S(2)}) copy-start(f32[4,8,128]{2,1,0:T(8,128)} %smooth_ref.5) | copy-start | bytes 49156
  0.7 6.0 %copy-start.3 = (s32[4,8,5]{1,0,2:T(4,128)S(1)}, s32[4,8,5]{1,0,2:T(4,128)}, u32[]{:S(2)}) copy-start(s32[4,8,5]{1,0,2:T(4,128)} %param.11) | copy-start | bytes 1924
  0.7 6.0 %copy-start.5 = (s32[4,8,128]{2,1,0:T(8,128)S(1)}, s32[4,8,128]{2,1,0:T(8,128)}, u32[]{:S(2)}) copy-start(s32[4,8,128]{2,1,0:T(8,128)} %group_ref.3) | copy-start | bytes 49156
  1.5 5.2 %copy-start = (f32[3,4,8,128]{3,2,1,0:T(8,128)S(1)}, f32[3,4,8,128]{3,2,1,0:T(8,128)}, u32[]{:S(2)}) copy-start(f32[3,4,8,128]{3,2,1,0:T(8,128)} %pos_ref.7) | copy-start | bytes 147460
  1.5 5.2 %copy-start.6 = (s32[1024]{0:T(1024)S(1)}, s32[1024]{0:T(1024)}, u32[]{:S(2)}) copy-start(s32[1024]{0:T(1024)} %param.13) | copy-start | bytes 12292
  1.5 8.9 %collective-permute-start = (f32[4,8,128]{2,1,0:T(8,128)S(1)}, f32[4,8,128]{2,1,0:T(8,128)S(1)}, u32[]{:S(2)}, u32[]{:S(2)}) collective-permute-start(f32[4,8,128]{2,1,0:T(8,128)S(1)} %select_bitcast_fusion.1), channel_id=1, source_target_pairs={{0,24},{8,16},{16,8},{24,0},{1,25},{9,17},{17,9},{25,1},{2,26},{10... | collective-permute-start | bytes 49160 | tf_op jit(solution)/shard_map/ppermute | solution.py:426
  6.6 3.7 %collective-permute-start.1 = (f32[4,8,128]{2,1,0:T(8,128)S(1)}, f32[4,8,128]{2,1,0:T(8,128)S(1)}, u32[]{:S(2)}, u32[]{:S(2)}) collective-permute-start(f32[4,8,128]{2,1,0:T(8,128)S(1)} %get-tuple-element.20), channel_id=1, source_target_pairs={{0,8},{8,0},{16,24},{24,16},{1,9},{9,1},{17,25},{25,17},{2,10},{10... | collective-permute-start | bytes 49160 | tf_op jit(solution)/shard_map/ppermute | solution.py:423
  6.7 2.6 %copy-start.4 = (f32[3,4,8,128]{3,2,1,0:T(8,128)S(1)}, f32[3,4,8,128]{3,2,1,0:T(8,128)}, u32[]{:S(2)}) copy-start(f32[3,4,8,128]{3,2,1,0:T(8,128)} %vel_ref.1) | copy-start | bytes 147460
  10.4 5.2 %collective-permute-start.3 = (f32[4,6,128]{2,1,0:T(8,128)S(1)}, f32[4,6,128]{2,1,0:T(8,128)S(1)}, u32[]{:S(2)}, u32[]{:S(2)}) collective-permute-start(f32[4,6,128]{2,1,0:T(8,128)S(1)} %get-tuple-element.30), channel_id=1, source_target_pairs={{0,1},{1,0},{2,3},{3,2},{4,5},{5,4},{6,7},{7,6},{8,9},{9,8},{10,11... | collective-permute-start | bytes 36872 | tf_op jit(solution)/shard_map/ppermute | solution.py:423
  10.5 5.2 %collective-permute-start.2 = (f32[4,6,128]{2,1,0:T(8,128)S(1)}, f32[4,6,128]{2,1,0:T(8,128)S(1)}, u32[]{:S(2)}, u32[]{:S(2)}) collective-permute-start(f32[4,6,128]{2,1,0:T(8,128)S(1)} %get-tuple-element.31), channel_id=1, source_target_pairs={{0,7},{1,2},{2,1},{3,4},{4,3},{5,6},{6,5},{7,0},{8,15},{9,10},{10,... | collective-permute-start | bytes 36872 | tf_op jit(solution)/shard_map/ppermute | solution.py:426
  18.2 1.3 %collective-permute-start.4 = (f32[4,17,128]{2,1,0:T(8,128)S(1)}, f32[4,17,128]{2,1,0:T(8,128)S(1)}, u32[]{:S(2)}, u32[]{:S(2)}) collective-permute-start(f32[4,17,128]{2,1,0:T(8,128)S(1)} %slice_bitcast_fusion), channel_id=1, source_target_pairs={{0,1},{1,0},{2,3},{3,2},{4,5},{5,4},{6,7},{7,6},{8,9},{9,8},{10,11... | collective-permute-start | bytes 104456 | tf_op jit(solution)/shard_map/ppermute | solution.py:417
  19.5 4.7 %collective-permute-start.7 = (f32[1,17,128]{2,1,0:T(8,128)S(1)}, f32[1,17,128]{2,1,0:T(8,128)S(1)}, u32[]{:S(2)}, u32[]{:S(2)}) collective-permute-start(f32[1,17,128]{2,1,0:T(8,128)S(1)} %get-tuple-element.23), channel_id=1, source_target_pairs={{0,6},{2,4},{4,2},{6,0},{1,7},{3,5},{5,3},{7,1},{8,14},{10,12},{12... | collective-permute-start | bytes 26120 | tf_op jit(solution)/shard_map/ppermute | solution.py:417
  21.1 3.7 %collective-permute-start.6 = (f32[1,17,128]{2,1,0:T(8,128)S(1)}, f32[1,17,128]{2,1,0:T(8,128)S(1)}, u32[]{:S(2)}, u32[]{:S(2)}) collective-permute-start(f32[1,17,128]{2,1,0:T(8,128)S(1)} %get-tuple-element.24), channel_id=1, source_target_pairs={{0,4},{2,6},{4,0},{6,2},{1,5},{3,7},{5,1},{7,3},{8,12},{10,14},{12... | collective-permute-start | bytes 26120 | tf_op jit(solution)/shard_map/ppermute | solution.py:417
  21.6 3.7 %collective-permute-start.5 = (f32[1,17,128]{2,1,0:T(8,128)S(1)}, f32[1,17,128]{2,1,0:T(8,128)S(1)}, u32[]{:S(2)}, u32[]{:S(2)}) collective-permute-start(f32[1,17,128]{2,1,0:T(8,128)S(1)} %get-tuple-element.25), channel_id=1, source_target_pairs={{0,2},{2,0},{4,6},{6,4},{1,3},{3,1},{5,7},{7,5},{8,10},{10,8},{12,... | collective-permute-start | bytes 26120 | tf_op jit(solution)/shard_map/ppermute | solution.py:417
  25.3 5.5 %collective-permute-start.10 = (f32[17,128]{1,0:T(8,128)S(1)}, f32[17,128]{1,0:T(8,128)S(1)}, u32[]{:S(2)}, u32[]{:S(2)}) collective-permute-start(f32[17,128]{1,0:T(8,128)S(1)} %fusion.4), channel_id=1, source_target_pairs={{0,24},{8,16},{16,8},{24,0},{1,25},{9,17},{17,9},{25,1},{2,26},{10... | collective-permute-start | bytes 26120 | tf_op jit(solution)/shard_map/ppermute | solution.py:417
  27.0 4.6 %collective-permute-start.9 = (f32[17,128]{1,0:T(8,128)S(1)}, f32[17,128]{1,0:T(8,128)S(1)}, u32[]{:S(2)}, u32[]{:S(2)}) collective-permute-start(f32[17,128]{1,0:T(8,128)S(1)} %fusion.4), channel_id=1, source_target_pairs={{0,16},{8,24},{16,0},{24,8},{1,17},{9,25},{17,1},{25,9},{2,18},{10... | collective-permute-start | bytes 26120 | tf_op jit(solution)/shard_map/ppermute | solution.py:417
  28.7 3.7 %collective-permute-start.8 = (f32[17,128]{1,0:T(8,128)S(1)}, f32[17,128]{1,0:T(8,128)S(1)}, u32[]{:S(2)}, u32[]{:S(2)}) collective-permute-start(f32[17,128]{1,0:T(8,128)S(1)} %fusion.4), channel_id=1, source_target_pairs={{0,8},{8,0},{16,24},{24,16},{1,9},{9,1},{17,25},{25,17},{2,10},{10... | collective-permute-start | bytes 26120 | tf_op jit(solution)/shard_map/ppermute | solution.py:417

commit v2 on v1

--- a/solution.py
+++ b/solution.py
@@ -14,7 +14,7 @@
 EARLY = 16
 DENSITY_FACTOR = 21.0 / (16.0 * math.pi) / 256.0
 VMEM = pl.BlockSpec(memory_space=pltpu.VMEM)
-SMEM = pl.BlockSpec(memory_space=pltpu.SMEM)
+ANY = pl.BlockSpec(memory_space=pl.ANY)
 NT = (((1,), (1,)), ((), ()))
 
 
@@ -193,7 +193,7 @@
         if first + width == count:
             for r, chunk in enumerate(chunks):
                 total[r * rows : (r + 1) * rows, :] = chunk
-        if number < len(pieces):
+        if number < len(pieces) and pieces[number] is not None:
             pieces[number]()
     for piece in pieces[len(steps) :]:
         piece()
@@ -229,21 +229,32 @@
     root_ref[number, k : k + 1, :] = root[0:1]
 
 
+def load_codes(far_ref, code_ref, sem):
+    copy = pltpu.make_async_copy(far_ref, code_ref, sem)
+    copy.start()
+    return copy
+
+
 def block_pairs(
-    x_first, x_step, x_count, code_ref, pos_ref, mass_ref, smooth_ref, prev_ref, next_ref,
-    out_ref, src_ref, nat_ref, shift_ref, tgt_ref, mat_ref, near_ref, root_ref, total_ref,
+    x_first, x_step, x_count, known_ref, far_code_ref, pos_ref, mass_ref, smooth_ref, prev_ref, next_ref,
+    out_ref, src_ref, code_ref, sem, nat_ref, shift_ref, tgt_ref, mat_ref, near_ref, root_ref, total_ref,
 ):
     blocks_x, blocks_y, _ = mass_ref.shape
     listed = code_ref.shape[0]
+    codes = load_codes(far_code_ref, code_ref, sem)
     for xe in range(blocks_x + 2):
         if xe == 0 or xe == blocks_x + 1:
             ref = prev_ref if xe == 0 else next_ref
             if ref is None:
                 continue
             store_source(nat_ref, xe * 64, blocks_y, [ref[c] for c in range(3)], ref[3])
-        else:
+        elif known_ref is None:
             columns = [pos_ref[c, xe - 1] for c in range(3)]
             store_source(nat_ref, xe * 64, blocks_y, columns, mass_ref[xe - 1])
+        else:
+            part = pl.ds(xe * blocks_y, blocks_y)
+            src_ref[part] = known_ref[part]
+            continue
         for y in range(blocks_y):
             src_ref[xe * blocks_y + y] = nat_ref[pl.ds(xe * 64 + y, 8, stride=8), :]
     put_shifts(shift_ref)
@@ -256,6 +267,7 @@
             tgt_ref[turn, row * blocks_y : (row + 1) * blocks_y, :] = line
     for number, (turn, y) in enumerate(blocks):
         mat_ref[number] = target_matrix(tgt_ref[turn, pl.ds(y, 24, stride=blocks_y), :])
+    codes.wait()
     for number, (turn, y) in enumerate(blocks):
         x = x_first + turn * x_step
         for k in range(listed):
@@ -263,20 +275,27 @@
             step_x = (code * 11) >> 5
             line = src_ref[(x + step_x) * blocks_y + y + code - 3 * step_x - 1]
             put_source(near_ref, root_ref, number, k, line, shift_ref[code], squares)
+    inner = blocks_y - 2
+    per_row = inner * ((listed + 1) // 2)
+
+    def row_sums(turn):
+        sums = column_sums([total_ref[turn * inner + k] for k in range(inner)])
+        out_ref[turn, 1 : blocks_y - 1, :] = sums
+
+    pieces = [None] * (x_count * per_row + 1)
+    for turn in range(x_count):
+        pieces[(turn + 1) * per_row] = functools.partial(row_sums, turn)
     pair_sums(
         [
             (mat_ref.at[n], near_ref.at[n], root_ref.at[n, pl.ds(0, listed)], total_ref.at[n])
             for n in range(len(blocks))
-        ]
-    )
-    inner = blocks_y - 2
-    for turn in range(x_count):
-        sums = column_sums([total_ref[turn * inner + k] for k in range(inner)])
-        out_ref[turn, 1 : blocks_y - 1, :] = sums
+        ],
+        pieces,
+    )
 
 
 def middle_kernel(
-    code_ref, pos_ref, mass_ref, smooth_ref, group_ref, row_ref, column_ref, out_ref, *scratch
+    code_ref, pos_ref, mass_ref, smooth_ref, group_ref, row_ref, column_ref, out_ref, src_ref, *scratch
 ):
     blocks_x, blocks_y, _ = mass_ref.shape
     for side in range(2):
@@ -286,22 +305,25 @@
                 column_ref[side, c, x : x + 1, :] = pos_ref[c, x, y : y + 1, :]
             column_ref[side, 3, x : x + 1, :] = mass_ref[x, y : y + 1, :]
     block_pairs(
-        1, 1, blocks_x - 2, code_ref, pos_ref, mass_ref, smooth_ref, None, None, out_ref, *scratch
+        1, 1, blocks_x - 2, None, code_ref, pos_ref, mass_ref, smooth_ref, None, None,
+        out_ref, src_ref, *scratch,
     )
 
 
 def edge_kernel(
-    code_ref, pos_ref, mass_ref, smooth_ref, prev_ref, next_ref, out_ref, src_ref, *scratch
+    code_ref, pos_ref, mass_ref, smooth_ref, prev_ref, next_ref, known_ref, out_ref, src_ref, *scratch
 ):
     blocks_x = mass_ref.shape[0]
     block_pairs(
-        0, blocks_x - 1, 2, code_ref, pos_ref, mass_ref, smooth_ref, prev_ref, next_ref,
+        0, blocks_x - 1, 2, known_ref, code_ref, pos_ref, mass_ref, smooth_ref, prev_ref, next_ref,
         out_ref, src_ref, *scratch,
     )
 
 
 def pair_scratch(blocks_x, blocks_y, x_count, listed):
     return [
+        pltpu.SMEM((listed, blocks_x, blocks_y), jnp.int32),
+        pltpu.SemaphoreType.DMA(()),
         pltpu.VMEM(((blocks_x + 2) * 64, LANES), F32),
         pltpu.VMEM((9, 8, LANES), F32),
         pltpu.VMEM((x_count, 24 * blocks_y, LANES), F32),
@@ -318,15 +340,16 @@
 
 
 def rim_kernel(
-    code_ref, middle_ref, edge_ref, known_ref, pos_ref, mass_ref, smooth_ref,
+    far_code_ref, middle_ref, edge_ref, known_ref, pos_ref, mass_ref, smooth_ref,
     low_ref, high_ref, rows_ref, hot_ref, early_ref,
-    sum_ref, table_ref, nat_ref, src_ref, md_ref, lhs_ref, row_sum_ref,
+    sum_ref, table_ref, code_ref, sem, nat_ref, src_ref, md_ref, lhs_ref, row_sum_ref,
     shift_ref, tgt_ref, mat_ref, near_ref, root_ref, total_ref,
 ):
     blocks_x, blocks_y, _ = mass_ref.shape
     owners = early_ref.shape[0]
     listed = code_ref.shape[0]
     wide = blocks_x + 2
+    codes = load_codes(far_code_ref, code_ref, sem)
     for side, ref in enumerate((low_ref, high_ref)):
         store_source(nat_ref, side * 64, wide, [ref[c] for c in range(3)], ref[3])
         for xe in range(wide):
@@ -349,6 +372,7 @@
         for side in range(2):
             y = side * (blocks_y - 1)
             mat_ref[2 * x + side] = target_matrix(tgt_ref[x, pl.ds(y, 24, stride=blocks_y), :])
+    codes.wait()
     for x in range(blocks_x):
         for side in range(2):
             y = side * (blocks_y - 1)
@@ -474,16 +498,16 @@
         packed[:, 0], packed[:, blocks_x - 1], "dom", lax.axis_index("dom") & 1
     )
     sources = ((blocks_x + 2) * blocks_y, 8, LANES)
-    columns, middle = pl.pallas_call(
+    columns, middle, own = pl.pallas_call(
         middle_kernel,
         out_shape=(
             shape((2, 4, blocks_x, LANES), F32),
             shape((blocks_x - 2, blocks_y, LANES), F32),
+            shape(sources, F32),
         ),
-        in_specs=[SMEM] + [VMEM] * 5,
-        out_specs=(VMEM,) * 2,
-        scratch_shapes=[pltpu.VMEM(sources, F32)]
-        + pair_scratch(blocks_x, blocks_y, blocks_x - 2, codes.shape[0]),
+        in_specs=[ANY] + [VMEM] * 5,
+        out_specs=(VMEM,) * 3,
+        scratch_shapes=pair_scratch(blocks_x, blocks_y, blocks_x - 2, codes.shape[0]),
         compiler_params=params(),
         cost_estimate=pl.CostEstimate(
             flops=4_000_000_000, bytes_accessed=400_000, transcendentals=1_300_000
@@ -518,7 +542,7 @@
     edge, known = pl.pallas_call(
         edge_kernel,
         out_shape=(shape((2, blocks_y, LANES), F32), shape(sources, F32)),
-        in_specs=[SMEM] + [VMEM] * 5,
+        in_specs=[ANY] + [VMEM] * 6,
         out_specs=(VMEM,) * 2,
         scratch_shapes=pair_scratch(blocks_x, blocks_y, 2, codes.shape[0]),
         compiler_params=params(),
@@ -526,13 +550,15 @@
             flops=4_000_000_000, bytes_accessed=400_000, transcendentals=1_300_000
         ),
         name="edge_pairs",
-    )(codes, positions, masses, smoothing, prev, following)
+    )(codes, positions, masses, smoothing, prev, following, own)
     sums, table = pl.pallas_call(
         rim_kernel,
         out_shape=(shape(masses.shape, F32), shape((2, owners // 2, EARLY + 1, LANES), F32)),
-        in_specs=[SMEM] + [VMEM] * 11,
+        in_specs=[ANY] + [VMEM] * 11,
         out_specs=(VMEM, VMEM),
         scratch_shapes=[
+            pltpu.SMEM(codes.shape, jnp.int32),
+            pltpu.SemaphoreType.DMA(()),
             pltpu.VMEM((128, LANES), F32),
             pltpu.VMEM((6 * (blocks_x + 2), 8, LANES), F32),
             pltpu.VMEM((owners, LANES), F32),

time: 33.2 us -> 33.1 us (level)
  no operation moved by 1% of the time
where the time goes in v2:
time: 33.1 us; the launch traced here: 32.9 us
  starting transfers between devices  15.7 us (47%)
  Pallas kernels  8.52 us (26%)
  waiting for transfers between devices  5.67 us (17%)
  other arithmetic  2.06 us (6%)
  between operations  0.86 us (3%)
    ppermute x7, starting transfers between devices, swap(): return lax.ppermute(value, axis, [(i, i ^ step) for i in range(count)])  8.01 us
    ppermute x2, starting transfers between devices, neighbours_of(): lax.ppermute(jnp.where(even, low_edge, high_edge), axis, [(i, (i + 1 if i...  7.66 us
    ppermute x7, waiting for transfers between devices, swap(): return lax.ppermute(value, axis, [(i, i ^ step) for i in range(count)])  5.61 us
    pallas_call x1, Pallas kernels, shards(): pl.pallas_call(middle_kernel, out_shape=(shape((2, 4, blocks_x, LANES), F...  2.56 us
    pallas_call x1, Pallas kernels, shards(): pl.pallas_call(edge_kernel, out_shape=(shape((2, blocks_y, LANES), F32),...  2.53 us
    pallas_call x1, Pallas kernels, shards(): pl.pallas_call(rim_kernel, out_shape=(shape(masses.shape, F32), shape((2,...  2.43 us
    pallas_call x1, Pallas kernels, shards(): pl.pallas_call(functools.partial(moments_kernel, blocks_x * dom_count, bl...  1.02 us
    select_n x2, other arithmetic, neighbours_of(): jnp.where(even, high_edge, low_edge)  0.8 us
  transfers between devices with their start and end apart: 11, of which 7 were waited for; matrix products, arithmetic and copies ran while one was open for 2% of the time, Pallas kernels for 19%

profile of v2, /device:TPU:0, one launch (start us, length us, event | category | flops | bytes accessed | tf_op | source)
XLA Modules:
  0.0 32.9 jit_solution(9420748533823059544)
XLA Ops:
  0.6 0.0 copy-start.1
  0.6 0.0 copy-start.2
  0.7 0.0 copy-start.3
  0.7 0.0 copy-start.5
  0.7 0.8 %select_bitcast_fusion = (f32[4,8,128]{2,1,0:T(8,128)S(1)}, f32[4,1,8,128]{3,2,0,1:T(8,128)S(1)}, f32[4,1,8,128]{3,2,0,1:T(8,128)S(1)}) fusion(pred[]{:T(512)S(6)} %eq.6, f32[1,4,8,128]{3,2,0,1:T(8,128)} %bitcast.17, f32[3,4,8,128]{3,2,1,0:T(8,128)} %pos_ref.7), kind=kLoop, calls=%fused_computation.8 | loop fusion | flops 12288 | bytes 114689 | tf_op jit(solution)/shard_map/jit(_where)/select_n | solution.py:448
  1.5 0.0 copy-start
  1.5 0.0 copy-start.6
  1.5 5.1 %collective-permute-start = (f32[4,8,128]{2,1,0:T(8,128)S(1)}, f32[4,8,128]{2,1,0:T(8,128)S(1)}, u32[]{:S(2)}, u32[]{:S(2)}) collective-permute-start(f32[4,8,128]{2,1,0:T(8,128)S(1)} %select_bitcast_fusion.1), channel_id=1, source_target_pairs={{0,24},{8,16},{16,8},{24,0},{1,25},{9,17},{17,9},{25,1},{2,26},{10... | collective-permute-start | bytes 49160 | tf_op jit(solution)/shard_map/ppermute | solution.py:450
  6.6 0.0 collective-permute-start.1
  6.6 0.0 copy-done.1
  6.6 0.0 copy-done.2
  6.6 0.0 copy-done.3
  6.6 0.0 copy-done.5
  6.6 0.0 copy-done
  6.6 0.0 copy-done.6
  6.7 0.0 copy-start.4
  6.7 2.6 %middle_pairs.1 = (f32[2,4,4,128]{3,2,1,0:T(4,128)S(1)}, f32[2,8,128]{2,1,0:T(8,128)S(1)}, f32[48,8,128]{2,1,0:T(8,128)S(1)}) custom-call(s32[5,4,8]{2,1,0:T(4,128)S(1)} %bitcast.18, f32[3,4,8,128]{3,2,1,0:T(8,128)S(1)} %copy-done, f32[4,8,128]{2,1,0:T(8,128)S(1)} %copy-done.1, f32[4,8,128]{2,1,0:T(8,128)S(1)} %copy-done.2, s32[4,8,128]{2,1,0:T(8,128)S(1)} %copy-done.5, ...), custom_call_target="tpu_custom_call" | custom-call | flops 4000000000 | bytes 400000 | tf_op jit(solution)/shard_map/middle_pairs/pallas_call | solution.py:501
  9.2 0.0 copy-done.4
  9.2 1.0 %moments_by_row.1 = (f32[8,16,128]{2,1,0:T(8,128)S(1)}, s32[4,8,128]{2,1,0:T(8,128)S(1)}, bf16[4,128,1024]{2,1,0:T(8,128)(2,1)S(1)}) custom-call(f32[2,8,128]{2,1,0:T(8,128)S(1)} %get-tuple-element.12.after_ref.middle_ref, f32[3,4,8,128]{3,2,1,0:T(8,128)S(1)} %copy-done, f32[3,4,8,128]{3,2,1,0:T(8,128)S(1)} %copy-done.4, f32[4,8,128]{2,1,0:T(8,128)S(1)} %copy-done.1, ...), custom_call_target="tpu_custom_call" | custom-call | flops 2000000000 | bytes 1400000 | tf_op jit(solution)/shard_map/moments_by_row/pallas_call | solution.py:517
  10.3 0.0 collective-permute-done
  10.3 0.1 collective-permute-done.1
  10.4 0.1 collective-permute-start.3
  10.5 2.5 %collective-permute-start.2 = (f32[4,6,128]{2,1,0:T(8,128)S(1)}, f32[4,6,128]{2,1,0:T(8,128)S(1)}, u32[]{:S(2)}, u32[]{:S(2)}) collective-permute-start(f32[4,6,128]{2,1,0:T(8,128)S(1)} %get-tuple-element.33), channel_id=1, source_target_pairs={{0,7},{1,2},{2,1},{3,4},{4,3},{5,6},{6,5},{7,0},{8,15},{9,10},{10,... | collective-permute-start | bytes 36872 | tf_op jit(solution)/shard_map/ppermute | solution.py:450
  13.0 2.5 %edge_pairs.1 = (f32[2,8,128]{2,1,0:T(8,128)S(1)}, f32[48,8,128]{2,1,0:T(8,128)S(1)}) custom-call(s32[5,4,8]{2,1,0:T(4,128)S(1)} %bitcast.19, f32[3,4,8,128]{3,2,1,0:T(8,128)S(1)} %copy-done, f32[4,8,128]{2,1,0:T(8,128)S(1)} %copy-done.1, f32[4,8,128]{2,1,0:T(8,128)S(1)} %copy-done.2, f32[4,8,128]{2,1,0:T(8,128)S(1)} %get-tuple-element.31.prev_ref, ...), custom_call_target="tpu_custom_call" | custom-call | flops 4000000000 | bytes 400000 | tf_op jit(solution)/shard_map/edge_pairs/pallas_call | solution.py:542
  15.5 0.0 collective-permute-done.3
  15.6 0.0 collective-permute-done.2
  15.6 2.4 %rim_pairs_and_table.1 = (f32[4,8,128]{2,1,0:T(8,128)S(1)}, f32[2,4,17,128]{3,2,1,0:T(8,128)S(1)}) custom-call(s32[5,4,8]{2,1,0:T(4,128)S(1)} %bitcast.20, f32[2,8,128]{2,1,0:T(8,128)S(1)} %get-tuple-element.12.after_ref.middle_ref, f32[2,8,128]{2,1,0:T(8,128)S(1)} %get-tuple-element.14.edge_ref, f32[48,8,128]{2,1,0:T(8,128)S(1)} %get-tuple-element.15.known_ref, ...), custom_call_target="tpu_custom_call" | custom-call | flops 200000000 | bytes 400000 | tf_op jit(solution)/shard_map/rim_pairs_and_table/pallas_call | solution.py:554
  18.0 0.1 collective-permute-start.4
  18.1 1.2 %collective-permute-done.4 = f32[4,17,128]{2,1,0:T(8,128)S(1)} collective-permute-done((f32[4,17,128]{2,1,0:T(8,128)S(1)}, f32[4,17,128]{2,1,0:T(8,128)S(1)}, u32[]{:S(2)}, u32[]{:S(2)}) %collective-permute-start.4) | collective-permute-done | bytes 34848 | tf_op jit(solution)/shard_map/ppermute | solution.py:441
  19.3 1.6 %collective-permute-start.7 = (f32[1,17,128]{2,1,0:T(8,128)S(1)}, f32[1,17,128]{2,1,0:T(8,128)S(1)}, u32[]{:S(2)}, u32[]{:S(2)}) collective-permute-start(f32[1,17,128]{2,1,0:T(8,128)S(1)} %get-tuple-element.25), channel_id=1, source_target_pairs={{0,6},{2,4},{4,2},{6,0},{1,7},{3,5},{5,3},{7,1},{8,14},{10,12},{12... | collective-permute-start | bytes 26120 | tf_op jit(solution)/shard_map/ppermute | solution.py:441
  21.0 0.5 %collective-permute-start.6 = (f32[1,17,128]{2,1,0:T(8,128)S(1)}, f32[1,17,128]{2,1,0:T(8,128)S(1)}, u32[]{:S(2)}, u32[]{:S(2)}) collective-permute-start(f32[1,17,128]{2,1,0:T(8,128)S(1)} %get-tuple-element.26), channel_id=1, source_target_pairs={{0,4},{2,6},{4,0},{6,2},{1,5},{3,7},{5,1},{7,3},{8,12},{10,14},{12... | collective-permute-start | bytes 26120 | tf_op jit(solution)/shard_map/ppermute | solution.py:441
  21.5 1.4 %collective-permute-start.5 = (f32[1,17,128]{2,1,0:T(8,128)S(1)}, f32[1,17,128]{2,1,0:T(8,128)S(1)}, u32[]{:S(2)}, u32[]{:S(2)}) collective-permute-start(f32[1,17,128]{2,1,0:T(8,128)S(1)} %get-tuple-element.27), channel_id=1, source_target_pairs={{0,2},{2,0},{4,6},{6,4},{1,3},{3,1},{5,7},{7,5},{8,10},{10,8},{12,... | collective-permute-start | bytes 26120 | tf_op jit(solution)/shard_map/ppermute | solution.py:441
  22.9 1.1 %collective-permute-done.7 = f32[1,17,128]{2,1,0:T(8,128)S(1)} collective-permute-done((f32[1,17,128]{2,1,0:T(8,128)S(1)}, f32[1,17,128]{2,1,0:T(8,128)S(1)}, u32[]{:S(2)}, u32[]{:S(2)}) %collective-permute-start.7) | collective-permute-done | bytes 8736 | tf_op jit(solution)/shard_map/ppermute | solution.py:441
  24.0 0.6 %collective-permute-done.6 = f32[1,17,128]{2,1,0:T(8,128)S(1)} collective-permute-done((f32[1,17,128]{2,1,0:T(8,128)S(1)}, f32[1,17,128]{2,1,0:T(8,128)S(1)}, u32[]{:S(2)}, u32[]{:S(2)}) %collective-permute-start.6) | collective-permute-done | bytes 8736 | tf_op jit(solution)/shard_map/ppermute | solution.py:441
  24.7 0.5 %collective-permute-done.5 = f32[1,17,128]{2,1,0:T(8,128)S(1)} collective-permute-done((f32[1,17,128]{2,1,0:T(8,128)S(1)}, f32[1,17,128]{2,1,0:T(8,128)S(1)}, u32[]{:S(2)}, u32[]{:S(2)}) %collective-permute-start.5) | collective-permute-done | bytes 8736 | tf_op jit(solution)/shard_map/ppermute | solution.py:441
  25.2 1.8 %collective-permute-start.10 = (f32[17,128]{1,0:T(8,128)S(1)}, f32[17,128]{1,0:T(8,128)S(1)}, u32[]{:S(2)}, u32[]{:S(2)}) collective-permute-start(f32[17,128]{1,0:T(8,128)S(1)} %fusion.4), channel_id=1, source_target_pairs={{0,24},{8,16},{16,8},{24,0},{1,25},{9,17},{17,9},{25,1},{2,26},{10... | collective-permute-start | bytes 26120 | tf_op jit(solution)/shard_map/ppermute | solution.py:441
  27.0 1.6 %collective-permute-start.9 = (f32[17,128]{1,0:T(8,128)S(1)}, f32[17,128]{1,0:T(8,128)S(1)}, u32[]{:S(2)}, u32[]{:S(2)}) collective-permute-start(f32[17,128]{1,0:T(8,128)S(1)} %fusion.4), channel_id=1, source_target_pairs={{0,16},{8,24},{16,0},{24,8},{1,17},{9,25},{17,1},{25,9},{2,18},{10... | collective-permute-start | bytes 26120 | tf_op jit(solution)/shard_map/ppermute | solution.py:441
  28.6 0.9 %collective-permute-start.8 = (f32[17,128]{1,0:T(8,128)S(1)}, f32[17,128]{1,0:T(8,128)S(1)}, u32[]{:S(2)}, u32[]{:S(2)}) collective-permute-start(f32[17,128]{1,0:T(8,128)S(1)} %fusion.4), channel_id=1, source_target_pairs={{0,8},{8,0},{16,24},{24,16},{1,9},{9,1},{17,25},{25,17},{2,10},{10... | collective-permute-start | bytes 26120 | tf_op jit(solution)/shard_map/ppermute | solution.py:441
  29.6 0.6 %fusion = f32[4,8,128]{2,1,0:T(8,128)} fusion(f32[4,8,128]{2,1,0:T(8,128)S(1)} %copy-done.2, f32[4,8,128]{2,1,0:T(8,128)S(1)} %get-tuple-element.20), kind=kLoop, calls=%fused_computation.3 | loop fusion | flops 16384 | bytes 49152 | tf_op jit(solution)/shard_map/div | solution.py:579
  30.2 0.5 %collective-permute-done.10 = f32[17,128]{1,0:T(8,128)S(1)} collective-permute-done((f32[17,128]{1,0:T(8,128)S(1)}, f32[17,128]{1,0:T(8,128)S(1)}, u32[]{:S(2)}, u32[]{:S(2)}) %collective-permute-start.10) | collective-permute-done | bytes 8736 | tf_op jit(solution)/shard_map/ppermute | solution.py:441
  30.7 0.9 %collective-permute-done.9 = f32[17,128]{1,0:T(8,128)S(1)} collective-permute-done((f32[17,128]{1,0:T(8,128)S(1)}, f32[17,128]{1,0:T(8,128)S(1)}, u32[]{:S(2)}, u32[]{:S(2)}) %collective-permute-start.9) | collective-permute-done | bytes 8736 | tf_op jit(solution)/shard_map/ppermute | solution.py:441
  31.6 0.7 %collective-permute-done.8 = f32[17,128]{1,0:T(8,128)S(1)} collective-permute-done((f32[17,128]{1,0:T(8,128)S(1)}, f32[17,128]{1,0:T(8,128)S(1)}, u32[]{:S(2)}, u32[]{:S(2)}) %collective-permute-start.8) | collective-permute-done | bytes 8736 | tf_op jit(solution)/shard_map/ppermute | solution.py:441
  32.3 0.6 %add_add_fusion = f32[17,128]{1,0:T(8,128)} fusion(f32[17,128]{1,0:T(8,128)S(1)} %collective-permute-done.9, f32[17,128]{1,0:T(8,128)S(1)} %collective-permute-done.10, f32[17,128]{1,0:T(8,128)S(1)} %fusion.4, f32[17,128]{1,0:T(8,128)S(1)} %collective-permute-done.8), kind=kLoop, calls=%fused_computation.15 | loop fusion | flops 6528 | bytes 43520 | tf_op jit(solution)/shard_map/add | solution.py:460
  (10 shorter events, 0.1 us)
Async XLA Ops:
  0.6 6.0 %copy-start.1 = (f32[4,8,128]{2,1,0:T(8,128)S(1)}, f32[4,8,128]{2,1,0:T(8,128)}, u32[]{:S(2)}) copy-start(f32[4,8,128]{2,1,0:T(8,128)} %mass_ref.7) | copy-start | bytes 49156
  0.6 6.0 %copy-start.2 = (f32[4,8,128]{2,1,0:T(8,128)S(1)}, f32[4,8,128]{2,1,0:T(8,128)}, u32[]{:S(2)}) copy-start(f32[4,8,128]{2,1,0:T(8,128)} %smooth_ref.5) | copy-start | bytes 49156
  0.7 6.0 %copy-start.3 = (s32[4,8,5]{1,0,2:T(4,128)S(1)}, s32[4,8,5]{1,0,2:T(4,128)}, u32[]{:S(2)}) copy-start(s32[4,8,5]{1,0,2:T(4,128)} %param.11) | copy-start | bytes 1924
  0.7 6.0 %copy-start.5 = (s32[4,8,128]{2,1,0:T(8,128)S(1)}, s32[4,8,128]{2,1,0:T(8,128)}, u32[]{:S(2)}) copy-start(s32[4,8,128]{2,1,0:T(8,128)} %group_ref.3) | copy-start | bytes 49156
  1.5 5.2 %copy-start = (f32[3,4,8,128]{3,2,1,0:T(8,128)S(1)}, f32[3,4,8,128]{3,2,1,0:T(8,128)}, u32[]{:S(2)}) copy-start(f32[3,4,8,128]{3,2,1,0:T(8,128)} %pos_ref.7) | copy-start | bytes 147460
  1.5 5.2 %copy-start.6 = (s32[1024]{0:T(1024)S(1)}, s32[1024]{0:T(1024)}, u32[]{:S(2)}) copy-start(s32[1024]{0:T(1024)} %param.13) | copy-start | bytes 12292
  1.5 8.8 %collective-permute-start = (f32[4,8,128]{2,1,0:T(8,128)S(1)}, f32[4,8,128]{2,1,0:T(8,128)S(1)}, u32[]{:S(2)}, u32[]{:S(2)}) collective-permute-start(f32[4,8,128]{2,1,0:T(8,128)S(1)} %select_bitcast_fusion.1), channel_id=1, source_target_pairs={{0,24},{8,16},{16,8},{24,0},{1,25},{9,17},{17,9},{25,1},{2,26},{10... | collective-permute-start | bytes 49160 | tf_op jit(solution)/shard_map/ppermute | solution.py:450
  6.6 3.7 %collective-permute-start.1 = (f32[4,8,128]{2,1,0:T(8,128)S(1)}, f32[4,8,128]{2,1,0:T(8,128)S(1)}, u32[]{:S(2)}, u32[]{:S(2)}) collective-permute-start(f32[4,8,128]{2,1,0:T(8,128)S(1)} %get-tuple-element.22), channel_id=1, source_target_pairs={{0,8},{8,0},{16,24},{24,16},{1,9},{9,1},{17,25},{25,17},{2,10},{10... | collective-permute-start | bytes 49160 | tf_op jit(solution)/shard_map/ppermute | solution.py:447
  6.7 2.6 %copy-start.4 = (f32[3,4,8,128]{3,2,1,0:T(8,128)S(1)}, f32[3,4,8,128]{3,2,1,0:T(8,128)}, u32[]{:S(2)}) copy-start(f32[3,4,8,128]{3,2,1,0:T(8,128)} %vel_ref.1) | copy-start | bytes 147460
  10.4 5.2 %collective-permute-start.3 = (f32[4,6,128]{2,1,0:T(8,128)S(1)}, f32[4,6,128]{2,1,0:T(8,128)S(1)}, u32[]{:S(2)}, u32[]{:S(2)}) collective-permute-start(f32[4,6,128]{2,1,0:T(8,128)S(1)} %get-tuple-element.32), channel_id=1, source_target_pairs={{0,1},{1,0},{2,3},{3,2},{4,5},{5,4},{6,7},{7,6},{8,9},{9,8},{10,11... | collective-permute-start | bytes 36872 | tf_op jit(solution)/shard_map/ppermute | solution.py:447
  10.5 5.1 %collective-permute-start.2 = (f32[4,6,128]{2,1,0:T(8,128)S(1)}, f32[4,6,128]{2,1,0:T(8,128)S(1)}, u32[]{:S(2)}, u32[]{:S(2)}) collective-permute-start(f32[4,6,128]{2,1,0:T(8,128)S(1)} %get-tuple-element.33), channel_id=1, source_target_pairs={{0,7},{1,2},{2,1},{3,4},{4,3},{5,6},{6,5},{7,0},{8,15},{9,10},{10,... | collective-permute-start | bytes 36872 | tf_op jit(solution)/shard_map/ppermute | solution.py:450
  18.0 1.3 %collective-permute-start.4 = (f32[4,17,128]{2,1,0:T(8,128)S(1)}, f32[4,17,128]{2,1,0:T(8,128)S(1)}, u32[]{:S(2)}, u32[]{:S(2)}) collective-permute-start(f32[4,17,128]{2,1,0:T(8,128)S(1)} %slice_bitcast_fusion), channel_id=1, source_target_pairs={{0,1},{1,0},{2,3},{3,2},{4,5},{5,4},{6,7},{7,6},{8,9},{9,8},{10,11... | collective-permute-start | bytes 104456 | tf_op jit(solution)/shard_map/ppermute | solution.py:441
  19.3 4.7 %collective-permute-start.7 = (f32[1,17,128]{2,1,0:T(8,128)S(1)}, f32[1,17,128]{2,1,0:T(8,128)S(1)}, u32[]{:S(2)}, u32[]{:S(2)}) collective-permute-start(f32[1,17,128]{2,1,0:T(8,128)S(1)} %get-tuple-element.25), channel_id=1, source_target_pairs={{0,6},{2,4},{4,2},{6,0},{1,7},{3,5},{5,3},{7,1},{8,14},{10,12},{12... | collective-permute-start | bytes 26120 | tf_op jit(solution)/shard_map/ppermute | solution.py:441
  21.0 3.7 %collective-permute-start.6 = (f32[1,17,128]{2,1,0:T(8,128)S(1)}, f32[1,17,128]{2,1,0:T(8,128)S(1)}, u32[]{:S(2)}, u32[]{:S(2)}) collective-permute-start(f32[1,17,128]{2,1,0:T(8,128)S(1)} %get-tuple-element.26), channel_id=1, source_target_pairs={{0,4},{2,6},{4,0},{6,2},{1,5},{3,7},{5,1},{7,3},{8,12},{10,14},{12... | collective-permute-start | bytes 26120 | tf_op jit(solution)/shard_map/ppermute | solution.py:441
  21.5 3.7 %collective-permute-start.5 = (f32[1,17,128]{2,1,0:T(8,128)S(1)}, f32[1,17,128]{2,1,0:T(8,128)S(1)}, u32[]{:S(2)}, u32[]{:S(2)}) collective-permute-start(f32[1,17,128]{2,1,0:T(8,128)S(1)} %get-tuple-element.27), channel_id=1, source_target_pairs={{0,2},{2,0},{4,6},{6,4},{1,3},{3,1},{5,7},{7,5},{8,10},{10,8},{12,... | collective-permute-start | bytes 26120 | tf_op jit(solution)/shard_map/ppermute | solution.py:441
  25.2 5.5 %collective-permute-start.10 = (f32[17,128]{1,0:T(8,128)S(1)}, f32[17,128]{1,0:T(8,128)S(1)}, u32[]{:S(2)}, u32[]{:S(2)}) collective-permute-start(f32[17,128]{1,0:T(8,128)S(1)} %fusion.4), channel_id=1, source_target_pairs={{0,24},{8,16},{16,8},{24,0},{1,25},{9,17},{17,9},{25,1},{2,26},{10... | collective-permute-start | bytes 26120 | tf_op jit(solution)/shard_map/ppermute | solution.py:441
  27.0 4.6 %collective-permute-start.9 = (f32[17,128]{1,0:T(8,128)S(1)}, f32[17,128]{1,0:T(8,128)S(1)}, u32[]{:S(2)}, u32[]{:S(2)}) collective-permute-start(f32[17,128]{1,0:T(8,128)S(1)} %fusion.4), channel_id=1, source_target_pairs={{0,16},{8,24},{16,0},{24,8},{1,17},{9,25},{17,1},{25,9},{2,18},{10... | collective-permute-start | bytes 26120 | tf_op jit(solution)/shard_map/ppermute | solution.py:441
  28.6 3.7 %collective-permute-start.8 = (f32[17,128]{1,0:T(8,128)S(1)}, f32[17,128]{1,0:T(8,128)S(1)}, u32[]{:S(2)}, u32[]{:S(2)}) collective-permute-start(f32[17,128]{1,0:T(8,128)S(1)} %fusion.4), channel_id=1, source_target_pairs={{0,8},{8,0},{16,24},{24,16},{1,9},{9,1},{17,25},{25,17},{2,10},{10... | collective-permute-start | bytes 26120 | tf_op jit(solution)/shard_map/ppermute | solution.py:441

commit v3 on v2

--- a/solution.py
+++ b/solution.py
@@ -152,50 +152,43 @@
         nat_ref[start + kind * 8 : start + kind * 8 + count, :] = line
 
 
-def pair_sums(sides, pieces=()):
+def pair_sums(sides, buffers, pieces=()):
     rows = 32
-    steps = []
-    for target, sources, roots, total in sides:
-        count = roots.shape[0]
-        for first in range(0, count, 2):
-            steps.append((target, sources, roots, total, first, min(2, count - first), count))
-
-    def product(step):
-        target, sources, _, _, first, width, _ = step
-        right = sources[:, first * LANES : (first + width) * LANES]
-        return jnp.dot(target[...], right, preferred_element_type=F32)
-
-    ready = product(steps[0])
-    chunks = None
-    for number, (_, _, roots, total, first, width, count) in enumerate(steps):
-        squared = ready
-        if number + 1 < len(steps):
-            ready = product(steps[number + 1])
-        if first == 0:
-            chunks = [None] * (LANES // rows)
+
+    def products(number):
+        target, sources, roots, _ = sides[number]
+        for first in range(0, roots.shape[0], 2):
+            lanes = slice(first * LANES, min(first + 2, roots.shape[0]) * LANES)
+            buffers[number % 2][:, lanes] = jnp.dot(
+                target[...], sources[:, lanes], preferred_element_type=F32
+            )
+
+    products(0)
+    for number, (_, _, roots, total) in enumerate(sides):
+        if number + 1 < len(sides):
+            products(number + 1)
         limits = []
-        for k in range(width):
-            root = roots[first + k : first + k + 1, :]
+        for k in range(roots.shape[0]):
+            root = roots[k : k + 1, :]
             reach = 4.0 * root
             limits.append(
                 [jnp.broadcast_to(line, (rows, LANES)) for line in (root, reach, reach * reach)]
             )
-        for r in range(len(chunks)):
+        for first in range(0, LANES, rows):
+            chunk = None
             for k, (root, reach, most) in enumerate(limits):
-                t = squared[r * rows : (r + 1) * rows, k * LANES : (k + 1) * LANES]
+                t = buffers[number % 2][first : first + rows, k * LANES : (k + 1) * LANES]
                 t = jnp.maximum(jnp.minimum(t, most), 1e-12)
                 u = t * lax.rsqrt(t)
                 f = reach - u
                 f = f * f
                 f = f * f
                 term = f * (root + u)
-                chunks[r] = term if chunks[r] is None else chunks[r] + term
-        if first + width == count:
-            for r, chunk in enumerate(chunks):
-                total[r * rows : (r + 1) * rows, :] = chunk
+                chunk = term if chunk is None else chunk + term
+            total[first : first + rows, :] = chunk
         if number < len(pieces) and pieces[number] is not None:
             pieces[number]()
-    for piece in pieces[len(steps) :]:
+    for piece in pieces[len(sides) :]:
         piece()
 
 
@@ -237,7 +230,7 @@
 
 def block_pairs(
     x_first, x_step, x_count, known_ref, far_code_ref, pos_ref, mass_ref, smooth_ref, prev_ref, next_ref,
-    out_ref, src_ref, code_ref, sem, nat_ref, shift_ref, tgt_ref, mat_ref, near_ref, root_ref, total_ref,
+    out_ref, src_ref, code_ref, sem, nat_ref, shift_ref, tgt_ref, mat_ref, near_ref, root_ref, total_ref, *buffers,
 ):
     blocks_x, blocks_y, _ = mass_ref.shape
     listed = code_ref.shape[0]
@@ -276,20 +269,20 @@
             line = src_ref[(x + step_x) * blocks_y + y + code - 3 * step_x - 1]
             put_source(near_ref, root_ref, number, k, line, shift_ref[code], squares)
     inner = blocks_y - 2
-    per_row = inner * ((listed + 1) // 2)
 
     def row_sums(turn):
         sums = column_sums([total_ref[turn * inner + k] for k in range(inner)])
         out_ref[turn, 1 : blocks_y - 1, :] = sums
 
-    pieces = [None] * (x_count * per_row + 1)
+    pieces = [None] * (x_count * inner + 1)
     for turn in range(x_count):
-        pieces[(turn + 1) * per_row] = functools.partial(row_sums, turn)
+        pieces[(turn + 1) * inner] = functools.partial(row_sums, turn)
     pair_sums(
         [
             (mat_ref.at[n], near_ref.at[n], root_ref.at[n, pl.ds(0, listed)], total_ref.at[n])
             for n in range(len(blocks))
         ],
+        buffers,
         pieces,
     )
 
@@ -336,6 +329,8 @@
         pltpu.VMEM((blocks, 48, listed * LANES), BF16),
         pltpu.VMEM((blocks, 8, LANES), F32),
         pltpu.VMEM((blocks, LANES, LANES), F32),
+        pltpu.VMEM((LANES, listed * LANES), F32),
+        pltpu.VMEM((LANES, listed * LANES), F32),
     ]
 
 
@@ -343,7 +338,7 @@
     far_code_ref, middle_ref, edge_ref, known_ref, pos_ref, mass_ref, smooth_ref,
     low_ref, high_ref, rows_ref, hot_ref, early_ref,
     sum_ref, table_ref, code_ref, sem, nat_ref, src_ref, md_ref, lhs_ref, row_sum_ref,
-    shift_ref, tgt_ref, mat_ref, near_ref, root_ref, total_ref,
+    shift_ref, tgt_ref, mat_ref, near_ref, root_ref, total_ref, *buffers,
 ):
     blocks_x, blocks_y, _ = mass_ref.shape
     owners = early_ref.shape[0]
@@ -412,7 +407,7 @@
         )
         row_sum_ref[...] = product if x == 0 else row_sum_ref[...] + product
 
-    pair_sums(sides, [functools.partial(inner_moments, x) for x in range(blocks_x)])
+    pair_sums(sides, buffers, [functools.partial(inner_moments, x) for x in range(blocks_x)])
     sums = column_sums([total_ref[number] for number in range(len(sides))])
     for x in range(blocks_x):
         for side in range(2):

time: 33.1 us -> 33.1 us (level)
  no operation moved by 1% of the time
where the time goes in v3:
time: 33.1 us; the launch traced here: 32.9 us
  starting transfers between devices  15.7 us (47%)
  Pallas kernels  8.55 us (26%)
  waiting for transfers between devices  5.66 us (17%)
  other arithmetic  2.06 us (6%)
  between operations  0.86 us (3%)
    ppermute x7, starting transfers between devices, swap(): return lax.ppermute(value, axis, [(i, i ^ step) for i in range(count)])  8.01 us
    ppermute x2, starting transfers between devices, neighbours_of(): lax.ppermute(jnp.where(even, low_edge, high_edge), axis, [(i, (i + 1 if i...  7.66 us
    ppermute x7, waiting for transfers between devices, swap(): return lax.ppermute(value, axis, [(i, i ^ step) for i in range(count)])  5.61 us
    pallas_call x1, Pallas kernels, shards(): pl.pallas_call(middle_kernel, out_shape=(shape((2, 4, blocks_x, LANES), F...  2.57 us
    pallas_call x1, Pallas kernels, shards(): pl.pallas_call(edge_kernel, out_shape=(shape((2, blocks_y, LANES), F32),...  2.54 us
    pallas_call x1, Pallas kernels, shards(): pl.pallas_call(rim_kernel, out_shape=(shape(masses.shape, F32), shape((2,...  2.43 us
    pallas_call x1, Pallas kernels, shards(): pl.pallas_call(functools.partial(moments_kernel, blocks_x * dom_count, bl...  1.02 us
    select_n x2, other arithmetic, neighbours_of(): jnp.where(even, high_edge, low_edge)  0.8 us
  transfers between devices with their start and end apart: 11, of which 7 were waited for; matrix products, arithmetic and copies ran while one was open for 2% of the time, Pallas kernels for 19%

profile of v3, /device:TPU:0, one launch (start us, length us, event | category | flops | bytes accessed | tf_op | source)
XLA Modules:
  0.0 32.9 jit_solution(10094524238832177157)
XLA Ops:
  0.6 0.0 copy-start.1
  0.6 0.0 copy-start.2
  0.7 0.0 copy-start.3
  0.7 0.0 copy-start.5
  0.7 0.8 %select_bitcast_fusion = (f32[4,8,128]{2,1,0:T(8,128)S(1)}, f32[4,1,8,128]{3,2,0,1:T(8,128)S(1)}, f32[4,1,8,128]{3,2,0,1:T(8,128)S(1)}) fusion(pred[]{:T(512)S(6)} %eq.6, f32[1,4,8,128]{3,2,0,1:T(8,128)} %bitcast.17, f32[3,4,8,128]{3,2,1,0:T(8,128)} %pos_ref.7), kind=kLoop, calls=%fused_computation.8 | loop fusion | flops 12288 | bytes 114689 | tf_op jit(solution)/shard_map/jit(_where)/select_n | solution.py:443
  1.5 0.0 copy-start
  1.5 0.0 copy-start.6
  1.5 5.1 %collective-permute-start = (f32[4,8,128]{2,1,0:T(8,128)S(1)}, f32[4,8,128]{2,1,0:T(8,128)S(1)}, u32[]{:S(2)}, u32[]{:S(2)}) collective-permute-start(f32[4,8,128]{2,1,0:T(8,128)S(1)} %select_bitcast_fusion.1), channel_id=1, source_target_pairs={{0,24},{8,16},{16,8},{24,0},{1,25},{9,17},{17,9},{25,1},{2,26},{10... | collective-permute-start | bytes 49160 | tf_op jit(solution)/shard_map/ppermute | solution.py:445
  6.6 0.0 collective-permute-start.1
  6.6 0.0 copy-done.1
  6.6 0.0 copy-done.2
  6.6 0.0 copy-done.3
  6.6 0.0 copy-done.5
  6.6 0.0 copy-done
  6.6 0.0 copy-done.6
  6.7 0.0 copy-start.4
  6.7 2.6 %middle_pairs.1 = (f32[2,4,4,128]{3,2,1,0:T(4,128)S(1)}, f32[2,8,128]{2,1,0:T(8,128)S(1)}, f32[48,8,128]{2,1,0:T(8,128)S(1)}) custom-call(s32[5,4,8]{2,1,0:T(4,128)S(1)} %bitcast.18, f32[3,4,8,128]{3,2,1,0:T(8,128)S(1)} %copy-done, f32[4,8,128]{2,1,0:T(8,128)S(1)} %copy-done.1, f32[4,8,128]{2,1,0:T(8,128)S(1)} %copy-done.2, s32[4,8,128]{2,1,0:T(8,128)S(1)} %copy-done.5, ...), custom_call_target="tpu_custom_call" | custom-call | flops 4000000000 | bytes 400000 | tf_op jit(solution)/shard_map/middle_pairs/pallas_call | solution.py:496
  9.3 0.0 copy-done.4
  9.3 1.0 %moments_by_row.1 = (f32[8,16,128]{2,1,0:T(8,128)S(1)}, s32[4,8,128]{2,1,0:T(8,128)S(1)}, bf16[4,128,1024]{2,1,0:T(8,128)(2,1)S(1)}) custom-call(f32[2,8,128]{2,1,0:T(8,128)S(1)} %get-tuple-element.12.after_ref.middle_ref, f32[3,4,8,128]{3,2,1,0:T(8,128)S(1)} %copy-done, f32[3,4,8,128]{3,2,1,0:T(8,128)S(1)} %copy-done.4, f32[4,8,128]{2,1,0:T(8,128)S(1)} %copy-done.1, ...), custom_call_target="tpu_custom_call" | custom-call | flops 2000000000 | bytes 1400000 | tf_op jit(solution)/shard_map/moments_by_row/pallas_call | solution.py:512
  10.3 0.0 collective-permute-done
  10.3 0.0 collective-permute-done.1
  10.4 0.1 collective-permute-start.3
  10.5 2.5 %collective-permute-start.2 = (f32[4,6,128]{2,1,0:T(8,128)S(1)}, f32[4,6,128]{2,1,0:T(8,128)S(1)}, u32[]{:S(2)}, u32[]{:S(2)}) collective-permute-start(f32[4,6,128]{2,1,0:T(8,128)S(1)} %get-tuple-element.33), channel_id=1, source_target_pairs={{0,7},{1,2},{2,1},{3,4},{4,3},{5,6},{6,5},{7,0},{8,15},{9,10},{10,... | collective-permute-start | bytes 36872 | tf_op jit(solution)/shard_map/ppermute | solution.py:445
  13.0 2.5 %edge_pairs.1 = (f32[2,8,128]{2,1,0:T(8,128)S(1)}, f32[48,8,128]{2,1,0:T(8,128)S(1)}) custom-call(s32[5,4,8]{2,1,0:T(4,128)S(1)} %bitcast.19, f32[3,4,8,128]{3,2,1,0:T(8,128)S(1)} %copy-done, f32[4,8,128]{2,1,0:T(8,128)S(1)} %copy-done.1, f32[4,8,128]{2,1,0:T(8,128)S(1)} %copy-done.2, f32[4,8,128]{2,1,0:T(8,128)S(1)} %get-tuple-element.31.prev_ref, ...), custom_call_target="tpu_custom_call" | custom-call | flops 4000000000 | bytes 400000 | tf_op jit(solution)/shard_map/edge_pairs/pallas_call | solution.py:537
  15.6 0.0 collective-permute-done.3
  15.6 0.0 collective-permute-done.2
  15.6 2.4 %rim_pairs_and_table.1 = (f32[4,8,128]{2,1,0:T(8,128)S(1)}, f32[2,4,17,128]{3,2,1,0:T(8,128)S(1)}) custom-call(s32[5,4,8]{2,1,0:T(4,128)S(1)} %bitcast.20, f32[2,8,128]{2,1,0:T(8,128)S(1)} %get-tuple-element.12.after_ref.middle_ref, f32[2,8,128]{2,1,0:T(8,128)S(1)} %get-tuple-element.14.edge_ref, f32[48,8,128]{2,1,0:T(8,128)S(1)} %get-tuple-element.15.known_ref, ...), custom_call_target="tpu_custom_call" | custom-call | flops 200000000 | bytes 400000 | tf_op jit(solution)/shard_map/rim_pairs_and_table/pallas_call | solution.py:549
  18.0 0.1 collective-permute-start.4
  18.1 1.2 %collective-permute-done.4 = f32[4,17,128]{2,1,0:T(8,128)S(1)} collective-permute-done((f32[4,17,128]{2,1,0:T(8,128)S(1)}, f32[4,17,128]{2,1,0:T(8,128)S(1)}, u32[]{:S(2)}, u32[]{:S(2)}) %collective-permute-start.4) | collective-permute-done | bytes 34848 | tf_op jit(solution)/shard_map/ppermute | solution.py:436
  19.4 1.6 %collective-permute-start.7 = (f32[1,17,128]{2,1,0:T(8,128)S(1)}, f32[1,17,128]{2,1,0:T(8,128)S(1)}, u32[]{:S(2)}, u32[]{:S(2)}) collective-permute-start(f32[1,17,128]{2,1,0:T(8,128)S(1)} %get-tuple-element.25), channel_id=1, source_target_pairs={{0,6},{2,4},{4,2},{6,0},{1,7},{3,5},{5,3},{7,1},{8,14},{10,12},{12... | collective-permute-start | bytes 26120 | tf_op jit(solution)/shard_map/ppermute | solution.py:436
  21.0 0.5 %collective-permute-start.6 = (f32[1,17,128]{2,1,0:T(8,128)S(1)}, f32[1,17,128]{2,1,0:T(8,128)S(1)}, u32[]{:S(2)}, u32[]{:S(2)}) collective-permute-start(f32[1,17,128]{2,1,0:T(8,128)S(1)} %get-tuple-element.26), channel_id=1, source_target_pairs={{0,4},{2,6},{4,0},{6,2},{1,5},{3,7},{5,1},{7,3},{8,12},{10,14},{12... | collective-permute-start | bytes 26120 | tf_op jit(solution)/shard_map/ppermute | solution.py:436
  21.5 1.4 %collective-permute-start.5 = (f32[1,17,128]{2,1,0:T(8,128)S(1)}, f32[1,17,128]{2,1,0:T(8,128)S(1)}, u32[]{:S(2)}, u32[]{:S(2)}) collective-permute-start(f32[1,17,128]{2,1,0:T(8,128)S(1)} %get-tuple-element.27), channel_id=1, source_target_pairs={{0,2},{2,0},{4,6},{6,4},{1,3},{3,1},{5,7},{7,5},{8,10},{10,8},{12,... | collective-permute-start | bytes 26120 | tf_op jit(solution)/shard_map/ppermute | solution.py:436
  22.9 1.1 %collective-permute-done.7 = f32[1,17,128]{2,1,0:T(8,128)S(1)} collective-permute-done((f32[1,17,128]{2,1,0:T(8,128)S(1)}, f32[1,17,128]{2,1,0:T(8,128)S(1)}, u32[]{:S(2)}, u32[]{:S(2)}) %collective-permute-start.7) | collective-permute-done | bytes 8736 | tf_op jit(solution)/shard_map/ppermute | solution.py:436
  24.0 0.6 %collective-permute-done.6 = f32[1,17,128]{2,1,0:T(8,128)S(1)} collective-permute-done((f32[1,17,128]{2,1,0:T(8,128)S(1)}, f32[1,17,128]{2,1,0:T(8,128)S(1)}, u32[]{:S(2)}, u32[]{:S(2)}) %collective-permute-start.6) | collective-permute-done | bytes 8736 | tf_op jit(solution)/shard_map/ppermute | solution.py:436
  24.7 0.5 %collective-permute-done.5 = f32[1,17,128]{2,1,0:T(8,128)S(1)} collective-permute-done((f32[1,17,128]{2,1,0:T(8,128)S(1)}, f32[1,17,128]{2,1,0:T(8,128)S(1)}, u32[]{:S(2)}, u32[]{:S(2)}) %collective-permute-start.5) | collective-permute-done | bytes 8736 | tf_op jit(solution)/shard_map/ppermute | solution.py:436
  25.2 1.8 %collective-permute-start.10 = (f32[17,128]{1,0:T(8,128)S(1)}, f32[17,128]{1,0:T(8,128)S(1)}, u32[]{:S(2)}, u32[]{:S(2)}) collective-permute-start(f32[17,128]{1,0:T(8,128)S(1)} %fusion.4), channel_id=1, source_target_pairs={{0,24},{8,16},{16,8},{24,0},{1,25},{9,17},{17,9},{25,1},{2,26},{10... | collective-permute-start | bytes 26120 | tf_op jit(solution)/shard_map/ppermute | solution.py:436
  27.0 1.7 %collective-permute-start.9 = (f32[17,128]{1,0:T(8,128)S(1)}, f32[17,128]{1,0:T(8,128)S(1)}, u32[]{:S(2)}, u32[]{:S(2)}) collective-permute-start(f32[17,128]{1,0:T(8,128)S(1)} %fusion.4), channel_id=1, source_target_pairs={{0,16},{8,24},{16,0},{24,8},{1,17},{9,25},{17,1},{25,9},{2,18},{10... | collective-permute-start | bytes 26120 | tf_op jit(solution)/shard_map/ppermute | solution.py:436
  28.6 0.9 %collective-permute-start.8 = (f32[17,128]{1,0:T(8,128)S(1)}, f32[17,128]{1,0:T(8,128)S(1)}, u32[]{:S(2)}, u32[]{:S(2)}) collective-permute-start(f32[17,128]{1,0:T(8,128)S(1)} %fusion.4), channel_id=1, source_target_pairs={{0,8},{8,0},{16,24},{24,16},{1,9},{9,1},{17,25},{25,17},{2,10},{10... | collective-permute-start | bytes 26120 | tf_op jit(solution)/shard_map/ppermute | solution.py:436
  29.6 0.6 %fusion = f32[4,8,128]{2,1,0:T(8,128)} fusion(f32[4,8,128]{2,1,0:T(8,128)S(1)} %copy-done.2, f32[4,8,128]{2,1,0:T(8,128)S(1)} %get-tuple-element.20), kind=kLoop, calls=%fused_computation.3 | loop fusion | flops 16384 | bytes 49152 | tf_op jit(solution)/shard_map/div | solution.py:574
  30.2 0.5 %collective-permute-done.10 = f32[17,128]{1,0:T(8,128)S(1)} collective-permute-done((f32[17,128]{1,0:T(8,128)S(1)}, f32[17,128]{1,0:T(8,128)S(1)}, u32[]{:S(2)}, u32[]{:S(2)}) %collective-permute-start.10) | collective-permute-done | bytes 8736 | tf_op jit(solution)/shard_map/ppermute | solution.py:436
  30.7 0.9 %collective-permute-done.9 = f32[17,128]{1,0:T(8,128)S(1)} collective-permute-done((f32[17,128]{1,0:T(8,128)S(1)}, f32[17,128]{1,0:T(8,128)S(1)}, u32[]{:S(2)}, u32[]{:S(2)}) %collective-permute-start.9) | collective-permute-done | bytes 8736 | tf_op jit(solution)/shard_map/ppermute | solution.py:436
  31.6 0.8 %collective-permute-done.8 = f32[17,128]{1,0:T(8,128)S(1)} collective-permute-done((f32[17,128]{1,0:T(8,128)S(1)}, f32[17,128]{1,0:T(8,128)S(1)}, u32[]{:S(2)}, u32[]{:S(2)}) %collective-permute-start.8) | collective-permute-done | bytes 8736 | tf_op jit(solution)/shard_map/ppermute | solution.py:436
  32.3 0.6 %add_add_fusion = f32[17,128]{1,0:T(8,128)} fusion(f32[17,128]{1,0:T(8,128)S(1)} %collective-permute-done.9, f32[17,128]{1,0:T(8,128)S(1)} %collective-permute-done.10, f32[17,128]{1,0:T(8,128)S(1)} %fusion.4, f32[17,128]{1,0:T(8,128)S(1)} %collective-permute-done.8), kind=kLoop, calls=%fused_computation.15 | loop fusion | flops 6528 | bytes 43520 | tf_op jit(solution)/shard_map/add | solution.py:455
  (10 shorter events, 0.1 us)
Async XLA Ops:
  0.6 6.0 %copy-start.1 = (f32[4,8,128]{2,1,0:T(8,128)S(1)}, f32[4,8,128]{2,1,0:T(8,128)}, u32[]{:S(2)}) copy-start(f32[4,8,128]{2,1,0:T(8,128)} %mass_ref.7) | copy-start | bytes 49156
  0.6 6.0 %copy-start.2 = (f32[4,8,128]{2,1,0:T(8,128)S(1)}, f32[4,8,128]{2,1,0:T(8,128)}, u32[]{:S(2)}) copy-start(f32[4,8,128]{2,1,0:T(8,128)} %smooth_ref.5) | copy-start | bytes 49156
  0.7 6.0 %copy-start.3 = (s32[4,8,5]{1,0,2:T(4,128)S(1)}, s32[4,8,5]{1,0,2:T(4,128)}, u32[]{:S(2)}) copy-start(s32[4,8,5]{1,0,2:T(4,128)} %param.11) | copy-start | bytes 1924
  0.7 6.0 %copy-start.5 = (s32[4,8,128]{2,1,0:T(8,128)S(1)}, s32[4,8,128]{2,1,0:T(8,128)}, u32[]{:S(2)}) copy-start(s32[4,8,128]{2,1,0:T(8,128)} %group_ref.3) | copy-start | bytes 49156
  1.5 5.2 %copy-start = (f32[3,4,8,128]{3,2,1,0:T(8,128)S(1)}, f32[3,4,8,128]{3,2,1,0:T(8,128)}, u32[]{:S(2)}) copy-start(f32[3,4,8,128]{3,2,1,0:T(8,128)} %pos_ref.7) | copy-start | bytes 147460
  1.5 5.2 %copy-start.6 = (s32[1024]{0:T(1024)S(1)}, s32[1024]{0:T(1024)}, u32[]{:S(2)}) copy-start(s32[1024]{0:T(1024)} %param.13) | copy-start | bytes 12292
  1.5 8.8 %collective-permute-start = (f32[4,8,128]{2,1,0:T(8,128)S(1)}, f32[4,8,128]{2,1,0:T(8,128)S(1)}, u32[]{:S(2)}, u32[]{:S(2)}) collective-permute-start(f32[4,8,128]{2,1,0:T(8,128)S(1)} %select_bitcast_fusion.1), channel_id=1, source_target_pairs={{0,24},{8,16},{16,8},{24,0},{1,25},{9,17},{17,9},{25,1},{2,26},{10... | collective-permute-start | bytes 49160 | tf_op jit(solution)/shard_map/ppermute | solution.py:445
  6.6 3.7 %collective-permute-start.1 = (f32[4,8,128]{2,1,0:T(8,128)S(1)}, f32[4,8,128]{2,1,0:T(8,128)S(1)}, u32[]{:S(2)}, u32[]{:S(2)}) collective-permute-start(f32[4,8,128]{2,1,0:T(8,128)S(1)} %get-tuple-element.22), channel_id=1, source_target_pairs={{0,8},{8,0},{16,24},{24,16},{1,9},{9,1},{17,25},{25,17},{2,10},{10... | collective-permute-start | bytes 49160 | tf_op jit(solution)/shard_map/ppermute | solution.py:442
  6.7 2.6 %copy-start.4 = (f32[3,4,8,128]{3,2,1,0:T(8,128)S(1)}, f32[3,4,8,128]{3,2,1,0:T(8,128)}, u32[]{:S(2)}) copy-start(f32[3,4,8,128]{3,2,1,0:T(8,128)} %vel_ref.1) | copy-start | bytes 147460
  10.4 5.2 %collective-permute-start.3 = (f32[4,6,128]{2,1,0:T(8,128)S(1)}, f32[4,6,128]{2,1,0:T(8,128)S(1)}, u32[]{:S(2)}, u32[]{:S(2)}) collective-permute-start(f32[4,6,128]{2,1,0:T(8,128)S(1)} %get-tuple-element.32), channel_id=1, source_target_pairs={{0,1},{1,0},{2,3},{3,2},{4,5},{5,4},{6,7},{7,6},{8,9},{9,8},{10,11... | collective-permute-start | bytes 36872 | tf_op jit(solution)/shard_map/ppermute | solution.py:442
  10.5 5.1 %collective-permute-start.2 = (f32[4,6,128]{2,1,0:T(8,128)S(1)}, f32[4,6,128]{2,1,0:T(8,128)S(1)}, u32[]{:S(2)}, u32[]{:S(2)}) collective-permute-start(f32[4,6,128]{2,1,0:T(8,128)S(1)} %get-tuple-element.33), channel_id=1, source_target_pairs={{0,7},{1,2},{2,1},{3,4},{4,3},{5,6},{6,5},{7,0},{8,15},{9,10},{10,... | collective-permute-start | bytes 36872 | tf_op jit(solution)/shard_map/ppermute | solution.py:445
  18.0 1.3 %collective-permute-start.4 = (f32[4,17,128]{2,1,0:T(8,128)S(1)}, f32[4,17,128]{2,1,0:T(8,128)S(1)}, u32[]{:S(2)}, u32[]{:S(2)}) collective-permute-start(f32[4,17,128]{2,1,0:T(8,128)S(1)} %slice_bitcast_fusion), channel_id=1, source_target_pairs={{0,1},{1,0},{2,3},{3,2},{4,5},{5,4},{6,7},{7,6},{8,9},{9,8},{10,11... | collective-permute-start | bytes 104456 | tf_op jit(solution)/shard_map/ppermute | solution.py:436
  19.4 4.7 %collective-permute-start.7 = (f32[1,17,128]{2,1,0:T(8,128)S(1)}, f32[1,17,128]{2,1,0:T(8,128)S(1)}, u32[]{:S(2)}, u32[]{:S(2)}) collective-permute-start(f32[1,17,128]{2,1,0:T(8,128)S(1)} %get-tuple-element.25), channel_id=1, source_target_pairs={{0,6},{2,4},{4,2},{6,0},{1,7},{3,5},{5,3},{7,1},{8,14},{10,12},{12... | collective-permute-start | bytes 26120 | tf_op jit(solution)/shard_map/ppermute | solution.py:436
  21.0 3.7 %collective-permute-start.6 = (f32[1,17,128]{2,1,0:T(8,128)S(1)}, f32[1,17,128]{2,1,0:T(8,128)S(1)}, u32[]{:S(2)}, u32[]{:S(2)}) collective-permute-start(f32[1,17,128]{2,1,0:T(8,128)S(1)} %get-tuple-element.26), channel_id=1, source_target_pairs={{0,4},{2,6},{4,0},{6,2},{1,5},{3,7},{5,1},{7,3},{8,12},{10,14},{12... | collective-permute-start | bytes 26120 | tf_op jit(solution)/shard_map/ppermute | solution.py:436
  21.5 3.7 %collective-permute-start.5 = (f32[1,17,128]{2,1,0:T(8,128)S(1)}, f32[1,17,128]{2,1,0:T(8,128)S(1)}, u32[]{:S(2)}, u32[]{:S(2)}) collective-permute-start(f32[1,17,128]{2,1,0:T(8,128)S(1)} %get-tuple-element.27), channel_id=1, source_target_pairs={{0,2},{2,0},{4,6},{6,4},{1,3},{3,1},{5,7},{7,5},{8,10},{10,8},{12,... | collective-permute-start | bytes 26120 | tf_op jit(solution)/shard_map/ppermute | solution.py:436
  25.2 5.5 %collective-permute-start.10 = (f32[17,128]{1,0:T(8,128)S(1)}, f32[17,128]{1,0:T(8,128)S(1)}, u32[]{:S(2)}, u32[]{:S(2)}) collective-permute-start(f32[17,128]{1,0:T(8,128)S(1)} %fusion.4), channel_id=1, source_target_pairs={{0,24},{8,16},{16,8},{24,0},{1,25},{9,17},{17,9},{25,1},{2,26},{10... | collective-permute-start | bytes 26120 | tf_op jit(solution)/shard_map/ppermute | solution.py:436
  27.0 4.6 %collective-permute-start.9 = (f32[17,128]{1,0:T(8,128)S(1)}, f32[17,128]{1,0:T(8,128)S(1)}, u32[]{:S(2)}, u32[]{:S(2)}) collective-permute-start(f32[17,128]{1,0:T(8,128)S(1)} %fusion.4), channel_id=1, source_target_pairs={{0,16},{8,24},{16,0},{24,8},{1,17},{9,25},{17,1},{25,9},{2,18},{10... | collective-permute-start | bytes 26120 | tf_op jit(solution)/shard_map/ppermute | solution.py:436
  28.6 3.7 %collective-permute-start.8 = (f32[17,128]{1,0:T(8,128)S(1)}, f32[17,128]{1,0:T(8,128)S(1)}, u32[]{:S(2)}, u32[]{:S(2)}) collective-permute-start(f32[17,128]{1,0:T(8,128)S(1)} %fusion.4), channel_id=1, source_target_pairs={{0,8},{8,0},{16,24},{24,16},{1,9},{9,1},{17,25},{25,17},{2,10},{10... | collective-permute-start | bytes 26120 | tf_op jit(solution)/shard_map/ppermute | solution.py:436

commit v4 on v2

--- a/solution.py
+++ b/solution.py
@@ -152,7 +152,7 @@
         nat_ref[start + kind * 8 : start + kind * 8 + count, :] = line
 
 
-def pair_sums(sides, pieces=()):
+def pair_sums(sides, pieces=(), add=False):
     rows = 32
     steps = []
     for target, sources, roots, total in sides:
@@ -173,6 +173,8 @@
             ready = product(steps[number + 1])
         if first == 0:
             chunks = [None] * (LANES // rows)
+            if add:
+                chunks = [total[r * rows : (r + 1) * rows, :] for r in range(len(chunks))]
         limits = []
         for k in range(width):
             root = roots[first + k : first + k + 1, :]
@@ -227,6 +229,14 @@
     root = jnp.broadcast_to(line[7:8], line.shape)
     near_ref[number, :, k * LANES : (k + 1) * LANES] = source_matrix(line + shift, root, squares)
     root_ref[number, k : k + 1, :] = root[0:1]
+
+
+def sides_of(count, first, end, mat_ref, near_ref, root_ref, total_ref):
+    lanes, rows = pl.ds(first * LANES, (end - first) * LANES), pl.ds(first, end - first)
+    return [
+        (mat_ref.at[n], near_ref.at[n, :, lanes], root_ref.at[n, rows], total_ref.at[n])
+        for n in range(count)
+    ]
 
 
 def load_codes(far_ref, code_ref, sem):
@@ -267,16 +277,20 @@
             tgt_ref[turn, row * blocks_y : (row + 1) * blocks_y, :] = line
     for number, (turn, y) in enumerate(blocks):
         mat_ref[number] = target_matrix(tgt_ref[turn, pl.ds(y, 24, stride=blocks_y), :])
+    for number, (turn, y) in enumerate(blocks):
+        line = src_ref[(x_first + turn * x_step + 1) * blocks_y + y]
+        put_source(near_ref, root_ref, number, 0, line, 0.0, squares)
+    pair_sums(sides_of(len(blocks), 0, 1, mat_ref, near_ref, root_ref, total_ref))
     codes.wait()
     for number, (turn, y) in enumerate(blocks):
         x = x_first + turn * x_step
-        for k in range(listed):
+        for k in range(1, listed):
             code = code_ref[k, x, y]
             step_x = (code * 11) >> 5
             line = src_ref[(x + step_x) * blocks_y + y + code - 3 * step_x - 1]
             put_source(near_ref, root_ref, number, k, line, shift_ref[code], squares)
     inner = blocks_y - 2
-    per_row = inner * ((listed + 1) // 2)
+    per_row = inner * (listed // 2)
 
     def row_sums(turn):
         sums = column_sums([total_ref[turn * inner + k] for k in range(inner)])
@@ -285,13 +299,8 @@
     pieces = [None] * (x_count * per_row + 1)
     for turn in range(x_count):
         pieces[(turn + 1) * per_row] = functools.partial(row_sums, turn)
-    pair_sums(
-        [
-            (mat_ref.at[n], near_ref.at[n], root_ref.at[n, pl.ds(0, listed)], total_ref.at[n])
-            for n in range(len(blocks))
-        ],
-        pieces,
-    )
+    sides = sides_of(len(blocks), 1, listed, mat_ref, near_ref, root_ref, total_ref)
+    pair_sums(sides, pieces, add=True)
 
 
 def middle_kernel(
@@ -372,19 +381,11 @@
         for side in range(2):
             y = side * (blocks_y - 1)
             mat_ref[2 * x + side] = target_matrix(tgt_ref[x, pl.ds(y, 24, stride=blocks_y), :])
-    codes.wait()
     for x in range(blocks_x):
         for side in range(2):
-            y = side * (blocks_y - 1)
-            for k in range(listed):
-                code = code_ref[k, x, y]
-                step_x = (code * 11) >> 5
-                line = src_ref[(3 * side + code - 3 * step_x) * wide + x + step_x]
-                put_source(near_ref, root_ref, 2 * x + side, k, line, shift_ref[code], squares)
-    sides = [
-        (mat_ref.at[n], near_ref.at[n], root_ref.at[n, pl.ds(0, listed)], total_ref.at[n])
-        for n in range(2 * blocks_x)
-    ]
+            line = src_ref[(3 * side + 1) * wide + x + 1]
+            put_source(near_ref, root_ref, 2 * x + side, 0, line, 0.0, squares)
+
     owner_ids = lax.broadcasted_iota(jnp.int32, (owners, LANES), 0)
     last = blocks_y - 1
 
@@ -412,8 +413,21 @@
         )
         row_sum_ref[...] = product if x == 0 else row_sum_ref[...] + product
 
-    pair_sums(sides, [functools.partial(inner_moments, x) for x in range(blocks_x)])
-    sums = column_sums([total_ref[number] for number in range(len(sides))])
+    products = (mat_ref, near_ref, root_ref, total_ref)
+    pair_sums(
+        sides_of(2 * blocks_x, 0, 1, *products),
+        [functools.partial(inner_moments, x) for x in range(blocks_x)],
+    )
+    codes.wait()
+    for x in range(blocks_x):
+        for side in range(2):
+            for k in range(1, listed):
+                code = code_ref[k, x, side * last]
+                step_x = (code * 11) >> 5
+                line = src_ref[(3 * side + code - 3 * step_x) * wide + x + step_x]
+                put_source(near_ref, root_ref, 2 * x + side, k, line, shift_ref[code], squares)
+    pair_sums(sides_of(2 * blocks_x, 1, listed, *products), add=True)
+    sums = column_sums([total_ref[number] for number in range(2 * blocks_x)])
     for x in range(blocks_x):
         for side in range(2):
             y = side * last

time: 33.1 us -> 32.5 us (0.982)
  Pallas kernels: 8.52 us -> 7.71 us
    pallas_call x1, Pallas kernels: 2.43 us -> 2.09 us  [shards(): pl.pallas_call(rim_kernel, out_shape=(shape(masses.shape, F32), shape((2,...]
  transfers between devices with their start and end apart: 11 -> 11, of which waited for: 7 -> 8; matrix products, arithmetic and copies ran while one was open for 2% -> 2% of each run, Pallas kernels for 19% -> 17%
where the time goes in v4:
time: 32.5 us; the launch traced here: 32.4 us
  starting transfers between devices  15.7 us (48%)
  Pallas kernels  7.71 us (24%)
  waiting for transfers between devices  5.93 us (18%)
  other arithmetic  2.06 us (6%)
  between operations  0.86 us (3%)
    ppermute x7, starting transfers between devices, swap(): return lax.ppermute(value, axis, [(i, i ^ step) for i in range(count)])  8.01 us
    ppermute x2, starting transfers between devices, neighbours_of(): lax.ppermute(jnp.where(even, low_edge, high_edge), axis, [(i, (i + 1 if i...  7.66 us
    ppermute x7, waiting for transfers between devices, swap(): return lax.ppermute(value, axis, [(i, i ^ step) for i in range(count)])  5.65 us
    pallas_call x1, Pallas kernels, shards(): pl.pallas_call(middle_kernel, out_shape=(shape((2, 4, blocks_x, LANES), F...  2.33 us
    pallas_call x1, Pallas kernels, shards(): pl.pallas_call(edge_kernel, out_shape=(shape((2, blocks_y, LANES), F32),...  2.27 us
    pallas_call x1, Pallas kernels, shards(): pl.pallas_call(rim_kernel, out_shape=(shape(masses.shape, F32), shape((2,...  2.09 us
    pallas_call x1, Pallas kernels, shards(): pl.pallas_call(functools.partial(moments_kernel, blocks_x * dom_count, bl...  1.02 us
    select_n x2, other arithmetic, neighbours_of(): jnp.where(even, high_edge, low_edge)  0.8 us
  transfers between devices with their start and end apart: 11, of which 8 were waited for; matrix products, arithmetic and copies ran while one was open for 2% of the time, Pallas kernels for 17%

profile of v4, /device:TPU:0, one launch (start us, length us, event | category | flops | bytes accessed | tf_op | source)
XLA Modules:
  0.0 32.4 jit_solution(13711211368174341517)
XLA Ops:
  0.6 0.0 copy-start.1
  0.6 0.0 copy-start.2
  0.7 0.0 copy-start.3
  0.7 0.0 copy-start.5
  0.7 0.8 %select_bitcast_fusion = (f32[4,8,128]{2,1,0:T(8,128)S(1)}, f32[4,1,8,128]{3,2,0,1:T(8,128)S(1)}, f32[4,1,8,128]{3,2,0,1:T(8,128)S(1)}) fusion(pred[]{:T(512)S(6)} %eq.6, f32[1,4,8,128]{3,2,0,1:T(8,128)} %bitcast.17, f32[3,4,8,128]{3,2,1,0:T(8,128)} %pos_ref.7), kind=kLoop, calls=%fused_computation.8 | loop fusion | flops 12288 | bytes 114689 | tf_op jit(solution)/shard_map/jit(_where)/select_n | solution.py:462
  1.5 0.0 copy-start
  1.5 0.0 copy-start.6
  1.5 5.1 %collective-permute-start = (f32[4,8,128]{2,1,0:T(8,128)S(1)}, f32[4,8,128]{2,1,0:T(8,128)S(1)}, u32[]{:S(2)}, u32[]{:S(2)}) collective-permute-start(f32[4,8,128]{2,1,0:T(8,128)S(1)} %select_bitcast_fusion.1), channel_id=1, source_target_pairs={{0,24},{8,16},{16,8},{24,0},{1,25},{9,17},{17,9},{25,1},{2,26},{10... | collective-permute-start | bytes 49160 | tf_op jit(solution)/shard_map/ppermute | solution.py:464
  6.6 0.0 collective-permute-start.1
  6.6 0.0 copy-done.1
  6.6 0.0 copy-done.2
  6.6 0.0 copy-done.3
  6.6 0.0 copy-done.5
  6.6 0.0 copy-done
  6.6 0.0 copy-done.6
  6.7 0.0 copy-start.4
  6.7 2.3 %middle_pairs.1 = (f32[2,4,4,128]{3,2,1,0:T(4,128)S(1)}, f32[2,8,128]{2,1,0:T(8,128)S(1)}, f32[48,8,128]{2,1,0:T(8,128)S(1)}) custom-call(s32[5,4,8]{2,1,0:T(4,128)S(1)} %bitcast.18, f32[3,4,8,128]{3,2,1,0:T(8,128)S(1)} %copy-done, f32[4,8,128]{2,1,0:T(8,128)S(1)} %copy-done.1, f32[4,8,128]{2,1,0:T(8,128)S(1)} %copy-done.2, s32[4,8,128]{2,1,0:T(8,128)S(1)} %copy-done.5, ...), custom_call_target="tpu_custom_call" | custom-call | flops 4000000000 | bytes 400000 | tf_op jit(solution)/shard_map/middle_pairs/pallas_call | solution.py:515
  9.0 0.0 copy-done.4
  9.0 1.0 %moments_by_row.1 = (f32[8,16,128]{2,1,0:T(8,128)S(1)}, s32[4,8,128]{2,1,0:T(8,128)S(1)}, bf16[4,128,1024]{2,1,0:T(8,128)(2,1)S(1)}) custom-call(f32[2,8,128]{2,1,0:T(8,128)S(1)} %get-tuple-element.12.after_ref.middle_ref, f32[3,4,8,128]{3,2,1,0:T(8,128)S(1)} %copy-done, f32[3,4,8,128]{3,2,1,0:T(8,128)S(1)} %copy-done.4, f32[4,8,128]{2,1,0:T(8,128)S(1)} %copy-done.1, ...), custom_call_target="tpu_custom_call" | custom-call | flops 2000000000 | bytes 1400000 | tf_op jit(solution)/shard_map/moments_by_row/pallas_call | solution.py:531
  10.1 0.0 collective-permute-done
  10.1 0.3 collective-permute-done.1
  10.4 0.1 collective-permute-start.3
  10.5 2.5 %collective-permute-start.2 = (f32[4,6,128]{2,1,0:T(8,128)S(1)}, f32[4,6,128]{2,1,0:T(8,128)S(1)}, u32[]{:S(2)}, u32[]{:S(2)}) collective-permute-start(f32[4,6,128]{2,1,0:T(8,128)S(1)} %get-tuple-element.33), channel_id=1, source_target_pairs={{0,7},{1,2},{2,1},{3,4},{4,3},{5,6},{6,5},{7,0},{8,15},{9,10},{10,... | collective-permute-start | bytes 36872 | tf_op jit(solution)/shard_map/ppermute | solution.py:464
  13.0 2.3 %edge_pairs.1 = (f32[2,8,128]{2,1,0:T(8,128)S(1)}, f32[48,8,128]{2,1,0:T(8,128)S(1)}) custom-call(s32[5,4,8]{2,1,0:T(4,128)S(1)} %bitcast.19, f32[3,4,8,128]{3,2,1,0:T(8,128)S(1)} %copy-done, f32[4,8,128]{2,1,0:T(8,128)S(1)} %copy-done.1, f32[4,8,128]{2,1,0:T(8,128)S(1)} %copy-done.2, f32[4,8,128]{2,1,0:T(8,128)S(1)} %get-tuple-element.31.prev_ref, ...), custom_call_target="tpu_custom_call" | custom-call | flops 4000000000 | bytes 400000 | tf_op jit(solution)/shard_map/edge_pairs/pallas_call | solution.py:556
  15.3 0.0 collective-permute-done.3
  15.3 0.0 collective-permute-done.2
  15.3 2.1 %rim_pairs_and_table.1 = (f32[4,8,128]{2,1,0:T(8,128)S(1)}, f32[2,4,17,128]{3,2,1,0:T(8,128)S(1)}) custom-call(s32[5,4,8]{2,1,0:T(4,128)S(1)} %bitcast.20, f32[2,8,128]{2,1,0:T(8,128)S(1)} %get-tuple-element.12.after_ref.middle_ref, f32[2,8,128]{2,1,0:T(8,128)S(1)} %get-tuple-element.14.edge_ref, f32[48,8,128]{2,1,0:T(8,128)S(1)} %get-tuple-element.15.known_ref, ...), custom_call_target="tpu_custom_call" | custom-call | flops 200000000 | bytes 400000 | tf_op jit(solution)/shard_map/rim_pairs_and_table/pallas_call | solution.py:568
  17.4 0.1 collective-permute-start.4
  17.5 1.2 %collective-permute-done.4 = f32[4,17,128]{2,1,0:T(8,128)S(1)} collective-permute-done((f32[4,17,128]{2,1,0:T(8,128)S(1)}, f32[4,17,128]{2,1,0:T(8,128)S(1)}, u32[]{:S(2)}, u32[]{:S(2)}) %collective-permute-start.4) | collective-permute-done | bytes 34848 | tf_op jit(solution)/shard_map/ppermute | solution.py:455
  18.8 1.9 %collective-permute-start.7 = (f32[1,17,128]{2,1,0:T(8,128)S(1)}, f32[1,17,128]{2,1,0:T(8,128)S(1)}, u32[]{:S(2)}, u32[]{:S(2)}) collective-permute-start(f32[1,17,128]{2,1,0:T(8,128)S(1)} %get-tuple-element.25), channel_id=1, source_target_pairs={{0,6},{2,4},{4,2},{6,0},{1,7},{3,5},{5,3},{7,1},{8,14},{10,12},{12... | collective-permute-start | bytes 26120 | tf_op jit(solution)/shard_map/ppermute | solution.py:455
  20.6 0.5 %collective-permute-start.6 = (f32[1,17,128]{2,1,0:T(8,128)S(1)}, f32[1,17,128]{2,1,0:T(8,128)S(1)}, u32[]{:S(2)}, u32[]{:S(2)}) collective-permute-start(f32[1,17,128]{2,1,0:T(8,128)S(1)} %get-tuple-element.26), channel_id=1, source_target_pairs={{0,4},{2,6},{4,0},{6,2},{1,5},{3,7},{5,1},{7,3},{8,12},{10,14},{12... | collective-permute-start | bytes 26120 | tf_op jit(solution)/shard_map/ppermute | solution.py:455
  21.1 1.2 %collective-permute-start.5 = (f32[1,17,128]{2,1,0:T(8,128)S(1)}, f32[1,17,128]{2,1,0:T(8,128)S(1)}, u32[]{:S(2)}, u32[]{:S(2)}) collective-permute-start(f32[1,17,128]{2,1,0:T(8,128)S(1)} %get-tuple-element.27), channel_id=1, source_target_pairs={{0,2},{2,0},{4,6},{6,4},{1,3},{3,1},{5,7},{7,5},{8,10},{10,8},{12,... | collective-permute-start | bytes 26120 | tf_op jit(solution)/shard_map/ppermute | solution.py:455
  22.3 1.1 %collective-permute-done.7 = f32[1,17,128]{2,1,0:T(8,128)S(1)} collective-permute-done((f32[1,17,128]{2,1,0:T(8,128)S(1)}, f32[1,17,128]{2,1,0:T(8,128)S(1)}, u32[]{:S(2)}, u32[]{:S(2)}) %collective-permute-start.7) | collective-permute-done | bytes 8736 | tf_op jit(solution)/shard_map/ppermute | solution.py:455
  23.4 0.9 %collective-permute-done.6 = f32[1,17,128]{2,1,0:T(8,128)S(1)} collective-permute-done((f32[1,17,128]{2,1,0:T(8,128)S(1)}, f32[1,17,128]{2,1,0:T(8,128)S(1)}, u32[]{:S(2)}, u32[]{:S(2)}) %collective-permute-start.6) | collective-permute-done | bytes 8736 | tf_op jit(solution)/shard_map/ppermute | solution.py:455
  24.3 0.5 %collective-permute-done.5 = f32[1,17,128]{2,1,0:T(8,128)S(1)} collective-permute-done((f32[1,17,128]{2,1,0:T(8,128)S(1)}, f32[1,17,128]{2,1,0:T(8,128)S(1)}, u32[]{:S(2)}, u32[]{:S(2)}) %collective-permute-start.5) | collective-permute-done | bytes 8736 | tf_op jit(solution)/shard_map/ppermute | solution.py:455
  24.8 1.8 %collective-permute-start.10 = (f32[17,128]{1,0:T(8,128)S(1)}, f32[17,128]{1,0:T(8,128)S(1)}, u32[]{:S(2)}, u32[]{:S(2)}) collective-permute-start(f32[17,128]{1,0:T(8,128)S(1)} %fusion.4), channel_id=1, source_target_pairs={{0,24},{8,16},{16,8},{24,0},{1,25},{9,17},{17,9},{25,1},{2,26},{10... | collective-permute-start | bytes 26120 | tf_op jit(solution)/shard_map/ppermute | solution.py:455
  26.6 1.4 %collective-permute-start.9 = (f32[17,128]{1,0:T(8,128)S(1)}, f32[17,128]{1,0:T(8,128)S(1)}, u32[]{:S(2)}, u32[]{:S(2)}) collective-permute-start(f32[17,128]{1,0:T(8,128)S(1)} %fusion.4), channel_id=1, source_target_pairs={{0,16},{8,24},{16,0},{24,8},{1,17},{9,25},{17,1},{25,9},{2,18},{10... | collective-permute-start | bytes 26120 | tf_op jit(solution)/shard_map/ppermute | solution.py:455
  28.1 1.2 %collective-permute-start.8 = (f32[17,128]{1,0:T(8,128)S(1)}, f32[17,128]{1,0:T(8,128)S(1)}, u32[]{:S(2)}, u32[]{:S(2)}) collective-permute-start(f32[17,128]{1,0:T(8,128)S(1)} %fusion.4), channel_id=1, source_target_pairs={{0,8},{8,0},{16,24},{24,16},{1,9},{9,1},{17,25},{25,17},{2,10},{10... | collective-permute-start | bytes 26120 | tf_op jit(solution)/shard_map/ppermute | solution.py:455
  29.2 0.6 %fusion = f32[4,8,128]{2,1,0:T(8,128)} fusion(f32[4,8,128]{2,1,0:T(8,128)S(1)} %copy-done.2, f32[4,8,128]{2,1,0:T(8,128)S(1)} %get-tuple-element.20), kind=kLoop, calls=%fused_computation.3 | loop fusion | flops 16384 | bytes 49152 | tf_op jit(solution)/shard_map/div | solution.py:593
  29.8 0.5 %collective-permute-done.10 = f32[17,128]{1,0:T(8,128)S(1)} collective-permute-done((f32[17,128]{1,0:T(8,128)S(1)}, f32[17,128]{1,0:T(8,128)S(1)}, u32[]{:S(2)}, u32[]{:S(2)}) %collective-permute-start.10) | collective-permute-done | bytes 8736 | tf_op jit(solution)/shard_map/ppermute | solution.py:455
  30.3 0.9 %collective-permute-done.9 = f32[17,128]{1,0:T(8,128)S(1)} collective-permute-done((f32[17,128]{1,0:T(8,128)S(1)}, f32[17,128]{1,0:T(8,128)S(1)}, u32[]{:S(2)}, u32[]{:S(2)}) %collective-permute-start.9) | collective-permute-done | bytes 8736 | tf_op jit(solution)/shard_map/ppermute | solution.py:455
  31.2 0.5 %collective-permute-done.8 = f32[17,128]{1,0:T(8,128)S(1)} collective-permute-done((f32[17,128]{1,0:T(8,128)S(1)}, f32[17,128]{1,0:T(8,128)S(1)}, u32[]{:S(2)}, u32[]{:S(2)}) %collective-permute-start.8) | collective-permute-done | bytes 8736 | tf_op jit(solution)/shard_map/ppermute | solution.py:455
  31.8 0.6 %add_add_fusion = f32[17,128]{1,0:T(8,128)} fusion(f32[17,128]{1,0:T(8,128)S(1)} %collective-permute-done.9, f32[17,128]{1,0:T(8,128)S(1)} %collective-permute-done.10, f32[17,128]{1,0:T(8,128)S(1)} %fusion.4, f32[17,128]{1,0:T(8,128)S(1)} %collective-permute-done.8), kind=kLoop, calls=%fused_computation.15 | loop fusion | flops 6528 | bytes 43520 | tf_op jit(solution)/shard_map/add | solution.py:474
  (10 shorter events, 0.1 us)
Async XLA Ops:
  0.6 6.0 %copy-start.1 = (f32[4,8,128]{2,1,0:T(8,128)S(1)}, f32[4,8,128]{2,1,0:T(8,128)}, u32[]{:S(2)}) copy-start(f32[4,8,128]{2,1,0:T(8,128)} %mass_ref.7) | copy-start | bytes 49156
  0.6 6.0 %copy-start.2 = (f32[4,8,128]{2,1,0:T(8,128)S(1)}, f32[4,8,128]{2,1,0:T(8,128)}, u32[]{:S(2)}) copy-start(f32[4,8,128]{2,1,0:T(8,128)} %smooth_ref.5) | copy-start | bytes 49156
  0.7 6.0 %copy-start.3 = (s32[4,8,5]{1,0,2:T(4,128)S(1)}, s32[4,8,5]{1,0,2:T(4,128)}, u32[]{:S(2)}) copy-start(s32[4,8,5]{1,0,2:T(4,128)} %param.11) | copy-start | bytes 1924
  0.7 6.0 %copy-start.5 = (s32[4,8,128]{2,1,0:T(8,128)S(1)}, s32[4,8,128]{2,1,0:T(8,128)}, u32[]{:S(2)}) copy-start(s32[4,8,128]{2,1,0:T(8,128)} %group_ref.3) | copy-start | bytes 49156
  1.5 5.2 %copy-start = (f32[3,4,8,128]{3,2,1,0:T(8,128)S(1)}, f32[3,4,8,128]{3,2,1,0:T(8,128)}, u32[]{:S(2)}) copy-start(f32[3,4,8,128]{3,2,1,0:T(8,128)} %pos_ref.7) | copy-start | bytes 147460
  1.5 5.2 %copy-start.6 = (s32[1024]{0:T(1024)S(1)}, s32[1024]{0:T(1024)}, u32[]{:S(2)}) copy-start(s32[1024]{0:T(1024)} %param.13) | copy-start | bytes 12292
  1.5 8.6 %collective-permute-start = (f32[4,8,128]{2,1,0:T(8,128)S(1)}, f32[4,8,128]{2,1,0:T(8,128)S(1)}, u32[]{:S(2)}, u32[]{:S(2)}) collective-permute-start(f32[4,8,128]{2,1,0:T(8,128)S(1)} %select_bitcast_fusion.1), channel_id=1, source_target_pairs={{0,24},{8,16},{16,8},{24,0},{1,25},{9,17},{17,9},{25,1},{2,26},{10... | collective-permute-start | bytes 49160 | tf_op jit(solution)/shard_map/ppermute | solution.py:464
  6.6 3.7 %collective-permute-start.1 = (f32[4,8,128]{2,1,0:T(8,128)S(1)}, f32[4,8,128]{2,1,0:T(8,128)S(1)}, u32[]{:S(2)}, u32[]{:S(2)}) collective-permute-start(f32[4,8,128]{2,1,0:T(8,128)S(1)} %get-tuple-element.22), channel_id=1, source_target_pairs={{0,8},{8,0},{16,24},{24,16},{1,9},{9,1},{17,25},{25,17},{2,10},{10... | collective-permute-start | bytes 49160 | tf_op jit(solution)/shard_map/ppermute | solution.py:461
  6.7 2.4 %copy-start.4 = (f32[3,4,8,128]{3,2,1,0:T(8,128)S(1)}, f32[3,4,8,128]{3,2,1,0:T(8,128)}, u32[]{:S(2)}) copy-start(f32[3,4,8,128]{3,2,1,0:T(8,128)} %vel_ref.1) | copy-start | bytes 147460
  10.4 4.9 %collective-permute-start.3 = (f32[4,6,128]{2,1,0:T(8,128)S(1)}, f32[4,6,128]{2,1,0:T(8,128)S(1)}, u32[]{:S(2)}, u32[]{:S(2)}) collective-permute-start(f32[4,6,128]{2,1,0:T(8,128)S(1)} %get-tuple-element.32), channel_id=1, source_target_pairs={{0,1},{1,0},{2,3},{3,2},{4,5},{5,4},{6,7},{7,6},{8,9},{9,8},{10,11... | collective-permute-start | bytes 36872 | tf_op jit(solution)/shard_map/ppermute | solution.py:461
  10.5 4.8 %collective-permute-start.2 = (f32[4,6,128]{2,1,0:T(8,128)S(1)}, f32[4,6,128]{2,1,0:T(8,128)S(1)}, u32[]{:S(2)}, u32[]{:S(2)}) collective-permute-start(f32[4,6,128]{2,1,0:T(8,128)S(1)} %get-tuple-element.33), channel_id=1, source_target_pairs={{0,7},{1,2},{2,1},{3,4},{4,3},{5,6},{6,5},{7,0},{8,15},{9,10},{10,... | collective-permute-start | bytes 36872 | tf_op jit(solution)/shard_map/ppermute | solution.py:464
  17.4 1.3 %collective-permute-start.4 = (f32[4,17,128]{2,1,0:T(8,128)S(1)}, f32[4,17,128]{2,1,0:T(8,128)S(1)}, u32[]{:S(2)}, u32[]{:S(2)}) collective-permute-start(f32[4,17,128]{2,1,0:T(8,128)S(1)} %slice_bitcast_fusion), channel_id=1, source_target_pairs={{0,1},{1,0},{2,3},{3,2},{4,5},{5,4},{6,7},{7,6},{8,9},{9,8},{10,11... | collective-permute-start | bytes 104456 | tf_op jit(solution)/shard_map/ppermute | solution.py:455
  18.8 4.7 %collective-permute-start.7 = (f32[1,17,128]{2,1,0:T(8,128)S(1)}, f32[1,17,128]{2,1,0:T(8,128)S(1)}, u32[]{:S(2)}, u32[]{:S(2)}) collective-permute-start(f32[1,17,128]{2,1,0:T(8,128)S(1)} %get-tuple-element.25), channel_id=1, source_target_pairs={{0,6},{2,4},{4,2},{6,0},{1,7},{3,5},{5,3},{7,1},{8,14},{10,12},{12... | collective-permute-start | bytes 26120 | tf_op jit(solution)/shard_map/ppermute | solution.py:455
  20.6 3.7 %collective-permute-start.6 = (f32[1,17,128]{2,1,0:T(8,128)S(1)}, f32[1,17,128]{2,1,0:T(8,128)S(1)}, u32[]{:S(2)}, u32[]{:S(2)}) collective-permute-start(f32[1,17,128]{2,1,0:T(8,128)S(1)} %get-tuple-element.26), channel_id=1, source_target_pairs={{0,4},{2,6},{4,0},{6,2},{1,5},{3,7},{5,1},{7,3},{8,12},{10,14},{12... | collective-permute-start | bytes 26120 | tf_op jit(solution)/shard_map/ppermute | solution.py:455
  21.1 3.7 %collective-permute-start.5 = (f32[1,17,128]{2,1,0:T(8,128)S(1)}, f32[1,17,128]{2,1,0:T(8,128)S(1)}, u32[]{:S(2)}, u32[]{:S(2)}) collective-permute-start(f32[1,17,128]{2,1,0:T(8,128)S(1)} %get-tuple-element.27), channel_id=1, source_target_pairs={{0,2},{2,0},{4,6},{6,4},{1,3},{3,1},{5,7},{7,5},{8,10},{10,8},{12,... | collective-permute-start | bytes 26120 | tf_op jit(solution)/shard_map/ppermute | solution.py:455
  24.8 5.5 %collective-permute-start.10 = (f32[17,128]{1,0:T(8,128)S(1)}, f32[17,128]{1,0:T(8,128)S(1)}, u32[]{:S(2)}, u32[]{:S(2)}) collective-permute-start(f32[17,128]{1,0:T(8,128)S(1)} %fusion.4), channel_id=1, source_target_pairs={{0,24},{8,16},{16,8},{24,0},{1,25},{9,17},{17,9},{25,1},{2,26},{10... | collective-permute-start | bytes 26120 | tf_op jit(solution)/shard_map/ppermute | solution.py:455
  26.6 4.6 %collective-permute-start.9 = (f32[17,128]{1,0:T(8,128)S(1)}, f32[17,128]{1,0:T(8,128)S(1)}, u32[]{:S(2)}, u32[]{:S(2)}) collective-permute-start(f32[17,128]{1,0:T(8,128)S(1)} %fusion.4), channel_id=1, source_target_pairs={{0,16},{8,24},{16,0},{24,8},{1,17},{9,25},{17,1},{25,9},{2,18},{10... | collective-permute-start | bytes 26120 | tf_op jit(solution)/shard_map/ppermute | solution.py:455
  28.1 3.7 %collective-permute-start.8 = (f32[17,128]{1,0:T(8,128)S(1)}, f32[17,128]{1,0:T(8,128)S(1)}, u32[]{:S(2)}, u32[]{:S(2)}) collective-permute-start(f32[17,128]{1,0:T(8,128)S(1)} %fusion.4), channel_id=1, source_target_pairs={{0,8},{8,0},{16,24},{24,16},{1,9},{9,1},{17,25},{25,17},{2,10},{10... | collective-permute-start | bytes 26120 | tf_op jit(solution)/shard_map/ppermute | solution.py:455

commit v5 on v4

--- a/solution.py
+++ b/solution.py
@@ -246,11 +246,10 @@
 
 
 def block_pairs(
-    x_first, x_step, x_count, known_ref, far_code_ref, pos_ref, mass_ref, smooth_ref, prev_ref, next_ref,
+    listed, x_first, x_step, x_count, known_ref, far_code_ref, pos_ref, mass_ref, smooth_ref, prev_ref, next_ref,
     out_ref, src_ref, code_ref, sem, nat_ref, shift_ref, tgt_ref, mat_ref, near_ref, root_ref, total_ref,
 ):
     blocks_x, blocks_y, _ = mass_ref.shape
-    listed = code_ref.shape[0]
     codes = load_codes(far_code_ref, code_ref, sem)
     for xe in range(blocks_x + 2):
         if xe == 0 or xe == blocks_x + 1:
@@ -284,8 +283,9 @@
     codes.wait()
     for number, (turn, y) in enumerate(blocks):
         x = x_first + turn * x_step
+        word = code_ref[x * blocks_y + y]
         for k in range(1, listed):
-            code = code_ref[k, x, y]
+            code = (word >> (4 * k)) & 15
             step_x = (code * 11) >> 5
             line = src_ref[(x + step_x) * blocks_y + y + code - 3 * step_x - 1]
             put_source(near_ref, root_ref, number, k, line, shift_ref[code], squares)
@@ -304,7 +304,7 @@
 
 
 def middle_kernel(
-    code_ref, pos_ref, mass_ref, smooth_ref, group_ref, row_ref, column_ref, out_ref, src_ref, *scratch
+    listed, code_ref, pos_ref, mass_ref, smooth_ref, group_ref, row_ref, column_ref, out_ref, src_ref, *scratch
 ):
     blocks_x, blocks_y, _ = mass_ref.shape
     for side in range(2):
@@ -314,24 +314,24 @@
                 column_ref[side, c, x : x + 1, :] = pos_ref[c, x, y : y + 1, :]
             column_ref[side, 3, x : x + 1, :] = mass_ref[x, y : y + 1, :]
     block_pairs(
-        1, 1, blocks_x - 2, None, code_ref, pos_ref, mass_ref, smooth_ref, None, None,
+        listed, 1, 1, blocks_x - 2, None, code_ref, pos_ref, mass_ref, smooth_ref, None, None,
         out_ref, src_ref, *scratch,
     )
 
 
 def edge_kernel(
-    code_ref, pos_ref, mass_ref, smooth_ref, prev_ref, next_ref, known_ref, out_ref, src_ref, *scratch
+    listed, code_ref, pos_ref, mass_ref, smooth_ref, prev_ref, next_ref, known_ref, out_ref, src_ref, *scratch
 ):
     blocks_x = mass_ref.shape[0]
     block_pairs(
-        0, blocks_x - 1, 2, known_ref, code_ref, pos_ref, mass_ref, smooth_ref, prev_ref, next_ref,
+        listed, 0, blocks_x - 1, 2, known_ref, code_ref, pos_ref, mass_ref, smooth_ref, prev_ref, next_ref,
         out_ref, src_ref, *scratch,
     )
 
 
 def pair_scratch(blocks_x, blocks_y, x_count, listed):
     return [
-        pltpu.SMEM((listed, blocks_x, blocks_y), jnp.int32),
+        pltpu.SMEM((blocks_x * blocks_y,), jnp.int32),
         pltpu.SemaphoreType.DMA(()),
         pltpu.VMEM(((blocks_x + 2) * 64, LANES), F32),
         pltpu.VMEM((9, 8, LANES), F32),
@@ -349,14 +349,13 @@
 
 
 def rim_kernel(
-    far_code_ref, middle_ref, edge_ref, known_ref, pos_ref, mass_ref, smooth_ref,
+    listed, far_code_ref, middle_ref, edge_ref, known_ref, pos_ref, mass_ref, smooth_ref,
     low_ref, high_ref, rows_ref, hot_ref, early_ref,
     sum_ref, table_ref, code_ref, sem, nat_ref, src_ref, md_ref, lhs_ref, row_sum_ref,
     shift_ref, tgt_ref, mat_ref, near_ref, root_ref, total_ref,
 ):
     blocks_x, blocks_y, _ = mass_ref.shape
     owners = early_ref.shape[0]
-    listed = code_ref.shape[0]
     wide = blocks_x + 2
     codes = load_codes(far_code_ref, code_ref, sem)
     for side, ref in enumerate((low_ref, high_ref)):
@@ -421,8 +420,9 @@
     codes.wait()
     for x in range(blocks_x):
         for side in range(2):
+            word = code_ref[x * blocks_y + side * last]
             for k in range(1, listed):
-                code = code_ref[k, x, side * last]
+                code = (word >> (4 * k)) & 15
                 step_x = (code * 11) >> 5
                 line = src_ref[(3 * side + code - 3 * step_x) * wide + x + step_x]
                 put_source(near_ref, root_ref, 2 * x + side, k, line, shift_ref[code], squares)
@@ -505,7 +505,8 @@
     owners = sub_count
     chunk = blocks_y * block_len
     shape = jax.ShapeDtypeStruct
-    codes = neighbours.transpose(2, 0, 1)
+    listed = neighbours.shape[2]
+    codes = sum(neighbours[:, :, k] << (4 * k) for k in range(listed)).reshape(-1)
     table_rows = group_row.reshape(-1, LANES)
     packed = jnp.concatenate([positions, masses[None]], axis=0)
     prev, following = neighbours_of(
@@ -513,7 +514,7 @@
     )
     sources = ((blocks_x + 2) * blocks_y, 8, LANES)
     columns, middle, own = pl.pallas_call(
-        middle_kernel,
+        functools.partial(middle_kernel, listed),
         out_shape=(
             shape((2, 4, blocks_x, LANES), F32),
             shape((blocks_x - 2, blocks_y, LANES), F32),
@@ -521,7 +522,7 @@
         ),
         in_specs=[ANY] + [VMEM] * 5,
         out_specs=(VMEM,) * 3,
-        scratch_shapes=pair_scratch(blocks_x, blocks_y, blocks_x - 2, codes.shape[0]),
+        scratch_shapes=pair_scratch(blocks_x, blocks_y, blocks_x - 2, listed),
         compiler_params=params(),
         cost_estimate=pl.CostEstimate(
             flops=4_000_000_000, bytes_accessed=400_000, transcendentals=1_300_000
@@ -554,11 +555,11 @@
     ]
     low, high = neighbours_of(*edges, ("chip", "core"), lax.axis_index("core"))
     edge, known = pl.pallas_call(
-        edge_kernel,
+        functools.partial(edge_kernel, listed),
         out_shape=(shape((2, blocks_y, LANES), F32), shape(sources, F32)),
         in_specs=[ANY] + [VMEM] * 6,
         out_specs=(VMEM,) * 2,
-        scratch_shapes=pair_scratch(blocks_x, blocks_y, 2, codes.shape[0]),
+        scratch_shapes=pair_scratch(blocks_x, blocks_y, 2, listed),
         compiler_params=params(),
         cost_estimate=pl.CostEstimate(
             flops=4_000_000_000, bytes_accessed=400_000, transcendentals=1_300_000
@@ -566,12 +567,12 @@
         name="edge_pairs",
     )(codes, positions, masses, smoothing, prev, following, own)
     sums, table = pl.pallas_call(
-        rim_kernel,
+        functools.partial(rim_kernel, listed),
         out_shape=(shape(masses.shape, F32), shape((2, owners // 2, EARLY + 1, LANES), F32)),
         in_specs=[ANY] + [VMEM] * 11,
         out_specs=(VMEM, VMEM),
         scratch_shapes=[
-            pltpu.SMEM(codes.shape, jnp.int32),
+            pltpu.SMEM((blocks_x * blocks_y,), jnp.int32),
             pltpu.SemaphoreType.DMA(()),
             pltpu.VMEM((128, LANES), F32),
             pltpu.VMEM((6 * (blocks_x + 2), 8, LANES), F32),
@@ -581,7 +582,7 @@
             pltpu.VMEM((9, 8, LANES), F32),
             pltpu.VMEM((blocks_x, 24 * blocks_y, LANES), F32),
         ]
-        + product_scratch(2 * blocks_x, codes.shape[0]),
+        + product_scratch(2 * blocks_x, listed),
         compiler_params=params(),
         cost_estimate=pl.CostEstimate(
             flops=200_000_000, bytes_accessed=400_000, transcendentals=400_000

time: 32.5 us -> 32.4 us (level)
  Pallas kernels: 7.71 us -> 7.32 us
    pallas_call x3, Pallas kernels: 6.69 us -> 6.31 us  [the longest x1 2.18 us: shards(): pl.pallas_call(functools.partial(middle_kernel, listed), out_shape=(shape...]
where the time goes in v5:
time: 32.4 us; the launch traced here: 32.2 us
  starting transfers between devices  15.7 us (48%)
  Pallas kernels  7.32 us (23%)
  waiting for transfers between devices  6.08 us (19%)
  other arithmetic  2.06 us (6%)
  between operations  0.85 us (3%)
    ppermute x7, starting transfers between devices, swap(): return lax.ppermute(value, axis, [(i, i ^ step) for i in range(count)])  8.01 us
    ppermute x2, starting transfers between devices, neighbours_of(): lax.ppermute(jnp.where(even, low_edge, high_edge), axis, [(i, (i + 1 if i...  7.66 us
    ppermute x7, waiting for transfers between devices, swap(): return lax.ppermute(value, axis, [(i, i ^ step) for i in range(count)])  5.73 us
    pallas_call x1, Pallas kernels, shards(): pl.pallas_call(functools.partial(middle_kernel, listed), out_shape=(shape...  2.18 us
    pallas_call x1, Pallas kernels, shards(): pl.pallas_call(functools.partial(edge_kernel, listed), out_shape=(shape((...  2.13 us
    pallas_call x1, Pallas kernels, shards(): pl.pallas_call(functools.partial(rim_kernel, listed), out_shape=(shape(ma...  2 us
    pallas_call x1, Pallas kernels, shards(): pl.pallas_call(functools.partial(moments_kernel, blocks_x * dom_count, bl...  1.02 us
    select_n x2, other arithmetic, neighbours_of(): jnp.where(even, high_edge, low_edge)  0.8 us
  transfers between devices with their start and end apart: 11, of which 8 were waited for; matrix products, arithmetic and copies ran while one was open for 2% of the time, Pallas kernels for 17%

profile of v5, /device:TPU:0, one launch (start us, length us, event | category | flops | bytes accessed | tf_op | source)
XLA Modules:
  0.0 32.2 jit_solution(8549271573354582978)
XLA Ops:
  0.6 0.0 copy-start.6
  0.6 0.0 copy-start.2
  0.7 0.0 copy-start.4
  0.7 0.8 %select_bitcast_fusion = (f32[4,8,128]{2,1,0:T(8,128)S(1)}, f32[4,1,8,128]{3,2,0,1:T(8,128)S(1)}, f32[4,1,8,128]{3,2,0,1:T(8,128)S(1)}) fusion(pred[]{:T(512)S(6)} %eq.6, f32[1,4,8,128]{3,2,0,1:T(8,128)} %bitcast.18, f32[3,4,8,128]{3,2,1,0:T(8,128)} %pos_ref.7), kind=kLoop, calls=%fused_computation.8 | loop fusion | flops 12288 | bytes 114689 | tf_op jit(solution)/shard_map/jit(_where)/select_n | solution.py:462
  1.4 0.0 copy-start
  1.4 0.0 copy-start.5
  1.5 0.0 copy-start.1
  1.5 5.1 %collective-permute-start = (f32[4,8,128]{2,1,0:T(8,128)S(1)}, f32[4,8,128]{2,1,0:T(8,128)S(1)}, u32[]{:S(2)}, u32[]{:S(2)}) collective-permute-start(f32[4,8,128]{2,1,0:T(8,128)S(1)} %select_bitcast_fusion.1), channel_id=1, source_target_pairs={{0,24},{8,16},{16,8},{24,0},{1,25},{9,17},{17,9},{25,1},{2,26},{10... | collective-permute-start | bytes 49160 | tf_op jit(solution)/shard_map/ppermute | solution.py:464
  6.6 0.0 collective-permute-start.1
  6.6 0.0 copy-done.6
  6.6 0.1 reshape.31.code_ref.far_code_ref
  6.7 0.0 copy-done.2
  6.7 0.0 copy-done.4
  6.7 0.0 copy-done
  6.7 0.0 copy-done.5
  6.7 0.0 copy-done.1
  6.7 0.0 copy-start.3
  6.7 2.2 %middle_pairs.1 = (f32[2,4,4,128]{3,2,1,0:T(4,128)S(1)}, f32[2,8,128]{2,1,0:T(8,128)S(1)}, f32[48,8,128]{2,1,0:T(8,128)S(1)}) custom-call(s32[32]{0:T(128)S(1)} %reshape.31.code_ref.far_code_ref, f32[3,4,8,128]{3,2,1,0:T(8,128)S(1)} %copy-done, f32[4,8,128]{2,1,0:T(8,128)S(1)} %copy-done.1, f32[4,8,128]{2,1,0:T(8,128)S(1)} %copy-done.2, ...), custom_call_target="tpu_custom_call" | custom-call | flops 4000000000 | bytes 400000 | tf_op jit(solution)/shard_map/middle_pairs/pallas_call | solution.py:516
  8.9 0.0 copy-done.3
  8.9 1.0 %moments_by_row.1 = (f32[8,16,128]{2,1,0:T(8,128)S(1)}, s32[4,8,128]{2,1,0:T(8,128)S(1)}, bf16[4,128,1024]{2,1,0:T(8,128)(2,1)S(1)}) custom-call(f32[2,8,128]{2,1,0:T(8,128)S(1)} %get-tuple-element.12.after_ref.middle_ref, f32[3,4,8,128]{3,2,1,0:T(8,128)S(1)} %copy-done, f32[3,4,8,128]{3,2,1,0:T(8,128)S(1)} %copy-done.3, f32[4,8,128]{2,1,0:T(8,128)S(1)} %copy-done.1, ...), custom_call_target="tpu_custom_call" | custom-call | flops 2000000000 | bytes 1400000 | tf_op jit(solution)/shard_map/moments_by_row/pallas_call | solution.py:532
  10.0 0.0 collective-permute-done
  10.0 0.3 %collective-permute-done.1 = f32[4,8,128]{2,1,0:T(8,128)S(1)} collective-permute-done((f32[4,8,128]{2,1,0:T(8,128)S(1)}, f32[4,8,128]{2,1,0:T(8,128)S(1)}, u32[]{:S(2)}, u32[]{:S(2)}) %collective-permute-start.1) | collective-permute-done | bytes 16416 | tf_op jit(solution)/shard_map/ppermute | solution.py:461
  10.4 0.1 collective-permute-start.3
  10.5 2.5 %collective-permute-start.2 = (f32[4,6,128]{2,1,0:T(8,128)S(1)}, f32[4,6,128]{2,1,0:T(8,128)S(1)}, u32[]{:S(2)}, u32[]{:S(2)}) collective-permute-start(f32[4,6,128]{2,1,0:T(8,128)S(1)} %get-tuple-element.33), channel_id=1, source_target_pairs={{0,7},{1,2},{2,1},{3,4},{4,3},{5,6},{6,5},{7,0},{8,15},{9,10},{10,... | collective-permute-start | bytes 36872 | tf_op jit(solution)/shard_map/ppermute | solution.py:464
  13.0 2.1 %edge_pairs.1 = (f32[2,8,128]{2,1,0:T(8,128)S(1)}, f32[48,8,128]{2,1,0:T(8,128)S(1)}) custom-call(s32[32]{0:T(128)S(1)} %reshape.31.code_ref.far_code_ref, f32[3,4,8,128]{3,2,1,0:T(8,128)S(1)} %copy-done, f32[4,8,128]{2,1,0:T(8,128)S(1)} %copy-done.1, f32[4,8,128]{2,1,0:T(8,128)S(1)} %copy-done.2, f32[4,8,128]{2,1,0:T(8,128)S(1)} %get-tuple-element.31.prev_ref, ...), custom_call_target="tpu_custom_call" | custom-call | flops 4000000000 | bytes 400000 | tf_op jit(solution)/shard_map/edge_pairs/pallas_call | solution.py:557
  15.1 0.0 collective-permute-done.3
  15.1 0.0 collective-permute-done.2
  15.2 2.0 %rim_pairs_and_table.1 = (f32[4,8,128]{2,1,0:T(8,128)S(1)}, f32[2,4,17,128]{3,2,1,0:T(8,128)S(1)}) custom-call(s32[32]{0:T(128)S(1)} %reshape.31.code_ref.far_code_ref, f32[2,8,128]{2,1,0:T(8,128)S(1)} %get-tuple-element.12.after_ref.middle_ref, f32[2,8,128]{2,1,0:T(8,128)S(1)} %get-tuple-element.14.edge_ref, f32[48,8,128]{2,1,0:T(8,128)S(1)} %get-tuple-element.15.known_ref, ...), custom_call_target="tpu_custom_call" | custom-call | flops 200000000 | bytes 400000 | tf_op jit(solution)/shard_map/rim_pairs_and_table/pallas_call | solution.py:569
  17.2 0.1 collective-permute-start.4
  17.3 1.2 %collective-permute-done.4 = f32[4,17,128]{2,1,0:T(8,128)S(1)} collective-permute-done((f32[4,17,128]{2,1,0:T(8,128)S(1)}, f32[4,17,128]{2,1,0:T(8,128)S(1)}, u32[]{:S(2)}, u32[]{:S(2)}) %collective-permute-start.4) | collective-permute-done | bytes 34848 | tf_op jit(solution)/shard_map/ppermute | solution.py:455
  18.5 2.0 %collective-permute-start.7 = (f32[1,17,128]{2,1,0:T(8,128)S(1)}, f32[1,17,128]{2,1,0:T(8,128)S(1)}, u32[]{:S(2)}, u32[]{:S(2)}) collective-permute-start(f32[1,17,128]{2,1,0:T(8,128)S(1)} %get-tuple-element.25), channel_id=1, source_target_pairs={{0,6},{2,4},{4,2},{6,0},{1,7},{3,5},{5,3},{7,1},{8,14},{10,12},{12... | collective-permute-start | bytes 26120 | tf_op jit(solution)/shard_map/ppermute | solution.py:455
  20.5 0.5 %collective-permute-start.6 = (f32[1,17,128]{2,1,0:T(8,128)S(1)}, f32[1,17,128]{2,1,0:T(8,128)S(1)}, u32[]{:S(2)}, u32[]{:S(2)}) collective-permute-start(f32[1,17,128]{2,1,0:T(8,128)S(1)} %get-tuple-element.26), channel_id=1, source_target_pairs={{0,4},{2,6},{4,0},{6,2},{1,5},{3,7},{5,1},{7,3},{8,12},{10,14},{12... | collective-permute-start | bytes 26120 | tf_op jit(solution)/shard_map/ppermute | solution.py:455
  21.0 1.0 %collective-permute-start.5 = (f32[1,17,128]{2,1,0:T(8,128)S(1)}, f32[1,17,128]{2,1,0:T(8,128)S(1)}, u32[]{:S(2)}, u32[]{:S(2)}) collective-permute-start(f32[1,17,128]{2,1,0:T(8,128)S(1)} %get-tuple-element.27), channel_id=1, source_target_pairs={{0,2},{2,0},{4,6},{6,4},{1,3},{3,1},{5,7},{7,5},{8,10},{10,8},{12,... | collective-permute-start | bytes 26120 | tf_op jit(solution)/shard_map/ppermute | solution.py:455
  22.1 1.1 %collective-permute-done.7 = f32[1,17,128]{2,1,0:T(8,128)S(1)} collective-permute-done((f32[1,17,128]{2,1,0:T(8,128)S(1)}, f32[1,17,128]{2,1,0:T(8,128)S(1)}, u32[]{:S(2)}, u32[]{:S(2)}) %collective-permute-start.7) | collective-permute-done | bytes 8736 | tf_op jit(solution)/shard_map/ppermute | solution.py:455
  23.2 1.0 %collective-permute-done.6 = f32[1,17,128]{2,1,0:T(8,128)S(1)} collective-permute-done((f32[1,17,128]{2,1,0:T(8,128)S(1)}, f32[1,17,128]{2,1,0:T(8,128)S(1)}, u32[]{:S(2)}, u32[]{:S(2)}) %collective-permute-start.6) | collective-permute-done | bytes 8736 | tf_op jit(solution)/shard_map/ppermute | solution.py:455
  24.2 0.5 %collective-permute-done.5 = f32[1,17,128]{2,1,0:T(8,128)S(1)} collective-permute-done((f32[1,17,128]{2,1,0:T(8,128)S(1)}, f32[1,17,128]{2,1,0:T(8,128)S(1)}, u32[]{:S(2)}, u32[]{:S(2)}) %collective-permute-start.5) | collective-permute-done | bytes 8736 | tf_op jit(solution)/shard_map/ppermute | solution.py:455
  24.7 1.8 %collective-permute-start.10 = (f32[17,128]{1,0:T(8,128)S(1)}, f32[17,128]{1,0:T(8,128)S(1)}, u32[]{:S(2)}, u32[]{:S(2)}) collective-permute-start(f32[17,128]{1,0:T(8,128)S(1)} %fusion.4), channel_id=1, source_target_pairs={{0,24},{8,16},{16,8},{24,0},{1,25},{9,17},{17,9},{25,1},{2,26},{10... | collective-permute-start | bytes 26120 | tf_op jit(solution)/shard_map/ppermute | solution.py:455
  26.6 1.3 %collective-permute-start.9 = (f32[17,128]{1,0:T(8,128)S(1)}, f32[17,128]{1,0:T(8,128)S(1)}, u32[]{:S(2)}, u32[]{:S(2)}) collective-permute-start(f32[17,128]{1,0:T(8,128)S(1)} %fusion.4), channel_id=1, source_target_pairs={{0,16},{8,24},{16,0},{24,8},{1,17},{9,25},{17,1},{25,9},{2,18},{10... | collective-permute-start | bytes 26120 | tf_op jit(solution)/shard_map/ppermute | solution.py:455
  27.9 1.2 %collective-permute-start.8 = (f32[17,128]{1,0:T(8,128)S(1)}, f32[17,128]{1,0:T(8,128)S(1)}, u32[]{:S(2)}, u32[]{:S(2)}) collective-permute-start(f32[17,128]{1,0:T(8,128)S(1)} %fusion.4), channel_id=1, source_target_pairs={{0,8},{8,0},{16,24},{24,16},{1,9},{9,1},{17,25},{25,17},{2,10},{10... | collective-permute-start | bytes 26120 | tf_op jit(solution)/shard_map/ppermute | solution.py:455
  29.1 0.6 %fusion = f32[4,8,128]{2,1,0:T(8,128)} fusion(f32[4,8,128]{2,1,0:T(8,128)S(1)} %copy-done.2, f32[4,8,128]{2,1,0:T(8,128)S(1)} %get-tuple-element.20), kind=kLoop, calls=%fused_computation.3 | loop fusion | flops 16384 | bytes 49152 | tf_op jit(solution)/shard_map/div | solution.py:594
  29.7 0.5 %collective-permute-done.10 = f32[17,128]{1,0:T(8,128)S(1)} collective-permute-done((f32[17,128]{1,0:T(8,128)S(1)}, f32[17,128]{1,0:T(8,128)S(1)}, u32[]{:S(2)}, u32[]{:S(2)}) %collective-permute-start.10) | collective-permute-done | bytes 8736 | tf_op jit(solution)/shard_map/ppermute | solution.py:455
  30.2 0.9 %collective-permute-done.9 = f32[17,128]{1,0:T(8,128)S(1)} collective-permute-done((f32[17,128]{1,0:T(8,128)S(1)}, f32[17,128]{1,0:T(8,128)S(1)}, u32[]{:S(2)}, u32[]{:S(2)}) %collective-permute-start.9) | collective-permute-done | bytes 8736 | tf_op jit(solution)/shard_map/ppermute | solution.py:455
  31.1 0.4 %collective-permute-done.8 = f32[17,128]{1,0:T(8,128)S(1)} collective-permute-done((f32[17,128]{1,0:T(8,128)S(1)}, f32[17,128]{1,0:T(8,128)S(1)}, u32[]{:S(2)}, u32[]{:S(2)}) %collective-permute-start.8) | collective-permute-done | bytes 8736 | tf_op jit(solution)/shard_map/ppermute | solution.py:455
  31.6 0.6 %add_add_fusion = f32[17,128]{1,0:T(8,128)} fusion(f32[17,128]{1,0:T(8,128)S(1)} %collective-permute-done.9, f32[17,128]{1,0:T(8,128)S(1)} %collective-permute-done.10, f32[17,128]{1,0:T(8,128)S(1)} %fusion.4, f32[17,128]{1,0:T(8,128)S(1)} %collective-permute-done.8), kind=kLoop, calls=%fused_computation.15 | loop fusion | flops 6528 | bytes 43520 | tf_op jit(solution)/shard_map/add | solution.py:474
  (11 shorter events, 0.1 us)
Async XLA Ops:
  0.6 6.0 %copy-start.6 = (s32[4,8,5]{1,0,2:T(4,128)S(1)}, s32[4,8,5]{1,0,2:T(4,128)}, u32[]{:S(2)}) copy-start(s32[4,8,5]{1,0,2:T(4,128)} %param.11) | copy-start | bytes 1924
  0.6 6.0 %copy-start.2 = (f32[4,8,128]{2,1,0:T(8,128)S(1)}, f32[4,8,128]{2,1,0:T(8,128)}, u32[]{:S(2)}) copy-start(f32[4,8,128]{2,1,0:T(8,128)} %smooth_ref.5) | copy-start | bytes 49156
  0.7 6.0 %copy-start.4 = (s32[4,8,128]{2,1,0:T(8,128)S(1)}, s32[4,8,128]{2,1,0:T(8,128)}, u32[]{:S(2)}) copy-start(s32[4,8,128]{2,1,0:T(8,128)} %group_ref.3) | copy-start | bytes 49156
  1.4 5.3 %copy-start = (f32[3,4,8,128]{3,2,1,0:T(8,128)S(1)}, f32[3,4,8,128]{3,2,1,0:T(8,128)}, u32[]{:S(2)}) copy-start(f32[3,4,8,128]{3,2,1,0:T(8,128)} %pos_ref.7) | copy-start | bytes 147460
  1.4 5.3 %copy-start.5 = (s32[1024]{0:T(1024)S(1)}, s32[1024]{0:T(1024)}, u32[]{:S(2)}) copy-start(s32[1024]{0:T(1024)} %param.13) | copy-start | bytes 12292
  1.5 5.2 %copy-start.1 = (f32[4,8,128]{2,1,0:T(8,128)S(1)}, f32[4,8,128]{2,1,0:T(8,128)}, u32[]{:S(2)}) copy-start(f32[4,8,128]{2,1,0:T(8,128)} %mass_ref.7) | copy-start | bytes 49156
  1.5 8.5 %collective-permute-start = (f32[4,8,128]{2,1,0:T(8,128)S(1)}, f32[4,8,128]{2,1,0:T(8,128)S(1)}, u32[]{:S(2)}, u32[]{:S(2)}) collective-permute-start(f32[4,8,128]{2,1,0:T(8,128)S(1)} %select_bitcast_fusion.1), channel_id=1, source_target_pairs={{0,24},{8,16},{16,8},{24,0},{1,25},{9,17},{17,9},{25,1},{2,26},{10... | collective-permute-start | bytes 49160 | tf_op jit(solution)/shard_map/ppermute | solution.py:464
  6.6 3.7 %collective-permute-start.1 = (f32[4,8,128]{2,1,0:T(8,128)S(1)}, f32[4,8,128]{2,1,0:T(8,128)S(1)}, u32[]{:S(2)}, u32[]{:S(2)}) collective-permute-start(f32[4,8,128]{2,1,0:T(8,128)S(1)} %get-tuple-element.22), channel_id=1, source_target_pairs={{0,8},{8,0},{16,24},{24,16},{1,9},{9,1},{17,25},{25,17},{2,10},{10... | collective-permute-start | bytes 49160 | tf_op jit(solution)/shard_map/ppermute | solution.py:461
  6.7 2.2 %copy-start.3 = (f32[3,4,8,128]{3,2,1,0:T(8,128)S(1)}, f32[3,4,8,128]{3,2,1,0:T(8,128)}, u32[]{:S(2)}) copy-start(f32[3,4,8,128]{3,2,1,0:T(8,128)} %vel_ref.1) | copy-start | bytes 147460
  10.4 4.8 %collective-permute-start.3 = (f32[4,6,128]{2,1,0:T(8,128)S(1)}, f32[4,6,128]{2,1,0:T(8,128)S(1)}, u32[]{:S(2)}, u32[]{:S(2)}) collective-permute-start(f32[4,6,128]{2,1,0:T(8,128)S(1)} %get-tuple-element.32), channel_id=1, source_target_pairs={{0,1},{1,0},{2,3},{3,2},{4,5},{5,4},{6,7},{7,6},{8,9},{9,8},{10,11... | collective-permute-start | bytes 36872 | tf_op jit(solution)/shard_map/ppermute | solution.py:461
  10.5 4.7 %collective-permute-start.2 = (f32[4,6,128]{2,1,0:T(8,128)S(1)}, f32[4,6,128]{2,1,0:T(8,128)S(1)}, u32[]{:S(2)}, u32[]{:S(2)}) collective-permute-start(f32[4,6,128]{2,1,0:T(8,128)S(1)} %get-tuple-element.33), channel_id=1, source_target_pairs={{0,7},{1,2},{2,1},{3,4},{4,3},{5,6},{6,5},{7,0},{8,15},{9,10},{10,... | collective-permute-start | bytes 36872 | tf_op jit(solution)/shard_map/ppermute | solution.py:464
  17.2 1.3 %collective-permute-start.4 = (f32[4,17,128]{2,1,0:T(8,128)S(1)}, f32[4,17,128]{2,1,0:T(8,128)S(1)}, u32[]{:S(2)}, u32[]{:S(2)}) collective-permute-start(f32[4,17,128]{2,1,0:T(8,128)S(1)} %slice_bitcast_fusion), channel_id=1, source_target_pairs={{0,1},{1,0},{2,3},{3,2},{4,5},{5,4},{6,7},{7,6},{8,9},{9,8},{10,11... | collective-permute-start | bytes 104456 | tf_op jit(solution)/shard_map/ppermute | solution.py:455
  18.5 4.7 %collective-permute-start.7 = (f32[1,17,128]{2,1,0:T(8,128)S(1)}, f32[1,17,128]{2,1,0:T(8,128)S(1)}, u32[]{:S(2)}, u32[]{:S(2)}) collective-permute-start(f32[1,17,128]{2,1,0:T(8,128)S(1)} %get-tuple-element.25), channel_id=1, source_target_pairs={{0,6},{2,4},{4,2},{6,0},{1,7},{3,5},{5,3},{7,1},{8,14},{10,12},{12... | collective-permute-start | bytes 26120 | tf_op jit(solution)/shard_map/ppermute | solution.py:455
  20.5 3.7 %collective-permute-start.6 = (f32[1,17,128]{2,1,0:T(8,128)S(1)}, f32[1,17,128]{2,1,0:T(8,128)S(1)}, u32[]{:S(2)}, u32[]{:S(2)}) collective-permute-start(f32[1,17,128]{2,1,0:T(8,128)S(1)} %get-tuple-element.26), channel_id=1, source_target_pairs={{0,4},{2,6},{4,0},{6,2},{1,5},{3,7},{5,1},{7,3},{8,12},{10,14},{12... | collective-permute-start | bytes 26120 | tf_op jit(solution)/shard_map/ppermute | solution.py:455
  21.0 3.7 %collective-permute-start.5 = (f32[1,17,128]{2,1,0:T(8,128)S(1)}, f32[1,17,128]{2,1,0:T(8,128)S(1)}, u32[]{:S(2)}, u32[]{:S(2)}) collective-permute-start(f32[1,17,128]{2,1,0:T(8,128)S(1)} %get-tuple-element.27), channel_id=1, source_target_pairs={{0,2},{2,0},{4,6},{6,4},{1,3},{3,1},{5,7},{7,5},{8,10},{10,8},{12,... | collective-permute-start | bytes 26120 | tf_op jit(solution)/shard_map/ppermute | solution.py:455
  24.7 5.5 %collective-permute-start.10 = (f32[17,128]{1,0:T(8,128)S(1)}, f32[17,128]{1,0:T(8,128)S(1)}, u32[]{:S(2)}, u32[]{:S(2)}) collective-permute-start(f32[17,128]{1,0:T(8,128)S(1)} %fusion.4), channel_id=1, source_target_pairs={{0,24},{8,16},{16,8},{24,0},{1,25},{9,17},{17,9},{25,1},{2,26},{10... | collective-permute-start | bytes 26120 | tf_op jit(solution)/shard_map/ppermute | solution.py:455
  26.6 4.6 %collective-permute-start.9 = (f32[17,128]{1,0:T(8,128)S(1)}, f32[17,128]{1,0:T(8,128)S(1)}, u32[]{:S(2)}, u32[]{:S(2)}) collective-permute-start(f32[17,128]{1,0:T(8,128)S(1)} %fusion.4), channel_id=1, source_target_pairs={{0,16},{8,24},{16,0},{24,8},{1,17},{9,25},{17,1},{25,9},{2,18},{10... | collective-permute-start | bytes 26120 | tf_op jit(solution)/shard_map/ppermute | solution.py:455
  27.9 3.7 %collective-permute-start.8 = (f32[17,128]{1,0:T(8,128)S(1)}, f32[17,128]{1,0:T(8,128)S(1)}, u32[]{:S(2)}, u32[]{:S(2)}) collective-permute-start(f32[17,128]{1,0:T(8,128)S(1)} %fusion.4), channel_id=1, source_target_pairs={{0,8},{8,0},{16,24},{24,16},{1,9},{9,1},{17,25},{25,17},{2,10},{10... | collective-permute-start | bytes 26120 | tf_op jit(solution)/shard_map/ppermute | solution.py:455

commit v6 on v5

--- a/solution.py
+++ b/solution.py
@@ -152,29 +152,29 @@
         nat_ref[start + kind * 8 : start + kind * 8 + count, :] = line
 
 
-def pair_sums(sides, pieces=(), add=False):
+def pair_sums(sides, pieces=()):
     rows = 32
     steps = []
-    for target, sources, roots, total in sides:
+    for target, sources, roots, total, base in sides:
         count = roots.shape[0]
         for first in range(0, count, 2):
-            steps.append((target, sources, roots, total, first, min(2, count - first), count))
+            steps.append((target, sources, roots, total, base, first, min(2, count - first), count))
 
     def product(step):
-        target, sources, _, _, first, width, _ = step
+        target, sources, _, _, _, first, width, _ = step
         right = sources[:, first * LANES : (first + width) * LANES]
         return jnp.dot(target[...], right, preferred_element_type=F32)
 
     ready = product(steps[0])
     chunks = None
-    for number, (_, _, roots, total, first, width, count) in enumerate(steps):
+    for number, (_, _, roots, total, base, first, width, count) in enumerate(steps):
         squared = ready
         if number + 1 < len(steps):
             ready = product(steps[number + 1])
         if first == 0:
             chunks = [None] * (LANES // rows)
-            if add:
-                chunks = [total[r * rows : (r + 1) * rows, :] for r in range(len(chunks))]
+            if base is not None:
+                chunks = [base[r * rows : (r + 1) * rows, :] for r in range(len(chunks))]
         limits = []
         for k in range(width):
             root = roots[first + k : first + k + 1, :]
@@ -231,12 +231,70 @@
     root_ref[number, k : k + 1, :] = root[0:1]
 
 
-def sides_of(count, first, end, mat_ref, near_ref, root_ref, total_ref):
+def sides_of(count, first, end, mat_ref, near_ref, root_ref, total_ref, base_ref=None):
     lanes, rows = pl.ds(first * LANES, (end - first) * LANES), pl.ds(first, end - first)
     return [
-        (mat_ref.at[n], near_ref.at[n, :, lanes], root_ref.at[n, rows], total_ref.at[n])
+        (
+            mat_ref.at[n], near_ref.at[n, :, lanes], root_ref.at[n, rows], total_ref.at[n],
+            None if base_ref is None else base_ref.at[n],
+        )
         for n in range(count)
     ]
+
+
+def put_moments(lhs_ref, ys, sums, mass, radius, rows):
+    owners = lhs_ref.shape[0] // 2
+    owner_ids = lax.broadcasted_iota(jnp.int32, (owners, LANES), 0)
+    moment = mass * (sums * DENSITY_FACTOR / (radius * radius * radius))
+    high_part = rounded(moment)
+    low_part = moment - high_part
+    owner = rows >> 7
+    for y in ys:
+        mine = jnp.broadcast_to(owner[y : y + 1, :], owner_ids.shape) == owner_ids
+        lhs_ref[:, y * LANES : (y + 1) * LANES] = jnp.concatenate(
+            [
+                jnp.where(mine, jnp.broadcast_to(part[y : y + 1, :], mine.shape), 0.0)
+                for part in (high_part, low_part)
+            ],
+            axis=0,
+        ).astype(BF16)
+
+
+def inner_moments(total_ref, first, hot, lhs_ref, sums, mass, radius, rows):
+    last = mass.shape[0] - 1
+    put_moments(lhs_ref, range(1, last), sums, mass, radius, rows)
+    lanes = slice(LANES, last * LANES)
+    product = lax.dot_general(hot[:, lanes], lhs_ref[:, lanes], NT, preferred_element_type=F32)
+    total_ref[...] = product if first else total_ref[...] + product
+
+
+def start_rim(
+    src_ref, pos_ref, mass_ref, smooth_ref, middle_ref, rows_ref, hot_ref,
+    mat_ref, self_ref, moment_ref, tgt_ref, near_ref, root_ref, lhs_ref,
+):
+    blocks_x, blocks_y, _ = mass_ref.shape
+    squares = square_mask()
+    rim = [(x, side * (blocks_y - 1)) for x in range(blocks_x) for side in range(2)]
+    for x in range(blocks_x):
+        lines = target_rows([pos_ref[c, x] for c in range(3)], smooth_ref[x])
+        for row, line in enumerate(lines):
+            tgt_ref[x, row * blocks_y : (row + 1) * blocks_y, :] = line
+    for n, (x, y) in enumerate(rim):
+        mat_ref[n] = target_matrix(tgt_ref[x, pl.ds(y, 24, stride=blocks_y), :])
+    for n, (x, y) in enumerate(rim):
+        put_source(near_ref, root_ref, n, 0, src_ref[(x + 1) * blocks_y + y], 0.0, squares)
+
+    def middle_moments(turn):
+        x = turn + 1
+        inner_moments(
+            moment_ref, turn == 0, hot_ref[x], lhs_ref.at[turn], middle_ref[turn],
+            mass_ref[x], smooth_ref[x], rows_ref[x],
+        )
+
+    pair_sums(
+        sides_of(len(rim), 0, 1, mat_ref, near_ref, root_ref, self_ref),
+        [functools.partial(middle_moments, turn) for turn in range(blocks_x - 2)],
+    )
 
 
 def load_codes(far_ref, code_ref, sem):
@@ -248,6 +306,7 @@
 def block_pairs(
     listed, x_first, x_step, x_count, known_ref, far_code_ref, pos_ref, mass_ref, smooth_ref, prev_ref, next_ref,
     out_ref, src_ref, code_ref, sem, nat_ref, shift_ref, tgt_ref, mat_ref, near_ref, root_ref, total_ref,
+    ahead=None,
 ):
     blocks_x, blocks_y, _ = mass_ref.shape
     codes = load_codes(far_code_ref, code_ref, sem)
@@ -280,6 +339,8 @@
         line = src_ref[(x_first + turn * x_step + 1) * blocks_y + y]
         put_source(near_ref, root_ref, number, 0, line, 0.0, squares)
     pair_sums(sides_of(len(blocks), 0, 1, mat_ref, near_ref, root_ref, total_ref))
+    if ahead is not None:
+        ahead()
     codes.wait()
     for number, (turn, y) in enumerate(blocks):
         x = x_first + turn * x_step
@@ -299,8 +360,8 @@
     pieces = [None] * (x_count * per_row + 1)
     for turn in range(x_count):
         pieces[(turn + 1) * per_row] = functools.partial(row_sums, turn)
-    sides = sides_of(len(blocks), 1, listed, mat_ref, near_ref, root_ref, total_ref)
-    pair_sums(sides, pieces, add=True)
+    sides = sides_of(len(blocks), 1, listed, mat_ref, near_ref, root_ref, total_ref, total_ref)
+    pair_sums(sides, pieces)
 
 
 def middle_kernel(
@@ -320,12 +381,19 @@
 
 
 def edge_kernel(
-    listed, code_ref, pos_ref, mass_ref, smooth_ref, prev_ref, next_ref, known_ref, out_ref, src_ref, *scratch
+    listed, code_ref, pos_ref, mass_ref, smooth_ref, prev_ref, next_ref, known_ref,
+    middle_ref, rows_ref, hot_ref,
+    out_ref, src_ref, rim_mat_ref, self_ref, moment_ref,
+    rim_tgt_ref, rim_near_ref, rim_root_ref, lhs_ref, *scratch
 ):
     blocks_x = mass_ref.shape[0]
+    ahead = functools.partial(
+        start_rim, src_ref, pos_ref, mass_ref, smooth_ref, middle_ref, rows_ref, hot_ref,
+        rim_mat_ref, self_ref, moment_ref, rim_tgt_ref, rim_near_ref, rim_root_ref, lhs_ref,
+    )
     block_pairs(
         listed, 0, blocks_x - 1, 2, known_ref, code_ref, pos_ref, mass_ref, smooth_ref, prev_ref, next_ref,
-        out_ref, src_ref, *scratch,
+        out_ref, src_ref, *scratch, ahead=ahead,
     )
 
 
@@ -349,14 +417,15 @@
 
 
 def rim_kernel(
-    listed, far_code_ref, middle_ref, edge_ref, known_ref, pos_ref, mass_ref, smooth_ref,
-    low_ref, high_ref, rows_ref, hot_ref, early_ref,
-    sum_ref, table_ref, code_ref, sem, nat_ref, src_ref, md_ref, lhs_ref, row_sum_ref,
-    shift_ref, tgt_ref, mat_ref, near_ref, root_ref, total_ref,
+    listed, far_code_ref, middle_ref, edge_ref, known_ref, mat_ref, self_ref, moment_ref,
+    mass_ref, smooth_ref, low_ref, high_ref, rows_ref, hot_ref, early_ref,
+    sum_ref, table_ref, code_ref, sem, nat_ref, src_ref, md_ref, lhs_ref, total_moment_ref,
+    shift_ref, near_ref, root_ref, total_ref,
 ):
     blocks_x, blocks_y, _ = mass_ref.shape
     owners = early_ref.shape[0]
     wide = blocks_x + 2
+    last = blocks_y - 1
     codes = load_codes(far_code_ref, code_ref, sem)
     for side, ref in enumerate((low_ref, high_ref)):
         store_source(nat_ref, side * 64, wide, [ref[c] for c in range(3)], ref[3])
@@ -371,52 +440,13 @@
     squares = square_mask()
     for x in range(blocks_x):
         edge = x == 0 or x == blocks_x - 1
-        turn = (1 if x else 0) if edge else x - 1
-        sum_ref[x] = (edge_ref if edge else middle_ref)[turn]
-        lines = target_rows([pos_ref[c, x] for c in range(3)], smooth_ref[x])
-        for row, line in enumerate(lines):
-            tgt_ref[x, row * blocks_y : (row + 1) * blocks_y, :] = line
-    for x in range(blocks_x):
-        for side in range(2):
-            y = side * (blocks_y - 1)
-            mat_ref[2 * x + side] = target_matrix(tgt_ref[x, pl.ds(y, 24, stride=blocks_y), :])
-    for x in range(blocks_x):
-        for side in range(2):
-            line = src_ref[(3 * side + 1) * wide + x + 1]
-            put_source(near_ref, root_ref, 2 * x + side, 0, line, 0.0, squares)
-
-    owner_ids = lax.broadcasted_iota(jnp.int32, (owners, LANES), 0)
-    last = blocks_y - 1
-
-    def put_moments(x, ys):
-        radius = smooth_ref[x]
-        moment = mass_ref[x] * (sum_ref[x] * DENSITY_FACTOR / (radius * radius * radius))
-        high_part = rounded(moment)
-        low_part = moment - high_part
-        owner = rows_ref[x] >> 7
-        for y in ys:
-            mine = jnp.broadcast_to(owner[y : y + 1, :], owner_ids.shape) == owner_ids
-            lhs_ref[x, :, y * LANES : (y + 1) * LANES] = jnp.concatenate(
-                [
-                    jnp.where(mine, jnp.broadcast_to(part[y : y + 1, :], mine.shape), 0.0)
-                    for part in (high_part, low_part)
-                ],
-                axis=0,
-            ).astype(BF16)
-
-    def inner_moments(x):
-        put_moments(x, range(1, last))
-        lanes = slice(LANES, last * LANES)
-        product = lax.dot_general(
-            hot_ref[x, :, lanes], lhs_ref[x, :, lanes], NT, preferred_element_type=F32
+        sum_ref[x] = (edge_ref if edge else middle_ref)[(1 if x else 0) if edge else x - 1]
+    total_moment_ref[...] = moment_ref[...]
+    for x in (0, blocks_x - 1):
+        inner_moments(
+            total_moment_ref, False, hot_ref[x], lhs_ref.at[x], sum_ref[x],
+            mass_ref[x], smooth_ref[x], rows_ref[x],
         )
-        row_sum_ref[...] = product if x == 0 else row_sum_ref[...] + product
-
-    products = (mat_ref, near_ref, root_ref, total_ref)
-    pair_sums(
-        sides_of(2 * blocks_x, 0, 1, *products),
-        [functools.partial(inner_moments, x) for x in range(blocks_x)],
-    )
     codes.wait()
     for x in range(blocks_x):
         for side in range(2):
@@ -426,15 +456,15 @@
                 step_x = (code * 11) >> 5
                 line = src_ref[(3 * side + code - 3 * step_x) * wide + x + step_x]
                 put_source(near_ref, root_ref, 2 * x + side, k, line, shift_ref[code], squares)
-    pair_sums(sides_of(2 * blocks_x, 1, listed, *products), add=True)
+    pair_sums(sides_of(2 * blocks_x, 1, listed, mat_ref, near_ref, root_ref, total_ref, self_ref))
     sums = column_sums([total_ref[number] for number in range(2 * blocks_x)])
     for x in range(blocks_x):
         for side in range(2):
             y = side * last
             sum_ref[x, y : y + 1, :] = sums[2 * x + side : 2 * x + side + 1, :]
-        put_moments(x, (0, last))
+        put_moments(lhs_ref.at[x], (0, last), sum_ref[x], mass_ref[x], smooth_ref[x], rows_ref[x])
     ends = [(x, slice(y * LANES, (y + 1) * LANES)) for x in range(blocks_x) for y in (0, last)]
-    total = row_sum_ref[...] + lax.dot_general(
+    total = total_moment_ref[...] + lax.dot_general(
         jnp.concatenate([hot_ref[x, :, lanes] for x, lanes in ends], axis=1),
         jnp.concatenate([lhs_ref[x, :, lanes] for x, lanes in ends], axis=1),
         NT,
@@ -554,22 +584,35 @@
         for side, y in ((0, 0), (1, blocks_y - 1))
     ]
     low, high = neighbours_of(*edges, ("chip", "core"), lax.axis_index("core"))
-    edge, known = pl.pallas_call(
+    rims = 2 * blocks_x
+    edge, known, rim_match, rim_self, middle_moment = pl.pallas_call(
         functools.partial(edge_kernel, listed),
-        out_shape=(shape((2, blocks_y, LANES), F32), shape(sources, F32)),
-        in_specs=[ANY] + [VMEM] * 6,
-        out_specs=(VMEM,) * 2,
-        scratch_shapes=pair_scratch(blocks_x, blocks_y, 2, listed),
+        out_shape=(
+            shape((2, blocks_y, LANES), F32),
+            shape(sources, F32),
+            shape((rims, LANES, 48), BF16),
+            shape((rims, LANES, LANES), F32),
+            shape((LANES, 2 * owners), F32),
+        ),
+        in_specs=[ANY] + [VMEM] * 9,
+        out_specs=(VMEM,) * 5,
+        scratch_shapes=[
+            pltpu.VMEM((blocks_x, 24 * blocks_y, LANES), F32),
+            pltpu.VMEM((rims, 48, LANES), BF16),
+            pltpu.VMEM((rims, 8, LANES), F32),
+            pltpu.VMEM((blocks_x - 2, 2 * owners, chunk), BF16),
+        ]
+        + pair_scratch(blocks_x, blocks_y, 2, listed),
         compiler_params=params(),
         cost_estimate=pl.CostEstimate(
             flops=4_000_000_000, bytes_accessed=400_000, transcendentals=1_300_000
         ),
         name="edge_pairs",
-    )(codes, positions, masses, smoothing, prev, following, own)
+    )(codes, positions, masses, smoothing, prev, following, own, middle, rows, hot)
     sums, table = pl.pallas_call(
         functools.partial(rim_kernel, listed),
         out_shape=(shape(masses.shape, F32), shape((2, owners // 2, EARLY + 1, LANES), F32)),
-        in_specs=[ANY] + [VMEM] * 11,
+        in_specs=[ANY] + [VMEM] * 13,
         out_specs=(VMEM, VMEM),
         scratch_shapes=[
             pltpu.SMEM((blocks_x * blocks_y,), jnp.int32),
@@ -580,16 +623,16 @@
             pltpu.VMEM((blocks_x, 2 * owners, chunk), BF16),
             pltpu.VMEM((LANES, 2 * owners), F32),
             pltpu.VMEM((9, 8, LANES), F32),
-            pltpu.VMEM((blocks_x, 24 * blocks_y, LANES), F32),
         ]
-        + product_scratch(2 * blocks_x, listed),
+        + product_scratch(rims, listed)[1:],
         compiler_params=params(),
         cost_estimate=pl.CostEstimate(
             flops=200_000_000, bytes_accessed=400_000, transcendentals=400_000
         ),
         name="rim_pairs_and_table",
     )(
-        codes, middle, edge, known, positions, masses, smoothing, low, high, rows, hot, early
+        codes, middle, edge, known, rim_match, rim_self, middle_moment,
+        masses, smoothing, low, high, rows, hot, early,
     )
     density = sums * DENSITY_FACTOR / (smoothing * smoothing * smoothing)
     return (density, summed(to_owner(table), "dom"))

time: 32.4 us -> 33.3 us (1.028)
  waiting for transfers between devices: 6.08 us -> 7.15 us
  starting transfers between devices: 15.7 us -> 15.3 us
    ppermute x2, starting transfers between devices: 0.07 us -> 3.09 us  [neighbours_of(): lax.ppermute(jnp.where(even, high_edge, low_edge), axis, [(i, i ^ 1) for...]
    ppermute x2, starting transfers between devices: 7.66 us -> 5.09 us  [neighbours_of(): lax.ppermute(jnp.where(even, low_edge, high_edge), axis, [(i, (i + 1 if i...]
    ppermute x7, waiting for transfers between devices: 5.73 us -> 7.14 us  [swap(): return lax.ppermute(value, axis, [(i, i ^ step) for i in range(count)])]
    ppermute x7, starting transfers between devices: 8.01 us -> 7.11 us  [swap(): return lax.ppermute(value, axis, [(i, i ^ step) for i in range(count)])]
    ppermute x2, waiting for transfers between devices: 0.35 us -> 0.01 us  [neighbours_of(): lax.ppermute(jnp.where(even, high_edge, low_edge), axis, [(i, i ^ 1) for...]
  transfers between devices with their start and end apart: 11 -> 11, of which waited for: 8 -> 7; matrix products, arithmetic and copies ran while one was open for 2% -> 2% of each run, Pallas kernels for 17% -> 17%
where the time goes in v6:
time: 33.3 us; the launch traced here: 33.1 us
  starting transfers between devices  15.3 us (46%)
  Pallas kernels  7.59 us (23%)
  waiting for transfers between devices  7.15 us (21%)
  other arithmetic  2.06 us (6%)
  between operations  0.85 us (3%)
    ppermute x7, waiting for transfers between devices, swap(): return lax.ppermute(value, axis, [(i, i ^ step) for i in range(count)])  7.14 us
    ppermute x7, starting transfers between devices, swap(): return lax.ppermute(value, axis, [(i, i ^ step) for i in range(count)])  7.11 us
    ppermute x2, starting transfers between devices, neighbours_of(): lax.ppermute(jnp.where(even, low_edge, high_edge), axis, [(i, (i + 1 if i...  5.09 us
    ppermute x2, starting transfers between devices, neighbours_of(): lax.ppermute(jnp.where(even, high_edge, low_edge), axis, [(i, i ^ 1) for...  3.09 us
    pallas_call x1, Pallas kernels, shards(): pl.pallas_call(functools.partial(edge_kernel, listed), out_shape=(shape((...  2.45 us
    pallas_call x1, Pallas kernels, shards(): pl.pallas_call(functools.partial(middle_kernel, listed), out_shape=(shape...  2.18 us
    pallas_call x1, Pallas kernels, shards(): pl.pallas_call(functools.partial(rim_kernel, listed), out_shape=(shape(ma...  1.95 us
    pallas_call x1, Pallas kernels, shards(): pl.pallas_call(functools.partial(moments_kernel, blocks_x * dom_count, bl...  1.02 us
  transfers between devices with their start and end apart: 11, of which 7 were waited for; matrix products, arithmetic and copies ran while one was open for 2% of the time, Pallas kernels for 17%

profile of v6, /device:TPU:0, one launch (start us, length us, event | category | flops | bytes accessed | tf_op | source)
XLA Modules:
  0.0 33.1 jit_solution(12426478924390482112)
XLA Ops:
  0.6 0.0 copy-start.2
  0.6 0.8 %select_bitcast_fusion = (f32[4,8,128]{2,1,0:T(8,128)S(1)}, f32[4,1,8,128]{3,2,0,1:T(8,128)S(1)}, f32[4,1,8,128]{3,2,0,1:T(8,128)S(1)}) fusion(pred[]{:T(512)S(6)} %eq.6, f32[1,4,8,128]{3,2,0,1:T(8,128)} %bitcast.18, f32[3,4,8,128]{3,2,1,0:T(8,128)} %pos_ref.5), kind=kLoop, calls=%fused_computation.8 | loop fusion | flops 12288 | bytes 114689 | tf_op jit(solution)/shard_map/jit(_where)/select_n | solution.py:492
  1.4 3.0 %collective-permute-start.1 = (f32[4,8,128]{2,1,0:T(8,128)S(1)}, f32[4,8,128]{2,1,0:T(8,128)S(1)}, u32[]{:S(2)}, u32[]{:S(2)}) collective-permute-start(f32[4,8,128]{2,1,0:T(8,128)S(1)} %get-tuple-element.28), channel_id=1, source_target_pairs={{0,8},{8,0},{16,24},{24,16},{1,9},{9,1},{17,25},{25,17},{2,10},{10... | collective-permute-start | bytes 49160 | tf_op jit(solution)/shard_map/ppermute | solution.py:491
  4.4 0.0 copy-start.6
  4.5 0.0 copy-start.1
  4.5 0.0 copy-start.4
  4.5 0.0 copy-start.5
  4.5 0.0 copy-start
  4.5 2.5 %collective-permute-start = (f32[4,8,128]{2,1,0:T(8,128)S(1)}, f32[4,8,128]{2,1,0:T(8,128)S(1)}, u32[]{:S(2)}, u32[]{:S(2)}) collective-permute-start(f32[4,8,128]{2,1,0:T(8,128)S(1)} %select_bitcast_fusion.1), channel_id=1, source_target_pairs={{0,24},{8,16},{16,8},{24,0},{1,25},{9,17},{17,9},{25,1},{2,26},{10... | collective-permute-start | bytes 49160 | tf_op jit(solution)/shard_map/ppermute | solution.py:494
  7.0 0.0 copy-done.6
  7.0 0.1 reshape.31.code_ref.far_code_ref
  7.1 0.0 copy-done.2
  7.1 0.0 copy-done.1
  7.1 0.0 copy-done.4
  7.1 0.0 copy-done.5
  7.1 0.0 copy-done
  7.2 0.0 copy-start.3
  7.2 2.2 %middle_pairs.1 = (f32[2,4,4,128]{3,2,1,0:T(4,128)S(1)}, f32[2,8,128]{2,1,0:T(8,128)S(1)}, f32[48,8,128]{2,1,0:T(8,128)S(1)}) custom-call(s32[32]{0:T(128)S(1)} %reshape.31.code_ref.far_code_ref, f32[3,4,8,128]{3,2,1,0:T(8,128)S(1)} %copy-done.2, f32[4,8,128]{2,1,0:T(8,128)S(1)} %copy-done, f32[4,8,128]{2,1,0:T(8,128)S(1)} %copy-done.1, ...), custom_call_target="tpu_custom_call" | custom-call | flops 4000000000 | bytes 400000 | tf_op jit(solution)/shard_map/middle_pairs/pallas_call | solution.py:546
  9.4 0.0 copy-done.3
  9.4 1.0 %moments_by_row.1 = (f32[8,16,128]{2,1,0:T(8,128)S(1)}, s32[4,8,128]{2,1,0:T(8,128)S(1)}, bf16[4,128,1024]{2,1,0:T(8,128)(2,1)S(1)}) custom-call(f32[2,8,128]{2,1,0:T(8,128)S(1)} %get-tuple-element.15.after_ref.middle_ref, f32[3,4,8,128]{3,2,1,0:T(8,128)S(1)} %copy-done.2, f32[3,4,8,128]{3,2,1,0:T(8,128)S(1)} %copy-done.3, f32[4,8,128]{2,1,0:T(8,128)S(1)} %copy-done, ...), custom_call_target="tpu_custom_call" | custom-call | flops 2000000000 | bytes 1400000 | tf_op jit(solution)/shard_map/moments_by_row/pallas_call | solution.py:562
  10.4 0.0 collective-permute-done.1
  10.4 0.0 collective-permute-done
  10.5 0.1 collective-permute-start.3
  10.6 2.5 %collective-permute-start.2 = (f32[4,6,128]{2,1,0:T(8,128)S(1)}, f32[4,6,128]{2,1,0:T(8,128)S(1)}, u32[]{:S(2)}, u32[]{:S(2)}) collective-permute-start(f32[4,6,128]{2,1,0:T(8,128)S(1)} %get-tuple-element.39), channel_id=1, source_target_pairs={{0,7},{1,2},{2,1},{3,4},{4,3},{5,6},{6,5},{7,0},{8,15},{9,10},{10,... | collective-permute-start | bytes 36872 | tf_op jit(solution)/shard_map/ppermute | solution.py:494
  13.1 2.4 %edge_pairs.1 = (f32[2,8,128]{2,1,0:T(8,128)S(1)}, f32[48,8,128]{2,1,0:T(8,128)S(1)}, bf16[8,128,48]{2,1,0:T(8,128)(2,1)S(1)}, f32[8,128,128]{2,1,0:T(8,128)S(1)}, f32[128,16]{1,0:T(8,128)S(1)}) custom-call(s32[32]{0:T(128)S(1)} %reshape.31.code_ref.far_code_ref, f32[3,4,8,128]{3,2,1,0:T(8,128)S(1)} %copy-done.2, f32[4,8,128]{2,1,0:T(8,128)S(1)} %copy-done, ...), custom_call_target="tpu_custom_call" | custom-call | flops 4000000000 | bytes 400000 | tf_op jit(solution)/shard_map/edge_pairs/pallas_call | solution.py:588
  15.6 0.0 collective-permute-done.3
  15.6 0.0 collective-permute-done.2
  15.6 1.9 %rim_pairs_and_table.1 = (f32[4,8,128]{2,1,0:T(8,128)S(1)}, f32[2,4,17,128]{3,2,1,0:T(8,128)S(1)}) custom-call(s32[32]{0:T(128)S(1)} %reshape.31.code_ref.far_code_ref, f32[2,8,128]{2,1,0:T(8,128)S(1)} %get-tuple-element.15.after_ref.middle_ref, f32[2,8,128]{2,1,0:T(8,128)S(1)} %get-tuple-element.19.edge_ref, f32[48,8,128]{2,1,0:T(8,128)S(1)} %get-tuple-element.20.known_ref, ...), custom_call_target="tpu_custom_call" | custom-call | flops 200000000 | bytes 400000 | tf_op jit(solution)/shard_map/rim_pairs_and_table/pallas_call | solution.py:612
  17.6 0.1 collective-permute-start.4
  17.6 1.2 %collective-permute-done.4 = f32[4,17,128]{2,1,0:T(8,128)S(1)} collective-permute-done((f32[4,17,128]{2,1,0:T(8,128)S(1)}, f32[4,17,128]{2,1,0:T(8,128)S(1)}, u32[]{:S(2)}, u32[]{:S(2)}) %collective-permute-start.4) | collective-permute-done | bytes 34848 | tf_op jit(solution)/shard_map/ppermute | solution.py:485
  18.9 0.7 %collective-permute-start.5 = (f32[1,17,128]{2,1,0:T(8,128)S(1)}, f32[1,17,128]{2,1,0:T(8,128)S(1)}, u32[]{:S(2)}, u32[]{:S(2)}) collective-permute-start(f32[1,17,128]{2,1,0:T(8,128)S(1)} %get-tuple-element.33), channel_id=1, source_target_pairs={{0,2},{2,0},{4,6},{6,4},{1,3},{3,1},{5,7},{7,5},{8,10},{10,8},{12,... | collective-permute-start | bytes 26120 | tf_op jit(solution)/shard_map/ppermute | solution.py:485
  19.6 1.5 %collective-permute-start.6 = (f32[1,17,128]{2,1,0:T(8,128)S(1)}, f32[1,17,128]{2,1,0:T(8,128)S(1)}, u32[]{:S(2)}, u32[]{:S(2)}) collective-permute-start(f32[1,17,128]{2,1,0:T(8,128)S(1)} %get-tuple-element.32), channel_id=1, source_target_pairs={{0,4},{2,6},{4,0},{6,2},{1,5},{3,7},{5,1},{7,3},{8,12},{10,14},{12... | collective-permute-start | bytes 26120 | tf_op jit(solution)/shard_map/ppermute | solution.py:485
  21.1 1.3 %collective-permute-start.7 = (f32[1,17,128]{2,1,0:T(8,128)S(1)}, f32[1,17,128]{2,1,0:T(8,128)S(1)}, u32[]{:S(2)}, u32[]{:S(2)}) collective-permute-start(f32[1,17,128]{2,1,0:T(8,128)S(1)} %get-tuple-element.31), channel_id=1, source_target_pairs={{0,6},{2,4},{4,2},{6,0},{1,7},{3,5},{5,3},{7,1},{8,14},{10,12},{12... | collective-permute-start | bytes 26120 | tf_op jit(solution)/shard_map/ppermute | solution.py:485
  22.4 0.2 collective-permute-done.5
  22.6 0.7 %collective-permute-done.6 = f32[1,17,128]{2,1,0:T(8,128)S(1)} collective-permute-done((f32[1,17,128]{2,1,0:T(8,128)S(1)}, f32[1,17,128]{2,1,0:T(8,128)S(1)}, u32[]{:S(2)}, u32[]{:S(2)}) %collective-permute-start.6) | collective-permute-done | bytes 8736 | tf_op jit(solution)/shard_map/ppermute | solution.py:485
  23.3 2.4 %collective-permute-done.7 = f32[1,17,128]{2,1,0:T(8,128)S(1)} collective-permute-done((f32[1,17,128]{2,1,0:T(8,128)S(1)}, f32[1,17,128]{2,1,0:T(8,128)S(1)}, u32[]{:S(2)}, u32[]{:S(2)}) %collective-permute-start.7) | collective-permute-done | bytes 8736 | tf_op jit(solution)/shard_map/ppermute | solution.py:485
  25.7 0.7 %collective-permute-start.9 = (f32[17,128]{1,0:T(8,128)S(1)}, f32[17,128]{1,0:T(8,128)S(1)}, u32[]{:S(2)}, u32[]{:S(2)}) collective-permute-start(f32[17,128]{1,0:T(8,128)S(1)} %fusion.4), channel_id=1, source_target_pairs={{0,16},{8,24},{16,0},{24,8},{1,17},{9,25},{17,1},{25,9},{2,18},{10... | collective-permute-start | bytes 26120 | tf_op jit(solution)/shard_map/ppermute | solution.py:485
  26.5 2.3 %collective-permute-start.10 = (f32[17,128]{1,0:T(8,128)S(1)}, f32[17,128]{1,0:T(8,128)S(1)}, u32[]{:S(2)}, u32[]{:S(2)}) collective-permute-start(f32[17,128]{1,0:T(8,128)S(1)} %fusion.4), channel_id=1, source_target_pairs={{0,24},{8,16},{16,8},{24,0},{1,25},{9,17},{17,9},{25,1},{2,26},{10... | collective-permute-start | bytes 26120 | tf_op jit(solution)/shard_map/ppermute | solution.py:485
  28.8 0.5 %collective-permute-start.8 = (f32[17,128]{1,0:T(8,128)S(1)}, f32[17,128]{1,0:T(8,128)S(1)}, u32[]{:S(2)}, u32[]{:S(2)}) collective-permute-start(f32[17,128]{1,0:T(8,128)S(1)} %fusion.4), channel_id=1, source_target_pairs={{0,8},{8,0},{16,24},{24,16},{1,9},{9,1},{17,25},{25,17},{2,10},{10... | collective-permute-start | bytes 26120 | tf_op jit(solution)/shard_map/ppermute | solution.py:485
  29.2 0.6 %fusion = f32[4,8,128]{2,1,0:T(8,128)} fusion(f32[4,8,128]{2,1,0:T(8,128)S(1)} %copy-done.1, f32[4,8,128]{2,1,0:T(8,128)S(1)} %get-tuple-element.26), kind=kLoop, calls=%fused_computation.3 | loop fusion | flops 16384 | bytes 49152 | tf_op jit(solution)/shard_map/div | solution.py:637
  29.8 0.5 %collective-permute-done.9 = f32[17,128]{1,0:T(8,128)S(1)} collective-permute-done((f32[17,128]{1,0:T(8,128)S(1)}, f32[17,128]{1,0:T(8,128)S(1)}, u32[]{:S(2)}, u32[]{:S(2)}) %collective-permute-start.9) | collective-permute-done | bytes 8736 | tf_op jit(solution)/shard_map/ppermute | solution.py:485
  30.3 1.6 %collective-permute-done.10 = f32[17,128]{1,0:T(8,128)S(1)} collective-permute-done((f32[17,128]{1,0:T(8,128)S(1)}, f32[17,128]{1,0:T(8,128)S(1)}, u32[]{:S(2)}, u32[]{:S(2)}) %collective-permute-start.10) | collective-permute-done | bytes 8736 | tf_op jit(solution)/shard_map/ppermute | solution.py:485
  31.9 0.5 %collective-permute-done.8 = f32[17,128]{1,0:T(8,128)S(1)} collective-permute-done((f32[17,128]{1,0:T(8,128)S(1)}, f32[17,128]{1,0:T(8,128)S(1)}, u32[]{:S(2)}, u32[]{:S(2)}) %collective-permute-start.8) | collective-permute-done | bytes 8736 | tf_op jit(solution)/shard_map/ppermute | solution.py:485
  32.5 0.6 %add_add_fusion = f32[17,128]{1,0:T(8,128)} fusion(f32[17,128]{1,0:T(8,128)S(1)} %collective-permute-done.9, f32[17,128]{1,0:T(8,128)S(1)} %collective-permute-done.10, f32[17,128]{1,0:T(8,128)S(1)} %fusion.4, f32[17,128]{1,0:T(8,128)S(1)} %collective-permute-done.8), kind=kLoop, calls=%fused_computation.15 | loop fusion | flops 6528 | bytes 43520 | tf_op jit(solution)/shard_map/add | solution.py:504
  (11 shorter events, 0.1 us)
Async XLA Ops:
  0.6 6.5 %copy-start.2 = (f32[3,4,8,128]{3,2,1,0:T(8,128)S(1)}, f32[3,4,8,128]{3,2,1,0:T(8,128)}, u32[]{:S(2)}) copy-start(f32[3,4,8,128]{3,2,1,0:T(8,128)} %pos_ref.5) | copy-start | bytes 147460
  1.4 9.0 %collective-permute-start.1 = (f32[4,8,128]{2,1,0:T(8,128)S(1)}, f32[4,8,128]{2,1,0:T(8,128)S(1)}, u32[]{:S(2)}, u32[]{:S(2)}) collective-permute-start(f32[4,8,128]{2,1,0:T(8,128)S(1)} %get-tuple-element.28), channel_id=1, source_target_pairs={{0,8},{8,0},{16,24},{24,16},{1,9},{9,1},{17,25},{25,17},{2,10},{10... | collective-permute-start | bytes 49160 | tf_op jit(solution)/shard_map/ppermute | solution.py:491
  4.4 2.6 %copy-start.6 = (s32[4,8,5]{1,0,2:T(4,128)S(1)}, s32[4,8,5]{1,0,2:T(4,128)}, u32[]{:S(2)}) copy-start(s32[4,8,5]{1,0,2:T(4,128)} %param.11) | copy-start | bytes 1924
  4.5 2.7 %copy-start.1 = (f32[4,8,128]{2,1,0:T(8,128)S(1)}, f32[4,8,128]{2,1,0:T(8,128)}, u32[]{:S(2)}) copy-start(f32[4,8,128]{2,1,0:T(8,128)} %smooth_ref.5) | copy-start | bytes 49156
  4.5 2.7 %copy-start.4 = (s32[4,8,128]{2,1,0:T(8,128)S(1)}, s32[4,8,128]{2,1,0:T(8,128)}, u32[]{:S(2)}) copy-start(s32[4,8,128]{2,1,0:T(8,128)} %group_ref.3) | copy-start | bytes 49156
  4.5 2.7 %copy-start.5 = (s32[1024]{0:T(1024)S(1)}, s32[1024]{0:T(1024)}, u32[]{:S(2)}) copy-start(s32[1024]{0:T(1024)} %param.13) | copy-start | bytes 12292
  4.5 2.7 %copy-start = (f32[4,8,128]{2,1,0:T(8,128)S(1)}, f32[4,8,128]{2,1,0:T(8,128)}, u32[]{:S(2)}) copy-start(f32[4,8,128]{2,1,0:T(8,128)} %mass_ref.7) | copy-start | bytes 49156
  4.5 5.9 %collective-permute-start = (f32[4,8,128]{2,1,0:T(8,128)S(1)}, f32[4,8,128]{2,1,0:T(8,128)S(1)}, u32[]{:S(2)}, u32[]{:S(2)}) collective-permute-start(f32[4,8,128]{2,1,0:T(8,128)S(1)} %select_bitcast_fusion.1), channel_id=1, source_target_pairs={{0,24},{8,16},{16,8},{24,0},{1,25},{9,17},{17,9},{25,1},{2,26},{10... | collective-permute-start | bytes 49160 | tf_op jit(solution)/shard_map/ppermute | solution.py:494
  7.2 2.2 %copy-start.3 = (f32[3,4,8,128]{3,2,1,0:T(8,128)S(1)}, f32[3,4,8,128]{3,2,1,0:T(8,128)}, u32[]{:S(2)}) copy-start(f32[3,4,8,128]{3,2,1,0:T(8,128)} %vel_ref.1) | copy-start | bytes 147460
  10.5 5.1 %collective-permute-start.3 = (f32[4,6,128]{2,1,0:T(8,128)S(1)}, f32[4,6,128]{2,1,0:T(8,128)S(1)}, u32[]{:S(2)}, u32[]{:S(2)}) collective-permute-start(f32[4,6,128]{2,1,0:T(8,128)S(1)} %get-tuple-element.38), channel_id=1, source_target_pairs={{0,1},{1,0},{2,3},{3,2},{4,5},{5,4},{6,7},{7,6},{8,9},{9,8},{10,11... | collective-permute-start | bytes 36872 | tf_op jit(solution)/shard_map/ppermute | solution.py:491
  10.6 5.0 %collective-permute-start.2 = (f32[4,6,128]{2,1,0:T(8,128)S(1)}, f32[4,6,128]{2,1,0:T(8,128)S(1)}, u32[]{:S(2)}, u32[]{:S(2)}) collective-permute-start(f32[4,6,128]{2,1,0:T(8,128)S(1)} %get-tuple-element.39), channel_id=1, source_target_pairs={{0,7},{1,2},{2,1},{3,4},{4,3},{5,6},{6,5},{7,0},{8,15},{9,10},{10,... | collective-permute-start | bytes 36872 | tf_op jit(solution)/shard_map/ppermute | solution.py:494
  17.6 1.3 %collective-permute-start.4 = (f32[4,17,128]{2,1,0:T(8,128)S(1)}, f32[4,17,128]{2,1,0:T(8,128)S(1)}, u32[]{:S(2)}, u32[]{:S(2)}) collective-permute-start(f32[4,17,128]{2,1,0:T(8,128)S(1)} %slice_bitcast_fusion), channel_id=1, source_target_pairs={{0,1},{1,0},{2,3},{3,2},{4,5},{5,4},{6,7},{7,6},{8,9},{9,8},{10,11... | collective-permute-start | bytes 104456 | tf_op jit(solution)/shard_map/ppermute | solution.py:485
  18.9 3.8 %collective-permute-start.5 = (f32[1,17,128]{2,1,0:T(8,128)S(1)}, f32[1,17,128]{2,1,0:T(8,128)S(1)}, u32[]{:S(2)}, u32[]{:S(2)}) collective-permute-start(f32[1,17,128]{2,1,0:T(8,128)S(1)} %get-tuple-element.33), channel_id=1, source_target_pairs={{0,2},{2,0},{4,6},{6,4},{1,3},{3,1},{5,7},{7,5},{8,10},{10,8},{12,... | collective-permute-start | bytes 26120 | tf_op jit(solution)/shard_map/ppermute | solution.py:485
  19.6 3.7 %collective-permute-start.6 = (f32[1,17,128]{2,1,0:T(8,128)S(1)}, f32[1,17,128]{2,1,0:T(8,128)S(1)}, u32[]{:S(2)}, u32[]{:S(2)}) collective-permute-start(f32[1,17,128]{2,1,0:T(8,128)S(1)} %get-tuple-element.32), channel_id=1, source_target_pairs={{0,4},{2,6},{4,0},{6,2},{1,5},{3,7},{5,1},{7,3},{8,12},{10,14},{12... | collective-permute-start | bytes 26120 | tf_op jit(solution)/shard_map/ppermute | solution.py:485
  21.1 4.6 %collective-permute-start.7 = (f32[1,17,128]{2,1,0:T(8,128)S(1)}, f32[1,17,128]{2,1,0:T(8,128)S(1)}, u32[]{:S(2)}, u32[]{:S(2)}) collective-permute-start(f32[1,17,128]{2,1,0:T(8,128)S(1)} %get-tuple-element.31), channel_id=1, source_target_pairs={{0,6},{2,4},{4,2},{6,0},{1,7},{3,5},{5,3},{7,1},{8,14},{10,12},{12... | collective-permute-start | bytes 26120 | tf_op jit(solution)/shard_map/ppermute | solution.py:485
  25.7 4.6 %collective-permute-start.9 = (f32[17,128]{1,0:T(8,128)S(1)}, f32[17,128]{1,0:T(8,128)S(1)}, u32[]{:S(2)}, u32[]{:S(2)}) collective-permute-start(f32[17,128]{1,0:T(8,128)S(1)} %fusion.4), channel_id=1, source_target_pairs={{0,16},{8,24},{16,0},{24,8},{1,17},{9,25},{17,1},{25,9},{2,18},{10... | collective-permute-start | bytes 26120 | tf_op jit(solution)/shard_map/ppermute | solution.py:485
  26.5 5.5 %collective-permute-start.10 = (f32[17,128]{1,0:T(8,128)S(1)}, f32[17,128]{1,0:T(8,128)S(1)}, u32[]{:S(2)}, u32[]{:S(2)}) collective-permute-start(f32[17,128]{1,0:T(8,128)S(1)} %fusion.4), channel_id=1, source_target_pairs={{0,24},{8,16},{16,8},{24,0},{1,25},{9,17},{17,9},{25,1},{2,26},{10... | collective-permute-start | bytes 26120 | tf_op jit(solution)/shard_map/ppermute | solution.py:485
  28.8 3.7 %collective-permute-start.8 = (f32[17,128]{1,0:T(8,128)S(1)}, f32[17,128]{1,0:T(8,128)S(1)}, u32[]{:S(2)}, u32[]{:S(2)}) collective-permute-start(f32[17,128]{1,0:T(8,128)S(1)} %fusion.4), channel_id=1, source_target_pairs={{0,8},{8,0},{16,24},{24,16},{1,9},{9,1},{17,25},{25,17},{2,10},{10... | collective-permute-start | bytes 26120 | tf_op jit(solution)/shard_map/ppermute | solution.py:485

commit v7 on v5

--- a/solution.py
+++ b/solution.py
@@ -14,7 +14,6 @@
 EARLY = 16
 DENSITY_FACTOR = 21.0 / (16.0 * math.pi) / 256.0
 VMEM = pl.BlockSpec(memory_space=pltpu.VMEM)
-ANY = pl.BlockSpec(memory_space=pl.ANY)
 NT = (((1,), (1,)), ((), ()))
 
 
@@ -239,18 +238,11 @@
     ]
 
 
-def load_codes(far_ref, code_ref, sem):
-    copy = pltpu.make_async_copy(far_ref, code_ref, sem)
-    copy.start()
-    return copy
-
-
 def block_pairs(
-    listed, x_first, x_step, x_count, known_ref, far_code_ref, pos_ref, mass_ref, smooth_ref, prev_ref, next_ref,
-    out_ref, src_ref, code_ref, sem, nat_ref, shift_ref, tgt_ref, mat_ref, near_ref, root_ref, total_ref,
+    listed, x_first, x_step, x_count, known_ref, code_ref, pos_ref, mass_ref, smooth_ref, prev_ref, next_ref,
+    out_ref, src_ref, nat_ref, shift_ref, tgt_ref, mat_ref, near_ref, root_ref, total_ref,
 ):
     blocks_x, blocks_y, _ = mass_ref.shape
-    codes = load_codes(far_code_ref, code_ref, sem)
     for xe in range(blocks_x + 2):
         if xe == 0 or xe == blocks_x + 1:
             ref = prev_ref if xe == 0 else next_ref
@@ -280,10 +272,10 @@
         line = src_ref[(x_first + turn * x_step + 1) * blocks_y + y]
         put_source(near_ref, root_ref, number, 0, line, 0.0, squares)
     pair_sums(sides_of(len(blocks), 0, 1, mat_ref, near_ref, root_ref, total_ref))
-    codes.wait()
+    words = code_ref[...]
     for number, (turn, y) in enumerate(blocks):
         x = x_first + turn * x_step
-        word = code_ref[x * blocks_y + y]
+        word = words[x, y]
         for k in range(1, listed):
             code = (word >> (4 * k)) & 15
             step_x = (code * 11) >> 5
@@ -331,8 +323,6 @@
 
 def pair_scratch(blocks_x, blocks_y, x_count, listed):
     return [
-        pltpu.SMEM((blocks_x * blocks_y,), jnp.int32),
-        pltpu.SemaphoreType.DMA(()),
         pltpu.VMEM(((blocks_x + 2) * 64, LANES), F32),
         pltpu.VMEM((9, 8, LANES), F32),
         pltpu.VMEM((x_count, 24 * blocks_y, LANES), F32),
@@ -349,15 +339,14 @@
 
 
 def rim_kernel(
-    listed, far_code_ref, middle_ref, edge_ref, known_ref, pos_ref, mass_ref, smooth_ref,
+    listed, code_ref, middle_ref, edge_ref, known_ref, pos_ref, mass_ref, smooth_ref,
     low_ref, high_ref, rows_ref, hot_ref, early_ref,
-    sum_ref, table_ref, code_ref, sem, nat_ref, src_ref, md_ref, lhs_ref, row_sum_ref,
+    sum_ref, table_ref, nat_ref, src_ref, md_ref, lhs_ref, row_sum_ref,
     shift_ref, tgt_ref, mat_ref, near_ref, root_ref, total_ref,
 ):
     blocks_x, blocks_y, _ = mass_ref.shape
     owners = early_ref.shape[0]
     wide = blocks_x + 2
-    codes = load_codes(far_code_ref, code_ref, sem)
     for side, ref in enumerate((low_ref, high_ref)):
         store_source(nat_ref, side * 64, wide, [ref[c] for c in range(3)], ref[3])
         for xe in range(wide):
@@ -417,10 +406,10 @@
         sides_of(2 * blocks_x, 0, 1, *products),
         [functools.partial(inner_moments, x) for x in range(blocks_x)],
     )
-    codes.wait()
+    words = code_ref[...]
     for x in range(blocks_x):
         for side in range(2):
-            word = code_ref[x * blocks_y + side * last]
+            word = words[x, side * last]
             for k in range(1, listed):
                 code = (word >> (4 * k)) & 15
                 step_x = (code * 11) >> 5
@@ -506,7 +495,7 @@
     chunk = blocks_y * block_len
     shape = jax.ShapeDtypeStruct
     listed = neighbours.shape[2]
-    codes = sum(neighbours[:, :, k] << (4 * k) for k in range(listed)).reshape(-1)
+    codes = sum(neighbours[:, :, k] << (4 * k) for k in range(listed))
     table_rows = group_row.reshape(-1, LANES)
     packed = jnp.concatenate([positions, masses[None]], axis=0)
     prev, following = neighbours_of(
@@ -520,7 +509,7 @@
             shape((blocks_x - 2, blocks_y, LANES), F32),
             shape(sources, F32),
         ),
-        in_specs=[ANY] + [VMEM] * 5,
+        in_specs=[VMEM] * 6,
         out_specs=(VMEM,) * 3,
         scratch_shapes=pair_scratch(blocks_x, blocks_y, blocks_x - 2, listed),
         compiler_params=params(),
@@ -557,7 +546,7 @@
     edge, known = pl.pallas_call(
         functools.partial(edge_kernel, listed),
         out_shape=(shape((2, blocks_y, LANES), F32), shape(sources, F32)),
-        in_specs=[ANY] + [VMEM] * 6,
+        in_specs=[VMEM] * 7,
         out_specs=(VMEM,) * 2,
         scratch_shapes=pair_scratch(blocks_x, blocks_y, 2, listed),
         compiler_params=params(),
@@ -569,11 +558,9 @@
     sums, table = pl.pallas_call(
         functools.partial(rim_kernel, listed),
         out_shape=(shape(masses.shape, F32), shape((2, owners // 2, EARLY + 1, LANES), F32)),
-        in_specs=[ANY] + [VMEM] * 11,
+        in_specs=[VMEM] * 12,
         out_specs=(VMEM, VMEM),
         scratch_shapes=[
-            pltpu.SMEM((blocks_x * blocks_y,), jnp.int32),
-            pltpu.SemaphoreType.DMA(()),
             pltpu.VMEM((128, LANES), F32),
             pltpu.VMEM((6 * (blocks_x + 2), 8, LANES), F32),
             pltpu.VMEM((owners, LANES), F32),

time: 32.4 us -> 32 us (0.988)
  waiting for transfers between devices: 6.08 us -> 5.51 us
  local copies, waits for them, and re-layouts: 0.14 us -> 0.68 us
  Pallas kernels: 7.32 us -> 6.99 us
    unnamed x14, local copies, waits for them, and re-layouts: 0.03 us -> 0.66 us
    ppermute x2, waiting for transfers between devices: 0.35 us -> 0.01 us  [neighbours_of(): lax.ppermute(jnp.where(even, high_edge, low_edge), axis, [(i, i ^ 1) for...]
  transfers between devices with their start and end apart: 11 -> 11, of which waited for: 8 -> 7; matrix products, arithmetic and copies ran while one was open for 2% -> 2% of each run, Pallas kernels for 17% -> 16%
where the time goes in v7:
time: 32 us; the launch traced here: 31.8 us
  starting transfers between devices  15.8 us (49%)
  Pallas kernels  6.99 us (22%)
  waiting for transfers between devices  5.51 us (17%)
  other arithmetic  2.07 us (6%)
  between operations  0.82 us (3%)
  local copies, waits for them, and re-layouts  0.68 us (2%)
    ppermute x7, starting transfers between devices, swap(): return lax.ppermute(value, axis, [(i, i ^ step) for i in range(count)])  8.01 us
    ppermute x2, starting transfers between devices, neighbours_of(): lax.ppermute(jnp.where(even, low_edge, high_edge), axis, [(i, (i + 1 if i...  7.67 us
    ppermute x7, waiting for transfers between devices, swap(): return lax.ppermute(value, axis, [(i, i ^ step) for i in range(count)])  5.5 us
    pallas_call x1, Pallas kernels, shards(): pl.pallas_call(functools.partial(middle_kernel, listed), out_shape=(shape...  2.07 us
    pallas_call x1, Pallas kernels, shards(): pl.pallas_call(functools.partial(edge_kernel, listed), out_shape=(shape((...  2.07 us
    pallas_call x1, Pallas kernels, shards(): pl.pallas_call(functools.partial(rim_kernel, listed), out_shape=(shape(ma...  1.82 us
    pallas_call x1, Pallas kernels, shards(): pl.pallas_call(functools.partial(moments_kernel, blocks_x * dom_count, bl...  1.03 us
    select_n x2, other arithmetic, neighbours_of(): jnp.where(even, high_edge, low_edge)  0.8 us
  transfers between devices with their start and end apart: 11, of which 7 were waited for; matrix products, arithmetic and copies ran while one was open for 2% of the time, Pallas kernels for 16%

profile of v7, /device:TPU:0, one launch (start us, length us, event | category | flops | bytes accessed | tf_op | source)
XLA Modules:
  0.0 31.8 jit_solution(5507385083070074484)
XLA Ops:
  0.6 0.0 copy-start.6
  0.6 0.0 copy-start.2
  0.7 0.0 copy-start.4
  0.7 0.8 %select_bitcast_fusion = (f32[4,8,128]{2,1,0:T(8,128)S(1)}, f32[4,1,8,128]{3,2,0,1:T(8,128)S(1)}, f32[4,1,8,128]{3,2,0,1:T(8,128)S(1)}) fusion(pred[]{:T(512)S(6)} %eq.6, f32[1,4,8,128]{3,2,0,1:T(8,128)} %bitcast.18, f32[3,4,8,128]{3,2,1,0:T(8,128)} %pos_ref.7), kind=kLoop, calls=%fused_computation.8 | loop fusion | flops 12288 | bytes 114689 | tf_op jit(solution)/shard_map/jit(_where)/select_n | solution.py:451
  1.4 0.0 copy-start
  1.4 0.0 copy-start.1
  1.5 5.1 %collective-permute-start = (f32[4,8,128]{2,1,0:T(8,128)S(1)}, f32[4,8,128]{2,1,0:T(8,128)S(1)}, u32[]{:S(2)}, u32[]{:S(2)}) collective-permute-start(f32[4,8,128]{2,1,0:T(8,128)S(1)} %select_bitcast_fusion.1), channel_id=1, source_target_pairs={{0,24},{8,16},{16,8},{24,0},{1,25},{9,17},{17,9},{25,1},{2,26},{10... | collective-permute-start | bytes 49160 | tf_op jit(solution)/shard_map/ppermute | solution.py:453
  6.6 0.0 copy-start.5
  6.6 0.0 collective-permute-start.1
  6.6 0.0 copy-done.6
  6.6 0.0 copy-done.2
  6.6 0.0 copy-done.4
  6.6 0.0 copy-done
  6.6 0.0 copy-done.1
  6.6 0.6 %copy-done.5 = s32[1024]{0:T(1024)S(1)} copy-done((s32[1024]{0:T(1024)S(1)}, s32[1024]{0:T(1024)}, u32[]{:S(2)}) %copy-start.5) | copy-done | bytes 4120
  7.3 0.0 copy-start.3
  7.3 2.1 %middle_pairs.1 = (f32[2,4,4,128]{3,2,1,0:T(4,128)S(1)}, f32[2,8,128]{2,1,0:T(8,128)S(1)}, f32[48,8,128]{2,1,0:T(8,128)S(1)}) custom-call(s32[4,8]{1,0:T(4,128)S(1)} %add_bitcast_fusion.code_ref, f32[3,4,8,128]{3,2,1,0:T(8,128)S(1)} %copy-done, f32[4,8,128]{2,1,0:T(8,128)S(1)} %copy-done.1, f32[4,8,128]{2,1,0:T(8,128)S(1)} %copy-done.2, ...), custom_call_target="tpu_custom_call" | custom-call | flops 4000000000 | bytes 400000 | tf_op jit(solution)/shard_map/middle_pairs/pallas_call | solution.py:505
  9.3 0.0 copy-done.3
  9.3 1.0 %moments_by_row.1 = (f32[8,16,128]{2,1,0:T(8,128)S(1)}, s32[4,8,128]{2,1,0:T(8,128)S(1)}, bf16[4,128,1024]{2,1,0:T(8,128)(2,1)S(1)}) custom-call(f32[2,8,128]{2,1,0:T(8,128)S(1)} %get-tuple-element.12.after_ref.middle_ref, f32[3,4,8,128]{3,2,1,0:T(8,128)S(1)} %copy-done, f32[3,4,8,128]{3,2,1,0:T(8,128)S(1)} %copy-done.3, f32[4,8,128]{2,1,0:T(8,128)S(1)} %copy-done.1, ...), custom_call_target="tpu_custom_call" | custom-call | flops 2000000000 | bytes 1400000 | tf_op jit(solution)/shard_map/moments_by_row/pallas_call | solution.py:521
  10.4 0.0 collective-permute-done
  10.4 0.0 collective-permute-done.1
  10.5 0.1 collective-permute-start.3
  10.5 2.6 %collective-permute-start.2 = (f32[4,6,128]{2,1,0:T(8,128)S(1)}, f32[4,6,128]{2,1,0:T(8,128)S(1)}, u32[]{:S(2)}, u32[]{:S(2)}) collective-permute-start(f32[4,6,128]{2,1,0:T(8,128)S(1)} %get-tuple-element.33), channel_id=1, source_target_pairs={{0,7},{1,2},{2,1},{3,4},{4,3},{5,6},{6,5},{7,0},{8,15},{9,10},{10,... | collective-permute-start | bytes 36872 | tf_op jit(solution)/shard_map/ppermute | solution.py:453
  13.1 2.1 %edge_pairs.1 = (f32[2,8,128]{2,1,0:T(8,128)S(1)}, f32[48,8,128]{2,1,0:T(8,128)S(1)}) custom-call(s32[4,8]{1,0:T(4,128)S(1)} %add_bitcast_fusion.code_ref, f32[3,4,8,128]{3,2,1,0:T(8,128)S(1)} %copy-done, f32[4,8,128]{2,1,0:T(8,128)S(1)} %copy-done.1, f32[4,8,128]{2,1,0:T(8,128)S(1)} %copy-done.2, f32[4,8,128]{2,1,0:T(8,128)S(1)} %get-tuple-element.31.prev_ref, ...), custom_call_target="tpu_custom_call" | custom-call | flops 4000000000 | bytes 400000 | tf_op jit(solution)/shard_map/edge_pairs/pallas_call | solution.py:546
  15.2 0.0 collective-permute-done.3
  15.2 0.0 collective-permute-done.2
  15.2 1.8 %rim_pairs_and_table.1 = (f32[4,8,128]{2,1,0:T(8,128)S(1)}, f32[2,4,17,128]{3,2,1,0:T(8,128)S(1)}) custom-call(s32[4,8]{1,0:T(4,128)S(1)} %add_bitcast_fusion.code_ref, f32[2,8,128]{2,1,0:T(8,128)S(1)} %get-tuple-element.12.after_ref.middle_ref, f32[2,8,128]{2,1,0:T(8,128)S(1)} %get-tuple-element.14.edge_ref, f32[48,8,128]{2,1,0:T(8,128)S(1)} %get-tuple-element.15.known_ref, ...), custom_call_target="tpu_custom_call" | custom-call | flops 200000000 | bytes 400000 | tf_op jit(solution)/shard_map/rim_pairs_and_table/pallas_call | solution.py:558
  17.0 0.1 collective-permute-start.4
  17.1 1.2 %collective-permute-done.4 = f32[4,17,128]{2,1,0:T(8,128)S(1)} collective-permute-done((f32[4,17,128]{2,1,0:T(8,128)S(1)}, f32[4,17,128]{2,1,0:T(8,128)S(1)}, u32[]{:S(2)}, u32[]{:S(2)}) %collective-permute-start.4) | collective-permute-done | bytes 34848 | tf_op jit(solution)/shard_map/ppermute | solution.py:444
  18.4 2.1 %collective-permute-start.7 = (f32[1,17,128]{2,1,0:T(8,128)S(1)}, f32[1,17,128]{2,1,0:T(8,128)S(1)}, u32[]{:S(2)}, u32[]{:S(2)}) collective-permute-start(f32[1,17,128]{2,1,0:T(8,128)S(1)} %get-tuple-element.25), channel_id=1, source_target_pairs={{0,6},{2,4},{4,2},{6,0},{1,7},{3,5},{5,3},{7,1},{8,14},{10,12},{12... | collective-permute-start | bytes 26120 | tf_op jit(solution)/shard_map/ppermute | solution.py:444
  20.5 0.5 %collective-permute-start.6 = (f32[1,17,128]{2,1,0:T(8,128)S(1)}, f32[1,17,128]{2,1,0:T(8,128)S(1)}, u32[]{:S(2)}, u32[]{:S(2)}) collective-permute-start(f32[1,17,128]{2,1,0:T(8,128)S(1)} %get-tuple-element.26), channel_id=1, source_target_pairs={{0,4},{2,6},{4,0},{6,2},{1,5},{3,7},{5,1},{7,3},{8,12},{10,14},{12... | collective-permute-start | bytes 26120 | tf_op jit(solution)/shard_map/ppermute | solution.py:444
  21.0 1.0 %collective-permute-start.5 = (f32[1,17,128]{2,1,0:T(8,128)S(1)}, f32[1,17,128]{2,1,0:T(8,128)S(1)}, u32[]{:S(2)}, u32[]{:S(2)}) collective-permute-start(f32[1,17,128]{2,1,0:T(8,128)S(1)} %get-tuple-element.27), channel_id=1, source_target_pairs={{0,2},{2,0},{4,6},{6,4},{1,3},{3,1},{5,7},{7,5},{8,10},{10,8},{12,... | collective-permute-start | bytes 26120 | tf_op jit(solution)/shard_map/ppermute | solution.py:444
  21.9 1.1 %collective-permute-done.7 = f32[1,17,128]{2,1,0:T(8,128)S(1)} collective-permute-done((f32[1,17,128]{2,1,0:T(8,128)S(1)}, f32[1,17,128]{2,1,0:T(8,128)S(1)}, u32[]{:S(2)}, u32[]{:S(2)}) %collective-permute-start.7) | collective-permute-done | bytes 8736 | tf_op jit(solution)/shard_map/ppermute | solution.py:444
  23.0 1.1 %collective-permute-done.6 = f32[1,17,128]{2,1,0:T(8,128)S(1)} collective-permute-done((f32[1,17,128]{2,1,0:T(8,128)S(1)}, f32[1,17,128]{2,1,0:T(8,128)S(1)}, u32[]{:S(2)}, u32[]{:S(2)}) %collective-permute-start.6) | collective-permute-done | bytes 8736 | tf_op jit(solution)/shard_map/ppermute | solution.py:444
  24.1 0.5 %collective-permute-done.5 = f32[1,17,128]{2,1,0:T(8,128)S(1)} collective-permute-done((f32[1,17,128]{2,1,0:T(8,128)S(1)}, f32[1,17,128]{2,1,0:T(8,128)S(1)}, u32[]{:S(2)}, u32[]{:S(2)}) %collective-permute-start.5) | collective-permute-done | bytes 8736 | tf_op jit(solution)/shard_map/ppermute | solution.py:444
  24.7 1.7 %collective-permute-start.10 = (f32[17,128]{1,0:T(8,128)S(1)}, f32[17,128]{1,0:T(8,128)S(1)}, u32[]{:S(2)}, u32[]{:S(2)}) collective-permute-start(f32[17,128]{1,0:T(8,128)S(1)} %fusion.4), channel_id=1, source_target_pairs={{0,24},{8,16},{16,8},{24,0},{1,25},{9,17},{17,9},{25,1},{2,26},{10... | collective-permute-start | bytes 26120 | tf_op jit(solution)/shard_map/ppermute | solution.py:444
  26.4 1.2 %collective-permute-start.9 = (f32[17,128]{1,0:T(8,128)S(1)}, f32[17,128]{1,0:T(8,128)S(1)}, u32[]{:S(2)}, u32[]{:S(2)}) collective-permute-start(f32[17,128]{1,0:T(8,128)S(1)} %fusion.4), channel_id=1, source_target_pairs={{0,16},{8,24},{16,0},{24,8},{1,17},{9,25},{17,1},{25,9},{2,18},{10... | collective-permute-start | bytes 26120 | tf_op jit(solution)/shard_map/ppermute | solution.py:444
  27.5 1.5 %collective-permute-start.8 = (f32[17,128]{1,0:T(8,128)S(1)}, f32[17,128]{1,0:T(8,128)S(1)}, u32[]{:S(2)}, u32[]{:S(2)}) collective-permute-start(f32[17,128]{1,0:T(8,128)S(1)} %fusion.4), channel_id=1, source_target_pairs={{0,8},{8,0},{16,24},{24,16},{1,9},{9,1},{17,25},{25,17},{2,10},{10... | collective-permute-start | bytes 26120 | tf_op jit(solution)/shard_map/ppermute | solution.py:444
  29.0 0.6 %fusion = f32[4,8,128]{2,1,0:T(8,128)} fusion(f32[4,8,128]{2,1,0:T(8,128)S(1)} %copy-done.2, f32[4,8,128]{2,1,0:T(8,128)S(1)} %get-tuple-element.20), kind=kLoop, calls=%fused_computation.3 | loop fusion | flops 16384 | bytes 49152 | tf_op jit(solution)/shard_map/div | solution.py:581
  29.7 0.5 %collective-permute-done.10 = f32[17,128]{1,0:T(8,128)S(1)} collective-permute-done((f32[17,128]{1,0:T(8,128)S(1)}, f32[17,128]{1,0:T(8,128)S(1)}, u32[]{:S(2)}, u32[]{:S(2)}) %collective-permute-start.10) | collective-permute-done | bytes 8736 | tf_op jit(solution)/shard_map/ppermute | solution.py:444
  30.1 0.8 %collective-permute-done.9 = f32[17,128]{1,0:T(8,128)S(1)} collective-permute-done((f32[17,128]{1,0:T(8,128)S(1)}, f32[17,128]{1,0:T(8,128)S(1)}, u32[]{:S(2)}, u32[]{:S(2)}) %collective-permute-start.9) | collective-permute-done | bytes 8736 | tf_op jit(solution)/shard_map/ppermute | solution.py:444
  31.0 0.3 collective-permute-done.8
  31.2 0.6 %add_add_fusion = f32[17,128]{1,0:T(8,128)} fusion(f32[17,128]{1,0:T(8,128)S(1)} %collective-permute-done.9, f32[17,128]{1,0:T(8,128)S(1)} %collective-permute-done.10, f32[17,128]{1,0:T(8,128)S(1)} %fusion.4, f32[17,128]{1,0:T(8,128)S(1)} %collective-permute-done.8), kind=kLoop, calls=%fused_computation.15 | loop fusion | flops 6528 | bytes 43520 | tf_op jit(solution)/shard_map/add | solution.py:463
  (11 shorter events, 0.1 us)
Async XLA Ops:
  0.6 6.0 %copy-start.6 = (s32[4,8,5]{1,0,2:T(4,128)S(1)}, s32[4,8,5]{1,0,2:T(4,128)}, u32[]{:S(2)}) copy-start(s32[4,8,5]{1,0,2:T(4,128)} %param.11) | copy-start | bytes 1924
  0.6 6.0 %copy-start.2 = (f32[4,8,128]{2,1,0:T(8,128)S(1)}, f32[4,8,128]{2,1,0:T(8,128)}, u32[]{:S(2)}) copy-start(f32[4,8,128]{2,1,0:T(8,128)} %smooth_ref.5) | copy-start | bytes 49156
  0.7 6.0 %copy-start.4 = (s32[4,8,128]{2,1,0:T(8,128)S(1)}, s32[4,8,128]{2,1,0:T(8,128)}, u32[]{:S(2)}) copy-start(s32[4,8,128]{2,1,0:T(8,128)} %group_ref.3) | copy-start | bytes 49156
  1.4 5.2 %copy-start = (f32[3,4,8,128]{3,2,1,0:T(8,128)S(1)}, f32[3,4,8,128]{3,2,1,0:T(8,128)}, u32[]{:S(2)}) copy-start(f32[3,4,8,128]{3,2,1,0:T(8,128)} %pos_ref.7) | copy-start | bytes 147460
  1.4 5.2 %copy-start.1 = (f32[4,8,128]{2,1,0:T(8,128)S(1)}, f32[4,8,128]{2,1,0:T(8,128)}, u32[]{:S(2)}) copy-start(f32[4,8,128]{2,1,0:T(8,128)} %mass_ref.7) | copy-start | bytes 49156
  1.5 8.9 %collective-permute-start = (f32[4,8,128]{2,1,0:T(8,128)S(1)}, f32[4,8,128]{2,1,0:T(8,128)S(1)}, u32[]{:S(2)}, u32[]{:S(2)}) collective-permute-start(f32[4,8,128]{2,1,0:T(8,128)S(1)} %select_bitcast_fusion.1), channel_id=1, source_target_pairs={{0,24},{8,16},{16,8},{24,0},{1,25},{9,17},{17,9},{25,1},{2,26},{10... | collective-permute-start | bytes 49160 | tf_op jit(solution)/shard_map/ppermute | solution.py:453
  6.6 0.7 %copy-start.5 = (s32[1024]{0:T(1024)S(1)}, s32[1024]{0:T(1024)}, u32[]{:S(2)}) copy-start(s32[1024]{0:T(1024)} %param.13) | copy-start | bytes 12292
  6.6 3.8 %collective-permute-start.1 = (f32[4,8,128]{2,1,0:T(8,128)S(1)}, f32[4,8,128]{2,1,0:T(8,128)S(1)}, u32[]{:S(2)}, u32[]{:S(2)}) collective-permute-start(f32[4,8,128]{2,1,0:T(8,128)S(1)} %get-tuple-element.22), channel_id=1, source_target_pairs={{0,8},{8,0},{16,24},{24,16},{1,9},{9,1},{17,25},{25,17},{2,10},{10... | collective-permute-start | bytes 49160 | tf_op jit(solution)/shard_map/ppermute | solution.py:450
  7.3 2.1 %copy-start.3 = (f32[3,4,8,128]{3,2,1,0:T(8,128)S(1)}, f32[3,4,8,128]{3,2,1,0:T(8,128)}, u32[]{:S(2)}) copy-start(f32[3,4,8,128]{3,2,1,0:T(8,128)} %vel_ref.1) | copy-start | bytes 147460
  10.5 4.7 %collective-permute-start.3 = (f32[4,6,128]{2,1,0:T(8,128)S(1)}, f32[4,6,128]{2,1,0:T(8,128)S(1)}, u32[]{:S(2)}, u32[]{:S(2)}) collective-permute-start(f32[4,6,128]{2,1,0:T(8,128)S(1)} %get-tuple-element.32), channel_id=1, source_target_pairs={{0,1},{1,0},{2,3},{3,2},{4,5},{5,4},{6,7},{7,6},{8,9},{9,8},{10,11... | collective-permute-start | bytes 36872 | tf_op jit(solution)/shard_map/ppermute | solution.py:450
  10.5 4.6 %collective-permute-start.2 = (f32[4,6,128]{2,1,0:T(8,128)S(1)}, f32[4,6,128]{2,1,0:T(8,128)S(1)}, u32[]{:S(2)}, u32[]{:S(2)}) collective-permute-start(f32[4,6,128]{2,1,0:T(8,128)S(1)} %get-tuple-element.33), channel_id=1, source_target_pairs={{0,7},{1,2},{2,1},{3,4},{4,3},{5,6},{6,5},{7,0},{8,15},{9,10},{10,... | collective-permute-start | bytes 36872 | tf_op jit(solution)/shard_map/ppermute | solution.py:453
  17.0 1.3 %collective-permute-start.4 = (f32[4,17,128]{2,1,0:T(8,128)S(1)}, f32[4,17,128]{2,1,0:T(8,128)S(1)}, u32[]{:S(2)}, u32[]{:S(2)}) collective-permute-start(f32[4,17,128]{2,1,0:T(8,128)S(1)} %slice_bitcast_fusion), channel_id=1, source_target_pairs={{0,1},{1,0},{2,3},{3,2},{4,5},{5,4},{6,7},{7,6},{8,9},{9,8},{10,11... | collective-permute-start | bytes 104456 | tf_op jit(solution)/shard_map/ppermute | solution.py:444
  18.4 4.7 %collective-permute-start.7 = (f32[1,17,128]{2,1,0:T(8,128)S(1)}, f32[1,17,128]{2,1,0:T(8,128)S(1)}, u32[]{:S(2)}, u32[]{:S(2)}) collective-permute-start(f32[1,17,128]{2,1,0:T(8,128)S(1)} %get-tuple-element.25), channel_id=1, source_target_pairs={{0,6},{2,4},{4,2},{6,0},{1,7},{3,5},{5,3},{7,1},{8,14},{10,12},{12... | collective-permute-start | bytes 26120 | tf_op jit(solution)/shard_map/ppermute | solution.py:444
  20.5 3.7 %collective-permute-start.6 = (f32[1,17,128]{2,1,0:T(8,128)S(1)}, f32[1,17,128]{2,1,0:T(8,128)S(1)}, u32[]{:S(2)}, u32[]{:S(2)}) collective-permute-start(f32[1,17,128]{2,1,0:T(8,128)S(1)} %get-tuple-element.26), channel_id=1, source_target_pairs={{0,4},{2,6},{4,0},{6,2},{1,5},{3,7},{5,1},{7,3},{8,12},{10,14},{12... | collective-permute-start | bytes 26120 | tf_op jit(solution)/shard_map/ppermute | solution.py:444
  21.0 3.7 %collective-permute-start.5 = (f32[1,17,128]{2,1,0:T(8,128)S(1)}, f32[1,17,128]{2,1,0:T(8,128)S(1)}, u32[]{:S(2)}, u32[]{:S(2)}) collective-permute-start(f32[1,17,128]{2,1,0:T(8,128)S(1)} %get-tuple-element.27), channel_id=1, source_target_pairs={{0,2},{2,0},{4,6},{6,4},{1,3},{3,1},{5,7},{7,5},{8,10},{10,8},{12,... | collective-permute-start | bytes 26120 | tf_op jit(solution)/shard_map/ppermute | solution.py:444
  24.7 5.5 %collective-permute-start.10 = (f32[17,128]{1,0:T(8,128)S(1)}, f32[17,128]{1,0:T(8,128)S(1)}, u32[]{:S(2)}, u32[]{:S(2)}) collective-permute-start(f32[17,128]{1,0:T(8,128)S(1)} %fusion.4), channel_id=1, source_target_pairs={{0,24},{8,16},{16,8},{24,0},{1,25},{9,17},{17,9},{25,1},{2,26},{10... | collective-permute-start | bytes 26120 | tf_op jit(solution)/shard_map/ppermute | solution.py:444
  26.4 4.6 %collective-permute-start.9 = (f32[17,128]{1,0:T(8,128)S(1)}, f32[17,128]{1,0:T(8,128)S(1)}, u32[]{:S(2)}, u32[]{:S(2)}) collective-permute-start(f32[17,128]{1,0:T(8,128)S(1)} %fusion.4), channel_id=1, source_target_pairs={{0,16},{8,24},{16,0},{24,8},{1,17},{9,25},{17,1},{25,9},{2,18},{10... | collective-permute-start | bytes 26120 | tf_op jit(solution)/shard_map/ppermute | solution.py:444
  27.5 3.7 %collective-permute-start.8 = (f32[17,128]{1,0:T(8,128)S(1)}, f32[17,128]{1,0:T(8,128)S(1)}, u32[]{:S(2)}, u32[]{:S(2)}) collective-permute-start(f32[17,128]{1,0:T(8,128)S(1)} %fusion.4), channel_id=1, source_target_pairs={{0,8},{8,0},{16,24},{24,16},{1,9},{9,1},{17,25},{25,17},{2,10},{10... | collective-permute-start | bytes 26120 | tf_op jit(solution)/shard_map/ppermute | solution.py:444

commit v8 on v6

--- a/solution.py
+++ b/solution.py
@@ -14,7 +14,6 @@
 EARLY = 16
 DENSITY_FACTOR = 21.0 / (16.0 * math.pi) / 256.0
 VMEM = pl.BlockSpec(memory_space=pltpu.VMEM)
-ANY = pl.BlockSpec(memory_space=pl.ANY)
 NT = (((1,), (1,)), ((), ()))
 
 
@@ -297,19 +296,12 @@
     )
 
 
-def load_codes(far_ref, code_ref, sem):
-    copy = pltpu.make_async_copy(far_ref, code_ref, sem)
-    copy.start()
-    return copy
-
-
 def block_pairs(
-    listed, x_first, x_step, x_count, known_ref, far_code_ref, pos_ref, mass_ref, smooth_ref, prev_ref, next_ref,
-    out_ref, src_ref, code_ref, sem, nat_ref, shift_ref, tgt_ref, mat_ref, near_ref, root_ref, total_ref,
+    listed, x_first, x_step, x_count, known_ref, code_ref, pos_ref, mass_ref, smooth_ref, prev_ref, next_ref,
+    out_ref, src_ref, nat_ref, shift_ref, tgt_ref, mat_ref, near_ref, root_ref, total_ref,
     ahead=None,
 ):
     blocks_x, blocks_y, _ = mass_ref.shape
-    codes = load_codes(far_code_ref, code_ref, sem)
     for xe in range(blocks_x + 2):
         if xe == 0 or xe == blocks_x + 1:
             ref = prev_ref if xe == 0 else next_ref
@@ -341,10 +333,10 @@
     pair_sums(sides_of(len(blocks), 0, 1, mat_ref, near_ref, root_ref, total_ref))
     if ahead is not None:
         ahead()
-    codes.wait()
+    words = code_ref[...]
     for number, (turn, y) in enumerate(blocks):
         x = x_first + turn * x_step
-        word = code_ref[x * blocks_y + y]
+        word = words[x, y]
         for k in range(1, listed):
             code = (word >> (4 * k)) & 15
             step_x = (code * 11) >> 5
@@ -399,8 +391,6 @@
 
 def pair_scratch(blocks_x, blocks_y, x_count, listed):
     return [
-        pltpu.SMEM((blocks_x * blocks_y,), jnp.int32),
-        pltpu.SemaphoreType.DMA(()),
         pltpu.VMEM(((blocks_x + 2) * 64, LANES), F32),
         pltpu.VMEM((9, 8, LANES), F32),
         pltpu.VMEM((x_count, 24 * blocks_y, LANES), F32),
@@ -417,16 +407,15 @@
 
 
 def rim_kernel(
-    listed, far_code_ref, middle_ref, edge_ref, known_ref, mat_ref, self_ref, moment_ref,
+    listed, code_ref, middle_ref, edge_ref, known_ref, mat_ref, self_ref, moment_ref,
     mass_ref, smooth_ref, low_ref, high_ref, rows_ref, hot_ref, early_ref,
-    sum_ref, table_ref, code_ref, sem, nat_ref, src_ref, md_ref, lhs_ref, total_moment_ref,
+    sum_ref, table_ref, nat_ref, src_ref, md_ref, lhs_ref, total_moment_ref,
     shift_ref, near_ref, root_ref, total_ref,
 ):
     blocks_x, blocks_y, _ = mass_ref.shape
     owners = early_ref.shape[0]
     wide = blocks_x + 2
     last = blocks_y - 1
-    codes = load_codes(far_code_ref, code_ref, sem)
     for side, ref in enumerate((low_ref, high_ref)):
         store_source(nat_ref, side * 64, wide, [ref[c] for c in range(3)], ref[3])
         for xe in range(wide):
@@ -447,10 +436,10 @@
             total_moment_ref, False, hot_ref[x], lhs_ref.at[x], sum_ref[x],
             mass_ref[x], smooth_ref[x], rows_ref[x],
         )
-    codes.wait()
+    words = code_ref[...]
     for x in range(blocks_x):
         for side in range(2):
-            word = code_ref[x * blocks_y + side * last]
+            word = words[x, side * last]
             for k in range(1, listed):
                 code = (word >> (4 * k)) & 15
                 step_x = (code * 11) >> 5
@@ -510,10 +499,11 @@
     while table.shape[0] > 1:
         ways = min(4, table.shape[0])
         part = table.shape[0] // ways
-        table = added(
-            [table[:part]]
-            + [swap(table[k * part : (k + 1) * part], "chip", k * part) for k in range(1, ways)]
-        )
+        got = [
+            swap(table[k * part : (k + 1) * part], "chip", k * part)
+            for k in reversed(range(1, ways))
+        ]
+        table = added([table[:part]] + got)
     return table[0]
 
 
@@ -536,7 +526,7 @@
     chunk = blocks_y * block_len
     shape = jax.ShapeDtypeStruct
     listed = neighbours.shape[2]
-    codes = sum(neighbours[:, :, k] << (4 * k) for k in range(listed)).reshape(-1)
+    codes = sum(neighbours[:, :, k] << (4 * k) for k in range(listed))
     table_rows = group_row.reshape(-1, LANES)
     packed = jnp.concatenate([positions, masses[None]], axis=0)
     prev, following = neighbours_of(
@@ -550,7 +540,7 @@
             shape((blocks_x - 2, blocks_y, LANES), F32),
             shape(sources, F32),
         ),
-        in_specs=[ANY] + [VMEM] * 5,
+        in_specs=[VMEM] * 6,
         out_specs=(VMEM,) * 3,
         scratch_shapes=pair_scratch(blocks_x, blocks_y, blocks_x - 2, listed),
         compiler_params=params(),
@@ -594,7 +584,7 @@
             shape((rims, LANES, LANES), F32),
             shape((LANES, 2 * owners), F32),
         ),
-        in_specs=[ANY] + [VMEM] * 9,
+        in_specs=[VMEM] * 10,
         out_specs=(VMEM,) * 5,
         scratch_shapes=[
             pltpu.VMEM((blocks_x, 24 * blocks_y, LANES), F32),
@@ -612,11 +602,9 @@
     sums, table = pl.pallas_call(
         functools.partial(rim_kernel, listed),
         out_shape=(shape(masses.shape, F32), shape((2, owners // 2, EARLY + 1, LANES), F32)),
-        in_specs=[ANY] + [VMEM] * 13,
+        in_specs=[VMEM] * 14,
         out_specs=(VMEM, VMEM),
         scratch_shapes=[
-            pltpu.SMEM((blocks_x * blocks_y,), jnp.int32),
-            pltpu.SemaphoreType.DMA(()),
             pltpu.VMEM((128, LANES), F32),
             pltpu.VMEM((6 * (blocks_x + 2), 8, LANES), F32),
             pltpu.VMEM((owners, LANES), F32),

time: 33.3 us -> 31.6 us (0.949)
  waiting for transfers between devices: 7.15 us -> 6.32 us
  Pallas kernels: 7.59 us -> 6.91 us
    ppermute x7, waiting for transfers between devices: 7.14 us -> 6.31 us  [swap(): return lax.ppermute(value, axis, [(i, i ^ step) for i in range(count)])]
    pallas_call x1, Pallas kernels: 1.95 us -> 1.47 us  [shards(): pl.pallas_call(functools.partial(rim_kernel, listed), out_shape=(shape(ma...]
where the time goes in v8:
time: 31.6 us; the launch traced here: 31.5 us
  starting transfers between devices  15.3 us (48%)
  Pallas kernels  6.91 us (22%)
  waiting for transfers between devices  6.32 us (20%)
  other arithmetic  2.07 us (7%)
  between operations  0.82 us (3%)
    ppermute x7, starting transfers between devices, swap(): return lax.ppermute(value, axis, [(i, i ^ step) for i in range(count)])  7.11 us
    ppermute x7, waiting for transfers between devices, swap(): return lax.ppermute(value, axis, [(i, i ^ step) for i in range(count)])  6.31 us
    ppermute x2, starting transfers between devices, neighbours_of(): lax.ppermute(jnp.where(even, low_edge, high_edge), axis, [(i, (i + 1 if i...  5.09 us
    ppermute x2, starting transfers between devices, neighbours_of(): lax.ppermute(jnp.where(even, high_edge, low_edge), axis, [(i, i ^ 1) for...  3.09 us
    pallas_call x1, Pallas kernels, shards(): pl.pallas_call(functools.partial(edge_kernel, listed), out_shape=(shape((...  2.33 us
    pallas_call x1, Pallas kernels, shards(): pl.pallas_call(functools.partial(middle_kernel, listed), out_shape=(shape...  2.08 us
    pallas_call x1, Pallas kernels, shards(): pl.pallas_call(functools.partial(rim_kernel, listed), out_shape=(shape(ma...  1.47 us
    pallas_call x1, Pallas kernels, shards(): pl.pallas_call(functools.partial(moments_kernel, blocks_x * dom_count, bl...  1.03 us
  transfers between devices with their start and end apart: 11, of which 7 were waited for; matrix products, arithmetic and copies ran while one was open for 2% of the time, Pallas kernels for 17%

profile of v8, /device:TPU:0, one launch (start us, length us, event | category | flops | bytes accessed | tf_op | source)
XLA Modules:
  0.0 31.5 jit_solution(15628676832705806290)
XLA Ops:
  0.6 0.0 copy-start.2
  0.6 0.8 %select_bitcast_fusion = (f32[4,8,128]{2,1,0:T(8,128)S(1)}, f32[4,1,8,128]{3,2,0,1:T(8,128)S(1)}, f32[4,1,8,128]{3,2,0,1:T(8,128)S(1)}) fusion(pred[]{:T(512)S(6)} %eq.6, f32[1,4,8,128]{3,2,0,1:T(8,128)} %bitcast.18, f32[3,4,8,128]{3,2,1,0:T(8,128)} %pos_ref.5), kind=kLoop, calls=%fused_computation.8 | loop fusion | flops 12288 | bytes 114689 | tf_op jit(solution)/shard_map/jit(_where)/select_n | solution.py:481
  1.4 3.0 %collective-permute-start.1 = (f32[4,8,128]{2,1,0:T(8,128)S(1)}, f32[4,8,128]{2,1,0:T(8,128)S(1)}, u32[]{:S(2)}, u32[]{:S(2)}) collective-permute-start(f32[4,8,128]{2,1,0:T(8,128)S(1)} %get-tuple-element.28), channel_id=1, source_target_pairs={{0,8},{8,0},{16,24},{24,16},{1,9},{9,1},{17,25},{25,17},{2,10},{10... | collective-permute-start | bytes 49160 | tf_op jit(solution)/shard_map/ppermute | solution.py:480
  4.4 0.0 copy-start.6
  4.5 0.0 copy-start
  4.5 0.0 copy-start.1
  4.5 0.0 copy-start.4
  4.5 0.0 copy-start.5
  4.5 2.5 %collective-permute-start = (f32[4,8,128]{2,1,0:T(8,128)S(1)}, f32[4,8,128]{2,1,0:T(8,128)S(1)}, u32[]{:S(2)}, u32[]{:S(2)}) collective-permute-start(f32[4,8,128]{2,1,0:T(8,128)S(1)} %select_bitcast_fusion.1), channel_id=1, source_target_pairs={{0,24},{8,16},{16,8},{24,0},{1,25},{9,17},{17,9},{25,1},{2,26},{10... | collective-permute-start | bytes 49160 | tf_op jit(solution)/shard_map/ppermute | solution.py:483
  7.0 0.0 copy-done.6
  7.0 0.0 copy-done.2
  7.0 0.0 copy-done
  7.0 0.0 copy-done.1
  7.1 0.0 copy-done.4
  7.1 0.0 copy-done.5
  7.1 0.0 copy-start.3
  7.1 2.1 %middle_pairs.1 = (f32[2,4,4,128]{3,2,1,0:T(4,128)S(1)}, f32[2,8,128]{2,1,0:T(8,128)S(1)}, f32[48,8,128]{2,1,0:T(8,128)S(1)}) custom-call(s32[4,8]{1,0:T(4,128)S(1)} %add_bitcast_fusion.code_ref, f32[3,4,8,128]{3,2,1,0:T(8,128)S(1)} %copy-done.2, f32[4,8,128]{2,1,0:T(8,128)S(1)} %copy-done, f32[4,8,128]{2,1,0:T(8,128)S(1)} %copy-done.1, ...), custom_call_target="tpu_custom_call" | custom-call | flops 4000000000 | bytes 400000 | tf_op jit(solution)/shard_map/middle_pairs/pallas_call | solution.py:536
  9.2 0.0 copy-done.3
  9.2 1.0 %moments_by_row.1 = (f32[8,16,128]{2,1,0:T(8,128)S(1)}, s32[4,8,128]{2,1,0:T(8,128)S(1)}, bf16[4,128,1024]{2,1,0:T(8,128)(2,1)S(1)}) custom-call(f32[2,8,128]{2,1,0:T(8,128)S(1)} %get-tuple-element.15.after_ref.middle_ref, f32[3,4,8,128]{3,2,1,0:T(8,128)S(1)} %copy-done.2, f32[3,4,8,128]{3,2,1,0:T(8,128)S(1)} %copy-done.3, f32[4,8,128]{2,1,0:T(8,128)S(1)} %copy-done, ...), custom_call_target="tpu_custom_call" | custom-call | flops 2000000000 | bytes 1400000 | tf_op jit(solution)/shard_map/moments_by_row/pallas_call | solution.py:552
  10.2 0.0 collective-permute-done.1
  10.2 0.0 collective-permute-done
  10.3 0.1 collective-permute-start.3
  10.4 2.5 %collective-permute-start.2 = (f32[4,6,128]{2,1,0:T(8,128)S(1)}, f32[4,6,128]{2,1,0:T(8,128)S(1)}, u32[]{:S(2)}, u32[]{:S(2)}) collective-permute-start(f32[4,6,128]{2,1,0:T(8,128)S(1)} %get-tuple-element.39), channel_id=1, source_target_pairs={{0,7},{1,2},{2,1},{3,4},{4,3},{5,6},{6,5},{7,0},{8,15},{9,10},{10,... | collective-permute-start | bytes 36872 | tf_op jit(solution)/shard_map/ppermute | solution.py:483
  12.9 2.3 %edge_pairs.1 = (f32[2,8,128]{2,1,0:T(8,128)S(1)}, f32[48,8,128]{2,1,0:T(8,128)S(1)}, bf16[8,128,48]{2,1,0:T(8,128)(2,1)S(1)}, f32[8,128,128]{2,1,0:T(8,128)S(1)}, f32[128,16]{1,0:T(8,128)S(1)}) custom-call(s32[4,8]{1,0:T(4,128)S(1)} %add_bitcast_fusion.code_ref, f32[3,4,8,128]{3,2,1,0:T(8,128)S(1)} %copy-done.2, f32[4,8,128]{2,1,0:T(8,128)S(1)} %copy-done, ...), custom_call_target="tpu_custom_call" | custom-call | flops 4000000000 | bytes 400000 | tf_op jit(solution)/shard_map/edge_pairs/pallas_call | solution.py:578
  15.3 0.0 collective-permute-done.3
  15.3 0.0 collective-permute-done.2
  15.3 1.5 %rim_pairs_and_table.1 = (f32[4,8,128]{2,1,0:T(8,128)S(1)}, f32[2,4,17,128]{3,2,1,0:T(8,128)S(1)}) custom-call(s32[4,8]{1,0:T(4,128)S(1)} %add_bitcast_fusion.code_ref, f32[2,8,128]{2,1,0:T(8,128)S(1)} %get-tuple-element.15.after_ref.middle_ref, f32[2,8,128]{2,1,0:T(8,128)S(1)} %get-tuple-element.19.edge_ref, f32[48,8,128]{2,1,0:T(8,128)S(1)} %get-tuple-element.20.known_ref, ...), custom_call_target="tpu_custom_call" | custom-call | flops 200000000 | bytes 400000 | tf_op jit(solution)/shard_map/rim_pairs_and_table/pallas_call | solution.py:602
  16.8 0.1 collective-permute-start.4
  16.8 1.2 %collective-permute-done.4 = f32[4,17,128]{2,1,0:T(8,128)S(1)} collective-permute-done((f32[4,17,128]{2,1,0:T(8,128)S(1)}, f32[4,17,128]{2,1,0:T(8,128)S(1)}, u32[]{:S(2)}, u32[]{:S(2)}) %collective-permute-start.4) | collective-permute-done | bytes 34848 | tf_op jit(solution)/shard_map/ppermute | solution.py:474
  18.1 1.8 %collective-permute-start.5 = (f32[1,17,128]{2,1,0:T(8,128)S(1)}, f32[1,17,128]{2,1,0:T(8,128)S(1)}, u32[]{:S(2)}, u32[]{:S(2)}) collective-permute-start(f32[1,17,128]{2,1,0:T(8,128)S(1)} %get-tuple-element.33), channel_id=1, source_target_pairs={{0,6},{2,4},{4,2},{6,0},{1,7},{3,5},{5,3},{7,1},{8,14},{10,12},{12... | collective-permute-start | bytes 26120 | tf_op jit(solution)/shard_map/ppermute | solution.py:474
  19.9 0.5 %collective-permute-start.6 = (f32[1,17,128]{2,1,0:T(8,128)S(1)}, f32[1,17,128]{2,1,0:T(8,128)S(1)}, u32[]{:S(2)}, u32[]{:S(2)}) collective-permute-start(f32[1,17,128]{2,1,0:T(8,128)S(1)} %get-tuple-element.32), channel_id=1, source_target_pairs={{0,4},{2,6},{4,0},{6,2},{1,5},{3,7},{5,1},{7,3},{8,12},{10,14},{12... | collective-permute-start | bytes 26120 | tf_op jit(solution)/shard_map/ppermute | solution.py:474
  20.4 1.2 %collective-permute-start.7 = (f32[1,17,128]{2,1,0:T(8,128)S(1)}, f32[1,17,128]{2,1,0:T(8,128)S(1)}, u32[]{:S(2)}, u32[]{:S(2)}) collective-permute-start(f32[1,17,128]{2,1,0:T(8,128)S(1)} %get-tuple-element.31), channel_id=1, source_target_pairs={{0,2},{2,0},{4,6},{6,4},{1,3},{3,1},{5,7},{7,5},{8,10},{10,8},{12,... | collective-permute-start | bytes 26120 | tf_op jit(solution)/shard_map/ppermute | solution.py:474
  21.6 1.2 %collective-permute-done.5 = f32[1,17,128]{2,1,0:T(8,128)S(1)} collective-permute-done((f32[1,17,128]{2,1,0:T(8,128)S(1)}, f32[1,17,128]{2,1,0:T(8,128)S(1)}, u32[]{:S(2)}, u32[]{:S(2)}) %collective-permute-start.5) | collective-permute-done | bytes 8736 | tf_op jit(solution)/shard_map/ppermute | solution.py:474
  22.8 0.8 %collective-permute-done.6 = f32[1,17,128]{2,1,0:T(8,128)S(1)} collective-permute-done((f32[1,17,128]{2,1,0:T(8,128)S(1)}, f32[1,17,128]{2,1,0:T(8,128)S(1)}, u32[]{:S(2)}, u32[]{:S(2)}) %collective-permute-start.6) | collective-permute-done | bytes 8736 | tf_op jit(solution)/shard_map/ppermute | solution.py:474
  23.6 0.5 %collective-permute-done.7 = f32[1,17,128]{2,1,0:T(8,128)S(1)} collective-permute-done((f32[1,17,128]{2,1,0:T(8,128)S(1)}, f32[1,17,128]{2,1,0:T(8,128)S(1)}, u32[]{:S(2)}, u32[]{:S(2)}) %collective-permute-start.7) | collective-permute-done | bytes 8736 | tf_op jit(solution)/shard_map/ppermute | solution.py:474
  24.1 0.7 %collective-permute-start.9 = (f32[17,128]{1,0:T(8,128)S(1)}, f32[17,128]{1,0:T(8,128)S(1)}, u32[]{:S(2)}, u32[]{:S(2)}) collective-permute-start(f32[17,128]{1,0:T(8,128)S(1)} %fusion.4), channel_id=1, source_target_pairs={{0,16},{8,24},{16,0},{24,8},{1,17},{9,25},{17,1},{25,9},{2,18},{10... | collective-permute-start | bytes 26120 | tf_op jit(solution)/shard_map/ppermute | solution.py:474
  24.8 2.3 %collective-permute-start.10 = (f32[17,128]{1,0:T(8,128)S(1)}, f32[17,128]{1,0:T(8,128)S(1)}, u32[]{:S(2)}, u32[]{:S(2)}) collective-permute-start(f32[17,128]{1,0:T(8,128)S(1)} %fusion.4), channel_id=1, source_target_pairs={{0,24},{8,16},{16,8},{24,0},{1,25},{9,17},{17,9},{25,1},{2,26},{10... | collective-permute-start | bytes 26120 | tf_op jit(solution)/shard_map/ppermute | solution.py:474
  27.2 0.4 %collective-permute-start.8 = (f32[17,128]{1,0:T(8,128)S(1)}, f32[17,128]{1,0:T(8,128)S(1)}, u32[]{:S(2)}, u32[]{:S(2)}) collective-permute-start(f32[17,128]{1,0:T(8,128)S(1)} %fusion.4), channel_id=1, source_target_pairs={{0,8},{8,0},{16,24},{24,16},{1,9},{9,1},{17,25},{25,17},{2,10},{10... | collective-permute-start | bytes 26120 | tf_op jit(solution)/shard_map/ppermute | solution.py:474
  27.6 0.6 %fusion = f32[4,8,128]{2,1,0:T(8,128)} fusion(f32[4,8,128]{2,1,0:T(8,128)S(1)} %copy-done.1, f32[4,8,128]{2,1,0:T(8,128)S(1)} %get-tuple-element.26), kind=kLoop, calls=%fused_computation.3 | loop fusion | flops 16384 | bytes 49152 | tf_op jit(solution)/shard_map/div | solution.py:625
  28.2 0.5 %collective-permute-done.9 = f32[17,128]{1,0:T(8,128)S(1)} collective-permute-done((f32[17,128]{1,0:T(8,128)S(1)}, f32[17,128]{1,0:T(8,128)S(1)}, u32[]{:S(2)}, u32[]{:S(2)}) %collective-permute-start.9) | collective-permute-done | bytes 8736 | tf_op jit(solution)/shard_map/ppermute | solution.py:474
  28.7 1.6 %collective-permute-done.10 = f32[17,128]{1,0:T(8,128)S(1)} collective-permute-done((f32[17,128]{1,0:T(8,128)S(1)}, f32[17,128]{1,0:T(8,128)S(1)}, u32[]{:S(2)}, u32[]{:S(2)}) %collective-permute-start.10) | collective-permute-done | bytes 8736 | tf_op jit(solution)/shard_map/ppermute | solution.py:474
  30.3 0.5 %collective-permute-done.8 = f32[17,128]{1,0:T(8,128)S(1)} collective-permute-done((f32[17,128]{1,0:T(8,128)S(1)}, f32[17,128]{1,0:T(8,128)S(1)}, u32[]{:S(2)}, u32[]{:S(2)}) %collective-permute-start.8) | collective-permute-done | bytes 8736 | tf_op jit(solution)/shard_map/ppermute | solution.py:474
  30.9 0.6 %add_add_fusion = f32[17,128]{1,0:T(8,128)} fusion(f32[17,128]{1,0:T(8,128)S(1)} %collective-permute-done.9, f32[17,128]{1,0:T(8,128)S(1)} %collective-permute-done.10, f32[17,128]{1,0:T(8,128)S(1)} %fusion.4, f32[17,128]{1,0:T(8,128)S(1)} %collective-permute-done.8), kind=kLoop, calls=%fused_computation.15 | loop fusion | flops 6528 | bytes 43520 | tf_op jit(solution)/shard_map/add | solution.py:493
  (11 shorter events, 0.1 us)
Async XLA Ops:
  0.6 6.4 %copy-start.2 = (f32[3,4,8,128]{3,2,1,0:T(8,128)S(1)}, f32[3,4,8,128]{3,2,1,0:T(8,128)}, u32[]{:S(2)}) copy-start(f32[3,4,8,128]{3,2,1,0:T(8,128)} %pos_ref.5) | copy-start | bytes 147460
  1.4 8.8 %collective-permute-start.1 = (f32[4,8,128]{2,1,0:T(8,128)S(1)}, f32[4,8,128]{2,1,0:T(8,128)S(1)}, u32[]{:S(2)}, u32[]{:S(2)}) collective-permute-start(f32[4,8,128]{2,1,0:T(8,128)S(1)} %get-tuple-element.28), channel_id=1, source_target_pairs={{0,8},{8,0},{16,24},{24,16},{1,9},{9,1},{17,25},{25,17},{2,10},{10... | collective-permute-start | bytes 49160 | tf_op jit(solution)/shard_map/ppermute | solution.py:480
  4.4 2.6 %copy-start.6 = (s32[4,8,5]{1,0,2:T(4,128)S(1)}, s32[4,8,5]{1,0,2:T(4,128)}, u32[]{:S(2)}) copy-start(s32[4,8,5]{1,0,2:T(4,128)} %param.11) | copy-start | bytes 1924
  4.5 2.6 %copy-start = (f32[4,8,128]{2,1,0:T(8,128)S(1)}, f32[4,8,128]{2,1,0:T(8,128)}, u32[]{:S(2)}) copy-start(f32[4,8,128]{2,1,0:T(8,128)} %mass_ref.7) | copy-start | bytes 49156
  4.5 2.6 %copy-start.1 = (f32[4,8,128]{2,1,0:T(8,128)S(1)}, f32[4,8,128]{2,1,0:T(8,128)}, u32[]{:S(2)}) copy-start(f32[4,8,128]{2,1,0:T(8,128)} %smooth_ref.5) | copy-start | bytes 49156
  4.5 2.6 %copy-start.4 = (s32[4,8,128]{2,1,0:T(8,128)S(1)}, s32[4,8,128]{2,1,0:T(8,128)}, u32[]{:S(2)}) copy-start(s32[4,8,128]{2,1,0:T(8,128)} %group_ref.3) | copy-start | bytes 49156
  4.5 2.6 %copy-start.5 = (s32[1024]{0:T(1024)S(1)}, s32[1024]{0:T(1024)}, u32[]{:S(2)}) copy-start(s32[1024]{0:T(1024)} %param.13) | copy-start | bytes 12292
  4.5 5.7 %collective-permute-start = (f32[4,8,128]{2,1,0:T(8,128)S(1)}, f32[4,8,128]{2,1,0:T(8,128)S(1)}, u32[]{:S(2)}, u32[]{:S(2)}) collective-permute-start(f32[4,8,128]{2,1,0:T(8,128)S(1)} %select_bitcast_fusion.1), channel_id=1, source_target_pairs={{0,24},{8,16},{16,8},{24,0},{1,25},{9,17},{17,9},{25,1},{2,26},{10... | collective-permute-start | bytes 49160 | tf_op jit(solution)/shard_map/ppermute | solution.py:483
  7.1 2.1 %copy-start.3 = (f32[3,4,8,128]{3,2,1,0:T(8,128)S(1)}, f32[3,4,8,128]{3,2,1,0:T(8,128)}, u32[]{:S(2)}) copy-start(f32[3,4,8,128]{3,2,1,0:T(8,128)} %vel_ref.1) | copy-start | bytes 147460
  10.3 5.0 %collective-permute-start.3 = (f32[4,6,128]{2,1,0:T(8,128)S(1)}, f32[4,6,128]{2,1,0:T(8,128)S(1)}, u32[]{:S(2)}, u32[]{:S(2)}) collective-permute-start(f32[4,6,128]{2,1,0:T(8,128)S(1)} %get-tuple-element.38), channel_id=1, source_target_pairs={{0,1},{1,0},{2,3},{3,2},{4,5},{5,4},{6,7},{7,6},{8,9},{9,8},{10,11... | collective-permute-start | bytes 36872 | tf_op jit(solution)/shard_map/ppermute | solution.py:480
  10.4 4.9 %collective-permute-start.2 = (f32[4,6,128]{2,1,0:T(8,128)S(1)}, f32[4,6,128]{2,1,0:T(8,128)S(1)}, u32[]{:S(2)}, u32[]{:S(2)}) collective-permute-start(f32[4,6,128]{2,1,0:T(8,128)S(1)} %get-tuple-element.39), channel_id=1, source_target_pairs={{0,7},{1,2},{2,1},{3,4},{4,3},{5,6},{6,5},{7,0},{8,15},{9,10},{10,... | collective-permute-start | bytes 36872 | tf_op jit(solution)/shard_map/ppermute | solution.py:483
  16.8 1.3 %collective-permute-start.4 = (f32[4,17,128]{2,1,0:T(8,128)S(1)}, f32[4,17,128]{2,1,0:T(8,128)S(1)}, u32[]{:S(2)}, u32[]{:S(2)}) collective-permute-start(f32[4,17,128]{2,1,0:T(8,128)S(1)} %slice_bitcast_fusion), channel_id=1, source_target_pairs={{0,1},{1,0},{2,3},{3,2},{4,5},{5,4},{6,7},{7,6},{8,9},{9,8},{10,11... | collective-permute-start | bytes 104456 | tf_op jit(solution)/shard_map/ppermute | solution.py:474
  18.1 4.7 %collective-permute-start.5 = (f32[1,17,128]{2,1,0:T(8,128)S(1)}, f32[1,17,128]{2,1,0:T(8,128)S(1)}, u32[]{:S(2)}, u32[]{:S(2)}) collective-permute-start(f32[1,17,128]{2,1,0:T(8,128)S(1)} %get-tuple-element.33), channel_id=1, source_target_pairs={{0,6},{2,4},{4,2},{6,0},{1,7},{3,5},{5,3},{7,1},{8,14},{10,12},{12... | collective-permute-start | bytes 26120 | tf_op jit(solution)/shard_map/ppermute | solution.py:474
  19.9 3.7 %collective-permute-start.6 = (f32[1,17,128]{2,1,0:T(8,128)S(1)}, f32[1,17,128]{2,1,0:T(8,128)S(1)}, u32[]{:S(2)}, u32[]{:S(2)}) collective-permute-start(f32[1,17,128]{2,1,0:T(8,128)S(1)} %get-tuple-element.32), channel_id=1, source_target_pairs={{0,4},{2,6},{4,0},{6,2},{1,5},{3,7},{5,1},{7,3},{8,12},{10,14},{12... | collective-permute-start | bytes 26120 | tf_op jit(solution)/shard_map/ppermute | solution.py:474
  20.4 3.7 %collective-permute-start.7 = (f32[1,17,128]{2,1,0:T(8,128)S(1)}, f32[1,17,128]{2,1,0:T(8,128)S(1)}, u32[]{:S(2)}, u32[]{:S(2)}) collective-permute-start(f32[1,17,128]{2,1,0:T(8,128)S(1)} %get-tuple-element.31), channel_id=1, source_target_pairs={{0,2},{2,0},{4,6},{6,4},{1,3},{3,1},{5,7},{7,5},{8,10},{10,8},{12,... | collective-permute-start | bytes 26120 | tf_op jit(solution)/shard_map/ppermute | solution.py:474
  24.1 4.6 %collective-permute-start.9 = (f32[17,128]{1,0:T(8,128)S(1)}, f32[17,128]{1,0:T(8,128)S(1)}, u32[]{:S(2)}, u32[]{:S(2)}) collective-permute-start(f32[17,128]{1,0:T(8,128)S(1)} %fusion.4), channel_id=1, source_target_pairs={{0,16},{8,24},{16,0},{24,8},{1,17},{9,25},{17,1},{25,9},{2,18},{10... | collective-permute-start | bytes 26120 | tf_op jit(solution)/shard_map/ppermute | solution.py:474
  24.8 5.5 %collective-permute-start.10 = (f32[17,128]{1,0:T(8,128)S(1)}, f32[17,128]{1,0:T(8,128)S(1)}, u32[]{:S(2)}, u32[]{:S(2)}) collective-permute-start(f32[17,128]{1,0:T(8,128)S(1)} %fusion.4), channel_id=1, source_target_pairs={{0,24},{8,16},{16,8},{24,0},{1,25},{9,17},{17,9},{25,1},{2,26},{10... | collective-permute-start | bytes 26120 | tf_op jit(solution)/shard_map/ppermute | solution.py:474
  27.2 3.7 %collective-permute-start.8 = (f32[17,128]{1,0:T(8,128)S(1)}, f32[17,128]{1,0:T(8,128)S(1)}, u32[]{:S(2)}, u32[]{:S(2)}) collective-permute-start(f32[17,128]{1,0:T(8,128)S(1)} %fusion.4), channel_id=1, source_target_pairs={{0,8},{8,0},{16,24},{24,16},{1,9},{9,1},{17,25},{25,17},{2,10},{10... | collective-permute-start | bytes 26120 | tf_op jit(solution)/shard_map/ppermute | solution.py:474

commit v9 on v8

--- a/solution.py
+++ b/solution.py
@@ -476,16 +476,16 @@
 
 def neighbours_of(low_edge, high_edge, axis, parity):
     count = lax.axis_size(axis)
-    even = parity == 0
-    inner = lax.ppermute(
-        jnp.where(even, high_edge, low_edge), axis, [(i, i ^ 1) for i in range(count)]
-    )
+    odd = parity == 1
     outer = lax.ppermute(
-        jnp.where(even, low_edge, high_edge),
+        jnp.where(odd, high_edge, low_edge),
         axis,
         [(i, (i + 1 if i & 1 else i - 1) % count) for i in range(count)],
     )
-    return jnp.where(even, outer, inner), jnp.where(even, inner, outer)
+    inner = lax.ppermute(
+        jnp.where(odd, low_edge, high_edge), axis, [(i, i ^ 1) for i in range(count)]
+    )
+    return jnp.where(odd, inner, outer), jnp.where(odd, outer, inner)
 
 
 def added(parts):

time: 31.6 us -> 32.3 us (1.022)
  waiting for transfers between devices: 6.32 us -> 7.14 us
  starting transfers between devices: 15.3 us -> 14.5 us
  local copies, waits for them, and re-layouts: 0.05 us -> 0.68 us
    ppermute x4, starting transfers between devices: 8.18 us -> 6.8 us  [the longest x2 6.72 us: neighbours_of(): lax.ppermute(jnp.where(odd, high_edge, low_edge), axis, [(i, (i + 1 if i...]
    ppermute x7, waiting for transfers between devices: 6.31 us -> 6.95 us  [swap(): return lax.ppermute(value, axis, [(i, i ^ step) for i in range(count)])]
    ppermute x7, starting transfers between devices: 7.11 us -> 7.74 us  [swap(): return lax.ppermute(value, axis, [(i, i ^ step) for i in range(count)])]
    unnamed x14, local copies, waits for them, and re-layouts: 0.03 us -> 0.66 us
  transfers between devices with their start and end apart: 11 -> 11, of which waited for: 7 -> 8; matrix products, arithmetic and copies ran while one was open for 2% -> 2% of each run, Pallas kernels for 17% -> 17%
where the time goes in v9:
time: 32.3 us; the launch traced here: 32.1 us
  starting transfers between devices  14.5 us (45%)
  waiting for transfers between devices  7.14 us (22%)
  Pallas kernels  6.9 us (21%)
  other arithmetic  2.06 us (6%)
  between operations  0.76 us (2%)
  local copies, waits for them, and re-layouts  0.68 us (2%)
    ppermute x7, starting transfers between devices, swap(): return lax.ppermute(value, axis, [(i, i ^ step) for i in range(count)])  7.74 us
    ppermute x7, waiting for transfers between devices, swap(): return lax.ppermute(value, axis, [(i, i ^ step) for i in range(count)])  6.95 us
    ppermute x2, starting transfers between devices, neighbours_of(): lax.ppermute(jnp.where(odd, high_edge, low_edge), axis, [(i, (i + 1 if i...  6.72 us
    pallas_call x1, Pallas kernels, shards(): pl.pallas_call(functools.partial(edge_kernel, listed), out_shape=(shape((...  2.33 us
    pallas_call x1, Pallas kernels, shards(): pl.pallas_call(functools.partial(middle_kernel, listed), out_shape=(shape...  2.07 us
    pallas_call x1, Pallas kernels, shards(): pl.pallas_call(functools.partial(rim_kernel, listed), out_shape=(shape(ma...  1.47 us
    pallas_call x1, Pallas kernels, shards(): pl.pallas_call(functools.partial(moments_kernel, blocks_x * dom_count, bl...  1.03 us
    select_n x2, other arithmetic, neighbours_of(): jnp.where(odd, high_edge, low_edge)  0.8 us
  transfers between devices with their start and end apart: 11, of which 8 were waited for; matrix products, arithmetic and copies ran while one was open for 2% of the time, Pallas kernels for 17%

profile of v9, /device:TPU:0, one launch (start us, length us, event | category | flops | bytes accessed | tf_op | source)
XLA Modules:
  0.0 32.1 jit_solution(2238159353172964228)
XLA Ops:
  0.6 0.0 copy-start.2
  0.6 0.8 %select_bitcast_fusion = (f32[4,8,128]{2,1,0:T(8,128)S(1)}, f32[4,1,8,128]{3,2,0,1:T(8,128)S(1)}, f32[4,1,8,128]{3,2,0,1:T(8,128)S(1)}) fusion(pred[]{:T(512)S(6)} %eq.6, f32[1,4,8,128]{3,2,0,1:T(8,128)} %bitcast.18, f32[3,4,8,128]{3,2,1,0:T(8,128)} %pos_ref.5), kind=kLoop, calls=%fused_computation.8 | loop fusion | flops 12288 | bytes 114689 | tf_op jit(solution)/shard_map/jit(_where)/select_n | solution.py:481
  1.4 5.0 %collective-permute-start.1 = (f32[4,8,128]{2,1,0:T(8,128)S(1)}, f32[4,8,128]{2,1,0:T(8,128)S(1)}, u32[]{:S(2)}, u32[]{:S(2)}) collective-permute-start(f32[4,8,128]{2,1,0:T(8,128)S(1)} %get-tuple-element.28), channel_id=1, source_target_pairs={{0,24},{8,16},{16,8},{24,0},{1,25},{9,17},{17,9},{25,1},{2,26},{10... | collective-permute-start | bytes 49160 | tf_op jit(solution)/shard_map/ppermute | solution.py:480
  6.5 0.0 copy-start.6
  6.5 0.0 copy-start
  6.5 0.0 copy-start.1
  6.5 0.0 copy-start.4
  6.5 0.0 copy-start.5
  6.5 0.1 collective-permute-start
  6.6 0.6 %copy-done.6 = s32[4,8,5]{1,0,2:T(4,128)S(1)} copy-done((s32[4,8,5]{1,0,2:T(4,128)S(1)}, s32[4,8,5]{1,0,2:T(4,128)}, u32[]{:S(2)}) %copy-start.6) | copy-done | bytes 664
  7.2 0.0 copy-done.2
  7.2 0.0 copy-done
  7.2 0.0 copy-done.1
  7.2 0.0 copy-done.4
  7.2 0.0 copy-done.5
  7.2 0.0 copy-start.3
  7.2 2.1 %middle_pairs.1 = (f32[2,4,4,128]{3,2,1,0:T(4,128)S(1)}, f32[2,8,128]{2,1,0:T(8,128)S(1)}, f32[48,8,128]{2,1,0:T(8,128)S(1)}) custom-call(s32[4,8]{1,0:T(4,128)S(1)} %add_bitcast_fusion.code_ref, f32[3,4,8,128]{3,2,1,0:T(8,128)S(1)} %copy-done.2, f32[4,8,128]{2,1,0:T(8,128)S(1)} %copy-done, f32[4,8,128]{2,1,0:T(8,128)S(1)} %copy-done.1, ...), custom_call_target="tpu_custom_call" | custom-call | flops 4000000000 | bytes 400000 | tf_op jit(solution)/shard_map/middle_pairs/pallas_call | solution.py:536
  9.3 0.0 copy-done.3
  9.3 1.0 %moments_by_row.1 = (f32[8,16,128]{2,1,0:T(8,128)S(1)}, s32[4,8,128]{2,1,0:T(8,128)S(1)}, bf16[4,128,1024]{2,1,0:T(8,128)(2,1)S(1)}) custom-call(f32[2,8,128]{2,1,0:T(8,128)S(1)} %get-tuple-element.15.after_ref.middle_ref, f32[3,4,8,128]{3,2,1,0:T(8,128)S(1)} %copy-done.2, f32[3,4,8,128]{3,2,1,0:T(8,128)S(1)} %copy-done.3, f32[4,8,128]{2,1,0:T(8,128)S(1)} %copy-done, ...), custom_call_target="tpu_custom_call" | custom-call | flops 2000000000 | bytes 1400000 | tf_op jit(solution)/shard_map/moments_by_row/pallas_call | solution.py:552
  10.4 0.0 collective-permute-done.1
  10.4 0.0 collective-permute-done
  10.4 1.7 %collective-permute-start.3 = (f32[4,6,128]{2,1,0:T(8,128)S(1)}, f32[4,6,128]{2,1,0:T(8,128)S(1)}, u32[]{:S(2)}, u32[]{:S(2)}) collective-permute-start(f32[4,6,128]{2,1,0:T(8,128)S(1)} %get-tuple-element.38), channel_id=1, source_target_pairs={{0,7},{1,2},{2,1},{3,4},{4,3},{5,6},{6,5},{7,0},{8,15},{9,10},{10,... | collective-permute-start | bytes 36872 | tf_op jit(solution)/shard_map/ppermute | solution.py:480
  12.1 0.0 collective-permute-start.2
  12.1 2.3 %edge_pairs.1 = (f32[2,8,128]{2,1,0:T(8,128)S(1)}, f32[48,8,128]{2,1,0:T(8,128)S(1)}, bf16[8,128,48]{2,1,0:T(8,128)(2,1)S(1)}, f32[8,128,128]{2,1,0:T(8,128)S(1)}, f32[128,16]{1,0:T(8,128)S(1)}) custom-call(s32[4,8]{1,0:T(4,128)S(1)} %add_bitcast_fusion.code_ref, f32[3,4,8,128]{3,2,1,0:T(8,128)S(1)} %copy-done.2, f32[4,8,128]{2,1,0:T(8,128)S(1)} %copy-done, ...), custom_call_target="tpu_custom_call" | custom-call | flops 4000000000 | bytes 400000 | tf_op jit(solution)/shard_map/edge_pairs/pallas_call | solution.py:578
  14.5 0.2 collective-permute-done.3
  14.6 0.0 collective-permute-done.2
  14.6 1.5 %rim_pairs_and_table.1 = (f32[4,8,128]{2,1,0:T(8,128)S(1)}, f32[2,4,17,128]{3,2,1,0:T(8,128)S(1)}) custom-call(s32[4,8]{1,0:T(4,128)S(1)} %add_bitcast_fusion.code_ref, f32[2,8,128]{2,1,0:T(8,128)S(1)} %get-tuple-element.15.after_ref.middle_ref, f32[2,8,128]{2,1,0:T(8,128)S(1)} %get-tuple-element.19.edge_ref, f32[48,8,128]{2,1,0:T(8,128)S(1)} %get-tuple-element.20.known_ref, ...), custom_call_target="tpu_custom_call" | custom-call | flops 200000000 | bytes 400000 | tf_op jit(solution)/shard_map/rim_pairs_and_table/pallas_call | solution.py:602
  16.1 0.4 %collective-permute-start.4 = (f32[4,17,128]{2,1,0:T(8,128)S(1)}, f32[4,17,128]{2,1,0:T(8,128)S(1)}, u32[]{:S(2)}, u32[]{:S(2)}) collective-permute-start(f32[4,17,128]{2,1,0:T(8,128)S(1)} %slice_bitcast_fusion), channel_id=1, source_target_pairs={{0,1},{1,0},{2,3},{3,2},{4,5},{5,4},{6,7},{7,6},{8,9},{9,8},{10,11... | collective-permute-start | bytes 104456 | tf_op jit(solution)/shard_map/ppermute | solution.py:474
  16.5 0.9 %collective-permute-done.4 = f32[4,17,128]{2,1,0:T(8,128)S(1)} collective-permute-done((f32[4,17,128]{2,1,0:T(8,128)S(1)}, f32[4,17,128]{2,1,0:T(8,128)S(1)}, u32[]{:S(2)}, u32[]{:S(2)}) %collective-permute-start.4) | collective-permute-done | bytes 34848 | tf_op jit(solution)/shard_map/ppermute | solution.py:474
  17.5 1.7 %collective-permute-start.5 = (f32[1,17,128]{2,1,0:T(8,128)S(1)}, f32[1,17,128]{2,1,0:T(8,128)S(1)}, u32[]{:S(2)}, u32[]{:S(2)}) collective-permute-start(f32[1,17,128]{2,1,0:T(8,128)S(1)} %get-tuple-element.33), channel_id=1, source_target_pairs={{0,6},{2,4},{4,2},{6,0},{1,7},{3,5},{5,3},{7,1},{8,14},{10,12},{12... | collective-permute-start | bytes 26120 | tf_op jit(solution)/shard_map/ppermute | solution.py:474
  19.1 1.2 %collective-permute-start.6 = (f32[1,17,128]{2,1,0:T(8,128)S(1)}, f32[1,17,128]{2,1,0:T(8,128)S(1)}, u32[]{:S(2)}, u32[]{:S(2)}) collective-permute-start(f32[1,17,128]{2,1,0:T(8,128)S(1)} %get-tuple-element.32), channel_id=1, source_target_pairs={{0,4},{2,6},{4,0},{6,2},{1,5},{3,7},{5,1},{7,3},{8,12},{10,14},{12... | collective-permute-start | bytes 26120 | tf_op jit(solution)/shard_map/ppermute | solution.py:474
  20.3 0.7 %collective-permute-start.7 = (f32[1,17,128]{2,1,0:T(8,128)S(1)}, f32[1,17,128]{2,1,0:T(8,128)S(1)}, u32[]{:S(2)}, u32[]{:S(2)}) collective-permute-start(f32[1,17,128]{2,1,0:T(8,128)S(1)} %get-tuple-element.31), channel_id=1, source_target_pairs={{0,2},{2,0},{4,6},{6,4},{1,3},{3,1},{5,7},{7,5},{8,10},{10,8},{12,... | collective-permute-start | bytes 26120 | tf_op jit(solution)/shard_map/ppermute | solution.py:474
  21.0 1.1 %collective-permute-done.5 = f32[1,17,128]{2,1,0:T(8,128)S(1)} collective-permute-done((f32[1,17,128]{2,1,0:T(8,128)S(1)}, f32[1,17,128]{2,1,0:T(8,128)S(1)}, u32[]{:S(2)}, u32[]{:S(2)}) %collective-permute-start.5) | collective-permute-done | bytes 8736 | tf_op jit(solution)/shard_map/ppermute | solution.py:474
  22.1 0.7 %collective-permute-done.6 = f32[1,17,128]{2,1,0:T(8,128)S(1)} collective-permute-done((f32[1,17,128]{2,1,0:T(8,128)S(1)}, f32[1,17,128]{2,1,0:T(8,128)S(1)}, u32[]{:S(2)}, u32[]{:S(2)}) %collective-permute-start.6) | collective-permute-done | bytes 8736 | tf_op jit(solution)/shard_map/ppermute | solution.py:474
  22.8 1.2 %collective-permute-done.7 = f32[1,17,128]{2,1,0:T(8,128)S(1)} collective-permute-done((f32[1,17,128]{2,1,0:T(8,128)S(1)}, f32[1,17,128]{2,1,0:T(8,128)S(1)}, u32[]{:S(2)}, u32[]{:S(2)}) %collective-permute-start.7) | collective-permute-done | bytes 8736 | tf_op jit(solution)/shard_map/ppermute | solution.py:474
  24.0 0.2 collective-permute-start.9
  24.2 3.6 %collective-permute-start.10 = (f32[17,128]{1,0:T(8,128)S(1)}, f32[17,128]{1,0:T(8,128)S(1)}, u32[]{:S(2)}, u32[]{:S(2)}) collective-permute-start(f32[17,128]{1,0:T(8,128)S(1)} %fusion.4), channel_id=1, source_target_pairs={{0,24},{8,16},{16,8},{24,0},{1,25},{9,17},{17,9},{25,1},{2,26},{10... | collective-permute-start | bytes 26120 | tf_op jit(solution)/shard_map/ppermute | solution.py:474
  27.8 0.0 collective-permute-start.8
  27.8 0.6 %fusion = f32[4,8,128]{2,1,0:T(8,128)} fusion(f32[4,8,128]{2,1,0:T(8,128)S(1)} %copy-done.1, f32[4,8,128]{2,1,0:T(8,128)S(1)} %get-tuple-element.26), kind=kLoop, calls=%fused_computation.3 | loop fusion | flops 16384 | bytes 49152 | tf_op jit(solution)/shard_map/div | solution.py:625
  28.4 0.2 collective-permute-done.9
  28.6 1.1 %collective-permute-done.10 = f32[17,128]{1,0:T(8,128)S(1)} collective-permute-done((f32[17,128]{1,0:T(8,128)S(1)}, f32[17,128]{1,0:T(8,128)S(1)}, u32[]{:S(2)}, u32[]{:S(2)}) %collective-permute-start.10) | collective-permute-done | bytes 8736 | tf_op jit(solution)/shard_map/ppermute | solution.py:474
  29.7 1.8 %collective-permute-done.8 = f32[17,128]{1,0:T(8,128)S(1)} collective-permute-done((f32[17,128]{1,0:T(8,128)S(1)}, f32[17,128]{1,0:T(8,128)S(1)}, u32[]{:S(2)}, u32[]{:S(2)}) %collective-permute-start.8) | collective-permute-done | bytes 8736 | tf_op jit(solution)/shard_map/ppermute | solution.py:474
  31.5 0.6 %add_add_fusion = f32[17,128]{1,0:T(8,128)} fusion(f32[17,128]{1,0:T(8,128)S(1)} %collective-permute-done.9, f32[17,128]{1,0:T(8,128)S(1)} %collective-permute-done.10, f32[17,128]{1,0:T(8,128)S(1)} %fusion.4, f32[17,128]{1,0:T(8,128)S(1)} %collective-permute-done.8), kind=kLoop, calls=%fused_computation.15 | loop fusion | flops 6528 | bytes 43520 | tf_op jit(solution)/shard_map/add | solution.py:493
  (11 shorter events, 0.1 us)
Async XLA Ops:
  0.6 6.5 %copy-start.2 = (f32[3,4,8,128]{3,2,1,0:T(8,128)S(1)}, f32[3,4,8,128]{3,2,1,0:T(8,128)}, u32[]{:S(2)}) copy-start(f32[3,4,8,128]{3,2,1,0:T(8,128)} %pos_ref.5) | copy-start | bytes 147460
  1.4 8.9 %collective-permute-start.1 = (f32[4,8,128]{2,1,0:T(8,128)S(1)}, f32[4,8,128]{2,1,0:T(8,128)S(1)}, u32[]{:S(2)}, u32[]{:S(2)}) collective-permute-start(f32[4,8,128]{2,1,0:T(8,128)S(1)} %get-tuple-element.28), channel_id=1, source_target_pairs={{0,24},{8,16},{16,8},{24,0},{1,25},{9,17},{17,9},{25,1},{2,26},{10... | collective-permute-start | bytes 49160 | tf_op jit(solution)/shard_map/ppermute | solution.py:480
  6.5 0.7 %copy-start.6 = (s32[4,8,5]{1,0,2:T(4,128)S(1)}, s32[4,8,5]{1,0,2:T(4,128)}, u32[]{:S(2)}) copy-start(s32[4,8,5]{1,0,2:T(4,128)} %param.11) | copy-start | bytes 1924
  6.5 0.7 %copy-start = (f32[4,8,128]{2,1,0:T(8,128)S(1)}, f32[4,8,128]{2,1,0:T(8,128)}, u32[]{:S(2)}) copy-start(f32[4,8,128]{2,1,0:T(8,128)} %mass_ref.7) | copy-start | bytes 49156
  6.5 0.7 %copy-start.1 = (f32[4,8,128]{2,1,0:T(8,128)S(1)}, f32[4,8,128]{2,1,0:T(8,128)}, u32[]{:S(2)}) copy-start(f32[4,8,128]{2,1,0:T(8,128)} %smooth_ref.5) | copy-start | bytes 49156
  6.5 0.8 %copy-start.4 = (s32[4,8,128]{2,1,0:T(8,128)S(1)}, s32[4,8,128]{2,1,0:T(8,128)}, u32[]{:S(2)}) copy-start(s32[4,8,128]{2,1,0:T(8,128)} %group_ref.3) | copy-start | bytes 49156
  6.5 0.7 %copy-start.5 = (s32[1024]{0:T(1024)S(1)}, s32[1024]{0:T(1024)}, u32[]{:S(2)}) copy-start(s32[1024]{0:T(1024)} %param.13) | copy-start | bytes 12292
  6.5 3.9 %collective-permute-start = (f32[4,8,128]{2,1,0:T(8,128)S(1)}, f32[4,8,128]{2,1,0:T(8,128)S(1)}, u32[]{:S(2)}, u32[]{:S(2)}) collective-permute-start(f32[4,8,128]{2,1,0:T(8,128)S(1)} %select_bitcast_fusion.1), channel_id=1, source_target_pairs={{0,8},{8,0},{16,24},{24,16},{1,9},{9,1},{17,25},{25,17},{2,10},{10... | collective-permute-start | bytes 49160 | tf_op jit(solution)/shard_map/ppermute | solution.py:485
  7.2 2.1 %copy-start.3 = (f32[3,4,8,128]{3,2,1,0:T(8,128)S(1)}, f32[3,4,8,128]{3,2,1,0:T(8,128)}, u32[]{:S(2)}) copy-start(f32[3,4,8,128]{3,2,1,0:T(8,128)} %vel_ref.1) | copy-start | bytes 147460
  10.4 4.2 %collective-permute-start.3 = (f32[4,6,128]{2,1,0:T(8,128)S(1)}, f32[4,6,128]{2,1,0:T(8,128)S(1)}, u32[]{:S(2)}, u32[]{:S(2)}) collective-permute-start(f32[4,6,128]{2,1,0:T(8,128)S(1)} %get-tuple-element.38), channel_id=1, source_target_pairs={{0,7},{1,2},{2,1},{3,4},{4,3},{5,6},{6,5},{7,0},{8,15},{9,10},{10,... | collective-permute-start | bytes 36872 | tf_op jit(solution)/shard_map/ppermute | solution.py:480
  12.1 2.5 %collective-permute-start.2 = (f32[4,6,128]{2,1,0:T(8,128)S(1)}, f32[4,6,128]{2,1,0:T(8,128)S(1)}, u32[]{:S(2)}, u32[]{:S(2)}) collective-permute-start(f32[4,6,128]{2,1,0:T(8,128)S(1)} %get-tuple-element.39), channel_id=1, source_target_pairs={{0,1},{1,0},{2,3},{3,2},{4,5},{5,4},{6,7},{7,6},{8,9},{9,8},{10,11... | collective-permute-start | bytes 36872 | tf_op jit(solution)/shard_map/ppermute | solution.py:485
  16.1 1.3 %collective-permute-start.4 = (f32[4,17,128]{2,1,0:T(8,128)S(1)}, f32[4,17,128]{2,1,0:T(8,128)S(1)}, u32[]{:S(2)}, u32[]{:S(2)}) collective-permute-start(f32[4,17,128]{2,1,0:T(8,128)S(1)} %slice_bitcast_fusion), channel_id=1, source_target_pairs={{0,1},{1,0},{2,3},{3,2},{4,5},{5,4},{6,7},{7,6},{8,9},{9,8},{10,11... | collective-permute-start | bytes 104456 | tf_op jit(solution)/shard_map/ppermute | solution.py:474
  17.5 4.7 %collective-permute-start.5 = (f32[1,17,128]{2,1,0:T(8,128)S(1)}, f32[1,17,128]{2,1,0:T(8,128)S(1)}, u32[]{:S(2)}, u32[]{:S(2)}) collective-permute-start(f32[1,17,128]{2,1,0:T(8,128)S(1)} %get-tuple-element.33), channel_id=1, source_target_pairs={{0,6},{2,4},{4,2},{6,0},{1,7},{3,5},{5,3},{7,1},{8,14},{10,12},{12... | collective-permute-start | bytes 26120 | tf_op jit(solution)/shard_map/ppermute | solution.py:474
  19.1 3.7 %collective-permute-start.6 = (f32[1,17,128]{2,1,0:T(8,128)S(1)}, f32[1,17,128]{2,1,0:T(8,128)S(1)}, u32[]{:S(2)}, u32[]{:S(2)}) collective-permute-start(f32[1,17,128]{2,1,0:T(8,128)S(1)} %get-tuple-element.32), channel_id=1, source_target_pairs={{0,4},{2,6},{4,0},{6,2},{1,5},{3,7},{5,1},{7,3},{8,12},{10,14},{12... | collective-permute-start | bytes 26120 | tf_op jit(solution)/shard_map/ppermute | solution.py:474
  20.3 3.7 %collective-permute-start.7 = (f32[1,17,128]{2,1,0:T(8,128)S(1)}, f32[1,17,128]{2,1,0:T(8,128)S(1)}, u32[]{:S(2)}, u32[]{:S(2)}) collective-permute-start(f32[1,17,128]{2,1,0:T(8,128)S(1)} %get-tuple-element.31), channel_id=1, source_target_pairs={{0,2},{2,0},{4,6},{6,4},{1,3},{3,1},{5,7},{7,5},{8,10},{10,8},{12,... | collective-permute-start | bytes 26120 | tf_op jit(solution)/shard_map/ppermute | solution.py:474
  24.0 4.6 %collective-permute-start.9 = (f32[17,128]{1,0:T(8,128)S(1)}, f32[17,128]{1,0:T(8,128)S(1)}, u32[]{:S(2)}, u32[]{:S(2)}) collective-permute-start(f32[17,128]{1,0:T(8,128)S(1)} %fusion.4), channel_id=1, source_target_pairs={{0,16},{8,24},{16,0},{24,8},{1,17},{9,25},{17,1},{25,9},{2,18},{10... | collective-permute-start | bytes 26120 | tf_op jit(solution)/shard_map/ppermute | solution.py:474
  24.2 5.5 %collective-permute-start.10 = (f32[17,128]{1,0:T(8,128)S(1)}, f32[17,128]{1,0:T(8,128)S(1)}, u32[]{:S(2)}, u32[]{:S(2)}) collective-permute-start(f32[17,128]{1,0:T(8,128)S(1)} %fusion.4), channel_id=1, source_target_pairs={{0,24},{8,16},{16,8},{24,0},{1,25},{9,17},{17,9},{25,1},{2,26},{10... | collective-permute-start | bytes 26120 | tf_op jit(solution)/shard_map/ppermute | solution.py:474
  27.8 3.7 %collective-permute-start.8 = (f32[17,128]{1,0:T(8,128)S(1)}, f32[17,128]{1,0:T(8,128)S(1)}, u32[]{:S(2)}, u32[]{:S(2)}) collective-permute-start(f32[17,128]{1,0:T(8,128)S(1)} %fusion.4), channel_id=1, source_target_pairs={{0,8},{8,0},{16,24},{24,16},{1,9},{9,1},{17,25},{25,17},{2,10},{10... | collective-permute-start | bytes 26120 | tf_op jit(solution)/shard_map/ppermute | solution.py:474

commit v10 on v8

--- a/solution.py
+++ b/solution.py
@@ -474,18 +474,17 @@
     return lax.ppermute(value, axis, [(i, i ^ step) for i in range(count)])
 
 
-def neighbours_of(low_edge, high_edge, axis, parity):
+def neighbours_of(low_edge, high_edge, axis, odd):
     count = lax.axis_size(axis)
-    even = parity == 0
     inner = lax.ppermute(
-        jnp.where(even, high_edge, low_edge), axis, [(i, i ^ 1) for i in range(count)]
+        jnp.where(odd, low_edge, high_edge), axis, [(i, i ^ 1) for i in range(count)]
     )
     outer = lax.ppermute(
-        jnp.where(even, low_edge, high_edge),
+        jnp.where(odd, high_edge, low_edge),
         axis,
         [(i, (i + 1 if i & 1 else i - 1) % count) for i in range(count)],
     )
-    return jnp.where(even, outer, inner), jnp.where(even, inner, outer)
+    return inner, outer
 
 
 def added(parts):
@@ -529,9 +528,10 @@
     codes = sum(neighbours[:, :, k] << (4 * k) for k in range(listed))
     table_rows = group_row.reshape(-1, LANES)
     packed = jnp.concatenate([positions, masses[None]], axis=0)
-    prev, following = neighbours_of(
-        packed[:, 0], packed[:, blocks_x - 1], "dom", lax.axis_index("dom") & 1
-    )
+    odd_dom, odd_sub = (lax.axis_index("dom") & 1) == 1, lax.axis_index("core") == 1
+    inner, outer = neighbours_of(packed[:, 0], packed[:, blocks_x - 1], "dom", odd_dom)
+    even_dom = jnp.logical_not(odd_dom)
+    prev, following = jnp.where(even_dom, outer, inner), jnp.where(even_dom, inner, outer)
     sources = ((blocks_x + 2) * blocks_y, 8, LANES)
     columns, middle, own = pl.pallas_call(
         functools.partial(middle_kernel, listed),
@@ -573,7 +573,8 @@
         jnp.concatenate([prev[:, y : y + 1], columns[side], following[:, y : y + 1]], axis=1)
         for side, y in ((0, 0), (1, blocks_y - 1))
     ]
-    low, high = neighbours_of(*edges, ("chip", "core"), lax.axis_index("core"))
+    inner, outer = neighbours_of(*edges, ("chip", "core"), odd_sub)
+    low, high = jnp.where(odd_sub, inner, outer), jnp.where(odd_sub, outer, inner)
     rims = 2 * blocks_x
     edge, known, rim_match, rim_self, middle_moment = pl.pallas_call(
         functools.partial(edge_kernel, listed),

time: 31.6 us -> 31.4 us (level)
  starting transfers between devices: 15.3 us -> 14.4 us
  waiting for transfers between devices: 6.32 us -> 6.97 us
    ppermute x4, starting transfers between devices: 8.18 us -> 7.23 us  [the longest x2 3.93 us: neighbours_of(): lax.ppermute(jnp.where(odd, high_edge, low_edge), axis, [(i, (i + 1 if i...]
    ppermute x7, waiting for transfers between devices: 6.31 us -> 6.76 us  [swap(): return lax.ppermute(value, axis, [(i, i ^ step) for i in range(count)])]
  transfers between devices with their start and end apart: 11 -> 11, of which waited for: 7 -> 8; matrix products, arithmetic and copies ran while one was open for 2% -> 2% of each run, Pallas kernels for 17% -> 17%
where the time goes in v10:
time: 31.4 us; the launch traced here: 31.2 us
  starting transfers between devices  14.4 us (46%)
  waiting for transfers between devices  6.97 us (22%)
  Pallas kernels  6.9 us (22%)
  other arithmetic  2.06 us (7%)
  between operations  0.79 us (3%)
    ppermute x7, starting transfers between devices, swap(): return lax.ppermute(value, axis, [(i, i ^ step) for i in range(count)])  7.17 us
    ppermute x7, waiting for transfers between devices, swap(): return lax.ppermute(value, axis, [(i, i ^ step) for i in range(count)])  6.76 us
    ppermute x2, starting transfers between devices, neighbours_of(): lax.ppermute(jnp.where(odd, high_edge, low_edge), axis, [(i, (i + 1 if i...  3.93 us
    ppermute x2, starting transfers between devices, neighbours_of(): lax.ppermute(jnp.where(odd, low_edge, high_edge), axis, [(i, i ^ 1) for i...  3.3 us
    pallas_call x1, Pallas kernels, shards(): pl.pallas_call(functools.partial(edge_kernel, listed), out_shape=(shape((...  2.33 us
    pallas_call x1, Pallas kernels, shards(): pl.pallas_call(functools.partial(middle_kernel, listed), out_shape=(shape...  2.08 us
    pallas_call x1, Pallas kernels, shards(): pl.pallas_call(functools.partial(rim_kernel, listed), out_shape=(shape(ma...  1.47 us
    pallas_call x1, Pallas kernels, shards(): pl.pallas_call(functools.partial(moments_kernel, blocks_x * dom_count, bl...  1.03 us
  transfers between devices with their start and end apart: 11, of which 8 were waited for; matrix products, arithmetic and copies ran while one was open for 2% of the time, Pallas kernels for 17%

profile of v10, /device:TPU:0, one launch (start us, length us, event | category | flops | bytes accessed | tf_op | source)
XLA Modules:
  0.0 31.2 jit_solution(18022454633125074527)
XLA Ops:
  0.6 0.0 copy-start.2
  0.6 0.8 %select_bitcast_fusion = (f32[4,8,128]{2,1,0:T(8,128)S(1)}, f32[4,1,8,128]{3,2,0,1:T(8,128)S(1)}, f32[4,1,8,128]{3,2,0,1:T(8,128)S(1)}) fusion(pred[]{:T(512)S(6)} %eq.6, f32[1,4,8,128]{3,2,0,1:T(8,128)} %bitcast.18, f32[3,4,8,128]{3,2,1,0:T(8,128)} %pos_ref.5), kind=kLoop, calls=%fused_computation.8 | loop fusion | flops 12288 | bytes 114689 | tf_op jit(solution)/shard_map/jit(_where)/select_n | solution.py:480
  1.4 3.0 %collective-permute-start.1 = (f32[4,8,128]{2,1,0:T(8,128)S(1)}, f32[4,8,128]{2,1,0:T(8,128)S(1)}, u32[]{:S(2)}, u32[]{:S(2)}) collective-permute-start(f32[4,8,128]{2,1,0:T(8,128)S(1)} %get-tuple-element.28), channel_id=1, source_target_pairs={{0,8},{8,0},{16,24},{24,16},{1,9},{9,1},{17,25},{25,17},{2,10},{10... | collective-permute-start | bytes 49160 | tf_op jit(solution)/shard_map/ppermute | solution.py:479
  4.4 0.0 copy-start.6
  4.4 0.0 copy-start
  4.5 0.0 copy-start.1
  4.5 0.0 copy-start.4
  4.5 0.0 copy-start.5
  4.5 2.5 %collective-permute-start = (f32[4,8,128]{2,1,0:T(8,128)S(1)}, f32[4,8,128]{2,1,0:T(8,128)S(1)}, u32[]{:S(2)}, u32[]{:S(2)}) collective-permute-start(f32[4,8,128]{2,1,0:T(8,128)S(1)} %select_bitcast_fusion.1), channel_id=1, source_target_pairs={{0,24},{8,16},{16,8},{24,0},{1,25},{9,17},{17,9},{25,1},{2,26},{10... | collective-permute-start | bytes 49160 | tf_op jit(solution)/shard_map/ppermute | solution.py:482
  7.0 0.0 copy-done.6
  7.0 0.0 copy-done.2
  7.0 0.0 copy-done
  7.0 0.0 copy-done.1
  7.1 0.0 copy-done.4
  7.1 0.0 copy-done.5
  7.1 0.0 copy-start.3
  7.1 2.1 %middle_pairs.1 = (f32[2,4,4,128]{3,2,1,0:T(4,128)S(1)}, f32[2,8,128]{2,1,0:T(8,128)S(1)}, f32[48,8,128]{2,1,0:T(8,128)S(1)}) custom-call(s32[4,8]{1,0:T(4,128)S(1)} %add_bitcast_fusion.code_ref, f32[3,4,8,128]{3,2,1,0:T(8,128)S(1)} %copy-done.2, f32[4,8,128]{2,1,0:T(8,128)S(1)} %copy-done, f32[4,8,128]{2,1,0:T(8,128)S(1)} %copy-done.1, ...), custom_call_target="tpu_custom_call" | custom-call | flops 4000000000 | bytes 400000 | tf_op jit(solution)/shard_map/middle_pairs/pallas_call | solution.py:536
  9.2 0.0 copy-done.3
  9.2 1.0 %moments_by_row.1 = (f32[8,16,128]{2,1,0:T(8,128)S(1)}, s32[4,8,128]{2,1,0:T(8,128)S(1)}, bf16[4,128,1024]{2,1,0:T(8,128)(2,1)S(1)}) custom-call(f32[2,8,128]{2,1,0:T(8,128)S(1)} %get-tuple-element.15.after_ref.middle_ref, f32[3,4,8,128]{3,2,1,0:T(8,128)S(1)} %copy-done.2, f32[3,4,8,128]{3,2,1,0:T(8,128)S(1)} %copy-done.3, f32[4,8,128]{2,1,0:T(8,128)S(1)} %copy-done, ...), custom_call_target="tpu_custom_call" | custom-call | flops 2000000000 | bytes 1400000 | tf_op jit(solution)/shard_map/moments_by_row/pallas_call | solution.py:552
  10.2 0.0 collective-permute-done.1
  10.2 0.0 collective-permute-done
  10.3 1.4 %collective-permute-start.3 = (f32[4,6,128]{2,1,0:T(8,128)S(1)}, f32[4,6,128]{2,1,0:T(8,128)S(1)}, u32[]{:S(2)}, u32[]{:S(2)}) collective-permute-start(f32[4,6,128]{2,1,0:T(8,128)S(1)} %get-tuple-element.38), channel_id=1, source_target_pairs={{0,7},{1,2},{2,1},{3,4},{4,3},{5,6},{6,5},{7,0},{8,15},{9,10},{10,... | collective-permute-start | bytes 36872 | tf_op jit(solution)/shard_map/ppermute | solution.py:482
  11.7 0.3 collective-permute-start.2
  12.0 2.3 %edge_pairs.1 = (f32[2,8,128]{2,1,0:T(8,128)S(1)}, f32[48,8,128]{2,1,0:T(8,128)S(1)}, bf16[8,128,48]{2,1,0:T(8,128)(2,1)S(1)}, f32[8,128,128]{2,1,0:T(8,128)S(1)}, f32[128,16]{1,0:T(8,128)S(1)}) custom-call(s32[4,8]{1,0:T(4,128)S(1)} %add_bitcast_fusion.code_ref, f32[3,4,8,128]{3,2,1,0:T(8,128)S(1)} %copy-done.2, f32[4,8,128]{2,1,0:T(8,128)S(1)} %copy-done, ...), custom_call_target="tpu_custom_call" | custom-call | flops 4000000000 | bytes 400000 | tf_op jit(solution)/shard_map/edge_pairs/pallas_call | solution.py:579
  14.3 0.2 collective-permute-done.3
  14.5 0.0 collective-permute-done.2
  14.5 1.5 %rim_pairs_and_table.1 = (f32[4,8,128]{2,1,0:T(8,128)S(1)}, f32[2,4,17,128]{3,2,1,0:T(8,128)S(1)}) custom-call(s32[4,8]{1,0:T(4,128)S(1)} %add_bitcast_fusion.code_ref, f32[2,8,128]{2,1,0:T(8,128)S(1)} %get-tuple-element.15.after_ref.middle_ref, f32[2,8,128]{2,1,0:T(8,128)S(1)} %get-tuple-element.19.edge_ref, f32[48,8,128]{2,1,0:T(8,128)S(1)} %get-tuple-element.20.known_ref, ...), custom_call_target="tpu_custom_call" | custom-call | flops 200000000 | bytes 400000 | tf_op jit(solution)/shard_map/rim_pairs_and_table/pallas_call | solution.py:603
  16.0 0.1 collective-permute-start.4
  16.1 1.2 %collective-permute-done.4 = f32[4,17,128]{2,1,0:T(8,128)S(1)} collective-permute-done((f32[4,17,128]{2,1,0:T(8,128)S(1)}, f32[4,17,128]{2,1,0:T(8,128)S(1)}, u32[]{:S(2)}, u32[]{:S(2)}) %collective-permute-start.4) | collective-permute-done | bytes 34848 | tf_op jit(solution)/shard_map/ppermute | solution.py:474
  17.3 1.5 %collective-permute-start.5 = (f32[1,17,128]{2,1,0:T(8,128)S(1)}, f32[1,17,128]{2,1,0:T(8,128)S(1)}, u32[]{:S(2)}, u32[]{:S(2)}) collective-permute-start(f32[1,17,128]{2,1,0:T(8,128)S(1)} %get-tuple-element.33), channel_id=1, source_target_pairs={{0,6},{2,4},{4,2},{6,0},{1,7},{3,5},{5,3},{7,1},{8,14},{10,12},{12... | collective-permute-start | bytes 26120 | tf_op jit(solution)/shard_map/ppermute | solution.py:474
  18.9 1.3 %collective-permute-start.6 = (f32[1,17,128]{2,1,0:T(8,128)S(1)}, f32[1,17,128]{2,1,0:T(8,128)S(1)}, u32[]{:S(2)}, u32[]{:S(2)}) collective-permute-start(f32[1,17,128]{2,1,0:T(8,128)S(1)} %get-tuple-element.32), channel_id=1, source_target_pairs={{0,4},{2,6},{4,0},{6,2},{1,5},{3,7},{5,1},{7,3},{8,12},{10,14},{12... | collective-permute-start | bytes 26120 | tf_op jit(solution)/shard_map/ppermute | solution.py:474
  20.2 0.7 %collective-permute-start.7 = (f32[1,17,128]{2,1,0:T(8,128)S(1)}, f32[1,17,128]{2,1,0:T(8,128)S(1)}, u32[]{:S(2)}, u32[]{:S(2)}) collective-permute-start(f32[1,17,128]{2,1,0:T(8,128)S(1)} %get-tuple-element.31), channel_id=1, source_target_pairs={{0,2},{2,0},{4,6},{6,4},{1,3},{3,1},{5,7},{7,5},{8,10},{10,8},{12,... | collective-permute-start | bytes 26120 | tf_op jit(solution)/shard_map/ppermute | solution.py:474
  20.9 1.1 %collective-permute-done.5 = f32[1,17,128]{2,1,0:T(8,128)S(1)} collective-permute-done((f32[1,17,128]{2,1,0:T(8,128)S(1)}, f32[1,17,128]{2,1,0:T(8,128)S(1)}, u32[]{:S(2)}, u32[]{:S(2)}) %collective-permute-start.5) | collective-permute-done | bytes 8736 | tf_op jit(solution)/shard_map/ppermute | solution.py:474
  22.0 0.6 %collective-permute-done.6 = f32[1,17,128]{2,1,0:T(8,128)S(1)} collective-permute-done((f32[1,17,128]{2,1,0:T(8,128)S(1)}, f32[1,17,128]{2,1,0:T(8,128)S(1)}, u32[]{:S(2)}, u32[]{:S(2)}) %collective-permute-start.6) | collective-permute-done | bytes 8736 | tf_op jit(solution)/shard_map/ppermute | solution.py:474
  22.6 1.3 %collective-permute-done.7 = f32[1,17,128]{2,1,0:T(8,128)S(1)} collective-permute-done((f32[1,17,128]{2,1,0:T(8,128)S(1)}, f32[1,17,128]{2,1,0:T(8,128)S(1)}, u32[]{:S(2)}, u32[]{:S(2)}) %collective-permute-start.7) | collective-permute-done | bytes 8736 | tf_op jit(solution)/shard_map/ppermute | solution.py:474
  23.9 0.7 %collective-permute-start.9 = (f32[17,128]{1,0:T(8,128)S(1)}, f32[17,128]{1,0:T(8,128)S(1)}, u32[]{:S(2)}, u32[]{:S(2)}) collective-permute-start(f32[17,128]{1,0:T(8,128)S(1)} %fusion.4), channel_id=1, source_target_pairs={{0,16},{8,24},{16,0},{24,8},{1,17},{9,25},{17,1},{25,9},{2,18},{10... | collective-permute-start | bytes 26120 | tf_op jit(solution)/shard_map/ppermute | solution.py:474
  24.6 2.3 %collective-permute-start.10 = (f32[17,128]{1,0:T(8,128)S(1)}, f32[17,128]{1,0:T(8,128)S(1)}, u32[]{:S(2)}, u32[]{:S(2)}) collective-permute-start(f32[17,128]{1,0:T(8,128)S(1)} %fusion.4), channel_id=1, source_target_pairs={{0,24},{8,16},{16,8},{24,0},{1,25},{9,17},{17,9},{25,1},{2,26},{10... | collective-permute-start | bytes 26120 | tf_op jit(solution)/shard_map/ppermute | solution.py:474
  26.9 0.5 %collective-permute-start.8 = (f32[17,128]{1,0:T(8,128)S(1)}, f32[17,128]{1,0:T(8,128)S(1)}, u32[]{:S(2)}, u32[]{:S(2)}) collective-permute-start(f32[17,128]{1,0:T(8,128)S(1)} %fusion.4), channel_id=1, source_target_pairs={{0,8},{8,0},{16,24},{24,16},{1,9},{9,1},{17,25},{25,17},{2,10},{10... | collective-permute-start | bytes 26120 | tf_op jit(solution)/shard_map/ppermute | solution.py:474
  27.3 0.6 %fusion = f32[4,8,128]{2,1,0:T(8,128)} fusion(f32[4,8,128]{2,1,0:T(8,128)S(1)} %copy-done.1, f32[4,8,128]{2,1,0:T(8,128)S(1)} %get-tuple-element.26), kind=kLoop, calls=%fused_computation.3 | loop fusion | flops 16384 | bytes 49152 | tf_op jit(solution)/shard_map/div | solution.py:626
  28.0 0.5 %collective-permute-done.9 = f32[17,128]{1,0:T(8,128)S(1)} collective-permute-done((f32[17,128]{1,0:T(8,128)S(1)}, f32[17,128]{1,0:T(8,128)S(1)}, u32[]{:S(2)}, u32[]{:S(2)}) %collective-permute-start.9) | collective-permute-done | bytes 8736 | tf_op jit(solution)/shard_map/ppermute | solution.py:474
  28.5 1.6 %collective-permute-done.10 = f32[17,128]{1,0:T(8,128)S(1)} collective-permute-done((f32[17,128]{1,0:T(8,128)S(1)}, f32[17,128]{1,0:T(8,128)S(1)}, u32[]{:S(2)}, u32[]{:S(2)}) %collective-permute-start.10) | collective-permute-done | bytes 8736 | tf_op jit(solution)/shard_map/ppermute | solution.py:474
  30.1 0.5 %collective-permute-done.8 = f32[17,128]{1,0:T(8,128)S(1)} collective-permute-done((f32[17,128]{1,0:T(8,128)S(1)}, f32[17,128]{1,0:T(8,128)S(1)}, u32[]{:S(2)}, u32[]{:S(2)}) %collective-permute-start.8) | collective-permute-done | bytes 8736 | tf_op jit(solution)/shard_map/ppermute | solution.py:474
  30.6 0.6 %add_add_fusion = f32[17,128]{1,0:T(8,128)} fusion(f32[17,128]{1,0:T(8,128)S(1)} %collective-permute-done.9, f32[17,128]{1,0:T(8,128)S(1)} %collective-permute-done.10, f32[17,128]{1,0:T(8,128)S(1)} %fusion.4, f32[17,128]{1,0:T(8,128)S(1)} %collective-permute-done.8), kind=kLoop, calls=%fused_computation.15 | loop fusion | flops 6528 | bytes 43520 | tf_op jit(solution)/shard_map/add | solution.py:492
  (11 shorter events, 0.1 us)
Async XLA Ops:
  0.6 6.4 %copy-start.2 = (f32[3,4,8,128]{3,2,1,0:T(8,128)S(1)}, f32[3,4,8,128]{3,2,1,0:T(8,128)}, u32[]{:S(2)}) copy-start(f32[3,4,8,128]{3,2,1,0:T(8,128)} %pos_ref.5) | copy-start | bytes 147460
  1.4 8.8 %collective-permute-start.1 = (f32[4,8,128]{2,1,0:T(8,128)S(1)}, f32[4,8,128]{2,1,0:T(8,128)S(1)}, u32[]{:S(2)}, u32[]{:S(2)}) collective-permute-start(f32[4,8,128]{2,1,0:T(8,128)S(1)} %get-tuple-element.28), channel_id=1, source_target_pairs={{0,8},{8,0},{16,24},{24,16},{1,9},{9,1},{17,25},{25,17},{2,10},{10... | collective-permute-start | bytes 49160 | tf_op jit(solution)/shard_map/ppermute | solution.py:479
  4.4 2.6 %copy-start.6 = (s32[4,8,5]{1,0,2:T(4,128)S(1)}, s32[4,8,5]{1,0,2:T(4,128)}, u32[]{:S(2)}) copy-start(s32[4,8,5]{1,0,2:T(4,128)} %param.11) | copy-start | bytes 1924
  4.4 2.6 %copy-start = (f32[4,8,128]{2,1,0:T(8,128)S(1)}, f32[4,8,128]{2,1,0:T(8,128)}, u32[]{:S(2)}) copy-start(f32[4,8,128]{2,1,0:T(8,128)} %mass_ref.7) | copy-start | bytes 49156
  4.5 2.6 %copy-start.1 = (f32[4,8,128]{2,1,0:T(8,128)S(1)}, f32[4,8,128]{2,1,0:T(8,128)}, u32[]{:S(2)}) copy-start(f32[4,8,128]{2,1,0:T(8,128)} %smooth_ref.5) | copy-start | bytes 49156
  4.5 2.6 %copy-start.4 = (s32[4,8,128]{2,1,0:T(8,128)S(1)}, s32[4,8,128]{2,1,0:T(8,128)}, u32[]{:S(2)}) copy-start(s32[4,8,128]{2,1,0:T(8,128)} %group_ref.3) | copy-start | bytes 49156
  4.5 2.6 %copy-start.5 = (s32[1024]{0:T(1024)S(1)}, s32[1024]{0:T(1024)}, u32[]{:S(2)}) copy-start(s32[1024]{0:T(1024)} %param.13) | copy-start | bytes 12292
  4.5 5.7 %collective-permute-start = (f32[4,8,128]{2,1,0:T(8,128)S(1)}, f32[4,8,128]{2,1,0:T(8,128)S(1)}, u32[]{:S(2)}, u32[]{:S(2)}) collective-permute-start(f32[4,8,128]{2,1,0:T(8,128)S(1)} %select_bitcast_fusion.1), channel_id=1, source_target_pairs={{0,24},{8,16},{16,8},{24,0},{1,25},{9,17},{17,9},{25,1},{2,26},{10... | collective-permute-start | bytes 49160 | tf_op jit(solution)/shard_map/ppermute | solution.py:482
  7.1 2.1 %copy-start.3 = (f32[3,4,8,128]{3,2,1,0:T(8,128)S(1)}, f32[3,4,8,128]{3,2,1,0:T(8,128)}, u32[]{:S(2)}) copy-start(f32[3,4,8,128]{3,2,1,0:T(8,128)} %vel_ref.1) | copy-start | bytes 147460
  10.3 4.2 %collective-permute-start.3 = (f32[4,6,128]{2,1,0:T(8,128)S(1)}, f32[4,6,128]{2,1,0:T(8,128)S(1)}, u32[]{:S(2)}, u32[]{:S(2)}) collective-permute-start(f32[4,6,128]{2,1,0:T(8,128)S(1)} %get-tuple-element.38), channel_id=1, source_target_pairs={{0,7},{1,2},{2,1},{3,4},{4,3},{5,6},{6,5},{7,0},{8,15},{9,10},{10,... | collective-permute-start | bytes 36872 | tf_op jit(solution)/shard_map/ppermute | solution.py:482
  11.7 2.8 %collective-permute-start.2 = (f32[4,6,128]{2,1,0:T(8,128)S(1)}, f32[4,6,128]{2,1,0:T(8,128)S(1)}, u32[]{:S(2)}, u32[]{:S(2)}) collective-permute-start(f32[4,6,128]{2,1,0:T(8,128)S(1)} %get-tuple-element.39), channel_id=1, source_target_pairs={{0,1},{1,0},{2,3},{3,2},{4,5},{5,4},{6,7},{7,6},{8,9},{9,8},{10,11... | collective-permute-start | bytes 36872 | tf_op jit(solution)/shard_map/ppermute | solution.py:479
  16.0 1.3 %collective-permute-start.4 = (f32[4,17,128]{2,1,0:T(8,128)S(1)}, f32[4,17,128]{2,1,0:T(8,128)S(1)}, u32[]{:S(2)}, u32[]{:S(2)}) collective-permute-start(f32[4,17,128]{2,1,0:T(8,128)S(1)} %slice_bitcast_fusion), channel_id=1, source_target_pairs={{0,1},{1,0},{2,3},{3,2},{4,5},{5,4},{6,7},{7,6},{8,9},{9,8},{10,11... | collective-permute-start | bytes 104456 | tf_op jit(solution)/shard_map/ppermute | solution.py:474
  17.3 4.7 %collective-permute-start.5 = (f32[1,17,128]{2,1,0:T(8,128)S(1)}, f32[1,17,128]{2,1,0:T(8,128)S(1)}, u32[]{:S(2)}, u32[]{:S(2)}) collective-permute-start(f32[1,17,128]{2,1,0:T(8,128)S(1)} %get-tuple-element.33), channel_id=1, source_target_pairs={{0,6},{2,4},{4,2},{6,0},{1,7},{3,5},{5,3},{7,1},{8,14},{10,12},{12... | collective-permute-start | bytes 26120 | tf_op jit(solution)/shard_map/ppermute | solution.py:474
  18.9 3.7 %collective-permute-start.6 = (f32[1,17,128]{2,1,0:T(8,128)S(1)}, f32[1,17,128]{2,1,0:T(8,128)S(1)}, u32[]{:S(2)}, u32[]{:S(2)}) collective-permute-start(f32[1,17,128]{2,1,0:T(8,128)S(1)} %get-tuple-element.32), channel_id=1, source_target_pairs={{0,4},{2,6},{4,0},{6,2},{1,5},{3,7},{5,1},{7,3},{8,12},{10,14},{12... | collective-permute-start | bytes 26120 | tf_op jit(solution)/shard_map/ppermute | solution.py:474
  20.2 3.7 %collective-permute-start.7 = (f32[1,17,128]{2,1,0:T(8,128)S(1)}, f32[1,17,128]{2,1,0:T(8,128)S(1)}, u32[]{:S(2)}, u32[]{:S(2)}) collective-permute-start(f32[1,17,128]{2,1,0:T(8,128)S(1)} %get-tuple-element.31), channel_id=1, source_target_pairs={{0,2},{2,0},{4,6},{6,4},{1,3},{3,1},{5,7},{7,5},{8,10},{10,8},{12,... | collective-permute-start | bytes 26120 | tf_op jit(solution)/shard_map/ppermute | solution.py:474
  23.9 4.6 %collective-permute-start.9 = (f32[17,128]{1,0:T(8,128)S(1)}, f32[17,128]{1,0:T(8,128)S(1)}, u32[]{:S(2)}, u32[]{:S(2)}) collective-permute-start(f32[17,128]{1,0:T(8,128)S(1)} %fusion.4), channel_id=1, source_target_pairs={{0,16},{8,24},{16,0},{24,8},{1,17},{9,25},{17,1},{25,9},{2,18},{10... | collective-permute-start | bytes 26120 | tf_op jit(solution)/shard_map/ppermute | solution.py:474
  24.6 5.5 %collective-permute-start.10 = (f32[17,128]{1,0:T(8,128)S(1)}, f32[17,128]{1,0:T(8,128)S(1)}, u32[]{:S(2)}, u32[]{:S(2)}) collective-permute-start(f32[17,128]{1,0:T(8,128)S(1)} %fusion.4), channel_id=1, source_target_pairs={{0,24},{8,16},{16,8},{24,0},{1,25},{9,17},{17,9},{25,1},{2,26},{10... | collective-permute-start | bytes 26120 | tf_op jit(solution)/shard_map/ppermute | solution.py:474
  26.9 3.7 %collective-permute-start.8 = (f32[17,128]{1,0:T(8,128)S(1)}, f32[17,128]{1,0:T(8,128)S(1)}, u32[]{:S(2)}, u32[]{:S(2)}) collective-permute-start(f32[17,128]{1,0:T(8,128)S(1)} %fusion.4), channel_id=1, source_target_pairs={{0,8},{8,0},{16,24},{24,16},{1,9},{9,1},{17,25},{25,17},{2,10},{10... | collective-permute-start | bytes 26120 | tf_op jit(solution)/shard_map/ppermute | solution.py:474

commit v11 on v10

--- a/solution.py
+++ b/solution.py
@@ -97,11 +97,11 @@
         hot_ref[x, :, lanes] = slot_one_hot(rows & (LANES - 1), y)
 
     def add_product(x):
-        product = lax.dot_general(lhs_ref[x], hot_ref[x], NT, preferred_element_type=F32)
+        product = lax.dot_general(hot_ref[x], lhs_ref[x], NT, preferred_element_type=F32)
         total_ref[...] = product if x == 0 else total_ref[...] + product
 
     def finish():
-        total = total_ref[...].reshape(owners, 2 * EARLY, LANES)
+        total = total_ref[...].T.reshape(owners, 2 * EARLY, LANES)
         table_ref[...] = total[:, :EARLY, :] + total[:, EARLY:, :]
 
     for x in range(blocks_x):
@@ -561,7 +561,7 @@
         scratch_shapes=[
             pltpu.VMEM((blocks_x * EARLY * blocks_y, LANES), F32),
             pltpu.VMEM((blocks_x, owners * 2 * EARLY, chunk), BF16),
-            pltpu.VMEM((owners * 2 * EARLY, LANES), F32),
+            pltpu.VMEM((LANES, owners * 2 * EARLY), F32),
         ],
         compiler_params=params(),
         cost_estimate=pl.CostEstimate(

time: 31.4 us -> 31.4 us (level)
  transfers between devices with their start and end apart: 11 -> 11, of which waited for: 8 -> 8; matrix products, arithmetic and copies ran while one was open for 2% -> 2% of each run, Pallas kernels for 17% -> 18%
where the time goes in v11:
time: 31.4 us; the launch traced here: 31.2 us
  starting transfers between devices  14.4 us (46%)
  waiting for transfers between devices  7 us (22%)
  Pallas kernels  6.95 us (22%)
  other arithmetic  2.06 us (7%)
  between operations  0.79 us (3%)
    ppermute x7, starting transfers between devices, swap(): return lax.ppermute(value, axis, [(i, i ^ step) for i in range(count)])  7.15 us
    ppermute x7, waiting for transfers between devices, swap(): return lax.ppermute(value, axis, [(i, i ^ step) for i in range(count)])  6.77 us
    ppermute x2, starting transfers between devices, neighbours_of(): lax.ppermute(jnp.where(odd, high_edge, low_edge), axis, [(i, (i + 1 if i...  3.92 us
    ppermute x2, starting transfers between devices, neighbours_of(): lax.ppermute(jnp.where(odd, low_edge, high_edge), axis, [(i, i ^ 1) for i...  3.31 us
    pallas_call x1, Pallas kernels, shards(): pl.pallas_call(functools.partial(edge_kernel, listed), out_shape=(shape((...  2.32 us
    pallas_call x1, Pallas kernels, shards(): pl.pallas_call(functools.partial(middle_kernel, listed), out_shape=(shape...  2.08 us
    pallas_call x1, Pallas kernels, shards(): pl.pallas_call(functools.partial(rim_kernel, listed), out_shape=(shape(ma...  1.47 us
    pallas_call x1, Pallas kernels, shards(): pl.pallas_call(functools.partial(moments_kernel, blocks_x * dom_count, bl...  1.07 us
  transfers between devices with their start and end apart: 11, of which 8 were waited for; matrix products, arithmetic and copies ran while one was open for 2% of the time, Pallas kernels for 18%

profile of v11, /device:TPU:0, one launch (start us, length us, event | category | flops | bytes accessed | tf_op | source)
XLA Modules:
  0.0 31.2 jit_solution(3588660052296489052)
XLA Ops:
  0.6 0.0 copy-start.2
  0.6 0.8 %select_bitcast_fusion = (f32[4,8,128]{2,1,0:T(8,128)S(1)}, f32[4,1,8,128]{3,2,0,1:T(8,128)S(1)}, f32[4,1,8,128]{3,2,0,1:T(8,128)S(1)}) fusion(pred[]{:T(512)S(6)} %eq.6, f32[1,4,8,128]{3,2,0,1:T(8,128)} %bitcast.18, f32[3,4,8,128]{3,2,1,0:T(8,128)} %pos_ref.5), kind=kLoop, calls=%fused_computation.8 | loop fusion | flops 12288 | bytes 114689 | tf_op jit(solution)/shard_map/jit(_where)/select_n | solution.py:480
  1.4 3.0 %collective-permute-start.1 = (f32[4,8,128]{2,1,0:T(8,128)S(1)}, f32[4,8,128]{2,1,0:T(8,128)S(1)}, u32[]{:S(2)}, u32[]{:S(2)}) collective-permute-start(f32[4,8,128]{2,1,0:T(8,128)S(1)} %get-tuple-element.28), channel_id=1, source_target_pairs={{0,8},{8,0},{16,24},{24,16},{1,9},{9,1},{17,25},{25,17},{2,10},{10... | collective-permute-start | bytes 49160 | tf_op jit(solution)/shard_map/ppermute | solution.py:479
  4.4 0.0 copy-start.6
  4.4 0.0 copy-start
  4.5 0.0 copy-start.1
  4.5 0.0 copy-start.4
  4.5 0.0 copy-start.5
  4.5 2.5 %collective-permute-start = (f32[4,8,128]{2,1,0:T(8,128)S(1)}, f32[4,8,128]{2,1,0:T(8,128)S(1)}, u32[]{:S(2)}, u32[]{:S(2)}) collective-permute-start(f32[4,8,128]{2,1,0:T(8,128)S(1)} %select_bitcast_fusion.1), channel_id=1, source_target_pairs={{0,24},{8,16},{16,8},{24,0},{1,25},{9,17},{17,9},{25,1},{2,26},{10... | collective-permute-start | bytes 49160 | tf_op jit(solution)/shard_map/ppermute | solution.py:482
  7.0 0.0 copy-done.6
  7.0 0.0 copy-done.2
  7.0 0.0 copy-done
  7.0 0.0 copy-done.1
  7.1 0.0 copy-done.4
  7.1 0.0 copy-done.5
  7.1 0.0 copy-start.3
  7.1 2.1 %middle_pairs.1 = (f32[2,4,4,128]{3,2,1,0:T(4,128)S(1)}, f32[2,8,128]{2,1,0:T(8,128)S(1)}, f32[48,8,128]{2,1,0:T(8,128)S(1)}) custom-call(s32[4,8]{1,0:T(4,128)S(1)} %add_bitcast_fusion.code_ref, f32[3,4,8,128]{3,2,1,0:T(8,128)S(1)} %copy-done.2, f32[4,8,128]{2,1,0:T(8,128)S(1)} %copy-done, f32[4,8,128]{2,1,0:T(8,128)S(1)} %copy-done.1, ...), custom_call_target="tpu_custom_call" | custom-call | flops 4000000000 | bytes 400000 | tf_op jit(solution)/shard_map/middle_pairs/pallas_call | solution.py:536
  9.2 0.0 copy-done.3
  9.2 1.1 %moments_by_row.1 = (f32[8,16,128]{2,1,0:T(8,128)S(1)}, s32[4,8,128]{2,1,0:T(8,128)S(1)}, bf16[4,128,1024]{2,1,0:T(8,128)(2,1)S(1)}) custom-call(f32[2,8,128]{2,1,0:T(8,128)S(1)} %get-tuple-element.15.after_ref.middle_ref, f32[3,4,8,128]{3,2,1,0:T(8,128)S(1)} %copy-done.2, f32[3,4,8,128]{3,2,1,0:T(8,128)S(1)} %copy-done.3, f32[4,8,128]{2,1,0:T(8,128)S(1)} %copy-done, ...), custom_call_target="tpu_custom_call" | custom-call | flops 2000000000 | bytes 1400000 | tf_op jit(solution)/shard_map/moments_by_row/pallas_call | solution.py:552
  10.3 0.0 collective-permute-done.1
  10.3 0.0 collective-permute-done
  10.3 1.4 %collective-permute-start.3 = (f32[4,6,128]{2,1,0:T(8,128)S(1)}, f32[4,6,128]{2,1,0:T(8,128)S(1)}, u32[]{:S(2)}, u32[]{:S(2)}) collective-permute-start(f32[4,6,128]{2,1,0:T(8,128)S(1)} %get-tuple-element.38), channel_id=1, source_target_pairs={{0,7},{1,2},{2,1},{3,4},{4,3},{5,6},{6,5},{7,0},{8,15},{9,10},{10,... | collective-permute-start | bytes 36872 | tf_op jit(solution)/shard_map/ppermute | solution.py:482
  11.7 0.3 collective-permute-start.2
  12.0 2.3 %edge_pairs.1 = (f32[2,8,128]{2,1,0:T(8,128)S(1)}, f32[48,8,128]{2,1,0:T(8,128)S(1)}, bf16[8,128,48]{2,1,0:T(8,128)(2,1)S(1)}, f32[8,128,128]{2,1,0:T(8,128)S(1)}, f32[128,16]{1,0:T(8,128)S(1)}) custom-call(s32[4,8]{1,0:T(4,128)S(1)} %add_bitcast_fusion.code_ref, f32[3,4,8,128]{3,2,1,0:T(8,128)S(1)} %copy-done.2, f32[4,8,128]{2,1,0:T(8,128)S(1)} %copy-done, ...), custom_call_target="tpu_custom_call" | custom-call | flops 4000000000 | bytes 400000 | tf_op jit(solution)/shard_map/edge_pairs/pallas_call | solution.py:579
  14.3 0.2 collective-permute-done.3
  14.5 0.0 collective-permute-done.2
  14.6 1.5 %rim_pairs_and_table.1 = (f32[4,8,128]{2,1,0:T(8,128)S(1)}, f32[2,4,17,128]{3,2,1,0:T(8,128)S(1)}) custom-call(s32[4,8]{1,0:T(4,128)S(1)} %add_bitcast_fusion.code_ref, f32[2,8,128]{2,1,0:T(8,128)S(1)} %get-tuple-element.15.after_ref.middle_ref, f32[2,8,128]{2,1,0:T(8,128)S(1)} %get-tuple-element.19.edge_ref, f32[48,8,128]{2,1,0:T(8,128)S(1)} %get-tuple-element.20.known_ref, ...), custom_call_target="tpu_custom_call" | custom-call | flops 200000000 | bytes 400000 | tf_op jit(solution)/shard_map/rim_pairs_and_table/pallas_call | solution.py:603
  16.0 0.1 collective-permute-start.4
  16.2 1.2 %collective-permute-done.4 = f32[4,17,128]{2,1,0:T(8,128)S(1)} collective-permute-done((f32[4,17,128]{2,1,0:T(8,128)S(1)}, f32[4,17,128]{2,1,0:T(8,128)S(1)}, u32[]{:S(2)}, u32[]{:S(2)}) %collective-permute-start.4) | collective-permute-done | bytes 34848 | tf_op jit(solution)/shard_map/ppermute | solution.py:474
  17.4 1.5 %collective-permute-start.5 = (f32[1,17,128]{2,1,0:T(8,128)S(1)}, f32[1,17,128]{2,1,0:T(8,128)S(1)}, u32[]{:S(2)}, u32[]{:S(2)}) collective-permute-start(f32[1,17,128]{2,1,0:T(8,128)S(1)} %get-tuple-element.33), channel_id=1, source_target_pairs={{0,6},{2,4},{4,2},{6,0},{1,7},{3,5},{5,3},{7,1},{8,14},{10,12},{12... | collective-permute-start | bytes 26120 | tf_op jit(solution)/shard_map/ppermute | solution.py:474
  18.9 1.3 %collective-permute-start.6 = (f32[1,17,128]{2,1,0:T(8,128)S(1)}, f32[1,17,128]{2,1,0:T(8,128)S(1)}, u32[]{:S(2)}, u32[]{:S(2)}) collective-permute-start(f32[1,17,128]{2,1,0:T(8,128)S(1)} %get-tuple-element.32), channel_id=1, source_target_pairs={{0,4},{2,6},{4,0},{6,2},{1,5},{3,7},{5,1},{7,3},{8,12},{10,14},{12... | collective-permute-start | bytes 26120 | tf_op jit(solution)/shard_map/ppermute | solution.py:474
  20.2 0.7 %collective-permute-start.7 = (f32[1,17,128]{2,1,0:T(8,128)S(1)}, f32[1,17,128]{2,1,0:T(8,128)S(1)}, u32[]{:S(2)}, u32[]{:S(2)}) collective-permute-start(f32[1,17,128]{2,1,0:T(8,128)S(1)} %get-tuple-element.31), channel_id=1, source_target_pairs={{0,2},{2,0},{4,6},{6,4},{1,3},{3,1},{5,7},{7,5},{8,10},{10,8},{12,... | collective-permute-start | bytes 26120 | tf_op jit(solution)/shard_map/ppermute | solution.py:474
  20.9 1.1 %collective-permute-done.5 = f32[1,17,128]{2,1,0:T(8,128)S(1)} collective-permute-done((f32[1,17,128]{2,1,0:T(8,128)S(1)}, f32[1,17,128]{2,1,0:T(8,128)S(1)}, u32[]{:S(2)}, u32[]{:S(2)}) %collective-permute-start.5) | collective-permute-done | bytes 8736 | tf_op jit(solution)/shard_map/ppermute | solution.py:474
  22.0 0.6 %collective-permute-done.6 = f32[1,17,128]{2,1,0:T(8,128)S(1)} collective-permute-done((f32[1,17,128]{2,1,0:T(8,128)S(1)}, f32[1,17,128]{2,1,0:T(8,128)S(1)}, u32[]{:S(2)}, u32[]{:S(2)}) %collective-permute-start.6) | collective-permute-done | bytes 8736 | tf_op jit(solution)/shard_map/ppermute | solution.py:474
  22.6 1.3 %collective-permute-done.7 = f32[1,17,128]{2,1,0:T(8,128)S(1)} collective-permute-done((f32[1,17,128]{2,1,0:T(8,128)S(1)}, f32[1,17,128]{2,1,0:T(8,128)S(1)}, u32[]{:S(2)}, u32[]{:S(2)}) %collective-permute-start.7) | collective-permute-done | bytes 8736 | tf_op jit(solution)/shard_map/ppermute | solution.py:474
  23.9 0.7 %collective-permute-start.9 = (f32[17,128]{1,0:T(8,128)S(1)}, f32[17,128]{1,0:T(8,128)S(1)}, u32[]{:S(2)}, u32[]{:S(2)}) collective-permute-start(f32[17,128]{1,0:T(8,128)S(1)} %fusion.4), channel_id=1, source_target_pairs={{0,16},{8,24},{16,0},{24,8},{1,17},{9,25},{17,1},{25,9},{2,18},{10... | collective-permute-start | bytes 26120 | tf_op jit(solution)/shard_map/ppermute | solution.py:474
  24.6 2.3 %collective-permute-start.10 = (f32[17,128]{1,0:T(8,128)S(1)}, f32[17,128]{1,0:T(8,128)S(1)}, u32[]{:S(2)}, u32[]{:S(2)}) collective-permute-start(f32[17,128]{1,0:T(8,128)S(1)} %fusion.4), channel_id=1, source_target_pairs={{0,24},{8,16},{16,8},{24,0},{1,25},{9,17},{17,9},{25,1},{2,26},{10... | collective-permute-start | bytes 26120 | tf_op jit(solution)/shard_map/ppermute | solution.py:474
  26.9 0.5 %collective-permute-start.8 = (f32[17,128]{1,0:T(8,128)S(1)}, f32[17,128]{1,0:T(8,128)S(1)}, u32[]{:S(2)}, u32[]{:S(2)}) collective-permute-start(f32[17,128]{1,0:T(8,128)S(1)} %fusion.4), channel_id=1, source_target_pairs={{0,8},{8,0},{16,24},{24,16},{1,9},{9,1},{17,25},{25,17},{2,10},{10... | collective-permute-start | bytes 26120 | tf_op jit(solution)/shard_map/ppermute | solution.py:474
  27.4 0.6 %fusion = f32[4,8,128]{2,1,0:T(8,128)} fusion(f32[4,8,128]{2,1,0:T(8,128)S(1)} %copy-done.1, f32[4,8,128]{2,1,0:T(8,128)S(1)} %get-tuple-element.26), kind=kLoop, calls=%fused_computation.3 | loop fusion | flops 16384 | bytes 49152 | tf_op jit(solution)/shard_map/div | solution.py:626
  28.0 0.5 %collective-permute-done.9 = f32[17,128]{1,0:T(8,128)S(1)} collective-permute-done((f32[17,128]{1,0:T(8,128)S(1)}, f32[17,128]{1,0:T(8,128)S(1)}, u32[]{:S(2)}, u32[]{:S(2)}) %collective-permute-start.9) | collective-permute-done | bytes 8736 | tf_op jit(solution)/shard_map/ppermute | solution.py:474
  28.5 1.6 %collective-permute-done.10 = f32[17,128]{1,0:T(8,128)S(1)} collective-permute-done((f32[17,128]{1,0:T(8,128)S(1)}, f32[17,128]{1,0:T(8,128)S(1)}, u32[]{:S(2)}, u32[]{:S(2)}) %collective-permute-start.10) | collective-permute-done | bytes 8736 | tf_op jit(solution)/shard_map/ppermute | solution.py:474
  30.1 0.5 %collective-permute-done.8 = f32[17,128]{1,0:T(8,128)S(1)} collective-permute-done((f32[17,128]{1,0:T(8,128)S(1)}, f32[17,128]{1,0:T(8,128)S(1)}, u32[]{:S(2)}, u32[]{:S(2)}) %collective-permute-start.8) | collective-permute-done | bytes 8736 | tf_op jit(solution)/shard_map/ppermute | solution.py:474
  30.6 0.6 %add_add_fusion = f32[17,128]{1,0:T(8,128)} fusion(f32[17,128]{1,0:T(8,128)S(1)} %collective-permute-done.9, f32[17,128]{1,0:T(8,128)S(1)} %collective-permute-done.10, f32[17,128]{1,0:T(8,128)S(1)} %fusion.4, f32[17,128]{1,0:T(8,128)S(1)} %collective-permute-done.8), kind=kLoop, calls=%fused_computation.15 | loop fusion | flops 6528 | bytes 43520 | tf_op jit(solution)/shard_map/add | solution.py:492
  (11 shorter events, 0.1 us)
Async XLA Ops:
  0.6 6.4 %copy-start.2 = (f32[3,4,8,128]{3,2,1,0:T(8,128)S(1)}, f32[3,4,8,128]{3,2,1,0:T(8,128)}, u32[]{:S(2)}) copy-start(f32[3,4,8,128]{3,2,1,0:T(8,128)} %pos_ref.5) | copy-start | bytes 147460
  1.4 8.8 %collective-permute-start.1 = (f32[4,8,128]{2,1,0:T(8,128)S(1)}, f32[4,8,128]{2,1,0:T(8,128)S(1)}, u32[]{:S(2)}, u32[]{:S(2)}) collective-permute-start(f32[4,8,128]{2,1,0:T(8,128)S(1)} %get-tuple-element.28), channel_id=1, source_target_pairs={{0,8},{8,0},{16,24},{24,16},{1,9},{9,1},{17,25},{25,17},{2,10},{10... | collective-permute-start | bytes 49160 | tf_op jit(solution)/shard_map/ppermute | solution.py:479
  4.4 2.6 %copy-start.6 = (s32[4,8,5]{1,0,2:T(4,128)S(1)}, s32[4,8,5]{1,0,2:T(4,128)}, u32[]{:S(2)}) copy-start(s32[4,8,5]{1,0,2:T(4,128)} %param.11) | copy-start | bytes 1924
  4.4 2.6 %copy-start = (f32[4,8,128]{2,1,0:T(8,128)S(1)}, f32[4,8,128]{2,1,0:T(8,128)}, u32[]{:S(2)}) copy-start(f32[4,8,128]{2,1,0:T(8,128)} %mass_ref.7) | copy-start | bytes 49156
  4.5 2.6 %copy-start.1 = (f32[4,8,128]{2,1,0:T(8,128)S(1)}, f32[4,8,128]{2,1,0:T(8,128)}, u32[]{:S(2)}) copy-start(f32[4,8,128]{2,1,0:T(8,128)} %smooth_ref.5) | copy-start | bytes 49156
  4.5 2.6 %copy-start.4 = (s32[4,8,128]{2,1,0:T(8,128)S(1)}, s32[4,8,128]{2,1,0:T(8,128)}, u32[]{:S(2)}) copy-start(s32[4,8,128]{2,1,0:T(8,128)} %group_ref.3) | copy-start | bytes 49156
  4.5 2.6 %copy-start.5 = (s32[1024]{0:T(1024)S(1)}, s32[1024]{0:T(1024)}, u32[]{:S(2)}) copy-start(s32[1024]{0:T(1024)} %param.13) | copy-start | bytes 12292
  4.5 5.8 %collective-permute-start = (f32[4,8,128]{2,1,0:T(8,128)S(1)}, f32[4,8,128]{2,1,0:T(8,128)S(1)}, u32[]{:S(2)}, u32[]{:S(2)}) collective-permute-start(f32[4,8,128]{2,1,0:T(8,128)S(1)} %select_bitcast_fusion.1), channel_id=1, source_target_pairs={{0,24},{8,16},{16,8},{24,0},{1,25},{9,17},{17,9},{25,1},{2,26},{10... | collective-permute-start | bytes 49160 | tf_op jit(solution)/shard_map/ppermute | solution.py:482
  7.1 2.1 %copy-start.3 = (f32[3,4,8,128]{3,2,1,0:T(8,128)S(1)}, f32[3,4,8,128]{3,2,1,0:T(8,128)}, u32[]{:S(2)}) copy-start(f32[3,4,8,128]{3,2,1,0:T(8,128)} %vel_ref.1) | copy-start | bytes 147460
  10.3 4.2 %collective-permute-start.3 = (f32[4,6,128]{2,1,0:T(8,128)S(1)}, f32[4,6,128]{2,1,0:T(8,128)S(1)}, u32[]{:S(2)}, u32[]{:S(2)}) collective-permute-start(f32[4,6,128]{2,1,0:T(8,128)S(1)} %get-tuple-element.38), channel_id=1, source_target_pairs={{0,7},{1,2},{2,1},{3,4},{4,3},{5,6},{6,5},{7,0},{8,15},{9,10},{10,... | collective-permute-start | bytes 36872 | tf_op jit(solution)/shard_map/ppermute | solution.py:482
  11.7 2.8 %collective-permute-start.2 = (f32[4,6,128]{2,1,0:T(8,128)S(1)}, f32[4,6,128]{2,1,0:T(8,128)S(1)}, u32[]{:S(2)}, u32[]{:S(2)}) collective-permute-start(f32[4,6,128]{2,1,0:T(8,128)S(1)} %get-tuple-element.39), channel_id=1, source_target_pairs={{0,1},{1,0},{2,3},{3,2},{4,5},{5,4},{6,7},{7,6},{8,9},{9,8},{10,11... | collective-permute-start | bytes 36872 | tf_op jit(solution)/shard_map/ppermute | solution.py:479
  16.0 1.3 %collective-permute-start.4 = (f32[4,17,128]{2,1,0:T(8,128)S(1)}, f32[4,17,128]{2,1,0:T(8,128)S(1)}, u32[]{:S(2)}, u32[]{:S(2)}) collective-permute-start(f32[4,17,128]{2,1,0:T(8,128)S(1)} %slice_bitcast_fusion), channel_id=1, source_target_pairs={{0,1},{1,0},{2,3},{3,2},{4,5},{5,4},{6,7},{7,6},{8,9},{9,8},{10,11... | collective-permute-start | bytes 104456 | tf_op jit(solution)/shard_map/ppermute | solution.py:474
  17.4 4.7 %collective-permute-start.5 = (f32[1,17,128]{2,1,0:T(8,128)S(1)}, f32[1,17,128]{2,1,0:T(8,128)S(1)}, u32[]{:S(2)}, u32[]{:S(2)}) collective-permute-start(f32[1,17,128]{2,1,0:T(8,128)S(1)} %get-tuple-element.33), channel_id=1, source_target_pairs={{0,6},{2,4},{4,2},{6,0},{1,7},{3,5},{5,3},{7,1},{8,14},{10,12},{12... | collective-permute-start | bytes 26120 | tf_op jit(solution)/shard_map/ppermute | solution.py:474
  18.9 3.7 %collective-permute-start.6 = (f32[1,17,128]{2,1,0:T(8,128)S(1)}, f32[1,17,128]{2,1,0:T(8,128)S(1)}, u32[]{:S(2)}, u32[]{:S(2)}) collective-permute-start(f32[1,17,128]{2,1,0:T(8,128)S(1)} %get-tuple-element.32), channel_id=1, source_target_pairs={{0,4},{2,6},{4,0},{6,2},{1,5},{3,7},{5,1},{7,3},{8,12},{10,14},{12... | collective-permute-start | bytes 26120 | tf_op jit(solution)/shard_map/ppermute | solution.py:474
  20.2 3.7 %collective-permute-start.7 = (f32[1,17,128]{2,1,0:T(8,128)S(1)}, f32[1,17,128]{2,1,0:T(8,128)S(1)}, u32[]{:S(2)}, u32[]{:S(2)}) collective-permute-start(f32[1,17,128]{2,1,0:T(8,128)S(1)} %get-tuple-element.31), channel_id=1, source_target_pairs={{0,2},{2,0},{4,6},{6,4},{1,3},{3,1},{5,7},{7,5},{8,10},{10,8},{12,... | collective-permute-start | bytes 26120 | tf_op jit(solution)/shard_map/ppermute | solution.py:474
  23.9 4.6 %collective-permute-start.9 = (f32[17,128]{1,0:T(8,128)S(1)}, f32[17,128]{1,0:T(8,128)S(1)}, u32[]{:S(2)}, u32[]{:S(2)}) collective-permute-start(f32[17,128]{1,0:T(8,128)S(1)} %fusion.4), channel_id=1, source_target_pairs={{0,16},{8,24},{16,0},{24,8},{1,17},{9,25},{17,1},{25,9},{2,18},{10... | collective-permute-start | bytes 26120 | tf_op jit(solution)/shard_map/ppermute | solution.py:474
  24.6 5.5 %collective-permute-start.10 = (f32[17,128]{1,0:T(8,128)S(1)}, f32[17,128]{1,0:T(8,128)S(1)}, u32[]{:S(2)}, u32[]{:S(2)}) collective-permute-start(f32[17,128]{1,0:T(8,128)S(1)} %fusion.4), channel_id=1, source_target_pairs={{0,24},{8,16},{16,8},{24,0},{1,25},{9,17},{17,9},{25,1},{2,26},{10... | collective-permute-start | bytes 26120 | tf_op jit(solution)/shard_map/ppermute | solution.py:474
  26.9 3.7 %collective-permute-start.8 = (f32[17,128]{1,0:T(8,128)S(1)}, f32[17,128]{1,0:T(8,128)S(1)}, u32[]{:S(2)}, u32[]{:S(2)}) collective-permute-start(f32[17,128]{1,0:T(8,128)S(1)} %fusion.4), channel_id=1, source_target_pairs={{0,8},{8,0},{16,24},{24,16},{1,9},{9,1},{17,25},{25,17},{2,10},{10... | collective-permute-start | bytes 26120 | tf_op jit(solution)/shard_map/ppermute | solution.py:474

commit v12 on v10

--- a/solution.py
+++ b/solution.py
@@ -302,21 +302,17 @@
     ahead=None,
 ):
     blocks_x, blocks_y, _ = mass_ref.shape
-    for xe in range(blocks_x + 2):
-        if xe == 0 or xe == blocks_x + 1:
-            ref = prev_ref if xe == 0 else next_ref
-            if ref is None:
-                continue
-            store_source(nat_ref, xe * 64, blocks_y, [ref[c] for c in range(3)], ref[3])
-        elif known_ref is None:
-            columns = [pos_ref[c, xe - 1] for c in range(3)]
-            store_source(nat_ref, xe * 64, blocks_y, columns, mass_ref[xe - 1])
-        else:
-            part = pl.ds(xe * blocks_y, blocks_y)
-            src_ref[part] = known_ref[part]
-            continue
+    def table_row(xe, columns, mass):
+        store_source(nat_ref, xe * 64, blocks_y, columns, mass)
         for y in range(blocks_y):
             src_ref[xe * blocks_y + y] = nat_ref[pl.ds(xe * 64 + y, 8, stride=8), :]
+
+    for x in range(blocks_x):
+        if known_ref is None:
+            table_row(x + 1, [pos_ref[c, x] for c in range(3)], mass_ref[x])
+        else:
+            part = pl.ds((x + 1) * blocks_y, blocks_y)
+            src_ref[part] = known_ref[part]
     put_shifts(shift_ref)
     squares = square_mask()
     blocks = [(turn, y) for turn in range(x_count) for y in range(1, blocks_y - 1)]
@@ -333,6 +329,9 @@
     pair_sums(sides_of(len(blocks), 0, 1, mat_ref, near_ref, root_ref, total_ref))
     if ahead is not None:
         ahead()
+    for xe, ref in ((0, prev_ref), (blocks_x + 1, next_ref)):
+        if ref is not None:
+            table_row(xe, [ref[c] for c in range(3)], ref[3])
     words = code_ref[...]
     for number, (turn, y) in enumerate(blocks):
         x = x_first + turn * x_step

time: 31.4 us -> 31.4 us (level)
  no operation moved by 1% of the time
where the time goes in v12:
time: 31.4 us; the launch traced here: 31.2 us
  starting transfers between devices  14.4 us (46%)
  waiting for transfers between devices  7 us (22%)
  Pallas kernels  6.9 us (22%)
  other arithmetic  2.06 us (7%)
  between operations  0.79 us (3%)
    ppermute x7, starting transfers between devices, swap(): return lax.ppermute(value, axis, [(i, i ^ step) for i in range(count)])  7.16 us
    ppermute x7, waiting for transfers between devices, swap(): return lax.ppermute(value, axis, [(i, i ^ step) for i in range(count)])  6.8 us
    ppermute x2, starting transfers between devices, neighbours_of(): lax.ppermute(jnp.where(odd, high_edge, low_edge), axis, [(i, (i + 1 if i...  3.93 us
    ppermute x2, starting transfers between devices, neighbours_of(): lax.ppermute(jnp.where(odd, low_edge, high_edge), axis, [(i, i ^ 1) for i...  3.31 us
    pallas_call x1, Pallas kernels, shards(): pl.pallas_call(functools.partial(edge_kernel, listed), out_shape=(shape((...  2.33 us
    pallas_call x1, Pallas kernels, shards(): pl.pallas_call(functools.partial(middle_kernel, listed), out_shape=(shape...  2.08 us
    pallas_call x1, Pallas kernels, shards(): pl.pallas_call(functools.partial(rim_kernel, listed), out_shape=(shape(ma...  1.47 us
    pallas_call x1, Pallas kernels, shards(): pl.pallas_call(functools.partial(moments_kernel, blocks_x * dom_count, bl...  1.03 us
  transfers between devices with their start and end apart: 11, of which 8 were waited for; matrix products, arithmetic and copies ran while one was open for 2% of the time, Pallas kernels for 17%

profile of v12, /device:TPU:0, one launch (start us, length us, event | category | flops | bytes accessed | tf_op | source)
XLA Modules:
  0.0 31.2 jit_solution(5108830983157590113)
XLA Ops:
  0.6 0.0 copy-start.2
  0.6 0.8 %select_bitcast_fusion = (f32[4,8,128]{2,1,0:T(8,128)S(1)}, f32[4,1,8,128]{3,2,0,1:T(8,128)S(1)}, f32[4,1,8,128]{3,2,0,1:T(8,128)S(1)}) fusion(pred[]{:T(512)S(6)} %eq.6, f32[1,4,8,128]{3,2,0,1:T(8,128)} %bitcast.18, f32[3,4,8,128]{3,2,1,0:T(8,128)} %pos_ref.5), kind=kLoop, calls=%fused_computation.8 | loop fusion | flops 12288 | bytes 114689 | tf_op jit(solution)/shard_map/jit(_where)/select_n | solution.py:479
  1.4 3.0 %collective-permute-start.1 = (f32[4,8,128]{2,1,0:T(8,128)S(1)}, f32[4,8,128]{2,1,0:T(8,128)S(1)}, u32[]{:S(2)}, u32[]{:S(2)}) collective-permute-start(f32[4,8,128]{2,1,0:T(8,128)S(1)} %get-tuple-element.28), channel_id=1, source_target_pairs={{0,8},{8,0},{16,24},{24,16},{1,9},{9,1},{17,25},{25,17},{2,10},{10... | collective-permute-start | bytes 49160 | tf_op jit(solution)/shard_map/ppermute | solution.py:478
  4.4 0.0 copy-start.6
  4.4 0.0 copy-start
  4.5 0.0 copy-start.1
  4.5 0.0 copy-start.4
  4.5 0.0 copy-start.5
  4.5 2.5 %collective-permute-start = (f32[4,8,128]{2,1,0:T(8,128)S(1)}, f32[4,8,128]{2,1,0:T(8,128)S(1)}, u32[]{:S(2)}, u32[]{:S(2)}) collective-permute-start(f32[4,8,128]{2,1,0:T(8,128)S(1)} %select_bitcast_fusion.1), channel_id=1, source_target_pairs={{0,24},{8,16},{16,8},{24,0},{1,25},{9,17},{17,9},{25,1},{2,26},{10... | collective-permute-start | bytes 49160 | tf_op jit(solution)/shard_map/ppermute | solution.py:481
  7.0 0.0 copy-done.6
  7.0 0.0 copy-done.2
  7.0 0.0 copy-done
  7.0 0.0 copy-done.1
  7.1 0.0 copy-done.4
  7.1 0.0 copy-done.5
  7.1 0.0 copy-start.3
  7.1 2.1 %middle_pairs.1 = (f32[2,4,4,128]{3,2,1,0:T(4,128)S(1)}, f32[2,8,128]{2,1,0:T(8,128)S(1)}, f32[48,8,128]{2,1,0:T(8,128)S(1)}) custom-call(s32[4,8]{1,0:T(4,128)S(1)} %add_bitcast_fusion.code_ref, f32[3,4,8,128]{3,2,1,0:T(8,128)S(1)} %copy-done.2, f32[4,8,128]{2,1,0:T(8,128)S(1)} %copy-done, f32[4,8,128]{2,1,0:T(8,128)S(1)} %copy-done.1, ...), custom_call_target="tpu_custom_call" | custom-call | flops 4000000000 | bytes 400000 | tf_op jit(solution)/shard_map/middle_pairs/pallas_call | solution.py:535
  9.2 0.0 copy-done.3
  9.2 1.0 %moments_by_row.1 = (f32[8,16,128]{2,1,0:T(8,128)S(1)}, s32[4,8,128]{2,1,0:T(8,128)S(1)}, bf16[4,128,1024]{2,1,0:T(8,128)(2,1)S(1)}) custom-call(f32[2,8,128]{2,1,0:T(8,128)S(1)} %get-tuple-element.15.after_ref.middle_ref, f32[3,4,8,128]{3,2,1,0:T(8,128)S(1)} %copy-done.2, f32[3,4,8,128]{3,2,1,0:T(8,128)S(1)} %copy-done.3, f32[4,8,128]{2,1,0:T(8,128)S(1)} %copy-done, ...), custom_call_target="tpu_custom_call" | custom-call | flops 2000000000 | bytes 1400000 | tf_op jit(solution)/shard_map/moments_by_row/pallas_call | solution.py:551
  10.2 0.0 collective-permute-done.1
  10.2 0.0 collective-permute-done
  10.3 1.4 %collective-permute-start.3 = (f32[4,6,128]{2,1,0:T(8,128)S(1)}, f32[4,6,128]{2,1,0:T(8,128)S(1)}, u32[]{:S(2)}, u32[]{:S(2)}) collective-permute-start(f32[4,6,128]{2,1,0:T(8,128)S(1)} %get-tuple-element.38), channel_id=1, source_target_pairs={{0,7},{1,2},{2,1},{3,4},{4,3},{5,6},{6,5},{7,0},{8,15},{9,10},{10,... | collective-permute-start | bytes 36872 | tf_op jit(solution)/shard_map/ppermute | solution.py:481
  11.7 0.3 collective-permute-start.2
  12.0 2.3 %edge_pairs.1 = (f32[2,8,128]{2,1,0:T(8,128)S(1)}, f32[48,8,128]{2,1,0:T(8,128)S(1)}, bf16[8,128,48]{2,1,0:T(8,128)(2,1)S(1)}, f32[8,128,128]{2,1,0:T(8,128)S(1)}, f32[128,16]{1,0:T(8,128)S(1)}) custom-call(s32[4,8]{1,0:T(4,128)S(1)} %add_bitcast_fusion.code_ref, f32[3,4,8,128]{3,2,1,0:T(8,128)S(1)} %copy-done.2, f32[4,8,128]{2,1,0:T(8,128)S(1)} %copy-done, ...), custom_call_target="tpu_custom_call" | custom-call | flops 4000000000 | bytes 400000 | tf_op jit(solution)/shard_map/edge_pairs/pallas_call | solution.py:578
  14.3 0.2 collective-permute-done.3
  14.5 0.0 collective-permute-done.2
  14.5 1.5 %rim_pairs_and_table.1 = (f32[4,8,128]{2,1,0:T(8,128)S(1)}, f32[2,4,17,128]{3,2,1,0:T(8,128)S(1)}) custom-call(s32[4,8]{1,0:T(4,128)S(1)} %add_bitcast_fusion.code_ref, f32[2,8,128]{2,1,0:T(8,128)S(1)} %get-tuple-element.15.after_ref.middle_ref, f32[2,8,128]{2,1,0:T(8,128)S(1)} %get-tuple-element.19.edge_ref, f32[48,8,128]{2,1,0:T(8,128)S(1)} %get-tuple-element.20.known_ref, ...), custom_call_target="tpu_custom_call" | custom-call | flops 200000000 | bytes 400000 | tf_op jit(solution)/shard_map/rim_pairs_and_table/pallas_call | solution.py:602
  16.0 0.1 collective-permute-start.4
  16.1 1.2 %collective-permute-done.4 = f32[4,17,128]{2,1,0:T(8,128)S(1)} collective-permute-done((f32[4,17,128]{2,1,0:T(8,128)S(1)}, f32[4,17,128]{2,1,0:T(8,128)S(1)}, u32[]{:S(2)}, u32[]{:S(2)}) %collective-permute-start.4) | collective-permute-done | bytes 34848 | tf_op jit(solution)/shard_map/ppermute | solution.py:473
  17.3 1.5 %collective-permute-start.5 = (f32[1,17,128]{2,1,0:T(8,128)S(1)}, f32[1,17,128]{2,1,0:T(8,128)S(1)}, u32[]{:S(2)}, u32[]{:S(2)}) collective-permute-start(f32[1,17,128]{2,1,0:T(8,128)S(1)} %get-tuple-element.33), channel_id=1, source_target_pairs={{0,6},{2,4},{4,2},{6,0},{1,7},{3,5},{5,3},{7,1},{8,14},{10,12},{12... | collective-permute-start | bytes 26120 | tf_op jit(solution)/shard_map/ppermute | solution.py:473
  18.9 1.3 %collective-permute-start.6 = (f32[1,17,128]{2,1,0:T(8,128)S(1)}, f32[1,17,128]{2,1,0:T(8,128)S(1)}, u32[]{:S(2)}, u32[]{:S(2)}) collective-permute-start(f32[1,17,128]{2,1,0:T(8,128)S(1)} %get-tuple-element.32), channel_id=1, source_target_pairs={{0,4},{2,6},{4,0},{6,2},{1,5},{3,7},{5,1},{7,3},{8,12},{10,14},{12... | collective-permute-start | bytes 26120 | tf_op jit(solution)/shard_map/ppermute | solution.py:473
  20.2 0.7 %collective-permute-start.7 = (f32[1,17,128]{2,1,0:T(8,128)S(1)}, f32[1,17,128]{2,1,0:T(8,128)S(1)}, u32[]{:S(2)}, u32[]{:S(2)}) collective-permute-start(f32[1,17,128]{2,1,0:T(8,128)S(1)} %get-tuple-element.31), channel_id=1, source_target_pairs={{0,2},{2,0},{4,6},{6,4},{1,3},{3,1},{5,7},{7,5},{8,10},{10,8},{12,... | collective-permute-start | bytes 26120 | tf_op jit(solution)/shard_map/ppermute | solution.py:473
  20.9 1.1 %collective-permute-done.5 = f32[1,17,128]{2,1,0:T(8,128)S(1)} collective-permute-done((f32[1,17,128]{2,1,0:T(8,128)S(1)}, f32[1,17,128]{2,1,0:T(8,128)S(1)}, u32[]{:S(2)}, u32[]{:S(2)}) %collective-permute-start.5) | collective-permute-done | bytes 8736 | tf_op jit(solution)/shard_map/ppermute | solution.py:473
  22.0 0.6 %collective-permute-done.6 = f32[1,17,128]{2,1,0:T(8,128)S(1)} collective-permute-done((f32[1,17,128]{2,1,0:T(8,128)S(1)}, f32[1,17,128]{2,1,0:T(8,128)S(1)}, u32[]{:S(2)}, u32[]{:S(2)}) %collective-permute-start.6) | collective-permute-done | bytes 8736 | tf_op jit(solution)/shard_map/ppermute | solution.py:473
  22.5 1.3 %collective-permute-done.7 = f32[1,17,128]{2,1,0:T(8,128)S(1)} collective-permute-done((f32[1,17,128]{2,1,0:T(8,128)S(1)}, f32[1,17,128]{2,1,0:T(8,128)S(1)}, u32[]{:S(2)}, u32[]{:S(2)}) %collective-permute-start.7) | collective-permute-done | bytes 8736 | tf_op jit(solution)/shard_map/ppermute | solution.py:473
  23.9 0.7 %collective-permute-start.9 = (f32[17,128]{1,0:T(8,128)S(1)}, f32[17,128]{1,0:T(8,128)S(1)}, u32[]{:S(2)}, u32[]{:S(2)}) collective-permute-start(f32[17,128]{1,0:T(8,128)S(1)} %fusion.4), channel_id=1, source_target_pairs={{0,16},{8,24},{16,0},{24,8},{1,17},{9,25},{17,1},{25,9},{2,18},{10... | collective-permute-start | bytes 26120 | tf_op jit(solution)/shard_map/ppermute | solution.py:473
  24.6 2.3 %collective-permute-start.10 = (f32[17,128]{1,0:T(8,128)S(1)}, f32[17,128]{1,0:T(8,128)S(1)}, u32[]{:S(2)}, u32[]{:S(2)}) collective-permute-start(f32[17,128]{1,0:T(8,128)S(1)} %fusion.4), channel_id=1, source_target_pairs={{0,24},{8,16},{16,8},{24,0},{1,25},{9,17},{17,9},{25,1},{2,26},{10... | collective-permute-start | bytes 26120 | tf_op jit(solution)/shard_map/ppermute | solution.py:473
  26.9 0.4 %collective-permute-start.8 = (f32[17,128]{1,0:T(8,128)S(1)}, f32[17,128]{1,0:T(8,128)S(1)}, u32[]{:S(2)}, u32[]{:S(2)}) collective-permute-start(f32[17,128]{1,0:T(8,128)S(1)} %fusion.4), channel_id=1, source_target_pairs={{0,8},{8,0},{16,24},{24,16},{1,9},{9,1},{17,25},{25,17},{2,10},{10... | collective-permute-start | bytes 26120 | tf_op jit(solution)/shard_map/ppermute | solution.py:473
  27.3 0.6 %fusion = f32[4,8,128]{2,1,0:T(8,128)} fusion(f32[4,8,128]{2,1,0:T(8,128)S(1)} %copy-done.1, f32[4,8,128]{2,1,0:T(8,128)S(1)} %get-tuple-element.26), kind=kLoop, calls=%fused_computation.3 | loop fusion | flops 16384 | bytes 49152 | tf_op jit(solution)/shard_map/div | solution.py:625
  28.0 0.5 %collective-permute-done.9 = f32[17,128]{1,0:T(8,128)S(1)} collective-permute-done((f32[17,128]{1,0:T(8,128)S(1)}, f32[17,128]{1,0:T(8,128)S(1)}, u32[]{:S(2)}, u32[]{:S(2)}) %collective-permute-start.9) | collective-permute-done | bytes 8736 | tf_op jit(solution)/shard_map/ppermute | solution.py:473
  28.4 1.6 %collective-permute-done.10 = f32[17,128]{1,0:T(8,128)S(1)} collective-permute-done((f32[17,128]{1,0:T(8,128)S(1)}, f32[17,128]{1,0:T(8,128)S(1)}, u32[]{:S(2)}, u32[]{:S(2)}) %collective-permute-start.10) | collective-permute-done | bytes 8736 | tf_op jit(solution)/shard_map/ppermute | solution.py:473
  30.1 0.5 %collective-permute-done.8 = f32[17,128]{1,0:T(8,128)S(1)} collective-permute-done((f32[17,128]{1,0:T(8,128)S(1)}, f32[17,128]{1,0:T(8,128)S(1)}, u32[]{:S(2)}, u32[]{:S(2)}) %collective-permute-start.8) | collective-permute-done | bytes 8736 | tf_op jit(solution)/shard_map/ppermute | solution.py:473
  30.6 0.6 %add_add_fusion = f32[17,128]{1,0:T(8,128)} fusion(f32[17,128]{1,0:T(8,128)S(1)} %collective-permute-done.9, f32[17,128]{1,0:T(8,128)S(1)} %collective-permute-done.10, f32[17,128]{1,0:T(8,128)S(1)} %fusion.4, f32[17,128]{1,0:T(8,128)S(1)} %collective-permute-done.8), kind=kLoop, calls=%fused_computation.15 | loop fusion | flops 6528 | bytes 43520 | tf_op jit(solution)/shard_map/add | solution.py:491
  (11 shorter events, 0.1 us)
Async XLA Ops:
  0.6 6.4 %copy-start.2 = (f32[3,4,8,128]{3,2,1,0:T(8,128)S(1)}, f32[3,4,8,128]{3,2,1,0:T(8,128)}, u32[]{:S(2)}) copy-start(f32[3,4,8,128]{3,2,1,0:T(8,128)} %pos_ref.5) | copy-start | bytes 147460
  1.4 8.8 %collective-permute-start.1 = (f32[4,8,128]{2,1,0:T(8,128)S(1)}, f32[4,8,128]{2,1,0:T(8,128)S(1)}, u32[]{:S(2)}, u32[]{:S(2)}) collective-permute-start(f32[4,8,128]{2,1,0:T(8,128)S(1)} %get-tuple-element.28), channel_id=1, source_target_pairs={{0,8},{8,0},{16,24},{24,16},{1,9},{9,1},{17,25},{25,17},{2,10},{10... | collective-permute-start | bytes 49160 | tf_op jit(solution)/shard_map/ppermute | solution.py:478
  4.4 2.6 %copy-start.6 = (s32[4,8,5]{1,0,2:T(4,128)S(1)}, s32[4,8,5]{1,0,2:T(4,128)}, u32[]{:S(2)}) copy-start(s32[4,8,5]{1,0,2:T(4,128)} %param.11) | copy-start | bytes 1924
  4.4 2.6 %copy-start = (f32[4,8,128]{2,1,0:T(8,128)S(1)}, f32[4,8,128]{2,1,0:T(8,128)}, u32[]{:S(2)}) copy-start(f32[4,8,128]{2,1,0:T(8,128)} %mass_ref.7) | copy-start | bytes 49156
  4.5 2.6 %copy-start.1 = (f32[4,8,128]{2,1,0:T(8,128)S(1)}, f32[4,8,128]{2,1,0:T(8,128)}, u32[]{:S(2)}) copy-start(f32[4,8,128]{2,1,0:T(8,128)} %smooth_ref.5) | copy-start | bytes 49156
  4.5 2.6 %copy-start.4 = (s32[4,8,128]{2,1,0:T(8,128)S(1)}, s32[4,8,128]{2,1,0:T(8,128)}, u32[]{:S(2)}) copy-start(s32[4,8,128]{2,1,0:T(8,128)} %group_ref.3) | copy-start | bytes 49156
  4.5 2.6 %copy-start.5 = (s32[1024]{0:T(1024)S(1)}, s32[1024]{0:T(1024)}, u32[]{:S(2)}) copy-start(s32[1024]{0:T(1024)} %param.13) | copy-start | bytes 12292
  4.5 5.7 %collective-permute-start = (f32[4,8,128]{2,1,0:T(8,128)S(1)}, f32[4,8,128]{2,1,0:T(8,128)S(1)}, u32[]{:S(2)}, u32[]{:S(2)}) collective-permute-start(f32[4,8,128]{2,1,0:T(8,128)S(1)} %select_bitcast_fusion.1), channel_id=1, source_target_pairs={{0,24},{8,16},{16,8},{24,0},{1,25},{9,17},{17,9},{25,1},{2,26},{10... | collective-permute-start | bytes 49160 | tf_op jit(solution)/shard_map/ppermute | solution.py:481
  7.1 2.1 %copy-start.3 = (f32[3,4,8,128]{3,2,1,0:T(8,128)S(1)}, f32[3,4,8,128]{3,2,1,0:T(8,128)}, u32[]{:S(2)}) copy-start(f32[3,4,8,128]{3,2,1,0:T(8,128)} %vel_ref.1) | copy-start | bytes 147460
  10.3 4.2 %collective-permute-start.3 = (f32[4,6,128]{2,1,0:T(8,128)S(1)}, f32[4,6,128]{2,1,0:T(8,128)S(1)}, u32[]{:S(2)}, u32[]{:S(2)}) collective-permute-start(f32[4,6,128]{2,1,0:T(8,128)S(1)} %get-tuple-element.38), channel_id=1, source_target_pairs={{0,7},{1,2},{2,1},{3,4},{4,3},{5,6},{6,5},{7,0},{8,15},{9,10},{10,... | collective-permute-start | bytes 36872 | tf_op jit(solution)/shard_map/ppermute | solution.py:481
  11.7 2.8 %collective-permute-start.2 = (f32[4,6,128]{2,1,0:T(8,128)S(1)}, f32[4,6,128]{2,1,0:T(8,128)S(1)}, u32[]{:S(2)}, u32[]{:S(2)}) collective-permute-start(f32[4,6,128]{2,1,0:T(8,128)S(1)} %get-tuple-element.39), channel_id=1, source_target_pairs={{0,1},{1,0},{2,3},{3,2},{4,5},{5,4},{6,7},{7,6},{8,9},{9,8},{10,11... | collective-permute-start | bytes 36872 | tf_op jit(solution)/shard_map/ppermute | solution.py:478
  16.0 1.3 %collective-permute-start.4 = (f32[4,17,128]{2,1,0:T(8,128)S(1)}, f32[4,17,128]{2,1,0:T(8,128)S(1)}, u32[]{:S(2)}, u32[]{:S(2)}) collective-permute-start(f32[4,17,128]{2,1,0:T(8,128)S(1)} %slice_bitcast_fusion), channel_id=1, source_target_pairs={{0,1},{1,0},{2,3},{3,2},{4,5},{5,4},{6,7},{7,6},{8,9},{9,8},{10,11... | collective-permute-start | bytes 104456 | tf_op jit(solution)/shard_map/ppermute | solution.py:473
  17.3 4.7 %collective-permute-start.5 = (f32[1,17,128]{2,1,0:T(8,128)S(1)}, f32[1,17,128]{2,1,0:T(8,128)S(1)}, u32[]{:S(2)}, u32[]{:S(2)}) collective-permute-start(f32[1,17,128]{2,1,0:T(8,128)S(1)} %get-tuple-element.33), channel_id=1, source_target_pairs={{0,6},{2,4},{4,2},{6,0},{1,7},{3,5},{5,3},{7,1},{8,14},{10,12},{12... | collective-permute-start | bytes 26120 | tf_op jit(solution)/shard_map/ppermute | solution.py:473
  18.9 3.7 %collective-permute-start.6 = (f32[1,17,128]{2,1,0:T(8,128)S(1)}, f32[1,17,128]{2,1,0:T(8,128)S(1)}, u32[]{:S(2)}, u32[]{:S(2)}) collective-permute-start(f32[1,17,128]{2,1,0:T(8,128)S(1)} %get-tuple-element.32), channel_id=1, source_target_pairs={{0,4},{2,6},{4,0},{6,2},{1,5},{3,7},{5,1},{7,3},{8,12},{10,14},{12... | collective-permute-start | bytes 26120 | tf_op jit(solution)/shard_map/ppermute | solution.py:473
  20.2 3.7 %collective-permute-start.7 = (f32[1,17,128]{2,1,0:T(8,128)S(1)}, f32[1,17,128]{2,1,0:T(8,128)S(1)}, u32[]{:S(2)}, u32[]{:S(2)}) collective-permute-start(f32[1,17,128]{2,1,0:T(8,128)S(1)} %get-tuple-element.31), channel_id=1, source_target_pairs={{0,2},{2,0},{4,6},{6,4},{1,3},{3,1},{5,7},{7,5},{8,10},{10,8},{12,... | collective-permute-start | bytes 26120 | tf_op jit(solution)/shard_map/ppermute | solution.py:473
  23.9 4.6 %collective-permute-start.9 = (f32[17,128]{1,0:T(8,128)S(1)}, f32[17,128]{1,0:T(8,128)S(1)}, u32[]{:S(2)}, u32[]{:S(2)}) collective-permute-start(f32[17,128]{1,0:T(8,128)S(1)} %fusion.4), channel_id=1, source_target_pairs={{0,16},{8,24},{16,0},{24,8},{1,17},{9,25},{17,1},{25,9},{2,18},{10... | collective-permute-start | bytes 26120 | tf_op jit(solution)/shard_map/ppermute | solution.py:473
  24.6 5.5 %collective-permute-start.10 = (f32[17,128]{1,0:T(8,128)S(1)}, f32[17,128]{1,0:T(8,128)S(1)}, u32[]{:S(2)}, u32[]{:S(2)}) collective-permute-start(f32[17,128]{1,0:T(8,128)S(1)} %fusion.4), channel_id=1, source_target_pairs={{0,24},{8,16},{16,8},{24,0},{1,25},{9,17},{17,9},{25,1},{2,26},{10... | collective-permute-start | bytes 26120 | tf_op jit(solution)/shard_map/ppermute | solution.py:473
  26.9 3.7 %collective-permute-start.8 = (f32[17,128]{1,0:T(8,128)S(1)}, f32[17,128]{1,0:T(8,128)S(1)}, u32[]{:S(2)}, u32[]{:S(2)}) collective-permute-start(f32[17,128]{1,0:T(8,128)S(1)} %fusion.4), channel_id=1, source_target_pairs={{0,8},{8,0},{16,24},{24,16},{1,9},{9,1},{17,25},{25,17},{2,10},{10... | collective-permute-start | bytes 26120 | tf_op jit(solution)/shard_map/ppermute | solution.py:473

commit v13 on v10

--- a/solution.py
+++ b/solution.py
@@ -500,7 +500,7 @@
         part = table.shape[0] // ways
         got = [
             swap(table[k * part : (k + 1) * part], "chip", k * part)
-            for k in reversed(range(1, ways))
+            for k in sorted(range(1, ways), key=lambda step: (step == 1, step))
         ]
         table = added([table[:part]] + got)
     return table[0]

time: 31.4 us -> 31.4 us (level)
  no operation moved by 1% of the time
where the time goes in v13:
time: 31.4 us; the launch traced here: 31.2 us
  starting transfers between devices  14.4 us (46%)
  waiting for transfers between devices  7.05 us (22%)
  Pallas kernels  6.91 us (22%)
  other arithmetic  2.06 us (7%)
  between operations  0.79 us (3%)
    ppermute x7, starting transfers between devices, swap(): return lax.ppermute(value, axis, [(i, i ^ step) for i in range(count)])  7.13 us
    ppermute x7, waiting for transfers between devices, swap(): return lax.ppermute(value, axis, [(i, i ^ step) for i in range(count)])  6.82 us
    ppermute x2, starting transfers between devices, neighbours_of(): lax.ppermute(jnp.where(odd, high_edge, low_edge), axis, [(i, (i + 1 if i...  3.92 us
    ppermute x2, starting transfers between devices, neighbours_of(): lax.ppermute(jnp.where(odd, low_edge, high_edge), axis, [(i, i ^ 1) for i...  3.31 us
    pallas_call x1, Pallas kernels, shards(): pl.pallas_call(functools.partial(edge_kernel, listed), out_shape=(shape((...  2.33 us
    pallas_call x1, Pallas kernels, shards(): pl.pallas_call(functools.partial(middle_kernel, listed), out_shape=(shape...  2.08 us
    pallas_call x1, Pallas kernels, shards(): pl.pallas_call(functools.partial(rim_kernel, listed), out_shape=(shape(ma...  1.47 us
    pallas_call x1, Pallas kernels, shards(): pl.pallas_call(functools.partial(moments_kernel, blocks_x * dom_count, bl...  1.03 us
  transfers between devices with their start and end apart: 11, of which 8 were waited for; matrix products, arithmetic and copies ran while one was open for 2% of the time, Pallas kernels for 17%

profile of v13, /device:TPU:0, one launch (start us, length us, event | category | flops | bytes accessed | tf_op | source)
XLA Modules:
  0.0 31.2 jit_solution(5397122313677033263)
XLA Ops:
  0.6 0.0 copy-start.2
  0.6 0.8 %select_bitcast_fusion = (f32[4,8,128]{2,1,0:T(8,128)S(1)}, f32[4,1,8,128]{3,2,0,1:T(8,128)S(1)}, f32[4,1,8,128]{3,2,0,1:T(8,128)S(1)}) fusion(pred[]{:T(512)S(6)} %eq.6, f32[1,4,8,128]{3,2,0,1:T(8,128)} %bitcast.18, f32[3,4,8,128]{3,2,1,0:T(8,128)} %pos_ref.5), kind=kLoop, calls=%fused_computation.8 | loop fusion | flops 12288 | bytes 114689 | tf_op jit(solution)/shard_map/jit(_where)/select_n | solution.py:480
  1.4 3.0 %collective-permute-start.1 = (f32[4,8,128]{2,1,0:T(8,128)S(1)}, f32[4,8,128]{2,1,0:T(8,128)S(1)}, u32[]{:S(2)}, u32[]{:S(2)}) collective-permute-start(f32[4,8,128]{2,1,0:T(8,128)S(1)} %get-tuple-element.28), channel_id=1, source_target_pairs={{0,8},{8,0},{16,24},{24,16},{1,9},{9,1},{17,25},{25,17},{2,10},{10... | collective-permute-start | bytes 49160 | tf_op jit(solution)/shard_map/ppermute | solution.py:479
  4.4 0.0 copy-start.6
  4.4 0.0 copy-start
  4.5 0.0 copy-start.1
  4.5 0.0 copy-start.4
  4.5 0.0 copy-start.5
  4.5 2.5 %collective-permute-start = (f32[4,8,128]{2,1,0:T(8,128)S(1)}, f32[4,8,128]{2,1,0:T(8,128)S(1)}, u32[]{:S(2)}, u32[]{:S(2)}) collective-permute-start(f32[4,8,128]{2,1,0:T(8,128)S(1)} %select_bitcast_fusion.1), channel_id=1, source_target_pairs={{0,24},{8,16},{16,8},{24,0},{1,25},{9,17},{17,9},{25,1},{2,26},{10... | collective-permute-start | bytes 49160 | tf_op jit(solution)/shard_map/ppermute | solution.py:482
  7.0 0.0 copy-done.6
  7.0 0.0 copy-done.2
  7.0 0.0 copy-done
  7.0 0.0 copy-done.1
  7.1 0.0 copy-done.4
  7.1 0.0 copy-done.5
  7.1 0.0 copy-start.3
  7.1 2.1 %middle_pairs.1 = (f32[2,4,4,128]{3,2,1,0:T(4,128)S(1)}, f32[2,8,128]{2,1,0:T(8,128)S(1)}, f32[48,8,128]{2,1,0:T(8,128)S(1)}) custom-call(s32[4,8]{1,0:T(4,128)S(1)} %add_bitcast_fusion.code_ref, f32[3,4,8,128]{3,2,1,0:T(8,128)S(1)} %copy-done.2, f32[4,8,128]{2,1,0:T(8,128)S(1)} %copy-done, f32[4,8,128]{2,1,0:T(8,128)S(1)} %copy-done.1, ...), custom_call_target="tpu_custom_call" | custom-call | flops 4000000000 | bytes 400000 | tf_op jit(solution)/shard_map/middle_pairs/pallas_call | solution.py:536
  9.2 0.0 copy-done.3
  9.2 1.0 %moments_by_row.1 = (f32[8,16,128]{2,1,0:T(8,128)S(1)}, s32[4,8,128]{2,1,0:T(8,128)S(1)}, bf16[4,128,1024]{2,1,0:T(8,128)(2,1)S(1)}) custom-call(f32[2,8,128]{2,1,0:T(8,128)S(1)} %get-tuple-element.15.after_ref.middle_ref, f32[3,4,8,128]{3,2,1,0:T(8,128)S(1)} %copy-done.2, f32[3,4,8,128]{3,2,1,0:T(8,128)S(1)} %copy-done.3, f32[4,8,128]{2,1,0:T(8,128)S(1)} %copy-done, ...), custom_call_target="tpu_custom_call" | custom-call | flops 2000000000 | bytes 1400000 | tf_op jit(solution)/shard_map/moments_by_row/pallas_call | solution.py:552
  10.2 0.0 collective-permute-done.1
  10.2 0.0 collective-permute-done
  10.3 1.4 %collective-permute-start.3 = (f32[4,6,128]{2,1,0:T(8,128)S(1)}, f32[4,6,128]{2,1,0:T(8,128)S(1)}, u32[]{:S(2)}, u32[]{:S(2)}) collective-permute-start(f32[4,6,128]{2,1,0:T(8,128)S(1)} %get-tuple-element.38), channel_id=1, source_target_pairs={{0,7},{1,2},{2,1},{3,4},{4,3},{5,6},{6,5},{7,0},{8,15},{9,10},{10,... | collective-permute-start | bytes 36872 | tf_op jit(solution)/shard_map/ppermute | solution.py:482
  11.7 0.3 collective-permute-start.2
  12.0 2.3 %edge_pairs.1 = (f32[2,8,128]{2,1,0:T(8,128)S(1)}, f32[48,8,128]{2,1,0:T(8,128)S(1)}, bf16[8,128,48]{2,1,0:T(8,128)(2,1)S(1)}, f32[8,128,128]{2,1,0:T(8,128)S(1)}, f32[128,16]{1,0:T(8,128)S(1)}) custom-call(s32[4,8]{1,0:T(4,128)S(1)} %add_bitcast_fusion.code_ref, f32[3,4,8,128]{3,2,1,0:T(8,128)S(1)} %copy-done.2, f32[4,8,128]{2,1,0:T(8,128)S(1)} %copy-done, ...), custom_call_target="tpu_custom_call" | custom-call | flops 4000000000 | bytes 400000 | tf_op jit(solution)/shard_map/edge_pairs/pallas_call | solution.py:579
  14.3 0.2 collective-permute-done.3
  14.5 0.0 collective-permute-done.2
  14.5 1.5 %rim_pairs_and_table.1 = (f32[4,8,128]{2,1,0:T(8,128)S(1)}, f32[2,4,17,128]{3,2,1,0:T(8,128)S(1)}) custom-call(s32[4,8]{1,0:T(4,128)S(1)} %add_bitcast_fusion.code_ref, f32[2,8,128]{2,1,0:T(8,128)S(1)} %get-tuple-element.15.after_ref.middle_ref, f32[2,8,128]{2,1,0:T(8,128)S(1)} %get-tuple-element.19.edge_ref, f32[48,8,128]{2,1,0:T(8,128)S(1)} %get-tuple-element.20.known_ref, ...), custom_call_target="tpu_custom_call" | custom-call | flops 200000000 | bytes 400000 | tf_op jit(solution)/shard_map/rim_pairs_and_table/pallas_call | solution.py:603
  16.0 0.1 collective-permute-start.4
  16.1 1.2 %collective-permute-done.4 = f32[4,17,128]{2,1,0:T(8,128)S(1)} collective-permute-done((f32[4,17,128]{2,1,0:T(8,128)S(1)}, f32[4,17,128]{2,1,0:T(8,128)S(1)}, u32[]{:S(2)}, u32[]{:S(2)}) %collective-permute-start.4) | collective-permute-done | bytes 34848 | tf_op jit(solution)/shard_map/ppermute | solution.py:474
  17.3 1.5 %collective-permute-start.5 = (f32[1,17,128]{2,1,0:T(8,128)S(1)}, f32[1,17,128]{2,1,0:T(8,128)S(1)}, u32[]{:S(2)}, u32[]{:S(2)}) collective-permute-start(f32[1,17,128]{2,1,0:T(8,128)S(1)} %get-tuple-element.33), channel_id=1, source_target_pairs={{0,4},{2,6},{4,0},{6,2},{1,5},{3,7},{5,1},{7,3},{8,12},{10,14},{12... | collective-permute-start | bytes 26120 | tf_op jit(solution)/shard_map/ppermute | solution.py:474
  18.8 1.3 %collective-permute-start.6 = (f32[1,17,128]{2,1,0:T(8,128)S(1)}, f32[1,17,128]{2,1,0:T(8,128)S(1)}, u32[]{:S(2)}, u32[]{:S(2)}) collective-permute-start(f32[1,17,128]{2,1,0:T(8,128)S(1)} %get-tuple-element.32), channel_id=1, source_target_pairs={{0,6},{2,4},{4,2},{6,0},{1,7},{3,5},{5,3},{7,1},{8,14},{10,12},{12... | collective-permute-start | bytes 26120 | tf_op jit(solution)/shard_map/ppermute | solution.py:474
  20.2 0.7 %collective-permute-start.7 = (f32[1,17,128]{2,1,0:T(8,128)S(1)}, f32[1,17,128]{2,1,0:T(8,128)S(1)}, u32[]{:S(2)}, u32[]{:S(2)}) collective-permute-start(f32[1,17,128]{2,1,0:T(8,128)S(1)} %get-tuple-element.31), channel_id=1, source_target_pairs={{0,2},{2,0},{4,6},{6,4},{1,3},{3,1},{5,7},{7,5},{8,10},{10,8},{12,... | collective-permute-start | bytes 26120 | tf_op jit(solution)/shard_map/ppermute | solution.py:474
  20.9 0.2 collective-permute-done.5
  21.1 2.3 %collective-permute-done.6 = f32[1,17,128]{2,1,0:T(8,128)S(1)} collective-permute-done((f32[1,17,128]{2,1,0:T(8,128)S(1)}, f32[1,17,128]{2,1,0:T(8,128)S(1)}, u32[]{:S(2)}, u32[]{:S(2)}) %collective-permute-start.6) | collective-permute-done | bytes 8736 | tf_op jit(solution)/shard_map/ppermute | solution.py:474
  23.4 0.4 %collective-permute-done.7 = f32[1,17,128]{2,1,0:T(8,128)S(1)} collective-permute-done((f32[1,17,128]{2,1,0:T(8,128)S(1)}, f32[1,17,128]{2,1,0:T(8,128)S(1)}, u32[]{:S(2)}, u32[]{:S(2)}) %collective-permute-start.7) | collective-permute-done | bytes 8736 | tf_op jit(solution)/shard_map/ppermute | solution.py:474
  23.9 0.7 %collective-permute-start.9 = (f32[17,128]{1,0:T(8,128)S(1)}, f32[17,128]{1,0:T(8,128)S(1)}, u32[]{:S(2)}, u32[]{:S(2)}) collective-permute-start(f32[17,128]{1,0:T(8,128)S(1)} %fusion.4), channel_id=1, source_target_pairs={{0,16},{8,24},{16,0},{24,8},{1,17},{9,25},{17,1},{25,9},{2,18},{10... | collective-permute-start | bytes 26120 | tf_op jit(solution)/shard_map/ppermute | solution.py:474
  24.6 2.3 %collective-permute-start.10 = (f32[17,128]{1,0:T(8,128)S(1)}, f32[17,128]{1,0:T(8,128)S(1)}, u32[]{:S(2)}, u32[]{:S(2)}) collective-permute-start(f32[17,128]{1,0:T(8,128)S(1)} %fusion.4), channel_id=1, source_target_pairs={{0,24},{8,16},{16,8},{24,0},{1,25},{9,17},{17,9},{25,1},{2,26},{10... | collective-permute-start | bytes 26120 | tf_op jit(solution)/shard_map/ppermute | solution.py:474
  26.9 0.4 %collective-permute-start.8 = (f32[17,128]{1,0:T(8,128)S(1)}, f32[17,128]{1,0:T(8,128)S(1)}, u32[]{:S(2)}, u32[]{:S(2)}) collective-permute-start(f32[17,128]{1,0:T(8,128)S(1)} %fusion.4), channel_id=1, source_target_pairs={{0,8},{8,0},{16,24},{24,16},{1,9},{9,1},{17,25},{25,17},{2,10},{10... | collective-permute-start | bytes 26120 | tf_op jit(solution)/shard_map/ppermute | solution.py:474
  27.4 0.6 %fusion = f32[4,8,128]{2,1,0:T(8,128)} fusion(f32[4,8,128]{2,1,0:T(8,128)S(1)} %copy-done.1, f32[4,8,128]{2,1,0:T(8,128)S(1)} %get-tuple-element.26), kind=kLoop, calls=%fused_computation.3 | loop fusion | flops 16384 | bytes 49152 | tf_op jit(solution)/shard_map/div | solution.py:626
  28.0 0.5 %collective-permute-done.9 = f32[17,128]{1,0:T(8,128)S(1)} collective-permute-done((f32[17,128]{1,0:T(8,128)S(1)}, f32[17,128]{1,0:T(8,128)S(1)}, u32[]{:S(2)}, u32[]{:S(2)}) %collective-permute-start.9) | collective-permute-done | bytes 8736 | tf_op jit(solution)/shard_map/ppermute | solution.py:474
  28.5 1.6 %collective-permute-done.10 = f32[17,128]{1,0:T(8,128)S(1)} collective-permute-done((f32[17,128]{1,0:T(8,128)S(1)}, f32[17,128]{1,0:T(8,128)S(1)}, u32[]{:S(2)}, u32[]{:S(2)}) %collective-permute-start.10) | collective-permute-done | bytes 8736 | tf_op jit(solution)/shard_map/ppermute | solution.py:474
  30.1 0.5 %collective-permute-done.8 = f32[17,128]{1,0:T(8,128)S(1)} collective-permute-done((f32[17,128]{1,0:T(8,128)S(1)}, f32[17,128]{1,0:T(8,128)S(1)}, u32[]{:S(2)}, u32[]{:S(2)}) %collective-permute-start.8) | collective-permute-done | bytes 8736 | tf_op jit(solution)/shard_map/ppermute | solution.py:474
  30.6 0.6 %add_add_fusion = f32[17,128]{1,0:T(8,128)} fusion(f32[17,128]{1,0:T(8,128)S(1)} %collective-permute-done.9, f32[17,128]{1,0:T(8,128)S(1)} %collective-permute-done.10, f32[17,128]{1,0:T(8,128)S(1)} %fusion.4, f32[17,128]{1,0:T(8,128)S(1)} %collective-permute-done.8), kind=kLoop, calls=%fused_computation.15 | loop fusion | flops 6528 | bytes 43520 | tf_op jit(solution)/shard_map/add | solution.py:492
  (11 shorter events, 0.1 us)
Async XLA Ops:
  0.6 6.4 %copy-start.2 = (f32[3,4,8,128]{3,2,1,0:T(8,128)S(1)}, f32[3,4,8,128]{3,2,1,0:T(8,128)}, u32[]{:S(2)}) copy-start(f32[3,4,8,128]{3,2,1,0:T(8,128)} %pos_ref.5) | copy-start | bytes 147460
  1.4 8.8 %collective-permute-start.1 = (f32[4,8,128]{2,1,0:T(8,128)S(1)}, f32[4,8,128]{2,1,0:T(8,128)S(1)}, u32[]{:S(2)}, u32[]{:S(2)}) collective-permute-start(f32[4,8,128]{2,1,0:T(8,128)S(1)} %get-tuple-element.28), channel_id=1, source_target_pairs={{0,8},{8,0},{16,24},{24,16},{1,9},{9,1},{17,25},{25,17},{2,10},{10... | collective-permute-start | bytes 49160 | tf_op jit(solution)/shard_map/ppermute | solution.py:479
  4.4 2.6 %copy-start.6 = (s32[4,8,5]{1,0,2:T(4,128)S(1)}, s32[4,8,5]{1,0,2:T(4,128)}, u32[]{:S(2)}) copy-start(s32[4,8,5]{1,0,2:T(4,128)} %param.11) | copy-start | bytes 1924
  4.4 2.6 %copy-start = (f32[4,8,128]{2,1,0:T(8,128)S(1)}, f32[4,8,128]{2,1,0:T(8,128)}, u32[]{:S(2)}) copy-start(f32[4,8,128]{2,1,0:T(8,128)} %mass_ref.7) | copy-start | bytes 49156
  4.5 2.6 %copy-start.1 = (f32[4,8,128]{2,1,0:T(8,128)S(1)}, f32[4,8,128]{2,1,0:T(8,128)}, u32[]{:S(2)}) copy-start(f32[4,8,128]{2,1,0:T(8,128)} %smooth_ref.5) | copy-start | bytes 49156
  4.5 2.6 %copy-start.4 = (s32[4,8,128]{2,1,0:T(8,128)S(1)}, s32[4,8,128]{2,1,0:T(8,128)}, u32[]{:S(2)}) copy-start(s32[4,8,128]{2,1,0:T(8,128)} %group_ref.3) | copy-start | bytes 49156
  4.5 2.6 %copy-start.5 = (s32[1024]{0:T(1024)S(1)}, s32[1024]{0:T(1024)}, u32[]{:S(2)}) copy-start(s32[1024]{0:T(1024)} %param.13) | copy-start | bytes 12292
  4.5 5.7 %collective-permute-start = (f32[4,8,128]{2,1,0:T(8,128)S(1)}, f32[4,8,128]{2,1,0:T(8,128)S(1)}, u32[]{:S(2)}, u32[]{:S(2)}) collective-permute-start(f32[4,8,128]{2,1,0:T(8,128)S(1)} %select_bitcast_fusion.1), channel_id=1, source_target_pairs={{0,24},{8,16},{16,8},{24,0},{1,25},{9,17},{17,9},{25,1},{2,26},{10... | collective-permute-start | bytes 49160 | tf_op jit(solution)/shard_map/ppermute | solution.py:482
  7.1 2.1 %copy-start.3 = (f32[3,4,8,128]{3,2,1,0:T(8,128)S(1)}, f32[3,4,8,128]{3,2,1,0:T(8,128)}, u32[]{:S(2)}) copy-start(f32[3,4,8,128]{3,2,1,0:T(8,128)} %vel_ref.1) | copy-start | bytes 147460
  10.3 4.2 %collective-permute-start.3 = (f32[4,6,128]{2,1,0:T(8,128)S(1)}, f32[4,6,128]{2,1,0:T(8,128)S(1)}, u32[]{:S(2)}, u32[]{:S(2)}) collective-permute-start(f32[4,6,128]{2,1,0:T(8,128)S(1)} %get-tuple-element.38), channel_id=1, source_target_pairs={{0,7},{1,2},{2,1},{3,4},{4,3},{5,6},{6,5},{7,0},{8,15},{9,10},{10,... | collective-permute-start | bytes 36872 | tf_op jit(solution)/shard_map/ppermute | solution.py:482
  11.7 2.8 %collective-permute-start.2 = (f32[4,6,128]{2,1,0:T(8,128)S(1)}, f32[4,6,128]{2,1,0:T(8,128)S(1)}, u32[]{:S(2)}, u32[]{:S(2)}) collective-permute-start(f32[4,6,128]{2,1,0:T(8,128)S(1)} %get-tuple-element.39), channel_id=1, source_target_pairs={{0,1},{1,0},{2,3},{3,2},{4,5},{5,4},{6,7},{7,6},{8,9},{9,8},{10,11... | collective-permute-start | bytes 36872 | tf_op jit(solution)/shard_map/ppermute | solution.py:479
  16.0 1.3 %collective-permute-start.4 = (f32[4,17,128]{2,1,0:T(8,128)S(1)}, f32[4,17,128]{2,1,0:T(8,128)S(1)}, u32[]{:S(2)}, u32[]{:S(2)}) collective-permute-start(f32[4,17,128]{2,1,0:T(8,128)S(1)} %slice_bitcast_fusion), channel_id=1, source_target_pairs={{0,1},{1,0},{2,3},{3,2},{4,5},{5,4},{6,7},{7,6},{8,9},{9,8},{10,11... | collective-permute-start | bytes 104456 | tf_op jit(solution)/shard_map/ppermute | solution.py:474
  17.3 3.8 %collective-permute-start.5 = (f32[1,17,128]{2,1,0:T(8,128)S(1)}, f32[1,17,128]{2,1,0:T(8,128)S(1)}, u32[]{:S(2)}, u32[]{:S(2)}) collective-permute-start(f32[1,17,128]{2,1,0:T(8,128)S(1)} %get-tuple-element.33), channel_id=1, source_target_pairs={{0,4},{2,6},{4,0},{6,2},{1,5},{3,7},{5,1},{7,3},{8,12},{10,14},{12... | collective-permute-start | bytes 26120 | tf_op jit(solution)/shard_map/ppermute | solution.py:474
  18.8 4.6 %collective-permute-start.6 = (f32[1,17,128]{2,1,0:T(8,128)S(1)}, f32[1,17,128]{2,1,0:T(8,128)S(1)}, u32[]{:S(2)}, u32[]{:S(2)}) collective-permute-start(f32[1,17,128]{2,1,0:T(8,128)S(1)} %get-tuple-element.32), channel_id=1, source_target_pairs={{0,6},{2,4},{4,2},{6,0},{1,7},{3,5},{5,3},{7,1},{8,14},{10,12},{12... | collective-permute-start | bytes 26120 | tf_op jit(solution)/shard_map/ppermute | solution.py:474
  20.2 3.7 %collective-permute-start.7 = (f32[1,17,128]{2,1,0:T(8,128)S(1)}, f32[1,17,128]{2,1,0:T(8,128)S(1)}, u32[]{:S(2)}, u32[]{:S(2)}) collective-permute-start(f32[1,17,128]{2,1,0:T(8,128)S(1)} %get-tuple-element.31), channel_id=1, source_target_pairs={{0,2},{2,0},{4,6},{6,4},{1,3},{3,1},{5,7},{7,5},{8,10},{10,8},{12,... | collective-permute-start | bytes 26120 | tf_op jit(solution)/shard_map/ppermute | solution.py:474
  23.9 4.6 %collective-permute-start.9 = (f32[17,128]{1,0:T(8,128)S(1)}, f32[17,128]{1,0:T(8,128)S(1)}, u32[]{:S(2)}, u32[]{:S(2)}) collective-permute-start(f32[17,128]{1,0:T(8,128)S(1)} %fusion.4), channel_id=1, source_target_pairs={{0,16},{8,24},{16,0},{24,8},{1,17},{9,25},{17,1},{25,9},{2,18},{10... | collective-permute-start | bytes 26120 | tf_op jit(solution)/shard_map/ppermute | solution.py:474
  24.6 5.5 %collective-permute-start.10 = (f32[17,128]{1,0:T(8,128)S(1)}, f32[17,128]{1,0:T(8,128)S(1)}, u32[]{:S(2)}, u32[]{:S(2)}) collective-permute-start(f32[17,128]{1,0:T(8,128)S(1)} %fusion.4), channel_id=1, source_target_pairs={{0,24},{8,16},{16,8},{24,0},{1,25},{9,17},{17,9},{25,1},{2,26},{10... | collective-permute-start | bytes 26120 | tf_op jit(solution)/shard_map/ppermute | solution.py:474
  26.9 3.7 %collective-permute-start.8 = (f32[17,128]{1,0:T(8,128)S(1)}, f32[17,128]{1,0:T(8,128)S(1)}, u32[]{:S(2)}, u32[]{:S(2)}) collective-permute-start(f32[17,128]{1,0:T(8,128)S(1)} %fusion.4), channel_id=1, source_target_pairs={{0,8},{8,0},{16,24},{24,16},{1,9},{9,1},{17,25},{25,17},{2,10},{10... | collective-permute-start | bytes 26120 | tf_op jit(solution)/shard_map/ppermute | solution.py:474
